TPU v7x, 32 devices: a whole 2x2x4 slice. The times are simulated.
32 devices in a mesh: wide: 8 (over z, x), narrow: 4 (over y, core).
Axes of the slice: x: 2, y: 2, z: 4, core: 2. Of those that a mesh axis runs over, the one named last changes fastest.
Arguments:
- tokens: bfloat16 [65536, 1024], P(('wide', 'narrow')), may hold values from -64 to 64
- slot_params: bfloat16 [1024, 128], replicated, may hold values from -2.5 to 2.5
- expert_in: bfloat16 [32, 1024, 4096], P('wide', None, 'narrow'), may hold values from -0.1875 to 0.1875
- expert_out: bfloat16 [32, 4096, 1024], P('wide', 'narrow'), may hold values from -0.09375 to 0.09375
Outputs:
- mixed: bfloat16 [65536, 1024], P(('wide', 'narrow'))
All inputs are finite; a program needn't handle non-finite values.
Results may differ from a plain program's by a relative error of at most 0.0071.
Values may be sent and summed in bfloat16 or wider, within the bound.
No kernel may reach another device: no remote copies, remote signals or barrier semaphores. Data moves between devices by JAX's collectives and lax.ppermute only.
A program may use at most 128 MiB of HBM per device.

v0:
```python
import jax
import jax.numpy as jnp
from jax import lax
from jax.sharding import PartitionSpec as P

SLOT_PER = 4


def divide_rows(summed, slot_totals):
    return (summed / slot_totals[:, None]).astype(jnp.bfloat16)


def shards(tokens, slot_params, expert_in, expert_out):
    logits = jnp.dot(tokens, slot_params, preferred_element_type=jnp.float32)
    local_peak = jnp.max(logits, axis=0)
    column_peak = lax.pmax(local_peak, ("wide", "narrow"))
    weights = jnp.exp(logits - column_peak)
    slot_totals = lax.psum(jnp.sum(weights, axis=0), ("wide", "narrow"))
    dispatch = weights.astype(jnp.bfloat16)
    slot_count = slot_params.shape[1]
    row_count = slot_count // lax.axis_size("wide")
    columns = dispatch
    partial_value = lax.psum_scatter(
        lax.dot_general(
            columns, tokens, (((0,), (0,)), ((), ())), preferred_element_type=jnp.float32
        ),
        "wide",
        scatter_dimension=0,
        tiled=True,
    )
    summed = lax.psum(partial_value, "narrow")
    owned_totals = lax.dynamic_slice_in_dim(
        slot_totals, lax.axis_index("wide") * row_count, row_count
    )
    slot_in = divide_rows(summed, owned_totals)
    slot_stack = slot_in.reshape(expert_in.shape[0], SLOT_PER, slot_in.shape[1])
    hidden = jax.nn.gelu(
        jnp.einsum("esd,edh->esh", slot_stack, expert_in, preferred_element_type=jnp.float32)
    ).astype(jnp.bfloat16)
    expert_sum = jnp.einsum("esh,ehd->esd", hidden, expert_out, preferred_element_type=jnp.float32)
    expert_sum = expert_sum.reshape(-1, expert_sum.shape[2])
    mixing = jax.nn.softmax(logits, axis=1).astype(jnp.bfloat16)
    whole_rows = lax.psum(expert_sum, "narrow").astype(jnp.bfloat16)
    columns = mixing
    mixed = jnp.dot(
        columns,
        lax.all_gather(whole_rows, "wide", axis=0, tiled=True),
        preferred_element_type=jnp.float32,
    )
    return mixed.astype(jnp.bfloat16)


def solution(mesh):
    return jax.shard_map(
        shards,
        mesh=mesh,
        in_specs=(
            P(("wide", "narrow"), None),
            P(),
            P("wide", None, "narrow"),
            P("wide", "narrow", None),
        ),
        out_specs=P(("wide", "narrow"), None),
        check_vma=False,
    )
```

profile of v0, /device:TPU:0, one launch (start us, length us, event | category | flops | bytes accessed | tf_op | source)
XLA Modules:
  0.0 220.3 jit_solution(17958340659097253474)
XLA Ops:
  6.5 0.0 copy-start
  6.5 0.0 reduce-scatter.2.cloned.1.call-start
  6.5 0.9 copy-done
  7.5 3.5 %fusion.26 = (f32[2048]{0:T(1024)S(1)}, f32[128]{0:T(128)S(1)}, f32[2048,128]{1,0:T(8,128)S(1)}) fusion(bf16[2048,1024]{1,0:T(8,128)(2,1)} %param.4, bf16[1024,128]{1,0:T(8,128)(2,1)S(1)} %copy-done), kind=kOutput, calls=%fused_computation.30 | convolution fusion | flops 537393024 | bytes 5513728 | tf_op jit(solution)/shard_map/dot_general | solution.py:14
  11.0 41.9 %pmax.7 = f32[128]{0:T(128)S(1)} all-reduce(f32[128]{0:T(128)S(1)} %get-tuple-element.8), channel_id=1, replica_groups=mesh['wide'=8,'narrow'=4] {'wide','narrow'}, use_global_device_ids=true, to_apply=%region_3.0 | all-reduce | flops 128 | bytes 1024 | tf_op jit(solution)/shard_map/pmax | solution.py:16
  52.9 3.7 %fusion.3 = f32[128,1024]{1,0:T(8,128)} fusion(bf16[2048,1024]{1,0:T(8,128)(2,1)} %param.4, f32[2048,128]{1,0:T(8,128)S(1)} %get-tuple-element.9, f32[128]{0:T(128)S(1)} %pmax.7), kind=kOutput, calls=%fused_computation.7 | convolution fusion | flops 537395200 | bytes 5767680 | tf_op jit(solution)/shard_map/dot_general | solution.py:24
  56.7 0.0 reduce-scatter.2.cloned.1.call-update
  56.7 0.0 all-reduce.2.cloned.1.call-start
  56.8 62.4 %reduce-scatter.2.cloned.1.call-done = f32[16,1024]{1,0:T(8,128)} async-done(((f32[128,1024]{1,0:T(8,128)}), f32[16,1024]{1,0:T(8,128)}) %reduce-scatter.2.cloned.1.call-update) | async-done | bytes 65552 | tf_op jit(solution)/shard_map/reduce_scatter | solution.py:23
  119.2 0.0 all-reduce.2.cloned.1.call-update
  119.2 0.6 fusion
  119.8 40.1 %psum.22 = f32[128]{0:T(128)S(1)} all-reduce(f32[128]{0:T(128)S(1)} %get-tuple-element.6), channel_id=1, replica_groups=mesh['wide'=8,'narrow'=4] {'wide','narrow'}, use_global_device_ids=true, to_apply=%region_7.0 | all-reduce | flops 128 | bytes 1024 | tf_op jit(solution)/shard_map/psum | solution.py:18
  159.9 0.1 dynamic_slice.3
  160.0 0.0 all-reduce.2.cloned.1.call-done
  160.0 0.9 divide_convert_fusion.2
  161.0 8.0 %fusion.16 = f32[4,4,1024]{2,1,0:T(4,128)S(1)} fusion(bf16[4,1024,1024]{2,1,0:T(8,128)(2,1)} %param.7, bf16[4,4,1024]{2,1,0:T(4,128)(2,1)S(1)} %reshape.10, bf16[4,1024,1024]{2,1,0:T(8,128)(2,1)} %param.6), kind=kOutput, calls=%fused_computation.21 | convolution fusion | flops 67256320 | bytes 16875520 | tf_op jit(solution)/shard_map/esh,ehd->esd/dot_general | solution.py:40
  169.0 10.7 %psum.23 = bf16[16,1024]{1,0:T(8,128)(2,1)S(1)} all-reduce(f32[16,1024]{1,0:T(8,128)S(1)} %reshape.11), channel_id=1, replica_groups=mesh['wide'=8,'narrow'=4] {'narrow'}, use_global_device_ids=true, to_apply=%region_8.0 | all-reduce | flops 16384 | bytes 98304 | tf_op jit(solution)/shard_map/psum | solution.py:43
  179.7 30.8 %all_gather.3 = bf16[128,1024]{1,0:T(8,128)(2,1)S(1)} all-gather(bf16[16,1024]{1,0:T(8,128)(2,1)S(1)} %psum.23), channel_id=1, replica_groups=mesh['wide'=8,'narrow'=4] {'wide'}, dimensions={0}, use_global_device_ids=true | all-gather | bytes 294912 | tf_op jit(solution)/shard_map/all_gather | solution.py:47
  210.6 2.9 %convolution_convert_fusion = bf16[2048,1024]{1,0:T(8,128)(2,1)} fusion(bf16[128,1024]{1,0:T(8,128)(2,1)S(1)} %all_gather.3, f32[2048,128]{1,0:T(8,128)S(1)} %get-tuple-element.9, f32[2048]{0:T(1024)S(1)} %get-tuple-element.5, f32[2048]{0:T(1024)S(1)} %get-tuple-element.7), kind=kOutput, calls=%fused_computation | convolution fusion | flops 539754496 | bytes 5521408 | tf_op jit(solution)/shard_map/dot_general | solution.py:45
  (2 shorter events, 0.1 us)
Async XLA Ops:
  6.5 1.0 copy-start
  6.5 112.6 %reduce-scatter.2.cloned.1.call-start = ((), (), s32[]{:S(2)}) async-start(), calls=%async_computation.1 | async-start | bytes 589824 | tf_op jit(solution)/shard_map/reduce_scatter | solution.py:23
  56.7 103.3 %all-reduce.2.cloned.1.call-start = ((), (), s32[]{:S(2)}) async-start(), calls=%async_computation.2 | async-start | bytes 131072 | tf_op jit(solution)/shard_map/psum | solution.py:31
Sparse Core Ops, SparseCore 0:
  56.8 62.2 reduce-scatter.1
  121.6 30.0 all-reduce.1
where the time goes:
time: 221 us; the launch traced here: 220 us
  blocking collectives  124 us (56%)
  waiting for transfers between devices  62.4 us (28%)
  matrix products  18.2 us (8%)
  between operations  13.4 us (6%)
    reduce_scatter x1, waiting for transfers between devices, shards(): lax.psum_scatter(lax.dot_general(columns, tokens, (((0,), (0,)), ((), ())...  62.4 us
    pmax x1, blocking collectives, shards(): column_peak = lax.pmax(local_peak, ('wide', 'narrow'))  41.9 us
    psum x1, blocking collectives, shards(): slot_totals = lax.psum(jnp.sum(weights, axis=0), ('wide', 'narrow'))  40.1 us
    all_gather x1, blocking collectives, shards(): lax.all_gather(whole_rows, 'wide', axis=0, tiled=True)  30.8 us
    psum x1, blocking collectives, shards(): whole_rows = lax.psum(expert_sum, 'narrow').astype(jnp.bfloat16)  10.7 us
    dot_general x1, matrix products, shards(): jnp.einsum('esh,ehd->esd', hidden, expert_out, preferred_element_type=jnp...  8.04 us
  transfers between devices with their start and end apart: 2, of which 1 were waited for; matrix products, arithmetic and copies ran while one was open for 0% of the time, Pallas kernels for 0%

commit v1 on v0

v1 whole, which is shorter than its diff:
```python
import jax
import jax.numpy as jnp
from jax import lax
from jax.sharding import PartitionSpec as P

SLOT_PER = 4
SIDE = 128


def pieces(value):
    high = lax.reduce_precision(value, 8, 7)
    rest = value - high
    middle = lax.reduce_precision(rest, 8, 7)
    return [high, middle, rest - middle]


def pack(mean, peak, total):
    columns = jnp.stack(pieces(peak) + pieces(total), axis=-1)
    side = jnp.pad(columns, ((0, 0), (0, SIDE - columns.shape[1])))
    return jnp.concatenate([mean, side], axis=1).astype(jnp.bfloat16)


def combine_parts(parts):
    width = parts.shape[2] - SIDE
    wide_parts = parts.astype(jnp.float32)
    side = wide_parts[:, :, width:]
    peaks = side[:, :, 0] + side[:, :, 1] + side[:, :, 2]
    totals = side[:, :, 3] + side[:, :, 4] + side[:, :, 5]
    peak = jnp.max(peaks, axis=0)
    shares = totals * jnp.exp(peaks - peak)
    total = jnp.sum(shares, axis=0)
    mean = jnp.sum(wide_parts[:, :, :width] * (shares / total)[:, :, None], axis=0)
    return mean, peak, total


def rotations(value, axis):
    size = lax.axis_size(axis)
    return [
        lax.ppermute(value, axis, [(i, (i + step) % size) for i in range(size)])
        for step in range(1, size)
    ]


def shards(tokens, slot_params, expert_in, expert_out):
    wide = lax.axis_size("wide")
    logits = jnp.dot(tokens, slot_params, preferred_element_type=jnp.float32)
    peak = jnp.max(logits, axis=0)
    weights = jnp.exp(logits - peak)
    total = jnp.sum(weights, axis=0)
    sums = lax.dot_general(
        weights.astype(jnp.bfloat16), tokens, (((0,), (0,)), ((), ())), preferred_element_type=jnp.float32
    )
    packed = pack(sums / total[:, None], peak, total)
    rows = packed.shape[0] // wide
    received = lax.all_to_all(packed, "wide", split_axis=0, concat_axis=0, tiled=True)
    packed = pack(*combine_parts(received.reshape(wide, rows, -1)))
    slot_in, _, _ = combine_parts(jnp.stack([packed] + rotations(packed, "narrow")))
    slot_in = slot_in.astype(jnp.bfloat16)
    slot_stack = slot_in.reshape(expert_in.shape[0], SLOT_PER, slot_in.shape[1])
    hidden = jax.nn.gelu(
        jnp.einsum("esd,edh->esh", slot_stack, expert_in, preferred_element_type=jnp.float32)
    ).astype(jnp.bfloat16)
    partial = jnp.einsum("esh,ehd->esd", hidden, expert_out, preferred_element_type=jnp.float32)
    partial = partial.reshape(rows, -1)
    others = rotations(partial.astype(jnp.bfloat16), "narrow")
    owned = (partial + sum(other.astype(jnp.float32) for other in others)).astype(jnp.bfloat16)
    blocks = jnp.stack([owned] + rotations(owned, "wide"))
    order = (lax.axis_index("wide") - jnp.arange(wide)) % wide
    slot_out = jnp.take(blocks, order, axis=0).reshape(wide * rows, -1)
    mixing = jax.nn.softmax(logits, axis=1).astype(jnp.bfloat16)
    mixed = jnp.dot(mixing, slot_out, preferred_element_type=jnp.float32)
    return mixed.astype(jnp.bfloat16)


def solution(mesh):
    return jax.shard_map(
        shards,
        mesh=mesh,
        in_specs=(
            P(("wide", "narrow"), None),
            P(),
            P("wide", None, "narrow"),
            P("wide", "narrow", None),
        ),
        out_specs=P(("wide", "narrow"), None),
        check_vma=False,
    )
```

time: 221 us -> 65.3 us (0.30)
  blocking collectives: 124 us -> 0 us
  waiting for transfers between devices: 62.4 us -> 15.3 us
  starting transfers between devices: 0.04 us -> 23.6 us
  between operations: 13.4 us -> 0.17 us
  local copies, waits for them, and re-layouts: 1.07 us -> 4.91 us
  other arithmetic: 1.55 us -> 5.38 us
  matrix products: 18.2 us -> 15.6 us
    reduce_scatter x1 -> x0, waiting for transfers between devices: 62.4 us -> none  [shards(): lax.psum_scatter(lax.dot_general(columns, tokens, (((0,), (0,)), ((), ())...]
    psum x2 -> x0, blocking collectives: 50.8 us -> none  [the longest x1 40.1 us: shards(): slot_totals = lax.psum(jnp.sum(weights, axis=0), ('wide', 'narrow'))]
    pmax x1 -> x0, blocking collectives: 41.9 us -> none  [shards(): column_peak = lax.pmax(local_peak, ('wide', 'narrow'))]
    all_gather x1 -> x0, blocking collectives: 30.8 us -> none  [shards(): lax.all_gather(whole_rows, 'wide', axis=0, tiled=True)]
    ppermute x0 -> x13, starting transfers between devices: none -> 16.3 us  [rotations(): lax.ppermute(value, axis, [(i, (i + step) % size) for i in range(size)])]
    all_to_all x0 -> x1, waiting for transfers between devices: none -> 9.64 us  [shards(): lax.all_to_all(packed, 'wide', split_axis=0, concat_axis=0, tiled=True)]
    all_to_all x0 -> x1, starting transfers between devices: none -> 7.25 us  [shards(): lax.all_to_all(packed, 'wide', split_axis=0, concat_axis=0, tiled=True)]
    ppermute x0 -> x13, waiting for transfers between devices: none -> 5.69 us  [rotations(): lax.ppermute(value, axis, [(i, (i + step) % size) for i in range(size)])]
  transfers between devices with their start and end apart: 2 -> 14, of which waited for: 1 -> 9; matrix products, arithmetic and copies ran while one was open for 0% -> 1% of each run, Pallas kernels for 0% -> 0%
where the time goes in v1:
time: 65.3 us; the launch traced here: 65 us
  starting transfers between devices  23.6 us (36%)
  matrix products  15.6 us (24%)
  waiting for transfers between devices  15.3 us (23%)
  other arithmetic  5.38 us (8%)
  local copies, waits for them, and re-layouts  4.91 us (8%)
    ppermute x13, starting transfers between devices, rotations(): lax.ppermute(value, axis, [(i, (i + step) % size) for i in range(size)])  16.3 us
    all_to_all x1, waiting for transfers between devices, shards(): lax.all_to_all(packed, 'wide', split_axis=0, concat_axis=0, tiled=True)  9.64 us
    dot_general x1, matrix products, shards(): jnp.einsum('esh,ehd->esd', hidden, expert_out, preferred_element_type=jnp...  8.04 us
    all_to_all x1, starting transfers between devices, shards(): lax.all_to_all(packed, 'wide', split_axis=0, concat_axis=0, tiled=True)  7.25 us
    ppermute x13, waiting for transfers between devices, rotations(): lax.ppermute(value, axis, [(i, (i + step) % size) for i in range(size)])  5.69 us
    dot_general x1, matrix products, shards(): logits = jnp.dot(tokens, slot_params, preferred_element_type=jnp.float32)  3.89 us
    dot_general x1, matrix products, shards(): mixed = jnp.dot(mixing, slot_out, preferred_element_type=jnp.float32)  2.9 us
    all_to_all x1, local copies, waits for them, and re-layouts, shards(): lax.all_to_all(packed, 'wide', split_axis=0, concat_axis=0, tiled=True)  2.59 us
  transfers between devices with their start and end apart: 14, of which 9 were waited for; matrix products, arithmetic and copies ran while one was open for 1% of the time, Pallas kernels for 0%

profile of v1, /device:TPU:0, one launch (start us, length us, event | category | flops | bytes accessed | tf_op | source)
XLA Modules:
  0.0 65.0 jit_solution(15129308496913667755)
XLA Ops:
  0.0 0.9 %copy-done = bf16[1024,128]{1,0:T(8,128)(2,1)S(1)} copy-done((bf16[1024,128]{1,0:T(8,128)(2,1)S(1)}, bf16[1024,128]{1,0:T(8,128)(2,1)}, u32[]{:S(2)}) %copy-start) | copy-done | bytes 262168
  1.0 3.9 %fusion.43 = (f32[2048]{0:T(1024)S(1)}, f32[128]{0:T(128)S(1)}, f32[2048,128]{1,0:T(8,128)S(1)}) fusion(bf16[2048,1024]{1,0:T(8,128)(2,1)} %param.4, bf16[1024,128]{1,0:T(8,128)(2,1)S(1)} %copy-done), kind=kOutput, calls=%fused_computation.101 | convolution fusion | flops 537393024 | bytes 5513728 | tf_op jit(solution)/shard_map/dot_general | solution.py:46
  4.8 0.6 fusion.2
  5.5 0.8 %fusion.1 = bf16[128,1024]{1,0:T(8,128)(2,1)S(1)} fusion(bf16[2048,1024]{1,0:T(8,128)(2,1)S(1)} %copy-done.1, f32[2048,128]{1,0:T(8,128)S(1)} %get-tuple-element.34, f32[128]{0:T(128)S(1)} %get-tuple-element.8, f32[128]{0:T(128)S(1)} %get-tuple-element.6), kind=kOutput, calls=%fused_computation.5 | convolution fusion | flops 537657344 | bytes 5506048 | tf_op jit(solution)/shard_map/dot_general | solution.py:50
  6.5 0.7 %pad_maximum_fusion = bf16[8,16,1152]{2,1,0:T(8,128)(2,1)} fusion(bf16[8,16,128]{2,1,0:T(8,128)(2,1)S(1)} %bitcast.98, bf16[8,16,1024]{2,1,0:T(8,128)(2,1)S(1)} %bitcast.88), kind=kLoop, calls=%fused_computation.15 | loop fusion | flops 589824 | bytes 589824 | tf_op jit(solution)/shard_map/concatenate | solution.py:20
  7.2 7.3 %all-to-all-start = ((bf16[8,16,1152]{2,1,0:T(8,128)(2,1)}), bf16[8,16,1152]{2,1,0:T(8,128)(2,1)S(1)}, u32[]{:S(2)}, u32[]{:S(2)}) async-start(bf16[8,16,1152]{2,1,0:T(8,128)(2,1)} %pad_maximum_fusion), calls=%async_computation | async-start | bytes 589824 | tf_op jit(solution)/shard_map/all_to_all | solution.py:55
  14.5 9.6 %all-to-all-done = bf16[8,16,1152]{2,1,0:T(8,128)(2,1)S(1)} async-done(((bf16[8,16,1152]{2,1,0:T(8,128)(2,1)}), bf16[8,16,1152]{2,1,0:T(8,128)(2,1)S(1)}, u32[]{:S(2)}, u32[]{:S(2)}) %all-to-all-start) | async-done | bytes 294944 | tf_op jit(solution)/shard_map/all_to_all | solution.py:55
  24.1 2.6 %copy.40 = bf16[8,16,1152]{1,0,2:T(8,128)(2,1)} copy(bf16[8,16,1152]{2,1,0:T(8,128)(2,1)S(1)} %all-to-all-done) | data formatting | bytes 589824 | tf_op jit(solution)/shard_map/all_to_all | solution.py:55
  26.7 1.8 %convert_element_type.56 = f32[8,16,1152]{1,0,2:T(8,128)S(1)} convert(bf16[8,16,1152]{1,0,2:T(8,128)(2,1)} %copy.40) | non-fusion elementwise | flops 147456 | bytes 884736 | tf_op jit(solution)/shard_map/convert_element_type | solution.py:25
  28.6 1.3 %fusion = bf16[16,1024]{0,1:T(8,128)(2,1)S(1)} fusion(f32[8,16,1152]{1,0,2:T(8,128)S(1)} %convert_element_type.56, f32[8,16]{1,0:T(8,128)S(1)} %divide_bitcast_fusion), kind=kLoop, calls=%fused_computation.2 | loop fusion | flops 245760 | bytes 557568 | tf_op jit(solution)/shard_map/reduce_sum | solution.py:32
  30.1 1.6 %collective-permute-start.1 = (bf16[16,1152]{1,0:T(8,128)(2,1)S(1)}, bf16[16,1152]{1,0:T(8,128)(2,1)S(1)}, u32[]{:S(2)}, u32[]{:S(2)}) collective-permute-start(bf16[16,1152]{1,0:T(8,128)(2,1)S(1)} %pad_maximum_fusion.1), channel_id=1, source_target_pairs={{0,2},{1,3},{2,0},{3,1},{4,6},{5,7},{6,4},{7,5},{8,10},{9,11},{10,... | collective-permute-start | bytes 110600 | tf_op jit(solution)/shard_map/ppermute | solution.py:39
  31.7 1.4 %collective-permute-start.2 = (bf16[16,1152]{1,0:T(8,128)(2,1)S(1)}, bf16[16,1152]{1,0:T(8,128)(2,1)S(1)}, u32[]{:S(2)}, u32[]{:S(2)}) collective-permute-start(bf16[16,1152]{1,0:T(8,128)(2,1)S(1)} %pad_maximum_fusion.1), channel_id=1, source_target_pairs={{0,3},{1,0},{2,1},{3,2},{4,7},{5,4},{6,5},{7,6},{8,11},{9,8},{10,9... | collective-permute-start | bytes 110600 | tf_op jit(solution)/shard_map/ppermute | solution.py:39
  33.5 0.7 %collective-permute-done.1 = bf16[16,1152]{1,0:T(8,128)(2,1)S(1)} collective-permute-done((bf16[16,1152]{1,0:T(8,128)(2,1)S(1)}, bf16[16,1152]{1,0:T(8,128)(2,1)S(1)}, u32[]{:S(2)}, u32[]{:S(2)}) %collective-permute-start.1) | collective-permute-done | bytes 36896 | tf_op jit(solution)/shard_map/ppermute | solution.py:39
  34.2 0.6 collective-permute-done.2
  34.9 0.2 fusion.44
  35.5 8.0 %fusion.18 = f32[4,4,1024]{2,1,0:T(4,128)S(1)} fusion(bf16[4,1024,1024]{2,1,0:T(8,128)(2,1)} %param.7, bf16[4,4,1024]{2,1,0:T(4,128)(2,1)S(1)} %convert_element_type.59, bf16[4,1024,1024]{2,1,0:T(8,128)(2,1)} %param.6), kind=kOutput, calls=%fused_computation.32 | convolution fusion | flops 67256320 | bytes 16875520 | tf_op jit(solution)/shard_map/esh,ehd->esd/dot_general | solution.py:63
  43.6 0.7 %collective-permute-start.3 = (bf16[16,1024]{1,0:T(8,128)(2,1)S(1)}, bf16[16,1024]{1,0:T(8,128)(2,1)S(1)}, u32[]{:S(2)}, u32[]{:S(2)}) collective-permute-start(bf16[16,1024]{1,0:T(8,128)(2,1)S(1)} %convert_element_type.61), channel_id=1, source_target_pairs={{0,1},{1,2},{2,3},{3,0},{4,5},{5,6},{6,7},{7,4},{8,9},{9,10},{10,1... | collective-permute-start | bytes 98312 | tf_op jit(solution)/shard_map/ppermute | solution.py:39
  44.3 1.5 %collective-permute-start.4 = (bf16[16,1024]{1,0:T(8,128)(2,1)S(1)}, bf16[16,1024]{1,0:T(8,128)(2,1)S(1)}, u32[]{:S(2)}, u32[]{:S(2)}) collective-permute-start(bf16[16,1024]{1,0:T(8,128)(2,1)S(1)} %convert_element_type.61), channel_id=1, source_target_pairs={{0,2},{1,3},{2,0},{3,1},{4,6},{5,7},{6,4},{7,5},{8,10},{9,11},{10,... | collective-permute-start | bytes 98312 | tf_op jit(solution)/shard_map/ppermute | solution.py:39
  45.8 0.4 collective-permute-start.5
  46.2 0.8 %collective-permute-done.3 = bf16[16,1024]{1,0:T(8,128)(2,1)S(1)} collective-permute-done((bf16[16,1024]{1,0:T(8,128)(2,1)S(1)}, bf16[16,1024]{1,0:T(8,128)(2,1)S(1)}, u32[]{:S(2)}, u32[]{:S(2)}) %collective-permute-start.3) | collective-permute-done | bytes 32800 | tf_op jit(solution)/shard_map/ppermute | solution.py:39
  47.0 1.2 %collective-permute-done.4 = bf16[16,1024]{1,0:T(8,128)(2,1)S(1)} collective-permute-done((bf16[16,1024]{1,0:T(8,128)(2,1)S(1)}, bf16[16,1024]{1,0:T(8,128)(2,1)S(1)}, u32[]{:S(2)}, u32[]{:S(2)}) %collective-permute-start.4) | collective-permute-done | bytes 32800 | tf_op jit(solution)/shard_map/ppermute | solution.py:39
  48.2 1.5 %collective-permute-start.6 = (bf16[16,1024]{1,0:T(8,128)(2,1)S(1)}, bf16[16,1024]{1,0:T(8,128)(2,1)S(1)}, u32[]{:S(2)}, u32[]{:S(2)}) collective-permute-start(bf16[16,1024]{1,0:T(8,128)(2,1)S(1)} %get-tuple-element.12), channel_id=1, source_target_pairs={{0,4},{4,8},{8,12},{12,16},{16,20},{20,24},{24,28},{28,0},{1,5},{5... | collective-permute-start | bytes 98312 | tf_op jit(solution)/shard_map/ppermute | solution.py:39
  49.9 1.7 %collective-permute-start.8 = (bf16[16,1024]{1,0:T(8,128)(2,1)S(1)}, bf16[16,1024]{1,0:T(8,128)(2,1)S(1)}, u32[]{:S(2)}, u32[]{:S(2)}) collective-permute-start(bf16[16,1024]{1,0:T(8,128)(2,1)S(1)} %get-tuple-element.12), channel_id=1, source_target_pairs={{0,12},{4,16},{8,20},{12,24},{16,28},{20,0},{24,4},{28,8},{1,13},{... | collective-permute-start | bytes 98312 | tf_op jit(solution)/shard_map/ppermute | solution.py:39
  51.6 3.1 %collective-permute-start.9 = (bf16[16,1024]{1,0:T(8,128)(2,1)S(1)}, bf16[16,1024]{1,0:T(8,128)(2,1)S(1)}, u32[]{:S(2)}, u32[]{:S(2)}) collective-permute-start(bf16[16,1024]{1,0:T(8,128)(2,1)S(1)} %get-tuple-element.12), channel_id=1, source_target_pairs={{0,16},{4,20},{8,24},{12,28},{16,0},{20,4},{24,8},{28,12},{1,17},{... | collective-permute-start | bytes 98312 | tf_op jit(solution)/shard_map/ppermute | solution.py:39
  54.8 1.0 %collective-permute-start.10 = (bf16[16,1024]{1,0:T(8,128)(2,1)S(1)}, bf16[16,1024]{1,0:T(8,128)(2,1)S(1)}, u32[]{:S(2)}, u32[]{:S(2)}) collective-permute-start(bf16[16,1024]{1,0:T(8,128)(2,1)S(1)} %get-tuple-element.12), channel_id=1, source_target_pairs={{0,20},{4,24},{8,28},{12,0},{16,4},{20,8},{24,12},{28,16},{1,21},{... | collective-permute-start | bytes 98312 | tf_op jit(solution)/shard_map/ppermute | solution.py:39
  55.7 1.8 %collective-permute-start.11 = (bf16[16,1024]{1,0:T(8,128)(2,1)S(1)}, bf16[16,1024]{1,0:T(8,128)(2,1)S(1)}, u32[]{:S(2)}, u32[]{:S(2)}) collective-permute-start(bf16[16,1024]{1,0:T(8,128)(2,1)S(1)} %get-tuple-element.12), channel_id=1, source_target_pairs={{0,24},{4,28},{8,0},{12,4},{16,8},{20,12},{24,16},{28,20},{1,25},{... | collective-permute-start | bytes 98312 | tf_op jit(solution)/shard_map/ppermute | solution.py:39
  57.5 1.6 %collective-permute-start.12 = (bf16[16,1024]{1,0:T(8,128)(2,1)S(1)}, bf16[16,1024]{1,0:T(8,128)(2,1)S(1)}, u32[]{:S(2)}, u32[]{:S(2)}) collective-permute-start(bf16[16,1024]{1,0:T(8,128)(2,1)S(1)} %get-tuple-element.12), channel_id=1, source_target_pairs={{0,28},{4,0},{8,4},{12,8},{16,12},{20,16},{24,20},{28,24},{1,29},{... | collective-permute-start | bytes 98312 | tf_op jit(solution)/shard_map/ppermute | solution.py:39
  59.2 0.5 collective-permute-done.10
  59.6 0.6 collective-permute-done.11
  60.3 1.2 %collective-permute-done.12 = bf16[16,1024]{1,0:T(8,128)(2,1)S(1)} collective-permute-done((bf16[16,1024]{1,0:T(8,128)(2,1)S(1)}, bf16[16,1024]{1,0:T(8,128)(2,1)S(1)}, u32[]{:S(2)}, u32[]{:S(2)}) %collective-permute-start.12) | collective-permute-done | bytes 32800 | tf_op jit(solution)/shard_map/ppermute | solution.py:39
  61.4 0.6 gather_fusion
  62.1 2.9 %convolution_convert_fusion = bf16[2048,1024]{1,0:T(8,128)(2,1)} fusion(bf16[128,1024]{1,0:T(8,128)(2,1)S(1)} %bitcast_select_fusion, f32[2048,128]{1,0:T(8,128)S(1)} %get-tuple-element.34, f32[2048]{0:T(1024)S(1)} %get-tuple-element.5, f32[2048]{0:T(1024)S(1)} %get-tuple-element.7), kind=kOutput, calls=%fused_computation.3 | convolution fusion | flops 539754496 | bytes 5521408 | tf_op jit(solution)/shard_map/dot_general | solution.py:71
  (49 shorter events, 1.8 us)
Async XLA Ops:
  0.0 1.0 %copy-start = (bf16[1024,128]{1,0:T(8,128)(2,1)S(1)}, bf16[1024,128]{1,0:T(8,128)(2,1)}, u32[]{:S(2)}) copy-start(bf16[1024,128]{1,0:T(8,128)(2,1)} %param.5) | copy-start | bytes 786436
  0.0 5.5 %copy-start.1 = (bf16[2048,1024]{1,0:T(8,128)(2,1)S(1)}, bf16[2048,1024]{1,0:T(8,128)(2,1)}, u32[]{:S(2)}) copy-start(bf16[2048,1024]{1,0:T(8,128)(2,1)} %param.4) | copy-start | bytes 12582916
  7.2 16.9 %all-to-all-start = ((bf16[8,16,1152]{2,1,0:T(8,128)(2,1)}), bf16[8,16,1152]{2,1,0:T(8,128)(2,1)S(1)}, u32[]{:S(2)}, u32[]{:S(2)}) async-start(bf16[8,16,1152]{2,1,0:T(8,128)(2,1)} %pad_maximum_fusion), calls=%async_computation | async-start | bytes 589824 | tf_op jit(solution)/shard_map/all_to_all | solution.py:55
  30.1 3.4 %collective-permute-start = (bf16[16,1152]{1,0:T(8,128)(2,1)S(1)}, bf16[16,1152]{1,0:T(8,128)(2,1)S(1)}, u32[]{:S(2)}, u32[]{:S(2)}) collective-permute-start(bf16[16,1152]{1,0:T(8,128)(2,1)S(1)} %pad_maximum_fusion.1), channel_id=1, source_target_pairs={{0,1},{1,2},{2,3},{3,0},{4,5},{5,6},{6,7},{7,4},{8,9},{9,10},{10,1... | collective-permute-start | bytes 110600 | tf_op jit(solution)/shard_map/ppermute | solution.py:39
  30.1 4.0 %collective-permute-start.1 = (bf16[16,1152]{1,0:T(8,128)(2,1)S(1)}, bf16[16,1152]{1,0:T(8,128)(2,1)S(1)}, u32[]{:S(2)}, u32[]{:S(2)}) collective-permute-start(bf16[16,1152]{1,0:T(8,128)(2,1)S(1)} %pad_maximum_fusion.1), channel_id=1, source_target_pairs={{0,2},{1,3},{2,0},{3,1},{4,6},{5,7},{6,4},{7,5},{8,10},{9,11},{10,... | collective-permute-start | bytes 110600 | tf_op jit(solution)/shard_map/ppermute | solution.py:39
  31.7 3.0 %collective-permute-start.2 = (bf16[16,1152]{1,0:T(8,128)(2,1)S(1)}, bf16[16,1152]{1,0:T(8,128)(2,1)S(1)}, u32[]{:S(2)}, u32[]{:S(2)}) collective-permute-start(bf16[16,1152]{1,0:T(8,128)(2,1)S(1)} %pad_maximum_fusion.1), channel_id=1, source_target_pairs={{0,3},{1,0},{2,1},{3,2},{4,7},{5,4},{6,5},{7,6},{8,11},{9,8},{10,9... | collective-permute-start | bytes 110600 | tf_op jit(solution)/shard_map/ppermute | solution.py:39
  43.6 3.4 %collective-permute-start.3 = (bf16[16,1024]{1,0:T(8,128)(2,1)S(1)}, bf16[16,1024]{1,0:T(8,128)(2,1)S(1)}, u32[]{:S(2)}, u32[]{:S(2)}) collective-permute-start(bf16[16,1024]{1,0:T(8,128)(2,1)S(1)} %convert_element_type.61), channel_id=1, source_target_pairs={{0,1},{1,2},{2,3},{3,0},{4,5},{5,6},{6,7},{7,4},{8,9},{9,10},{10,1... | collective-permute-start | bytes 98312 | tf_op jit(solution)/shard_map/ppermute | solution.py:39
  44.3 3.9 %collective-permute-start.4 = (bf16[16,1024]{1,0:T(8,128)(2,1)S(1)}, bf16[16,1024]{1,0:T(8,128)(2,1)S(1)}, u32[]{:S(2)}, u32[]{:S(2)}) collective-permute-start(bf16[16,1024]{1,0:T(8,128)(2,1)S(1)} %convert_element_type.61), channel_id=1, source_target_pairs={{0,2},{1,3},{2,0},{3,1},{4,6},{5,7},{6,4},{7,5},{8,10},{9,11},{10,... | collective-permute-start | bytes 98312 | tf_op jit(solution)/shard_map/ppermute | solution.py:39
  45.8 2.4 %collective-permute-start.5 = (bf16[16,1024]{1,0:T(8,128)(2,1)S(1)}, bf16[16,1024]{1,0:T(8,128)(2,1)S(1)}, u32[]{:S(2)}, u32[]{:S(2)}) collective-permute-start(bf16[16,1024]{1,0:T(8,128)(2,1)S(1)} %convert_element_type.61), channel_id=1, source_target_pairs={{0,3},{1,0},{2,1},{3,2},{4,7},{5,4},{6,5},{7,6},{8,11},{9,8},{10,9... | collective-permute-start | bytes 98312 | tf_op jit(solution)/shard_map/ppermute | solution.py:39
  48.2 7.5 %collective-permute-start.6 = (bf16[16,1024]{1,0:T(8,128)(2,1)S(1)}, bf16[16,1024]{1,0:T(8,128)(2,1)S(1)}, u32[]{:S(2)}, u32[]{:S(2)}) collective-permute-start(bf16[16,1024]{1,0:T(8,128)(2,1)S(1)} %get-tuple-element.12), channel_id=1, source_target_pairs={{0,4},{4,8},{8,12},{12,16},{16,20},{20,24},{24,28},{28,0},{1,5},{5... | collective-permute-start | bytes 98312 | tf_op jit(solution)/shard_map/ppermute | solution.py:39
  49.9 7.7 %collective-permute-start.7 = (bf16[16,1024]{1,0:T(8,128)(2,1)S(1)}, bf16[16,1024]{1,0:T(8,128)(2,1)S(1)}, u32[]{:S(2)}, u32[]{:S(2)}) collective-permute-start(bf16[16,1024]{1,0:T(8,128)(2,1)S(1)} %get-tuple-element.12), channel_id=1, source_target_pairs={{0,8},{4,12},{8,16},{12,20},{16,24},{20,28},{24,0},{28,4},{1,9},{5... | collective-permute-start | bytes 98312 | tf_op jit(solution)/shard_map/ppermute | solution.py:39
  49.9 9.3 %collective-permute-start.8 = (bf16[16,1024]{1,0:T(8,128)(2,1)S(1)}, bf16[16,1024]{1,0:T(8,128)(2,1)S(1)}, u32[]{:S(2)}, u32[]{:S(2)}) collective-permute-start(bf16[16,1024]{1,0:T(8,128)(2,1)S(1)} %get-tuple-element.12), channel_id=1, source_target_pairs={{0,12},{4,16},{8,20},{12,24},{16,28},{20,0},{24,4},{28,8},{1,13},{... | collective-permute-start | bytes 98312 | tf_op jit(solution)/shard_map/ppermute | solution.py:39
  51.6 7.6 %collective-permute-start.9 = (bf16[16,1024]{1,0:T(8,128)(2,1)S(1)}, bf16[16,1024]{1,0:T(8,128)(2,1)S(1)}, u32[]{:S(2)}, u32[]{:S(2)}) collective-permute-start(bf16[16,1024]{1,0:T(8,128)(2,1)S(1)} %get-tuple-element.12), channel_id=1, source_target_pairs={{0,16},{4,20},{8,24},{12,28},{16,0},{20,4},{24,8},{28,12},{1,17},{... | collective-permute-start | bytes 98312 | tf_op jit(solution)/shard_map/ppermute | solution.py:39
  54.8 4.9 %collective-permute-start.10 = (bf16[16,1024]{1,0:T(8,128)(2,1)S(1)}, bf16[16,1024]{1,0:T(8,128)(2,1)S(1)}, u32[]{:S(2)}, u32[]{:S(2)}) collective-permute-start(bf16[16,1024]{1,0:T(8,128)(2,1)S(1)} %get-tuple-element.12), channel_id=1, source_target_pairs={{0,20},{4,24},{8,28},{12,0},{16,4},{20,8},{24,12},{28,16},{1,21},{... | collective-permute-start | bytes 98312 | tf_op jit(solution)/shard_map/ppermute | solution.py:39
  55.7 4.6 %collective-permute-start.11 = (bf16[16,1024]{1,0:T(8,128)(2,1)S(1)}, bf16[16,1024]{1,0:T(8,128)(2,1)S(1)}, u32[]{:S(2)}, u32[]{:S(2)}) collective-permute-start(bf16[16,1024]{1,0:T(8,128)(2,1)S(1)} %get-tuple-element.12), channel_id=1, source_target_pairs={{0,24},{4,28},{8,0},{12,4},{16,8},{20,12},{24,16},{28,20},{1,25},{... | collective-permute-start | bytes 98312 | tf_op jit(solution)/shard_map/ppermute | solution.py:39
  57.5 3.9 %collective-permute-start.12 = (bf16[16,1024]{1,0:T(8,128)(2,1)S(1)}, bf16[16,1024]{1,0:T(8,128)(2,1)S(1)}, u32[]{:S(2)}, u32[]{:S(2)}) collective-permute-start(bf16[16,1024]{1,0:T(8,128)(2,1)S(1)} %get-tuple-element.12), channel_id=1, source_target_pairs={{0,28},{4,0},{8,4},{12,8},{16,12},{20,16},{24,20},{28,24},{1,29},{... | collective-permute-start | bytes 98312 | tf_op jit(solution)/shard_map/ppermute | solution.py:39

commit v2 on v0

v2 whole, which is shorter than its diff:
```python
import functools

import jax
import jax.numpy as jnp
from jax import lax
from jax.experimental import pallas as pl
from jax.experimental.pallas import tpu as pltpu
from jax.sharding import PartitionSpec as P

SLOT_PER = 4
SIDE = 128
CHUNK = 256
F32 = jnp.float32
BF16 = jnp.bfloat16
VMEM = pl.BlockSpec(memory_space=pltpu.VMEM)
SMEM = pl.BlockSpec(memory_space=pltpu.SMEM)
ANY = pl.BlockSpec(memory_space=pl.ANY)
MIB = 1024 * 1024


def params(mib):
    return pltpu.CompilerParams(vmem_limit_bytes=mib * MIB)


def dot(lhs, rhs, dims):
    return lax.dot_general(lhs, rhs, ((dims[0], dims[1]), ((), ())), preferred_element_type=F32)


def side_state(peak, total):
    lane = lax.broadcasted_iota(jnp.int32, (peak.shape[0], SIDE), 1)
    return jnp.where(lane == 0, peak, jnp.where(lane == 1, total, 0.0))


def side_message(peak, total):
    lane = lax.broadcasted_iota(jnp.int32, (peak.shape[0], SIDE), 1)
    out = jnp.zeros((peak.shape[0], SIDE), F32)
    for index, value in enumerate((peak, total)):
        for piece in range(3):
            part = value.astype(BF16).astype(F32)
            out = jnp.where(lane == 3 * index + piece, part, out)
            value = value - part
    return out.astype(BF16)


def gather_kernel(place, tokens, slot_params, logits, keep, side, send, held, table, sems):
    chunks = tokens.shape[0] // CHUNK
    copies = [
        pltpu.make_async_copy(tokens.at[pl.ds(i * CHUNK, CHUNK)], held.at[pl.ds(i * CHUNK, CHUNK)], sems.at[i])
        for i in range(chunks)
    ]
    for copy in copies:
        copy.start()
    slots = slot_params.shape[1]
    row = lax.broadcasted_iota(jnp.int32, (slots, slots), 0)
    column = lax.broadcasted_iota(jnp.int32, (slots, slots), 1)
    swap = jnp.where(row == (column ^ place[0]), 1.0, 0.0).astype(BF16)
    table[...] = dot(swap, slot_params[...], ((1,), (1,))).astype(BF16)
    peak = None
    for i in range(chunks):
        copies[i].wait()
        part = dot(table[...], held[pl.ds(i * CHUNK, CHUNK), :], ((1,), (1,)))
        logits[:, pl.ds(i * CHUNK, CHUNK)] = part
        part_peak = jnp.max(part, axis=1, keepdims=True)
        peak = part_peak if peak is None else jnp.maximum(peak, part_peak)
    weights = jnp.exp(logits[...] - peak)
    total = jnp.sum(weights, axis=1, keepdims=True)
    sums = dot(weights.astype(BF16), held[...], ((1,), (0,)))
    half = sums.shape[1] // 2
    low, high = sums[:, :half], sums[:, half:]
    first = place[1] == 0
    keep[...] = jnp.where(first, low, high)
    side[...] = side_state(peak, total)
    send[:, :half] = jnp.where(first, high, low).astype(BF16)
    send[:, half:] = side_message(peak, total)


def merge(keep, side, received, rows):
    width = keep.shape[1]
    mine, other = side[rows, :], received[rows, width:].astype(F32)
    peak_mine, total_mine = mine[:, 0:1], mine[:, 1:2]
    peak_other = other[:, 0:1] + other[:, 1:2] + other[:, 2:3]
    total_other = other[:, 3:4] + other[:, 4:5] + other[:, 5:6]
    peak = jnp.maximum(peak_mine, peak_other)
    scale_mine, scale_other = jnp.exp(peak_mine - peak), jnp.exp(peak_other - peak)
    total = total_mine * scale_mine + total_other * scale_other
    sums = keep[rows, :] * scale_mine + received[rows, :width].astype(F32) * scale_other
    return sums, peak, total


def merge_kernel(rows, keep, side, received, keep_out, side_out, send):
    width = keep.shape[1]
    blocks = keep.shape[0] // rows
    for block in range(blocks):
        sums, peak, total = merge(keep, side, received, pl.ds(block * rows, rows))
        target = pl.ds(block // 2 * rows, rows)
        if block % 2 == 0:
            keep_out[target, :] = sums
            side_out[target, :] = side_state(peak, total)
        if block % 2 == 1 or blocks == 1:
            send[target, :width] = sums.astype(BF16)
            send[target, width:] = side_message(peak, total)


def merge_call(keep, side, received, rows):
    left = max(keep.shape[0] // 2, rows)
    width = keep.shape[1]
    return pl.pallas_call(
        functools.partial(merge_kernel, rows),
        out_shape=(
            jax.ShapeDtypeStruct((left, width), F32),
            jax.ShapeDtypeStruct((left, SIDE), F32),
            jax.ShapeDtypeStruct((left, width + SIDE), BF16),
        ),
        in_specs=[VMEM] * 3,
        out_specs=(VMEM,) * 3,
        name="merge",
    )(keep, side, received)


def finish_kernel(keep, side, received, slot_in):
    sums, _, total = merge(keep, side, received, pl.ds(0, keep.shape[0]))
    slot_in[...] = (sums / total).astype(BF16)


def expert_kernel(place, mine, other, expert_in, expert_out, keep, send, first_held, second_held, sems):
    experts = expert_in.shape[0]
    first_copies = [
        pltpu.make_async_copy(expert_in.at[e], first_held.at[e], sems.at[0, e]) for e in range(experts)
    ]
    second_copies = [
        pltpu.make_async_copy(expert_out.at[e], second_held.at[e], sems.at[1, e]) for e in range(experts)
    ]
    for e in range(experts):
        first_copies[e].start()
        second_copies[e].start()
    half = mine.shape[1]
    first = place[1] == 0
    slot_in = jnp.concatenate(
        [jnp.where(first, mine[...], other[...]), jnp.where(first, other[...], mine[...])], axis=1
    )
    row = lax.broadcasted_iota(jnp.int32, (mine.shape[0], 1), 0)
    result = jnp.zeros((mine.shape[0], expert_out.shape[2]), F32)
    for e in range(experts):
        first_copies[e].wait()
        hidden = jax.nn.gelu(dot(slot_in, first_held[e], ((1,), (0,)))).astype(BF16)
        second_copies[e].wait()
        out = dot(hidden, second_held[e], ((1,), (0,)))
        result = jnp.where(row // SLOT_PER == e, out, result)
    low, high = result[:, :half], result[:, half:]
    keep[...] = jnp.where(first, low, high)
    send[...] = jnp.where(first, high, low).astype(BF16)


def combine_kernel(logits, combine):
    value = logits[...]
    weights = jnp.exp(value - jnp.max(value, axis=0, keepdims=True))
    weights = weights / jnp.sum(weights, axis=0, keepdims=True)
    combine[...] = weights.T.astype(BF16)


def mix_kernel(place, combine, slot_out, mixed):
    mixed[...] = dot(combine[...], slot_out[...], ((1,), (0,))).astype(BF16)


def mix_second_kernel(place, combine, slot_out, before, mixed):
    mixed[...] = dot(combine[...], slot_out[...], ((1,), (0,))).astype(BF16)


def mix_call(which, combine, slot_out, before=None):
    tokens, slots = combine.shape
    width = slot_out.shape[1]
    block = 512
    in_specs = [
        pl.BlockSpec((block, slots), lambda i, which: (i, 0)),
        pl.BlockSpec((slots, width), lambda i, which: (0, 0)),
    ]
    operands = [which, combine, slot_out]
    if before is not None:
        in_specs.append(ANY)
        operands.append(before)
    return pl.pallas_call(
        mix_kernel if before is None else mix_second_kernel,
        out_shape=jax.ShapeDtypeStruct((tokens, 2 * width), BF16),
        grid_spec=pltpu.PrefetchScalarGridSpec(
            num_scalar_prefetch=1,
            grid=(tokens // block,),
            in_specs=in_specs,
            out_specs=pl.BlockSpec((block, width), lambda i, which: (i, which[0])),
        ),
        input_output_aliases={} if before is None else {3: 0},
        cost_estimate=pl.CostEstimate(
            flops=2 * tokens * slots * width, bytes_accessed=2 * tokens * (width + slots), transcendentals=0
        ),
        compiler_params=params(16),
        name="mix",
    )(*operands)


def exchange(value, axis, bit):
    return lax.ppermute(value, axis, [(i, i ^ bit) for i in range(lax.axis_size(axis))])


def bits(axis, first=1):
    found, bit = [], first
    while bit < lax.axis_size(axis):
        found.append(bit)
        bit *= 2
    return found


def shards(tokens, slot_params, expert_in, expert_out):
    count, model = tokens.shape
    slots = slot_params.shape[1]
    rows = slots // lax.axis_size("wide")
    half = model // 2
    side_of = lax.axis_index("narrow") % 2
    place = jnp.stack([lax.axis_index("wide") * rows, side_of]).astype(jnp.int32)

    logits, keep, side, send = pl.pallas_call(
        gather_kernel,
        out_shape=(
            jax.ShapeDtypeStruct((slots, count), F32),
            jax.ShapeDtypeStruct((slots, half), F32),
            jax.ShapeDtypeStruct((slots, SIDE), F32),
            jax.ShapeDtypeStruct((slots, half + SIDE), BF16),
        ),
        in_specs=[SMEM, ANY, VMEM],
        out_specs=(VMEM,) * 4,
        scratch_shapes=[
            pltpu.VMEM((count, model), BF16),
            pltpu.VMEM((slots, model), BF16),
            pltpu.SemaphoreType.DMA((count // CHUNK,)),
        ],
        compiler_params=params(40),
        name="gather",
    )(place, tokens, slot_params)
    received = exchange(send, "narrow", 1)
    combine = pl.pallas_call(
        combine_kernel,
        out_shape=jax.ShapeDtypeStruct((count, slots), BF16),
        grid=(count // 512,),
        in_specs=[pl.BlockSpec((slots, 512), lambda i: (0, i))],
        out_specs=pl.BlockSpec((512, slots), lambda i: (i, 0)),
        cost_estimate=pl.CostEstimate(
            flops=8 * count * slots, bytes_accessed=6 * count * slots, transcendentals=count * slots
        ),
        compiler_params=params(16),
        name="combine",
    )(logits)
    for bit in bits("wide"):
        keep, side, send = merge_call(keep, side, received, rows)
        received = exchange(send, "wide", bit)
    for bit in bits("narrow", 2):
        keep, side, send = merge_call(keep, side, received, rows)
        received = exchange(send, "narrow", bit)
    mine = pl.pallas_call(
        finish_kernel,
        out_shape=jax.ShapeDtypeStruct((rows, half), BF16),
        in_specs=[VMEM] * 3,
        out_specs=VMEM,
        name="finish",
    )(keep, side, received)
    other = exchange(mine, "narrow", 1)
    keep, send = pl.pallas_call(
        expert_kernel,
        out_shape=(jax.ShapeDtypeStruct((rows, half), F32), jax.ShapeDtypeStruct((rows, half), BF16)),
        in_specs=[SMEM, VMEM, VMEM, ANY, ANY],
        out_specs=(VMEM, VMEM),
        scratch_shapes=[
            pltpu.VMEM(expert_in.shape, BF16),
            pltpu.VMEM(expert_out.shape, BF16),
            pltpu.SemaphoreType.DMA((2, expert_in.shape[0])),
        ],
        compiler_params=params(40),
        name="experts",
    )(place, mine, other, expert_in, expert_out)
    keep = keep + exchange(send, "narrow", 1).astype(F32)
    for bit in bits("narrow", 2):
        keep = keep + exchange(keep.astype(BF16), "narrow", bit).astype(F32)
    block = keep.astype(BF16)
    for bit in reversed(bits("wide")):
        other = exchange(block, "wide", bit)
        pieces = zip(block.reshape(-1, rows, half), other.reshape(-1, rows, half))
        block = jnp.concatenate([part for pair in pieces for part in pair], axis=0)
    other = exchange(block, "narrow", 1)
    mixed = mix_call(place[1:], combine, block)
    return mix_call(1 - place[1:], combine, other, mixed)


def solution(mesh):
    return jax.shard_map(
        shards,
        mesh=mesh,
        in_specs=(
            P(("wide", "narrow"), None),
            P(),
            P("wide", None, "narrow"),
            P("wide", "narrow", None),
        ),
        out_specs=P(("wide", "narrow"), None),
        check_vma=False,
    )
```

time: 221 us -> 78.1 us (0.35)
  blocking collectives: 124 us -> 0 us
  waiting for transfers between devices: 62.4 us -> 21.5 us
  Pallas kernels: 0 us -> 25.8 us
  starting transfers between devices: 0.04 us -> 18.3 us
  matrix products: 18.2 us -> 0 us
  between operations: 13.4 us -> 0.11 us
  local copies, waits for them, and re-layouts: 1.07 us -> 11.7 us
    reduce_scatter x1 -> x0, waiting for transfers between devices: 62.4 us -> none  [shards(): lax.psum_scatter(lax.dot_general(columns, tokens, (((0,), (0,)), ((), ())...]
    psum x2 -> x0, blocking collectives: 50.8 us -> none  [the longest x1 40.1 us: shards(): slot_totals = lax.psum(jnp.sum(weights, axis=0), ('wide', 'narrow'))]
    pmax x1 -> x0, blocking collectives: 41.9 us -> none  [shards(): column_peak = lax.pmax(local_peak, ('wide', 'narrow'))]
    all_gather x1 -> x0, blocking collectives: 30.8 us -> none  [shards(): lax.all_gather(whole_rows, 'wide', axis=0, tiled=True)]
    pallas_call x0 -> x10, Pallas kernels: none -> 25.8 us  [the longest x4 7.39 us: merge_call(): pl.pallas_call(functools.partial(merge_kernel, rows), out_shape=(jax.Shap...]
    ppermute x0 -> x12, waiting for transfers between devices: none -> 21.5 us  [exchange(): lax.ppermute(value, axis, [(i, i ^ bit) for i in range(lax.axis_size(axis...]
    ppermute x0 -> x12, starting transfers between devices: none -> 18.3 us  [exchange(): lax.ppermute(value, axis, [(i, i ^ bit) for i in range(lax.axis_size(axis...]
    dot_general x4 -> x0, matrix products: 18.2 us -> none  [the longest x1 8.04 us: shards(): jnp.einsum('esh,ehd->esd', hidden, expert_out, preferred_element_type=jnp...]
  transfers between devices with their start and end apart: 2 -> 12, of which waited for: 1 -> 11; matrix products, arithmetic and copies ran while one was open for 0% -> 0% of each run, Pallas kernels for 0% -> 4%
where the time goes in v2:
time: 78.1 us; the launch traced here: 77.5 us
  Pallas kernels  25.8 us (33%)
  waiting for transfers between devices  21.5 us (28%)
  starting transfers between devices  18.3 us (23%)
  local copies, waits for them, and re-layouts  11.7 us (15%)
    ppermute x12, waiting for transfers between devices, exchange(): lax.ppermute(value, axis, [(i, i ^ bit) for i in range(lax.axis_size(axis...  21.5 us
    ppermute x12, starting transfers between devices, exchange(): lax.ppermute(value, axis, [(i, i ^ bit) for i in range(lax.axis_size(axis...  18.3 us
    unnamed x28, local copies, waits for them, and re-layouts  11.7 us
    pallas_call x4, Pallas kernels, merge_call(): pl.pallas_call(functools.partial(merge_kernel, rows), out_shape=(jax.Shap...  7.39 us
    pallas_call x1, Pallas kernels, shards(): pl.pallas_call(gather_kernel, out_shape=(jax.ShapeDtypeStruct((slots, cou...  5.91 us
    pallas_call x1, Pallas kernels, shards(): pl.pallas_call(expert_kernel, out_shape=(jax.ShapeDtypeStruct((rows, half...  5.12 us
    pallas_call x2, Pallas kernels, mix_call(): pl.pallas_call(mix_kernel if before is None else mix_second_kernel, out_s...  4.89 us
    pallas_call x1, Pallas kernels, shards(): pl.pallas_call(finish_kernel, out_shape=jax.ShapeDtypeStruct((rows, half)...  1.68 us
  transfers between devices with their start and end apart: 12, of which 11 were waited for; matrix products, arithmetic and copies ran while one was open for 0% of the time, Pallas kernels for 4%

profile of v2, /device:TPU:0, one launch (start us, length us, event | category | flops | bytes accessed | tf_op | source)
XLA Modules:
  0.0 77.5 jit_solution(11786470044573994477)
XLA Ops:
  0.1 2.2 %copy-done.1 = bf16[2048,1024]{1,0:T(8,128)(2,1)S(1)} copy-done((bf16[2048,1024]{1,0:T(8,128)(2,1)S(1)}, bf16[2048,1024]{1,0:T(8,128)(2,1)}, u32[]{:S(2)}) %copy-start.1) | copy-done | bytes 4194328
  2.3 0.9 %copy-done.2 = bf16[1024,128]{1,0:T(8,128)(2,1)S(1)} copy-done((bf16[1024,128]{1,0:T(8,128)(2,1)S(1)}, bf16[1024,128]{1,0:T(8,128)(2,1)}, u32[]{:S(2)}) %copy-start.2) | copy-done | bytes 262168
  3.2 5.9 %gather.1 = (f32[128,2048]{1,0:T(8,128)S(1)}, f32[128,512]{1,0:T(8,128)S(1)}, f32[128,128]{1,0:T(8,128)S(1)}, bf16[128,640]{1,0:T(8,128)(2,1)S(1)}) custom-call(s32[2]{0:T(128)S(1)} %pad_add_fusion.place, bf16[2048,1024]{1,0:T(8,128)(2,1)S(1)} %copy-done.1, bf16[1024,128]{1,0:T(8,128)(2,1)S(1)} %copy-done.2), custom_call_target="tpu_custom_call" | custom-call | tf_op jit(solution)/shard_map/gather/pallas_call | solution.py:219
  10.9 1.0 %collective-permute-done.received = bf16[128,640]{1,0:T(8,128)(2,1)S(1)} collective-permute-done((bf16[128,640]{1,0:T(8,128)(2,1)S(1)}, bf16[128,640]{1,0:T(8,128)(2,1)S(1)}, u32[]{:S(2)}, u32[]{:S(2)}) %collective-permute-start) | collective-permute-done | bytes 163872 | tf_op jit(solution)/shard_map/ppermute | solution.py:200
  12.6 2.0 %merge.4 = (f32[64,512]{1,0:T(8,128)}, f32[64,128]{1,0:T(8,128)}, bf16[64,640]{1,0:T(8,128)(2,1)}) custom-call(f32[128,512]{1,0:T(8,128)} %copy-done.3, f32[128,128]{1,0:T(8,128)} %copy-done.5, bf16[128,640]{1,0:T(8,128)(2,1)} %copy-done.6), custom_call_target="tpu_custom_call" | custom-call | tf_op jit(solution)/shard_map/merge/pallas_call | solution.py:107
  14.7 2.9 %collective-permute-start.1 = (bf16[64,640]{1,0:T(8,128)(2,1)}, bf16[64,640]{1,0:T(8,128)(2,1)S(1)}, u32[]{:S(2)}, u32[]{:S(2)}) collective-permute-start(bf16[64,640]{1,0:T(8,128)(2,1)} %get-tuple-element.29), channel_id=1, source_target_pairs={{0,4},{4,0},{8,12},{12,8},{16,20},{20,16},{24,28},{28,24},{1,5},{5... | collective-permute-start | bytes 245768 | tf_op jit(solution)/shard_map/ppermute | solution.py:200
  17.5 3.0 %collective-permute-done.1.received = bf16[64,640]{1,0:T(8,128)(2,1)S(1)} collective-permute-done((bf16[64,640]{1,0:T(8,128)(2,1)}, bf16[64,640]{1,0:T(8,128)(2,1)S(1)}, u32[]{:S(2)}, u32[]{:S(2)}) %collective-permute-start.1) | collective-permute-done | bytes 81952 | tf_op jit(solution)/shard_map/ppermute | solution.py:200
  21.1 1.9 %merge.5 = (f32[32,512]{1,0:T(8,128)}, f32[32,128]{1,0:T(8,128)}, bf16[32,640]{1,0:T(8,128)(2,1)}) custom-call(f32[64,512]{1,0:T(8,128)} %get-tuple-element.27.keep, f32[64,128]{1,0:T(8,128)} %get-tuple-element.28.side, bf16[64,640]{1,0:T(8,128)(2,1)} %copy-done.7), custom_call_target="tpu_custom_call" | custom-call | tf_op jit(solution)/shard_map/merge/pallas_call | solution.py:107
  23.0 1.8 %collective-permute-start.2 = (bf16[32,640]{1,0:T(8,128)(2,1)}, bf16[32,640]{1,0:T(8,128)(2,1)S(1)}, u32[]{:S(2)}, u32[]{:S(2)}) collective-permute-start(bf16[32,640]{1,0:T(8,128)(2,1)} %get-tuple-element.32), channel_id=1, source_target_pairs={{0,8},{4,12},{8,0},{12,4},{16,24},{20,28},{24,16},{28,20},{1,9},{5... | collective-permute-start | bytes 122888 | tf_op jit(solution)/shard_map/ppermute | solution.py:200
  24.8 2.4 %collective-permute-done.2.received = bf16[32,640]{1,0:T(8,128)(2,1)S(1)} collective-permute-done((bf16[32,640]{1,0:T(8,128)(2,1)}, bf16[32,640]{1,0:T(8,128)(2,1)S(1)}, u32[]{:S(2)}, u32[]{:S(2)}) %collective-permute-start.2) | collective-permute-done | bytes 40992 | tf_op jit(solution)/shard_map/ppermute | solution.py:200
  27.8 1.8 %merge.6 = (f32[16,512]{1,0:T(8,128)}, f32[16,128]{1,0:T(8,128)}, bf16[16,640]{1,0:T(8,128)(2,1)}) custom-call(f32[32,512]{1,0:T(8,128)} %get-tuple-element.30.keep, f32[32,128]{1,0:T(8,128)} %get-tuple-element.31.side, bf16[32,640]{1,0:T(8,128)(2,1)} %copy-done.8), custom_call_target="tpu_custom_call" | custom-call | tf_op jit(solution)/shard_map/merge/pallas_call | solution.py:107
  29.6 2.8 %collective-permute-start.3 = (bf16[16,640]{1,0:T(8,128)(2,1)}, bf16[16,640]{1,0:T(8,128)(2,1)S(1)}, u32[]{:S(2)}, u32[]{:S(2)}) collective-permute-start(bf16[16,640]{1,0:T(8,128)(2,1)} %get-tuple-element.35), channel_id=1, source_target_pairs={{0,16},{4,20},{8,24},{12,28},{16,0},{20,4},{24,8},{28,12},{1,17},{... | collective-permute-start | bytes 61448 | tf_op jit(solution)/shard_map/ppermute | solution.py:200
  32.4 2.1 %collective-permute-done.3.received = bf16[16,640]{1,0:T(8,128)(2,1)S(1)} collective-permute-done((bf16[16,640]{1,0:T(8,128)(2,1)}, bf16[16,640]{1,0:T(8,128)(2,1)S(1)}, u32[]{:S(2)}, u32[]{:S(2)}) %collective-permute-start.3) | collective-permute-done | bytes 20512 | tf_op jit(solution)/shard_map/ppermute | solution.py:200
  35.1 1.7 %merge.7 = (f32[16,512]{1,0:T(8,128)}, f32[16,128]{1,0:T(8,128)}, bf16[16,640]{1,0:T(8,128)(2,1)}) custom-call(f32[16,512]{1,0:T(8,128)} %get-tuple-element.33.keep, f32[16,128]{1,0:T(8,128)} %get-tuple-element.34.side, bf16[16,640]{1,0:T(8,128)(2,1)} %copy-done.9), custom_call_target="tpu_custom_call" | custom-call | tf_op jit(solution)/shard_map/merge/pallas_call | solution.py:107
  36.8 1.8 %collective-permute-start.4 = (bf16[16,640]{1,0:T(8,128)(2,1)}, bf16[16,640]{1,0:T(8,128)(2,1)S(1)}, u32[]{:S(2)}, u32[]{:S(2)}) collective-permute-start(bf16[16,640]{1,0:T(8,128)(2,1)} %get-tuple-element.38), channel_id=1, source_target_pairs={{0,2},{1,3},{2,0},{3,1},{4,6},{5,7},{6,4},{7,5},{8,10},{9,11},{10,... | collective-permute-start | bytes 61448 | tf_op jit(solution)/shard_map/ppermute | solution.py:200
  38.5 2.2 %collective-permute-done.4.received = bf16[16,640]{1,0:T(8,128)(2,1)S(1)} collective-permute-done((bf16[16,640]{1,0:T(8,128)(2,1)}, bf16[16,640]{1,0:T(8,128)(2,1)S(1)}, u32[]{:S(2)}, u32[]{:S(2)}) %collective-permute-start.4) | collective-permute-done | bytes 20512 | tf_op jit(solution)/shard_map/ppermute | solution.py:200
  41.4 1.7 %finish.1.mine = bf16[16,512]{1,0:T(8,128)(2,1)} custom-call(f32[16,512]{1,0:T(8,128)} %get-tuple-element.36.keep, f32[16,128]{1,0:T(8,128)} %get-tuple-element.37.side, bf16[16,640]{1,0:T(8,128)(2,1)} %copy-done.10), custom_call_target="tpu_custom_call" | custom-call | tf_op jit(solution)/shard_map/finish/pallas_call | solution.py:256
  43.1 1.4 %collective-permute-done.5.other = bf16[16,512]{1,0:T(8,128)(2,1)S(1)} collective-permute-done((bf16[16,512]{1,0:T(8,128)(2,1)}, bf16[16,512]{1,0:T(8,128)(2,1)S(1)}, u32[]{:S(2)}, u32[]{:S(2)}) %collective-permute-start.5) | collective-permute-done | bytes 16416 | tf_op jit(solution)/shard_map/ppermute | solution.py:200
  44.5 3.4 %copy-done = bf16[4,1024,1024]{2,1,0:T(8,128)(2,1)S(1)} copy-done((bf16[4,1024,1024]{2,1,0:T(8,128)(2,1)S(1)}, bf16[4,1024,1024]{2,1,0:T(8,128)(2,1)}, u32[]{:S(2)}) %copy-start) | copy-done | bytes 8388632
  48.6 5.1 %experts.1 = (f32[16,512]{1,0:T(8,128)S(1)}, bf16[16,512]{1,0:T(8,128)(2,1)S(1)}) custom-call(s32[2]{0:T(128)S(1)} %pad_add_fusion.place, bf16[16,512]{1,0:T(8,128)(2,1)S(1)} %copy-done.4, bf16[16,512]{1,0:T(8,128)(2,1)S(1)} %collective-permute-done.5.other, bf16[4,1024,1024]{2,1,0:T(8,128)(2,1)S(1)} %copy-done, bf16[4,1024,1024]{2,1,0:T(8,128)(2,1)} %expert_out.1), custom_call_target="tpu_custom_call" | custom-call | tf_op jit(solution)/shard_map/experts/pallas_call | solution.py:264
  53.9 1.0 %collective-permute-done.6 = bf16[16,512]{1,0:T(8,128)(2,1)S(1)} collective-permute-done((bf16[16,512]{1,0:T(8,128)(2,1)S(1)}, bf16[16,512]{1,0:T(8,128)(2,1)S(1)}, u32[]{:S(2)}, u32[]{:S(2)}) %collective-permute-start.6) | collective-permute-done | bytes 16416 | tf_op jit(solution)/shard_map/ppermute | solution.py:200
  54.9 1.8 %collective-permute-start.7 = (bf16[16,512]{1,0:T(8,128)(2,1)S(1)}, bf16[16,512]{1,0:T(8,128)(2,1)S(1)}, u32[]{:S(2)}, u32[]{:S(2)}) collective-permute-start(bf16[16,512]{1,0:T(8,128)(2,1)S(1)} %fusion), channel_id=1, source_target_pairs={{0,2},{1,3},{2,0},{3,1},{4,6},{5,7},{6,4},{7,5},{8,10},{9,11},{10,... | collective-permute-start | bytes 49160 | tf_op jit(solution)/shard_map/ppermute | solution.py:200
  56.7 2.0 %collective-permute-done.7 = bf16[16,512]{1,0:T(8,128)(2,1)S(1)} collective-permute-done((bf16[16,512]{1,0:T(8,128)(2,1)S(1)}, bf16[16,512]{1,0:T(8,128)(2,1)S(1)}, u32[]{:S(2)}, u32[]{:S(2)}) %collective-permute-start.7) | collective-permute-done | bytes 16416 | tf_op jit(solution)/shard_map/ppermute | solution.py:200
  58.7 2.9 %collective-permute-start.8 = (bf16[16,512]{1,0:T(8,128)(2,1)S(1)}, bf16[16,512]{1,0:T(8,128)(2,1)S(1)}, u32[]{:S(2)}, u32[]{:S(2)}) collective-permute-start(bf16[16,512]{1,0:T(8,128)(2,1)S(1)} %get-tuple-element.42), channel_id=1, source_target_pairs={{0,16},{4,20},{8,24},{12,28},{16,0},{20,4},{24,8},{28,12},{1,17},{... | collective-permute-start | bytes 49160 | tf_op jit(solution)/shard_map/ppermute | solution.py:200
  61.6 1.8 %collective-permute-done.8 = bf16[16,512]{1,0:T(8,128)(2,1)S(1)} collective-permute-done((bf16[16,512]{1,0:T(8,128)(2,1)S(1)}, bf16[16,512]{1,0:T(8,128)(2,1)S(1)}, u32[]{:S(2)}, u32[]{:S(2)}) %collective-permute-start.8) | collective-permute-done | bytes 16416 | tf_op jit(solution)/shard_map/ppermute | solution.py:200
  63.4 1.8 %collective-permute-start.9 = (bf16[32,512]{1,0:T(8,128)(2,1)S(1)}, bf16[32,512]{1,0:T(8,128)(2,1)S(1)}, u32[]{:S(2)}, u32[]{:S(2)}) collective-permute-start(bf16[32,512]{1,0:T(8,128)(2,1)S(1)} %pad_maximum_fusion.1), channel_id=1, source_target_pairs={{0,8},{4,12},{8,0},{12,4},{16,24},{20,28},{24,16},{28,20},{1,9},{5... | collective-permute-start | bytes 98312 | tf_op jit(solution)/shard_map/ppermute | solution.py:200
  65.2 2.1 %collective-permute-done.9 = bf16[32,512]{1,0:T(8,128)(2,1)S(1)} collective-permute-done((bf16[32,512]{1,0:T(8,128)(2,1)S(1)}, bf16[32,512]{1,0:T(8,128)(2,1)S(1)}, u32[]{:S(2)}, u32[]{:S(2)}) %collective-permute-start.9) | collective-permute-done | bytes 32800 | tf_op jit(solution)/shard_map/ppermute | solution.py:200
  67.3 1.8 %collective-permute-start.10 = (bf16[64,512]{1,0:T(8,128)(2,1)S(1)}, bf16[64,512]{1,0:T(8,128)(2,1)S(1)}, u32[]{:S(2)}, u32[]{:S(2)}) collective-permute-start(bf16[64,512]{1,0:T(8,128)(2,1)S(1)} %pad_maximum_fusion), channel_id=1, source_target_pairs={{0,4},{4,0},{8,12},{12,8},{16,20},{20,16},{24,28},{28,24},{1,5},{5... | collective-permute-start | bytes 196616 | tf_op jit(solution)/shard_map/ppermute | solution.py:200
  69.1 2.5 %collective-permute-done.10 = bf16[64,512]{1,0:T(8,128)(2,1)S(1)} collective-permute-done((bf16[64,512]{1,0:T(8,128)(2,1)S(1)}, bf16[64,512]{1,0:T(8,128)(2,1)S(1)}, u32[]{:S(2)}, u32[]{:S(2)}) %collective-permute-start.10) | collective-permute-done | bytes 65568 | tf_op jit(solution)/shard_map/ppermute | solution.py:200
  71.8 0.8 %combine.1 = bf16[2048,128]{1,0:T(8,128)(2,1)S(1)} custom-call(f32[128,2048]{1,0:T(8,128)S(1)} %get-tuple-element.23.logits), custom_call_target="tpu_custom_call" | custom-call | flops 2097152 | bytes 1572864 | tf_op jit(solution)/shard_map/combine/pallas_call | solution.py:238
  72.6 2.5 %mix.2.before = bf16[2048,1024]{1,0:T(8,128)(2,1)} custom-call(s32[1]{0:T(128)} %bitcast.place, bf16[2048,128]{1,0:T(8,128)(2,1)S(1)} %combine.1, bf16[128,512]{1,0:T(8,128)(2,1)S(1)} %constant_dynamic-update-slice_fusion.slot_out), custom_call_target="tpu_custom_call" | custom-call | flops 268435456 | bytes 2621440 | tf_op jit(solution)/shard_map/mix/pallas_call | solution.py:181
  75.1 2.4 %mix.3 = bf16[2048,1024]{1,0:T(8,128)(2,1)} custom-call(s32[1]{0:T(128)S(6)} %sub.3.place, bf16[2048,128]{1,0:T(8,128)(2,1)S(1)} %combine.1, bf16[128,512]{1,0:T(8,128)(2,1)S(1)} %collective-permute-done.11.slot_out, bf16[2048,1024]{1,0:T(8,128)(2,1)} %mix.2.before), custom_call_target="tpu_custom_call", output_to_operand_aliasing={{}: (3, {})} | custom-call | flops 268435456 | bytes 2621440 | tf_op jit(solution)/shard_map/mix/pallas_call | solution.py:181
  (37 shorter events, 6.1 us)
Async XLA Ops:
  0.1 2.2 %copy-start.1 = (bf16[2048,1024]{1,0:T(8,128)(2,1)S(1)}, bf16[2048,1024]{1,0:T(8,128)(2,1)}, u32[]{:S(2)}) copy-start(bf16[2048,1024]{1,0:T(8,128)(2,1)} %tokens.1) | copy-start | bytes 12582916
  2.3 0.9 %copy-start.2 = (bf16[1024,128]{1,0:T(8,128)(2,1)S(1)}, bf16[1024,128]{1,0:T(8,128)(2,1)}, u32[]{:S(2)}) copy-start(bf16[1024,128]{1,0:T(8,128)(2,1)} %slot_params.1) | copy-start | bytes 786436
  9.1 0.7 copy-start.3
  9.8 0.6 copy-start.5
  10.5 1.5 %collective-permute-start = (bf16[128,640]{1,0:T(8,128)(2,1)S(1)}, bf16[128,640]{1,0:T(8,128)(2,1)S(1)}, u32[]{:S(2)}, u32[]{:S(2)}) collective-permute-start(bf16[128,640]{1,0:T(8,128)(2,1)S(1)} %get-tuple-element.26), channel_id=1, source_target_pairs={{0,1},{1,0},{2,3},{3,2},{4,5},{5,4},{6,7},{7,6},{8,9},{9,8},{10,11... | collective-permute-start | bytes 491528 | tf_op jit(solution)/shard_map/ppermute | solution.py:200
  11.9 0.7 copy-start.6
  14.7 5.8 %collective-permute-start.1 = (bf16[64,640]{1,0:T(8,128)(2,1)}, bf16[64,640]{1,0:T(8,128)(2,1)S(1)}, u32[]{:S(2)}, u32[]{:S(2)}) collective-permute-start(bf16[64,640]{1,0:T(8,128)(2,1)} %get-tuple-element.29), channel_id=1, source_target_pairs={{0,4},{4,0},{8,12},{12,8},{16,20},{20,16},{24,28},{28,24},{1,5},{5... | collective-permute-start | bytes 245768 | tf_op jit(solution)/shard_map/ppermute | solution.py:200
  20.5 0.6 copy-start.7
  23.0 4.2 %collective-permute-start.2 = (bf16[32,640]{1,0:T(8,128)(2,1)}, bf16[32,640]{1,0:T(8,128)(2,1)S(1)}, u32[]{:S(2)}, u32[]{:S(2)}) collective-permute-start(bf16[32,640]{1,0:T(8,128)(2,1)} %get-tuple-element.32), channel_id=1, source_target_pairs={{0,8},{4,12},{8,0},{12,4},{16,24},{20,28},{24,16},{28,20},{1,9},{5... | collective-permute-start | bytes 122888 | tf_op jit(solution)/shard_map/ppermute | solution.py:200
  27.2 0.6 copy-start.8
  29.6 4.9 %collective-permute-start.3 = (bf16[16,640]{1,0:T(8,128)(2,1)}, bf16[16,640]{1,0:T(8,128)(2,1)S(1)}, u32[]{:S(2)}, u32[]{:S(2)}) collective-permute-start(bf16[16,640]{1,0:T(8,128)(2,1)} %get-tuple-element.35), channel_id=1, source_target_pairs={{0,16},{4,20},{8,24},{12,28},{16,0},{20,4},{24,8},{28,12},{1,17},{... | collective-permute-start | bytes 61448 | tf_op jit(solution)/shard_map/ppermute | solution.py:200
  34.5 0.6 copy-start.9
  36.8 4.0 %collective-permute-start.4 = (bf16[16,640]{1,0:T(8,128)(2,1)}, bf16[16,640]{1,0:T(8,128)(2,1)S(1)}, u32[]{:S(2)}, u32[]{:S(2)}) collective-permute-start(bf16[16,640]{1,0:T(8,128)(2,1)} %get-tuple-element.38), channel_id=1, source_target_pairs={{0,2},{1,3},{2,0},{3,1},{4,6},{5,7},{6,4},{7,5},{8,10},{9,11},{10,... | collective-permute-start | bytes 61448 | tf_op jit(solution)/shard_map/ppermute | solution.py:200
  40.8 0.6 copy-start.10
  43.1 1.4 %collective-permute-start.5 = (bf16[16,512]{1,0:T(8,128)(2,1)}, bf16[16,512]{1,0:T(8,128)(2,1)S(1)}, u32[]{:S(2)}, u32[]{:S(2)}) collective-permute-start(bf16[16,512]{1,0:T(8,128)(2,1)} %finish.1.mine), channel_id=1, source_target_pairs={{0,1},{1,0},{2,3},{3,2},{4,5},{5,4},{6,7},{7,6},{8,9},{9,8},{10,11... | collective-permute-start | bytes 49160 | tf_op jit(solution)/shard_map/ppermute | solution.py:200
  44.5 3.4 %copy-start = (bf16[4,1024,1024]{2,1,0:T(8,128)(2,1)S(1)}, bf16[4,1024,1024]{2,1,0:T(8,128)(2,1)}, u32[]{:S(2)}) copy-start(bf16[4,1024,1024]{2,1,0:T(8,128)(2,1)} %expert_in.1) | copy-start | bytes 25165828
  47.8 0.7 copy-start.4
  53.7 1.2 %collective-permute-start.6 = (bf16[16,512]{1,0:T(8,128)(2,1)S(1)}, bf16[16,512]{1,0:T(8,128)(2,1)S(1)}, u32[]{:S(2)}, u32[]{:S(2)}) collective-permute-start(bf16[16,512]{1,0:T(8,128)(2,1)S(1)} %get-tuple-element.40), channel_id=1, source_target_pairs={{0,1},{1,0},{2,3},{3,2},{4,5},{5,4},{6,7},{7,6},{8,9},{9,8},{10,11... | collective-permute-start | bytes 49160 | tf_op jit(solution)/shard_map/ppermute | solution.py:200
  54.9 3.7 %collective-permute-start.7 = (bf16[16,512]{1,0:T(8,128)(2,1)S(1)}, bf16[16,512]{1,0:T(8,128)(2,1)S(1)}, u32[]{:S(2)}, u32[]{:S(2)}) collective-permute-start(bf16[16,512]{1,0:T(8,128)(2,1)S(1)} %fusion), channel_id=1, source_target_pairs={{0,2},{1,3},{2,0},{3,1},{4,6},{5,7},{6,4},{7,5},{8,10},{9,11},{10,... | collective-permute-start | bytes 49160 | tf_op jit(solution)/shard_map/ppermute | solution.py:200
  58.7 4.7 %collective-permute-start.8 = (bf16[16,512]{1,0:T(8,128)(2,1)S(1)}, bf16[16,512]{1,0:T(8,128)(2,1)S(1)}, u32[]{:S(2)}, u32[]{:S(2)}) collective-permute-start(bf16[16,512]{1,0:T(8,128)(2,1)S(1)} %get-tuple-element.42), channel_id=1, source_target_pairs={{0,16},{4,20},{8,24},{12,28},{16,0},{20,4},{24,8},{28,12},{1,17},{... | collective-permute-start | bytes 49160 | tf_op jit(solution)/shard_map/ppermute | solution.py:200
  63.4 3.9 %collective-permute-start.9 = (bf16[32,512]{1,0:T(8,128)(2,1)S(1)}, bf16[32,512]{1,0:T(8,128)(2,1)S(1)}, u32[]{:S(2)}, u32[]{:S(2)}) collective-permute-start(bf16[32,512]{1,0:T(8,128)(2,1)S(1)} %pad_maximum_fusion.1), channel_id=1, source_target_pairs={{0,8},{4,12},{8,0},{12,4},{16,24},{20,28},{24,16},{28,20},{1,9},{5... | collective-permute-start | bytes 98312 | tf_op jit(solution)/shard_map/ppermute | solution.py:200
  67.3 4.3 %collective-permute-start.10 = (bf16[64,512]{1,0:T(8,128)(2,1)S(1)}, bf16[64,512]{1,0:T(8,128)(2,1)S(1)}, u32[]{:S(2)}, u32[]{:S(2)}) collective-permute-start(bf16[64,512]{1,0:T(8,128)(2,1)S(1)} %pad_maximum_fusion), channel_id=1, source_target_pairs={{0,4},{4,0},{8,12},{12,8},{16,20},{20,16},{24,28},{28,24},{1,5},{5... | collective-permute-start | bytes 196616 | tf_op jit(solution)/shard_map/ppermute | solution.py:200
  71.7 3.4 %collective-permute-start.11 = (bf16[128,512]{1,0:T(8,128)(2,1)S(1)}, bf16[128,512]{1,0:T(8,128)(2,1)S(1)}, u32[]{:S(2)}, u32[]{:S(2)}) collective-permute-start(bf16[128,512]{1,0:T(8,128)(2,1)S(1)} %constant_dynamic-update-slice_fusion.slot_out), channel_id=1, source_target_pairs={{0,1},{1,0},{2,3},{3,2},{4,5},{5,4},{6,7},{7,6},{8,9},{9,8},{10,11... | collective-permute-start | bytes 393224 | tf_op jit(solution)/shard_map/ppermute | solution.py:200

commit v3 on v0

v3 whole, which is shorter than its diff:
```python
import jax
import jax.numpy as jnp
from jax import lax
from jax.experimental import pallas as pl
from jax.experimental.pallas import tpu as pltpu
from jax.sharding import PartitionSpec as P

SLOT_PER = 4
SIDE = 128
CHUNK = 256
F32 = jnp.float32
BF16 = jnp.bfloat16
VMEM = pl.BlockSpec(memory_space=pltpu.VMEM)
SMEM = pl.BlockSpec(memory_space=pltpu.SMEM)
ANY = pl.BlockSpec(memory_space=pl.ANY)
MIB = 1024 * 1024


def params(mib):
    return pltpu.CompilerParams(vmem_limit_bytes=mib * MIB)


def cost(flops, moved, transcendentals=0):
    return pl.CostEstimate(flops=flops, bytes_accessed=moved, transcendentals=transcendentals)


def dot(lhs, rhs):
    return jnp.dot(lhs, rhs, preferred_element_type=F32)


def side_state(peak, total):
    lane = lax.broadcasted_iota(jnp.int32, (peak.shape[0], SIDE), 1)
    return jnp.where(lane == 0, peak, jnp.where(lane == 1, total, 0.0))


def side_message(peak, total):
    lane = lax.broadcasted_iota(jnp.int32, (peak.shape[0], SIDE), 1)
    out = jnp.zeros((peak.shape[0], SIDE), F32)
    for index, value in enumerate((peak, total)):
        for piece in range(3):
            part = value.astype(BF16).astype(F32)
            out = jnp.where(lane == 3 * index + piece, part, out)
            value = value - part
    return out.astype(BF16)


def read_message(side):
    value = side.astype(F32)
    return (
        value[:, 0:1] + value[:, 1:2] + value[:, 2:3],
        value[:, 3:4] + value[:, 4:5] + value[:, 5:6],
    )


def gather_kernel(place, tokens, slot_params, logits, keep, side, send, held, table, sems):
    chunks = tokens.shape[0] // CHUNK
    slots = slot_params.shape[1]
    table_copy = pltpu.make_async_copy(slot_params, table, sems.at[chunks])
    table_copy.start()
    copies = [
        pltpu.make_async_copy(tokens.at[pl.ds(i * CHUNK, CHUNK)], held.at[pl.ds(i * CHUNK, CHUNK)], sems.at[i])
        for i in range(chunks)
    ]
    for copy in copies:
        copy.start()
    high = jnp.full((8, slots), -jnp.inf, F32)
    table_copy.wait()
    for i in range(chunks):
        copies[i].wait()
        part = dot(held[pl.ds(i * CHUNK, CHUNK), :], table[...])
        logits[pl.ds(i * CHUNK, CHUNK), :] = part
        high = jnp.maximum(high, jnp.max(part.reshape(CHUNK // 8, 8, slots), axis=0))
    peak = jnp.max(high, axis=0, keepdims=True)
    total = jnp.zeros((8, slots), F32)
    turned = []
    for i in range(chunks):
        weights = jnp.exp(logits[pl.ds(i * CHUNK, CHUNK), :] - peak)
        total = total + jnp.sum(weights.reshape(CHUNK // 8, 8, slots), axis=0)
        turned.append(weights.T.astype(BF16))
    sums = dot(jnp.concatenate(turned, axis=1), held[...])
    total = jnp.sum(total, axis=0, keepdims=True)
    peak = jnp.broadcast_to(peak, (8, slots)).T[:, 0:1]
    total = jnp.broadcast_to(total, (8, slots)).T[:, 0:1]
    half = sums.shape[1] // 2
    left, right = sums[:, :half], sums[:, half:]
    first = place[0] == 0
    keep[...] = jnp.where(first, left, right)
    side[...] = side_state(peak, total)
    send[:, :half] = jnp.where(first, right, left).astype(BF16)
    send[:, half:] = side_message(peak, total)


def merge(keep, side, received):
    width = keep.shape[1]
    peak_mine, total_mine = side[:, 0:1], side[:, 1:2]
    peak_other, total_other = read_message(received[:, width:])
    peak = jnp.maximum(peak_mine, peak_other)
    scale_mine, scale_other = jnp.exp(peak_mine - peak), jnp.exp(peak_other - peak)
    total = total_mine * scale_mine + total_other * scale_other
    sums = keep[...] * scale_mine + received[:, :width].astype(F32) * scale_other
    return sums, peak, total


def pair_kernel(keep, side, received, send):
    width = keep.shape[1]
    sums, peak, total = merge(keep, side, received)
    send[:, :width] = sums.astype(BF16)
    send[:, width:] = side_message(peak, total)


def merge_all_kernel(received, combine, keep, side, send):
    groups, width = received.shape[0], received.shape[2] - SIDE
    states = [read_message(received[g, :, width:]) for g in range(groups)]
    peak = states[0][0]
    for other, _ in states[1:]:
        peak = jnp.maximum(peak, other)
    total = jnp.zeros_like(peak)
    sums = jnp.zeros(keep.shape, F32)
    for g, (peak_other, total_other) in enumerate(states):
        scale = jnp.exp(peak_other - peak)
        total = total + total_other * scale
        sums = sums + received[g, :, :width].astype(F32) * scale
    keep[...] = sums
    side[...] = side_state(peak, total)
    send[:, :width] = sums.astype(BF16)
    send[:, width:] = side_message(peak, total)


def finish_kernel(keep, side, received, first_held, slot_in):
    sums, _, total = merge(keep, side, received)
    slot_in[...] = (sums / total).astype(BF16)


def step_kernel(keep, side, received, keep_out, side_out, send):
    width = keep.shape[1]
    sums, peak, total = merge(keep, side, received)
    keep_out[...] = sums
    side_out[...] = side_state(peak, total)
    send[:, :width] = sums.astype(BF16)
    send[:, width:] = side_message(peak, total)


def load_kernel(after, weights, held, sems):
    copies = [pltpu.make_async_copy(weights.at[e], held.at[e], sems.at[e]) for e in range(weights.shape[0])]
    for copy in copies:
        copy.start()
    for copy in copies:
        copy.wait()


def load_call(after, weights, room):
    return pl.pallas_call(
        load_kernel,
        out_shape=jax.ShapeDtypeStruct(weights.shape, weights.dtype),
        in_specs=[ANY, ANY],
        out_specs=VMEM,
        scratch_shapes=[pltpu.SemaphoreType.DMA((weights.shape[0],))],
        cost_estimate=cost(0, 2 * weights.size),
        compiler_params=params(room),
        name="load",
    )(after, weights)


def expert_kernel(place, mine, other, expert_in, expert_out, keep, send, held, sems):
    experts = expert_in.shape[0]
    copies = [pltpu.make_async_copy(expert_out.at[e], held.at[e], sems.at[e]) for e in range(experts)]
    for copy in copies:
        copy.start()
    half = mine.shape[1]
    first = place[0] == 0
    slot_in = jnp.concatenate(
        [jnp.where(first, mine[...], other[...]), jnp.where(first, other[...], mine[...])], axis=1
    )
    hidden = [jax.nn.gelu(dot(slot_in, expert_in[e])).astype(BF16) for e in range(experts)]
    row = lax.broadcasted_iota(jnp.int32, (mine.shape[0], 1), 0)
    result = jnp.zeros((mine.shape[0], expert_out.shape[2]), F32)
    for e in range(experts):
        copies[e].wait()
        result = jnp.where(row // SLOT_PER == e, dot(hidden[e], held[e]), result)
    left, right = result[:, :half], result[:, half:]
    keep[...] = jnp.where(first, left, right)
    send[...] = jnp.where(first, right, left).astype(BF16)


def combine_kernel(logits, after, combine):
    value = logits[...]
    weights = jnp.exp(value - jnp.max(value, axis=1, keepdims=True))
    combine[...] = (weights / jnp.sum(weights, axis=1, keepdims=True)).astype(BF16)


def mix_kernel(place, combine, slot_out, *refs):
    mixed, held, sems = refs[-3:]
    width = slot_out.shape[1]
    block = held.shape[0] // sems.shape[0]
    columns = pl.ds(pl.multiple_of(place[0] * width, width), width)
    copies = []
    for i in range(sems.shape[0]):
        rows = pl.ds(i * block, block)
        held[rows, :] = dot(combine[rows, :], slot_out[...]).astype(BF16)
        copies.append(pltpu.make_async_copy(held.at[rows], mixed.at[rows, columns], sems.at[i]))
        copies[-1].start()
    for copy in copies:
        copy.wait()


def mix_call(which, combine, slot_out, before=None):
    tokens, slots = combine.shape
    width = slot_out.shape[1]
    more = [] if before is None else [before]
    return pl.pallas_call(
        mix_kernel,
        out_shape=jax.ShapeDtypeStruct((tokens, 2 * width), BF16),
        in_specs=[SMEM, VMEM, VMEM] + [ANY] * len(more),
        out_specs=ANY,
        scratch_shapes=[pltpu.VMEM((tokens, width), BF16), pltpu.SemaphoreType.DMA((8,))],
        input_output_aliases={3: 0} if more else {},
        cost_estimate=cost(2 * tokens * slots * width, 2 * tokens * (width + slots)),
        compiler_params=params(16),
        name="mix",
    )(which, combine, slot_out, *more)


def exchange(value, axis, bit):
    return lax.ppermute(value, axis, [(i, i ^ bit) for i in range(lax.axis_size(axis))])


def later_bits(axis):
    found, bit = [], 2
    while bit < lax.axis_size(axis):
        found.append(bit)
        bit *= 2
    return found


def shards(tokens, slot_params, expert_in, expert_out):
    count, model = tokens.shape
    slots = slot_params.shape[1]
    groups = lax.axis_size("wide")
    rows = slots // groups
    half = model // 2
    place = (lax.axis_index("narrow") % 2).astype(jnp.int32).reshape(1)

    def state(height):
        return (
            jax.ShapeDtypeStruct((height, half), F32),
            jax.ShapeDtypeStruct((height, SIDE), F32),
            jax.ShapeDtypeStruct((height, half + SIDE), BF16),
        )

    logits, keep, side, send = pl.pallas_call(
        gather_kernel,
        out_shape=(jax.ShapeDtypeStruct((count, slots), F32),) + state(slots),
        in_specs=[SMEM, ANY, ANY],
        out_specs=(VMEM,) * 4,
        scratch_shapes=[
            pltpu.VMEM((count, model), BF16),
            pltpu.VMEM((model, slots), BF16),
            pltpu.SemaphoreType.DMA((count // CHUNK + 1,)),
        ],
        compiler_params=params(52),
        name="gather",
    )(place, tokens, slot_params)
    received = exchange(send, "narrow", 1)
    send = pl.pallas_call(
        pair_kernel,
        out_shape=state(slots)[2],
        in_specs=[VMEM] * 3,
        out_specs=VMEM,
        compiler_params=params(8),
        name="pair",
    )(keep, side, received)
    received = lax.all_to_all(send.reshape(groups, rows, -1), "wide", split_axis=0, concat_axis=0, tiled=True)
    combine = pl.pallas_call(
        combine_kernel,
        out_shape=jax.ShapeDtypeStruct((count, slots), BF16),
        in_specs=[VMEM, ANY],
        out_specs=VMEM,
        cost_estimate=cost(8 * count * slots, 6 * count * slots, count * slots),
        compiler_params=params(8),
        name="combine",
    )(logits, send)
    keep, side, send = pl.pallas_call(
        merge_all_kernel,
        out_shape=state(rows),
        in_specs=[VMEM, ANY],
        out_specs=(VMEM,) * 3,
        compiler_params=params(8),
        name="merge",
    )(received, combine)
    first_held = load_call(send, expert_in, 44)
    more = later_bits("narrow")
    for bit in more[:-1]:
        received = exchange(send, "narrow", bit)
        keep, side, send = pl.pallas_call(
            step_kernel,
            out_shape=state(rows),
            in_specs=[VMEM] * 3,
            out_specs=(VMEM,) * 3,
            compiler_params=params(8),
            name="step",
        )(keep, side, received)
    received = exchange(send, "narrow", more[-1])
    mine = pl.pallas_call(
        finish_kernel,
        out_shape=jax.ShapeDtypeStruct((rows, half), BF16),
        in_specs=[VMEM] * 3 + [ANY],
        out_specs=VMEM,
        compiler_params=params(8),
        name="finish",
    )(keep, side, received, first_held)
    other = exchange(mine, "narrow", 1)
    keep, send = pl.pallas_call(
        expert_kernel,
        out_shape=(jax.ShapeDtypeStruct((rows, half), F32), jax.ShapeDtypeStruct((rows, half), BF16)),
        in_specs=[SMEM, VMEM, VMEM, VMEM, ANY],
        out_specs=(VMEM, VMEM),
        scratch_shapes=[
            pltpu.VMEM(expert_out.shape, BF16),
            pltpu.SemaphoreType.DMA((expert_out.shape[0],)),
        ],
        compiler_params=params(42),
        name="experts",
    )(place, mine, other, first_held, expert_out)
    keep = keep + exchange(send, "narrow", 1).astype(F32)
    for bit in more:
        keep = keep + exchange(keep.astype(BF16), "narrow", bit).astype(F32)
    block = jnp.broadcast_to(keep.astype(BF16), (groups, rows, half))
    block = lax.all_to_all(block, "wide", split_axis=0, concat_axis=0, tiled=True).reshape(slots, half)
    other = exchange(block, "narrow", 1)
    mixed = mix_call(place, combine, block)
    return mix_call(1 - place, combine, other, mixed)


def solution(mesh):
    return jax.shard_map(
        shards,
        mesh=mesh,
        in_specs=(
            P(("wide", "narrow"), None),
            P(),
            P("wide", None, "narrow"),
            P("wide", "narrow", None),
        ),
        out_specs=P(("wide", "narrow"), None),
        check_vma=False,
    )
```

time: 221 us -> 53.3 us (0.24)
  blocking collectives: 124 us -> 10.1 us
  waiting for transfers between devices: 62.4 us -> 13.6 us
  matrix products: 18.2 us -> 0 us
  Pallas kernels: 0 us -> 18.1 us
  between operations: 13.4 us -> 0.09 us
  starting transfers between devices: 0.04 us -> 10.1 us
    reduce_scatter x1 -> x0, waiting for transfers between devices: 62.4 us -> none  [shards(): lax.psum_scatter(lax.dot_general(columns, tokens, (((0,), (0,)), ((), ())...]
    psum x2 -> x0, blocking collectives: 50.8 us -> none  [the longest x1 40.1 us: shards(): slot_totals = lax.psum(jnp.sum(weights, axis=0), ('wide', 'narrow'))]
    pmax x1 -> x0, blocking collectives: 41.9 us -> none  [shards(): column_peak = lax.pmax(local_peak, ('wide', 'narrow'))]
    all_gather x1 -> x0, blocking collectives: 30.8 us -> none  [shards(): lax.all_gather(whole_rows, 'wide', axis=0, tiled=True)]
    dot_general x4 -> x0, matrix products: 18.2 us -> none  [the longest x1 8.04 us: shards(): jnp.einsum('esh,ehd->esd', hidden, expert_out, preferred_element_type=jnp...]
    pallas_call x0 -> x9, Pallas kernels: none -> 18.1 us  [the longest x1 4.98 us: shards(): pl.pallas_call(expert_kernel, out_shape=(jax.ShapeDtypeStruct((rows, half...]
    all_to_all x0 -> x1, blocking collectives: none -> 10.1 us  [shards(): lax.all_to_all(block, 'wide', split_axis=0, concat_axis=0, tiled=True)]
    all_to_all x0 -> x1, starting transfers between devices: none -> 7.17 us  [shards(): lax.all_to_all(send.reshape(groups, rows, -1), 'wide', split_axis=0, conc...]
  transfers between devices with their start and end apart: 2 -> 7, of which waited for: 1 -> 5; matrix products, arithmetic and copies ran while one was open for 0% -> 0% of each run, Pallas kernels for 0% -> 11%
where the time goes in v3:
time: 53.3 us; the launch traced here: 53 us
  Pallas kernels  18.1 us (34%)
  waiting for transfers between devices  13.6 us (26%)
  starting transfers between devices  10.1 us (19%)
  blocking collectives  10.1 us (19%)
  local copies, waits for them, and re-layouts  0.96 us (2%)
    all_to_all x1, blocking collectives, shards(): lax.all_to_all(block, 'wide', split_axis=0, concat_axis=0, tiled=True)  10.1 us
    all_to_all x1, starting transfers between devices, shards(): lax.all_to_all(send.reshape(groups, rows, -1), 'wide', split_axis=0, conc...  7.17 us
    all_to_all x1, waiting for transfers between devices, shards(): lax.all_to_all(send.reshape(groups, rows, -1), 'wide', split_axis=0, conc...  7.15 us
    ppermute x6, waiting for transfers between devices, exchange(): lax.ppermute(value, axis, [(i, i ^ bit) for i in range(lax.axis_size(axis...  6.45 us
    pallas_call x1, Pallas kernels, shards(): pl.pallas_call(expert_kernel, out_shape=(jax.ShapeDtypeStruct((rows, half...  4.98 us
    pallas_call x1, Pallas kernels, shards(): pl.pallas_call(gather_kernel, out_shape=(jax.ShapeDtypeStruct((count, slo...  4.3 us
    pallas_call x1, Pallas kernels, load_call(): pl.pallas_call(load_kernel, out_shape=jax.ShapeDtypeStruct(weights.shape,...  3.5 us
    pallas_call x2, Pallas kernels, mix_call(): pl.pallas_call(mix_kernel, out_shape=jax.ShapeDtypeStruct((tokens, 2 * wi...  3.18 us
  transfers between devices with their start and end apart: 7, of which 5 were waited for; matrix products, arithmetic and copies ran while one was open for 0% of the time, Pallas kernels for 11%

profile of v3, /device:TPU:0, one launch (start us, length us, event | category | flops | bytes accessed | tf_op | source)
XLA Modules:
  0.0 53.0 jit_solution(10179024166397622620)
XLA Ops:
  0.0 0.0 copy-start
  0.0 0.9 %copy-done = bf16[1024,128]{1,0:T(8,128)(2,1)S(1)} copy-done((bf16[1024,128]{1,0:T(8,128)(2,1)S(1)}, bf16[1024,128]{1,0:T(8,128)(2,1)}, u32[]{:S(2)}) %copy-start) | copy-done | bytes 262168
  1.0 4.3 %gather.1 = (f32[2048,128]{1,0:T(8,128)S(1)}, f32[128,512]{1,0:T(8,128)S(1)}, f32[128,128]{1,0:T(8,128)S(1)}, bf16[128,640]{1,0:T(8,128)(2,1)S(1)}) custom-call(s32[1]{0:T(128)} %bitcast.place, bf16[2048,1024]{1,0:T(8,128)(2,1)} %tokens.1, bf16[1024,128]{1,0:T(8,128)(2,1)S(1)} %copy-done), custom_call_target="tpu_custom_call" | custom-call | tf_op jit(solution)/shard_map/gather/pallas_call | solution.py:250
  5.3 0.5 collective-permute-start
  5.8 1.0 %collective-permute-done.received = bf16[128,640]{1,0:T(8,128)(2,1)S(1)} collective-permute-done((bf16[128,640]{1,0:T(8,128)(2,1)S(1)}, bf16[128,640]{1,0:T(8,128)(2,1)S(1)}, u32[]{:S(2)}, u32[]{:S(2)}) %collective-permute-start) | collective-permute-done | bytes 163872 | tf_op jit(solution)/shard_map/ppermute | solution.py:224
  6.8 1.0 %pair.1.after = bf16[128,640]{1,0:T(8,128)(2,1)} custom-call(f32[128,512]{1,0:T(8,128)S(1)} %get-tuple-element.15.keep, f32[128,128]{1,0:T(8,128)S(1)} %get-tuple-element.16.side, bf16[128,640]{1,0:T(8,128)(2,1)S(1)} %collective-permute-done.received), custom_call_target="tpu_custom_call" | custom-call | tf_op jit(solution)/shard_map/pair/pallas_call | solution.py:264
  7.8 7.2 %all-to-all-start = ((bf16[8,16,640]{2,1,0:T(8,128)(2,1)}), bf16[8,16,640]{2,1,0:T(8,128)(2,1)S(1)}, u32[]{:S(2)}, u32[]{:S(2)}) async-start(bf16[8,16,640]{2,1,0:T(8,128)(2,1)} %bitcast.1), calls=%async_computation | async-start | bytes 327680 | tf_op jit(solution)/shard_map/all_to_all | solution.py:272
  15.0 0.6 %combine.1 = bf16[2048,128]{1,0:T(8,128)(2,1)S(1)} custom-call(f32[2048,128]{1,0:T(8,128)S(1)} %get-tuple-element.14.logits, bf16[128,640]{1,0:T(8,128)(2,1)} %pair.1.after), custom_call_target="tpu_custom_call" | custom-call | flops 2097152 | bytes 1572864 | tf_op jit(solution)/shard_map/combine/pallas_call | solution.py:273
  15.6 7.2 %all-to-all-done.received = bf16[8,16,640]{2,1,0:T(8,128)(2,1)S(1)} async-done(((bf16[8,16,640]{2,1,0:T(8,128)(2,1)}), bf16[8,16,640]{2,1,0:T(8,128)(2,1)S(1)}, u32[]{:S(2)}, u32[]{:S(2)}) %all-to-all-start) | async-done | bytes 163872 | tf_op jit(solution)/shard_map/all_to_all | solution.py:272
  22.8 0.3 merge.1
  23.0 1.6 %collective-permute-start.1 = (bf16[16,640]{1,0:T(8,128)(2,1)S(1)}, bf16[16,640]{1,0:T(8,128)(2,1)S(1)}, u32[]{:S(2)}, u32[]{:S(2)}) collective-permute-start(bf16[16,640]{1,0:T(8,128)(2,1)S(1)} %get-tuple-element.20.after), channel_id=1, source_target_pairs={{0,2},{1,3},{2,0},{3,1},{4,6},{5,7},{6,4},{7,5},{8,10},{9,11},{10,... | collective-permute-start | bytes 61448 | tf_op jit(solution)/shard_map/ppermute | solution.py:224
  24.6 3.5 %load.1.first_held.expert_in = bf16[4,1024,1024]{2,1,0:T(8,128)(2,1)S(1)} custom-call(bf16[16,640]{1,0:T(8,128)(2,1)S(1)} %get-tuple-element.20.after, bf16[4,1024,1024]{2,1,0:T(8,128)(2,1)} %weights.1), custom_call_target="tpu_custom_call" | custom-call | bytes 8388608 | tf_op jit(solution)/shard_map/load/pallas_call | solution.py:152
  28.1 0.0 collective-permute-done.1.received
  28.1 0.3 finish.1.mine
  28.4 0.1 collective-permute-start.2
  28.5 1.2 %collective-permute-done.2.other = bf16[16,512]{1,0:T(8,128)(2,1)S(1)} collective-permute-done((bf16[16,512]{1,0:T(8,128)(2,1)S(1)}, bf16[16,512]{1,0:T(8,128)(2,1)S(1)}, u32[]{:S(2)}, u32[]{:S(2)}) %collective-permute-start.2) | collective-permute-done | bytes 16416 | tf_op jit(solution)/shard_map/ppermute | solution.py:224
  29.7 5.0 %experts.1 = (f32[16,512]{1,0:T(8,128)S(1)}, bf16[16,512]{1,0:T(8,128)(2,1)S(1)}) custom-call(s32[1]{0:T(128)} %bitcast.place, bf16[16,512]{1,0:T(8,128)(2,1)S(1)} %finish.1.mine, bf16[16,512]{1,0:T(8,128)(2,1)S(1)} %collective-permute-done.2.other, bf16[4,1024,1024]{2,1,0:T(8,128)(2,1)S(1)} %load.1.first_held.expert_in, bf16[4,1024,1024]{2,1,0:T(8,128)(2,1)} %expert_out.1), custom_call_target="tpu_custom_call" | custom-call | tf_op jit(solution)/shard_map/experts/pallas_call | solution.py:312
  34.7 0.2 collective-permute-start.3
  34.9 1.0 %collective-permute-done.3 = bf16[16,512]{1,0:T(8,128)(2,1)S(1)} collective-permute-done((bf16[16,512]{1,0:T(8,128)(2,1)S(1)}, bf16[16,512]{1,0:T(8,128)(2,1)S(1)}, u32[]{:S(2)}, u32[]{:S(2)}) %collective-permute-start.3) | collective-permute-done | bytes 16416 | tf_op jit(solution)/shard_map/ppermute | solution.py:224
  35.9 0.5 collective-permute-start.4
  36.4 3.2 %collective-permute-done.4 = bf16[16,512]{1,0:T(8,128)(2,1)S(1)} collective-permute-done((bf16[16,512]{1,0:T(8,128)(2,1)S(1)}, bf16[16,512]{1,0:T(8,128)(2,1)S(1)}, u32[]{:S(2)}, u32[]{:S(2)}) %collective-permute-start.4) | collective-permute-done | bytes 16416 | tf_op jit(solution)/shard_map/ppermute | solution.py:224
  39.7 10.1 %all_to_all.10 = bf16[8,16,512]{2,1,0:T(8,128)(2,1)S(1)} all-to-all(bf16[8,16,512]{2,1,0:T(8,128)(2,1)S(1)} %broadcast_in_dim.3), channel_id=1, replica_groups=mesh['wide'=8,'narrow'=4] {'wide'}, dimensions={0} | all-to-all | bytes 262144 | tf_op jit(solution)/shard_map/all_to_all | solution.py:328
  49.8 0.0 collective-permute-start.5
  49.8 1.6 %mix.2.refs_0_ = bf16[2048,1024]{1,0:T(8,128)(2,1)} custom-call(s32[1]{0:T(128)} %bitcast.place, bf16[2048,128]{1,0:T(8,128)(2,1)S(1)} %combine.1, bf16[128,512]{1,0:T(8,128)(2,1)S(1)} %bitcast.4), custom_call_target="tpu_custom_call" | custom-call | flops 268435456 | bytes 2621440 | tf_op jit(solution)/shard_map/mix/pallas_call | solution.py:210
  51.4 0.0 collective-permute-done.5.slot_out
  51.4 1.6 %mix.3 = bf16[2048,1024]{1,0:T(8,128)(2,1)} custom-call(s32[1]{0:T(128)S(6)} %sub.3.place, bf16[2048,128]{1,0:T(8,128)(2,1)S(1)} %combine.1, bf16[128,512]{1,0:T(8,128)(2,1)S(1)} %collective-permute-done.5.slot_out, bf16[2048,1024]{1,0:T(8,128)(2,1)} %mix.2.refs_0_), custom_call_target="tpu_custom_call", output_to_operand_aliasing={{}: (3, {})} | custom-call | flops 268435456 | bytes 2621440 | tf_op jit(solution)/shard_map/mix/pallas_call | solution.py:210
  (3 shorter events, 0.0 us)
Async XLA Ops:
  0.0 0.9 %copy-start = (bf16[1024,128]{1,0:T(8,128)(2,1)S(1)}, bf16[1024,128]{1,0:T(8,128)(2,1)}, u32[]{:S(2)}) copy-start(bf16[1024,128]{1,0:T(8,128)(2,1)} %slot_params.1) | copy-start | bytes 786436
  5.3 1.5 %collective-permute-start = (bf16[128,640]{1,0:T(8,128)(2,1)S(1)}, bf16[128,640]{1,0:T(8,128)(2,1)S(1)}, u32[]{:S(2)}, u32[]{:S(2)}) collective-permute-start(bf16[128,640]{1,0:T(8,128)(2,1)S(1)} %get-tuple-element.17), channel_id=1, source_target_pairs={{0,1},{1,0},{2,3},{3,2},{4,5},{5,4},{6,7},{7,6},{8,9},{9,8},{10,11... | collective-permute-start | bytes 491528 | tf_op jit(solution)/shard_map/ppermute | solution.py:224
  7.8 14.9 %all-to-all-start = ((bf16[8,16,640]{2,1,0:T(8,128)(2,1)}), bf16[8,16,640]{2,1,0:T(8,128)(2,1)S(1)}, u32[]{:S(2)}, u32[]{:S(2)}) async-start(bf16[8,16,640]{2,1,0:T(8,128)(2,1)} %bitcast.1), calls=%async_computation | async-start | bytes 327680 | tf_op jit(solution)/shard_map/all_to_all | solution.py:272
  23.0 5.1 %collective-permute-start.1 = (bf16[16,640]{1,0:T(8,128)(2,1)S(1)}, bf16[16,640]{1,0:T(8,128)(2,1)S(1)}, u32[]{:S(2)}, u32[]{:S(2)}) collective-permute-start(bf16[16,640]{1,0:T(8,128)(2,1)S(1)} %get-tuple-element.20.after), channel_id=1, source_target_pairs={{0,2},{1,3},{2,0},{3,1},{4,6},{5,7},{6,4},{7,5},{8,10},{9,11},{10,... | collective-permute-start | bytes 61448 | tf_op jit(solution)/shard_map/ppermute | solution.py:224
  28.4 1.2 %collective-permute-start.2 = (bf16[16,512]{1,0:T(8,128)(2,1)S(1)}, bf16[16,512]{1,0:T(8,128)(2,1)S(1)}, u32[]{:S(2)}, u32[]{:S(2)}) collective-permute-start(bf16[16,512]{1,0:T(8,128)(2,1)S(1)} %finish.1.mine), channel_id=1, source_target_pairs={{0,1},{1,0},{2,3},{3,2},{4,5},{5,4},{6,7},{7,6},{8,9},{9,8},{10,11... | collective-permute-start | bytes 49160 | tf_op jit(solution)/shard_map/ppermute | solution.py:224
  34.7 1.2 %collective-permute-start.3 = (bf16[16,512]{1,0:T(8,128)(2,1)S(1)}, bf16[16,512]{1,0:T(8,128)(2,1)S(1)}, u32[]{:S(2)}, u32[]{:S(2)}) collective-permute-start(bf16[16,512]{1,0:T(8,128)(2,1)S(1)} %get-tuple-element.22), channel_id=1, source_target_pairs={{0,1},{1,0},{2,3},{3,2},{4,5},{5,4},{6,7},{7,6},{8,9},{9,8},{10,11... | collective-permute-start | bytes 49160 | tf_op jit(solution)/shard_map/ppermute | solution.py:224
  35.9 3.7 %collective-permute-start.4 = (bf16[16,512]{1,0:T(8,128)(2,1)S(1)}, bf16[16,512]{1,0:T(8,128)(2,1)S(1)}, u32[]{:S(2)}, u32[]{:S(2)}) collective-permute-start(bf16[16,512]{1,0:T(8,128)(2,1)S(1)} %fusion), channel_id=1, source_target_pairs={{0,2},{1,3},{2,0},{3,1},{4,6},{5,7},{6,4},{7,5},{8,10},{9,11},{10,... | collective-permute-start | bytes 49160 | tf_op jit(solution)/shard_map/ppermute | solution.py:224
  49.8 1.6 %collective-permute-start.5 = (bf16[128,512]{1,0:T(8,128)(2,1)S(1)}, bf16[128,512]{1,0:T(8,128)(2,1)S(1)}, u32[]{:S(2)}, u32[]{:S(2)}) collective-permute-start(bf16[128,512]{1,0:T(8,128)(2,1)S(1)} %bitcast.3), channel_id=1, source_target_pairs={{0,1},{1,0},{2,3},{3,2},{4,5},{5,4},{6,7},{7,6},{8,9},{9,8},{10,11... | collective-permute-start | bytes 393224 | tf_op jit(solution)/shard_map/ppermute | solution.py:224

commit v4 on v3

v4 whole, which is shorter than its diff:
```python
import jax
import jax.numpy as jnp
from jax import lax
from jax.experimental import pallas as pl
from jax.experimental.pallas import tpu as pltpu
from jax.sharding import Mesh, PartitionSpec as P

SLOT_PER = 4
SIDE = 128
CHUNK = 256
F32 = jnp.float32
BF16 = jnp.bfloat16
VMEM = pl.BlockSpec(memory_space=pltpu.VMEM)
SMEM = pl.BlockSpec(memory_space=pltpu.SMEM)
HBM = pl.BlockSpec(memory_space=pltpu.HBM)
MIB = 1024 * 1024


def params(mib):
    return pltpu.CompilerParams(vmem_limit_bytes=mib * MIB)


def cost(flops, moved, transcendentals=0):
    return pl.CostEstimate(flops=flops, bytes_accessed=moved, transcendentals=transcendentals)


def in_hbm(value):
    return pltpu.with_memory_space_constraint(value, pltpu.HBM)


def dot(lhs, rhs):
    return jnp.dot(lhs, rhs, preferred_element_type=F32)


def side_state(peak, total):
    lane = lax.broadcasted_iota(jnp.int32, (peak.shape[0], SIDE), 1)
    return jnp.where(lane == 0, peak, jnp.where(lane == 1, total, 0.0))


def side_message(peak, total):
    lane = lax.broadcasted_iota(jnp.int32, (peak.shape[0], SIDE), 1)
    out = jnp.zeros((peak.shape[0], SIDE), F32)
    for index, value in enumerate((peak, total)):
        for piece in range(3):
            part = value.astype(BF16).astype(F32)
            out = jnp.where(lane == 3 * index + piece, part, out)
            value = value - part
    return out.astype(BF16)


def read_message(side):
    value = side.astype(F32)
    return (
        value[:, 0:1] + value[:, 1:2] + value[:, 2:3],
        value[:, 3:4] + value[:, 4:5] + value[:, 5:6],
    )


def gather_kernel(place, tokens, slot_params, logits, keep, side, send, held, table, own, sems, out_sems):
    chunks = tokens.shape[0] // CHUNK
    slots = slot_params.shape[1]
    spans = [pl.ds(i * CHUNK, CHUNK) for i in range(chunks)]
    table_copy = pltpu.make_async_copy(slot_params, table, sems.at[chunks])
    table_copy.start()
    copies = [pltpu.make_async_copy(tokens.at[span], held.at[span], sems.at[i]) for i, span in enumerate(spans)]
    for copy in copies:
        copy.start()
    high = jnp.full((8, slots), -jnp.inf, F32)
    table_copy.wait()
    out_copies = []
    for i, span in enumerate(spans):
        copies[i].wait()
        part = dot(held[span, :], table[...])
        own[span, :] = part
        high = jnp.maximum(high, jnp.max(part.reshape(CHUNK // 8, 8, slots), axis=0))
        out_copies.append(pltpu.make_async_copy(own.at[span], logits.at[span], out_sems.at[i]))
        out_copies[-1].start()
    peak = jnp.max(high, axis=0, keepdims=True)
    total = jnp.zeros((8, slots), F32)
    turned = []
    for span in spans:
        weights = jnp.exp(own[span, :] - peak)
        total = total + jnp.sum(weights.reshape(CHUNK // 8, 8, slots), axis=0)
        turned.append(weights.T.astype(BF16))
    sums = dot(jnp.concatenate(turned, axis=1), held[...])
    total = jnp.sum(total, axis=0, keepdims=True)
    peak = jnp.broadcast_to(peak, (8, slots)).T[:, 0:1]
    total = jnp.broadcast_to(total, (8, slots)).T[:, 0:1]
    half = sums.shape[1] // 2
    left, right = sums[:, :half], sums[:, half:]
    first = place[0] == 0
    keep[...] = jnp.where(first, left, right)
    side[...] = side_state(peak, total)
    send[:, :half] = jnp.where(first, right, left).astype(BF16)
    send[:, half:] = side_message(peak, total)
    for copy in out_copies:
        copy.wait()


def pair_kernel(keep, side, received, send):
    groups, rest, rows, _ = send.shape
    width = keep.shape[1]
    for g in range(groups):
        span = pl.ds(g * rows, rows)
        peak_mine, total_mine = side[span, 0:1], side[span, 1:2]
        peak_other, total_other = read_message(received[span, width:])
        peak = jnp.maximum(peak_mine, peak_other)
        scale_mine, scale_other = jnp.exp(peak_mine - peak), jnp.exp(peak_other - peak)
        total = total_mine * scale_mine + total_other * scale_other
        sums = keep[span, :] * scale_mine + received[span, :width].astype(F32) * scale_other
        sums, message = sums.astype(BF16), side_message(peak, total)
        for r in range(rest):
            send[g, r, :, :width] = sums
            send[g, r, :, width:] = message


def finish_kernel(received, combine, slot_in):
    width = slot_in.shape[1]
    states = [read_message(received[d, :, width:]) for d in range(received.shape[0])]
    peak = states[0][0]
    for other, _ in states[1:]:
        peak = jnp.maximum(peak, other)
    total = jnp.zeros_like(peak)
    sums = jnp.zeros(slot_in.shape, F32)
    for d, (peak_other, total_other) in enumerate(states):
        scale = jnp.exp(peak_other - peak)
        total = total + total_other * scale
        sums = sums + received[d, :, :width].astype(F32) * scale
    slot_in[...] = (sums / total).astype(BF16)


def expert_kernel(place, mine, other, expert_in, expert_out, keep, send, in_held, out_held, sems):
    experts, depth = expert_in.shape[:2]
    parts = 2
    span = depth // parts
    in_copies, out_copies = [], []
    for e in range(experts):
        in_copies.append(
            [
                pltpu.make_async_copy(
                    expert_in.at[e, pl.ds(p * span, span)], in_held.at[e, pl.ds(p * span, span)], sems.at[e, p]
                )
                for p in range(parts)
            ]
        )
        out_copies.append(pltpu.make_async_copy(expert_out.at[e], out_held.at[e], sems.at[e, parts]))
        for copy in in_copies[-1]:
            copy.start()
        out_copies[-1].start()
    half = mine.shape[1]
    first = place[0] == 0
    slot_in = jnp.concatenate(
        [jnp.where(first, mine[...], other[...]), jnp.where(first, other[...], mine[...])], axis=1
    )
    row = lax.broadcasted_iota(jnp.int32, (mine.shape[0], 1), 0)
    result = jnp.zeros((mine.shape[0], expert_out.shape[2]), F32)
    for e in range(experts):
        hidden = 0.0
        for p in range(parts):
            in_copies[e][p].wait()
            hidden = hidden + dot(slot_in[:, p * span : (p + 1) * span], in_held[e, pl.ds(p * span, span), :])
        hidden = jax.nn.gelu(hidden).astype(BF16)
        out_copies[e].wait()
        result = jnp.where(row // SLOT_PER == e, dot(hidden, out_held[e]), result)
    left, right = result[:, :half], result[:, half:]
    keep[...] = jnp.where(first, left, right)
    send[...] = jnp.where(first, right, left).astype(BF16)


def combine_kernel(logits, after, combine):
    value = logits[...]
    weights = jnp.exp(value - jnp.max(value, axis=1, keepdims=True))
    combine[...] = (weights / jnp.sum(weights, axis=1, keepdims=True)).astype(BF16)


def mix_kernel(place, combine, slot_out, *refs):
    mixed, held, sems = refs[-3:]
    width = slot_out.shape[1]
    block = held.shape[0] // sems.shape[0]
    columns = pl.ds(pl.multiple_of(place[0] * width, width), width)
    copies = []
    for i in range(sems.shape[0]):
        rows = pl.ds(i * block, block)
        held[rows, :] = dot(combine[rows, :], slot_out[...]).astype(BF16)
        copies.append(pltpu.make_async_copy(held.at[rows], mixed.at[rows, columns], sems.at[i]))
        copies[-1].start()
    for copy in copies:
        copy.wait()


def mix_call(which, combine, slot_out, before=None):
    tokens, slots = combine.shape
    width = slot_out.shape[1]
    more = [] if before is None else [before]
    return pl.pallas_call(
        mix_kernel,
        out_shape=jax.ShapeDtypeStruct((tokens, 2 * width), BF16),
        in_specs=[SMEM, VMEM, VMEM] + [HBM] * len(more),
        out_specs=HBM,
        scratch_shapes=[pltpu.VMEM((tokens, width), BF16), pltpu.SemaphoreType.DMA((8,))],
        input_output_aliases={3: 0} if more else {},
        cost_estimate=cost(2 * tokens * slots * width, 2 * tokens * (width + slots)),
        compiler_params=params(16),
        name="mix",
    )(which, combine, slot_out, *more)


def swap_pair(value):
    return lax.ppermute(value, "pair", [(0, 1), (1, 0)])


def shards(tokens, slot_params, expert_in, expert_out):
    count, model = tokens.shape
    slots = slot_params.shape[1]
    groups, rest = lax.axis_size("wide"), lax.axis_size("rest")
    rows = slots // groups
    half = model // 2
    place = lax.axis_index("pair").astype(jnp.int32).reshape(1)

    logits, keep, side, send = pl.pallas_call(
        gather_kernel,
        out_shape=(
            pltpu.HBM((count, slots), F32),
            jax.ShapeDtypeStruct((slots, half), F32),
            jax.ShapeDtypeStruct((slots, SIDE), F32),
            jax.ShapeDtypeStruct((slots, half + SIDE), BF16),
        ),
        in_specs=[SMEM, HBM, HBM],
        out_specs=(HBM, VMEM, VMEM, VMEM),
        scratch_shapes=[
            pltpu.VMEM((count, model), BF16),
            pltpu.VMEM((model, slots), BF16),
            pltpu.VMEM((count, slots), F32),
            pltpu.SemaphoreType.DMA((count // CHUNK + 1,)),
            pltpu.SemaphoreType.DMA((count // CHUNK,)),
        ],
        compiler_params=params(40),
        name="gather",
    )(place, in_hbm(tokens), in_hbm(slot_params))
    received = swap_pair(send)
    send = pl.pallas_call(
        pair_kernel,
        out_shape=jax.ShapeDtypeStruct((groups, rest, rows, half + SIDE), BF16),
        in_specs=[VMEM] * 3,
        out_specs=VMEM,
        compiler_params=params(16),
        name="pair",
    )(keep, side, received)
    received = lax.all_to_all(
        send.reshape(groups * rest, rows, -1), ("wide", "rest"), split_axis=0, concat_axis=0, tiled=True
    )
    block = 512
    combine = pl.pallas_call(
        combine_kernel,
        out_shape=jax.ShapeDtypeStruct((count, slots), BF16),
        grid=(count // block,),
        in_specs=[pl.BlockSpec((block, slots), lambda i: (i, 0)), HBM],
        out_specs=pl.BlockSpec((block, slots), lambda i: (i, 0)),
        cost_estimate=cost(8 * count * slots, 6 * count * slots, count * slots),
        compiler_params=params(16),
        name="combine",
    )(in_hbm(logits), send)
    mine = pl.pallas_call(
        finish_kernel,
        out_shape=jax.ShapeDtypeStruct((rows, half), BF16),
        in_specs=[VMEM, pl.BlockSpec(memory_space=pl.ANY)],
        out_specs=VMEM,
        compiler_params=params(16),
        name="finish",
    )(received, combine)
    other = swap_pair(mine)
    keep, send = pl.pallas_call(
        expert_kernel,
        out_shape=(jax.ShapeDtypeStruct((rows, half), F32), jax.ShapeDtypeStruct((rows, half), BF16)),
        in_specs=[SMEM, VMEM, VMEM, HBM, HBM],
        out_specs=(VMEM, VMEM),
        scratch_shapes=[
            pltpu.VMEM(expert_in.shape, BF16),
            pltpu.VMEM(expert_out.shape, BF16),
            pltpu.SemaphoreType.DMA((expert_in.shape[0], 3)),
        ],
        compiler_params=params(40),
        name="experts",
    )(place, mine, other, in_hbm(expert_in), in_hbm(expert_out))
    partial = (keep + swap_pair(send).astype(F32)).astype(BF16)
    partials = jnp.broadcast_to(partial, (groups * rest, rows, half))
    partials = lax.all_to_all(partials, ("wide", "rest"), split_axis=0, concat_axis=0, tiled=True)
    slot_out = jnp.sum(partials.reshape(groups, rest, rows, half).astype(F32), axis=1)
    slot_out = slot_out.astype(BF16).reshape(slots, half)
    other = swap_pair(slot_out)
    mixed = mix_call(place, combine, slot_out)
    return mix_call(1 - place, combine, other, mixed)


def solution(mesh):
    wide, narrow = mesh.shape["wide"], mesh.shape["narrow"]
    cut = Mesh(mesh.devices.reshape(wide, narrow // 2, 2), ("wide", "rest", "pair"))
    narrow_axes = ("rest", "pair")
    return jax.shard_map(
        shards,
        mesh=cut,
        in_specs=(
            P(("wide",) + narrow_axes, None),
            P(),
            P("wide", None, narrow_axes),
            P("wide", narrow_axes, None),
        ),
        out_specs=P(("wide",) + narrow_axes, None),
        check_vma=False,
    )
```

time: 53.3 us -> 53.3 us (level)
  blocking collectives: 10.1 us -> 13.5 us
  waiting for transfers between devices: 13.6 us -> 12.2 us
  starting transfers between devices: 10.1 us -> 9.11 us
  local copies, waits for them, and re-layouts: 0.96 us -> 0.02 us
    pallas_call x4 -> x2, Pallas kernels: 9.08 us -> 5.57 us  [the longest x1 4.45 us: shards(): pl.pallas_call(gather_kernel, out_shape=(pltpu.HBM((count, slots), F32),...]
    all_to_all x1, blocking collectives: 10.1 us -> 13.5 us  [shards(): lax.all_to_all(partials, ('wide', 'rest'), split_axis=0, concat_axis=0, t...]
    ppermute x6 -> x4, waiting for transfers between devices: 6.45 us -> 3.22 us  [swap_pair(): return lax.ppermute(value, 'pair', [(0, 1), (1, 0)])]
    pallas_call x1, Pallas kernels: 0.62 us -> 2.66 us  [shards(): pl.pallas_call(combine_kernel, out_shape=jax.ShapeDtypeStruct((count, slo...]
    ppermute x6 -> x4, starting transfers between devices: 2.9 us -> 0.88 us  [swap_pair(): return lax.ppermute(value, 'pair', [(0, 1), (1, 0)])]
    all_to_all x1, waiting for transfers between devices: 7.15 us -> 8.96 us  [shards(): lax.all_to_all(send.reshape(groups * rest, rows, -1), ('wide', 'rest'), s...]
    pallas_call x1, Pallas kernels: 4.98 us -> 6.37 us  [shards(): pl.pallas_call(expert_kernel, out_shape=(jax.ShapeDtypeStruct((rows, half...]
    all_to_all x1, starting transfers between devices: 7.17 us -> 8.23 us  [shards(): lax.all_to_all(send.reshape(groups * rest, rows, -1), ('wide', 'rest'), s...]
  transfers between devices with their start and end apart: 7 -> 5, of which waited for: 5 -> 4; matrix products, arithmetic and copies ran while one was open for 0% -> 0% of each run, Pallas kernels for 11% -> 8%
where the time goes in v4:
time: 53.3 us; the launch traced here: 53 us
  Pallas kernels  18.1 us (34%)
  blocking collectives  13.5 us (25%)
  waiting for transfers between devices  12.2 us (23%)
  starting transfers between devices  9.11 us (17%)
    all_to_all x1, blocking collectives, shards(): lax.all_to_all(partials, ('wide', 'rest'), split_axis=0, concat_axis=0, t...  13.5 us
    all_to_all x1, waiting for transfers between devices, shards(): lax.all_to_all(send.reshape(groups * rest, rows, -1), ('wide', 'rest'), s...  8.96 us
    all_to_all x1, starting transfers between devices, shards(): lax.all_to_all(send.reshape(groups * rest, rows, -1), ('wide', 'rest'), s...  8.23 us
    pallas_call x1, Pallas kernels, shards(): pl.pallas_call(expert_kernel, out_shape=(jax.ShapeDtypeStruct((rows, half...  6.37 us
    pallas_call x1, Pallas kernels, shards(): pl.pallas_call(gather_kernel, out_shape=(pltpu.HBM((count, slots), F32),...  4.45 us
    ppermute x4, waiting for transfers between devices, swap_pair(): return lax.ppermute(value, 'pair', [(0, 1), (1, 0)])  3.22 us
    pallas_call x2, Pallas kernels, mix_call(): pl.pallas_call(mix_kernel, out_shape=jax.ShapeDtypeStruct((tokens, 2 * wi...  3.18 us
    pallas_call x1, Pallas kernels, shards(): pl.pallas_call(combine_kernel, out_shape=jax.ShapeDtypeStruct((count, slo...  2.66 us
  transfers between devices with their start and end apart: 5, of which 4 were waited for; matrix products, arithmetic and copies ran while one was open for 0% of the time, Pallas kernels for 8%

profile of v4, /device:TPU:0, one launch (start us, length us, event | category | flops | bytes accessed | tf_op | source)
XLA Modules:
  0.0 53.0 jit_solution(16226889096472260836)
XLA Ops:
  0.0 4.4 %gather.1 = (f32[2048,128]{1,0:T(8,128)}, f32[128,512]{1,0:T(8,128)S(1)}, f32[128,128]{1,0:T(8,128)S(1)}, bf16[128,640]{1,0:T(8,128)(2,1)S(1)}) custom-call(s32[1]{0:T(128)} %bitcast.place, bf16[2048,1024]{1,0:T(8,128)(2,1)} %tokens.1, bf16[1024,128]{1,0:T(8,128)(2,1)} %slot_params.1), custom_call_target="tpu_custom_call" | custom-call | tf_op jit(solution)/shard_map/gather/pallas_call | solution.py:220
  4.5 0.5 collective-permute-start
  5.0 1.0 %collective-permute-done.received = bf16[128,640]{1,0:T(8,128)(2,1)S(1)} collective-permute-done((bf16[128,640]{1,0:T(8,128)(2,1)S(1)}, bf16[128,640]{1,0:T(8,128)(2,1)S(1)}, u32[]{:S(2)}, u32[]{:S(2)}) %collective-permute-start) | collective-permute-done | bytes 163872 | tf_op jit(solution)/shard_map/ppermute | solution.py:209
  6.0 1.1 %pair.1.after = bf16[8,2,16,640]{3,2,1,0:T(8,128)(2,1)} custom-call(f32[128,512]{1,0:T(8,128)S(1)} %get-tuple-element.12.keep, f32[128,128]{1,0:T(8,128)S(1)} %get-tuple-element.13.side, bf16[128,640]{1,0:T(8,128)(2,1)S(1)} %collective-permute-done.received), custom_call_target="tpu_custom_call" | custom-call | tf_op jit(solution)/shard_map/pair/pallas_call | solution.py:241
  7.1 8.2 %all-to-all-start = ((bf16[16,16,640]{2,1,0:T(8,128)(2,1)}), bf16[16,16,640]{2,1,0:T(8,128)(2,1)S(1)}, u32[]{:S(2)}, u32[]{:S(2)}) async-start(bf16[16,16,640]{2,1,0:T(8,128)(2,1)} %bitcast.1), calls=%async_computation | async-start | bytes 655360 | tf_op jit(solution)/shard_map/all_to_all | solution.py:249
  15.4 2.7 %combine.1 = bf16[2048,128]{1,0:T(8,128)(2,1)S(1)} custom-call(f32[2048,128]{1,0:T(8,128)} %get-tuple-element.11.logits, bf16[8,2,16,640]{3,2,1,0:T(8,128)(2,1)} %pair.1.after), custom_call_target="tpu_custom_call" | custom-call | flops 2097152 | bytes 1572864 | tf_op jit(solution)/shard_map/combine/pallas_call | solution.py:253
  18.0 9.0 %all-to-all-done.received = bf16[16,16,640]{2,1,0:T(8,128)(2,1)S(1)} async-done(((bf16[16,16,640]{2,1,0:T(8,128)(2,1)}), bf16[16,16,640]{2,1,0:T(8,128)(2,1)S(1)}, u32[]{:S(2)}, u32[]{:S(2)}) %all-to-all-start) | async-done | bytes 327712 | tf_op jit(solution)/shard_map/all_to_all | solution.py:249
  27.0 0.3 finish.1.mine
  27.3 0.1 collective-permute-start.1
  27.4 1.2 %collective-permute-done.1.other = bf16[16,512]{1,0:T(8,128)(2,1)S(1)} collective-permute-done((bf16[16,512]{1,0:T(8,128)(2,1)S(1)}, bf16[16,512]{1,0:T(8,128)(2,1)S(1)}, u32[]{:S(2)}, u32[]{:S(2)}) %collective-permute-start.1) | collective-permute-done | bytes 16416 | tf_op jit(solution)/shard_map/ppermute | solution.py:209
  28.5 6.4 %experts.1 = (f32[16,512]{1,0:T(8,128)S(1)}, bf16[16,512]{1,0:T(8,128)(2,1)S(1)}) custom-call(s32[1]{0:T(128)} %bitcast.place, bf16[16,512]{1,0:T(8,128)(2,1)S(1)} %finish.1.mine, bf16[16,512]{1,0:T(8,128)(2,1)S(1)} %collective-permute-done.1.other, bf16[4,1024,1024]{2,1,0:T(8,128)(2,1)} %expert_in.1, bf16[4,1024,1024]{2,1,0:T(8,128)(2,1)} %expert_out.1), custom_call_target="tpu_custom_call" | custom-call | tf_op jit(solution)/shard_map/experts/pallas_call | solution.py:272
  34.9 0.2 collective-permute-start.2
  35.1 1.0 %collective-permute-done.2 = bf16[16,512]{1,0:T(8,128)(2,1)S(1)} collective-permute-done((bf16[16,512]{1,0:T(8,128)(2,1)S(1)}, bf16[16,512]{1,0:T(8,128)(2,1)S(1)}, u32[]{:S(2)}, u32[]{:S(2)}) %collective-permute-start.2) | collective-permute-done | bytes 16416 | tf_op jit(solution)/shard_map/ppermute | solution.py:209
  36.2 13.5 %all_to_all.10 = bf16[16,16,512]{2,1,0:T(8,128)(2,1)S(1)} all-to-all(bf16[16,16,512]{2,1,0:T(8,128)(2,1)S(1)} %broadcast_in_dim.3), channel_id=1, replica_groups=mesh['wide'=8,'rest'=2,'pair'=2] {'wide','rest'}, dimensions={0} | all-to-all | bytes 524288 | tf_op jit(solution)/shard_map/all_to_all | solution.py:287
  49.7 0.1 collective-permute-start.3
  49.8 1.6 %mix.2.refs_0_ = bf16[2048,1024]{1,0:T(8,128)(2,1)} custom-call(s32[1]{0:T(128)} %bitcast.place, bf16[2048,128]{1,0:T(8,128)(2,1)S(1)} %combine.1, bf16[128,512]{1,0:T(8,128)(2,1)S(1)} %bitcast.6), custom_call_target="tpu_custom_call" | custom-call | flops 268435456 | bytes 2621440 | tf_op jit(solution)/shard_map/mix/pallas_call | solution.py:195
  51.4 0.0 collective-permute-done.3.slot_out
  51.4 1.6 %mix.3 = bf16[2048,1024]{1,0:T(8,128)(2,1)} custom-call(s32[1]{0:T(128)S(6)} %sub.3.place, bf16[2048,128]{1,0:T(8,128)(2,1)S(1)} %combine.1, bf16[128,512]{1,0:T(8,128)(2,1)S(1)} %collective-permute-done.3.slot_out, bf16[2048,1024]{1,0:T(8,128)(2,1)} %mix.2.refs_0_), custom_call_target="tpu_custom_call", output_to_operand_aliasing={{}: (3, {})} | custom-call | flops 268435456 | bytes 2621440 | tf_op jit(solution)/shard_map/mix/pallas_call | solution.py:195
  (3 shorter events, 0.1 us)
Async XLA Ops:
  4.5 1.5 %collective-permute-start = (bf16[128,640]{1,0:T(8,128)(2,1)S(1)}, bf16[128,640]{1,0:T(8,128)(2,1)S(1)}, u32[]{:S(2)}, u32[]{:S(2)}) collective-permute-start(bf16[128,640]{1,0:T(8,128)(2,1)S(1)} %get-tuple-element.14), channel_id=1, source_target_pairs={{0,1},{1,0},{2,3},{3,2},{4,5},{5,4},{6,7},{7,6},{8,9},{9,8},{10,11... | collective-permute-start | bytes 491528 | tf_op jit(solution)/shard_map/ppermute | solution.py:209
  7.1 19.9 %all-to-all-start = ((bf16[16,16,640]{2,1,0:T(8,128)(2,1)}), bf16[16,16,640]{2,1,0:T(8,128)(2,1)S(1)}, u32[]{:S(2)}, u32[]{:S(2)}) async-start(bf16[16,16,640]{2,1,0:T(8,128)(2,1)} %bitcast.1), calls=%async_computation | async-start | bytes 655360 | tf_op jit(solution)/shard_map/all_to_all | solution.py:249
  27.3 1.2 %collective-permute-start.1 = (bf16[16,512]{1,0:T(8,128)(2,1)S(1)}, bf16[16,512]{1,0:T(8,128)(2,1)S(1)}, u32[]{:S(2)}, u32[]{:S(2)}) collective-permute-start(bf16[16,512]{1,0:T(8,128)(2,1)S(1)} %finish.1.mine), channel_id=1, source_target_pairs={{0,1},{1,0},{2,3},{3,2},{4,5},{5,4},{6,7},{7,6},{8,9},{9,8},{10,11... | collective-permute-start | bytes 49160 | tf_op jit(solution)/shard_map/ppermute | solution.py:209
  34.9 1.2 %collective-permute-start.2 = (bf16[16,512]{1,0:T(8,128)(2,1)S(1)}, bf16[16,512]{1,0:T(8,128)(2,1)S(1)}, u32[]{:S(2)}, u32[]{:S(2)}) collective-permute-start(bf16[16,512]{1,0:T(8,128)(2,1)S(1)} %get-tuple-element.16), channel_id=1, source_target_pairs={{0,1},{1,0},{2,3},{3,2},{4,5},{5,4},{6,7},{7,6},{8,9},{9,8},{10,11... | collective-permute-start | bytes 49160 | tf_op jit(solution)/shard_map/ppermute | solution.py:209
  49.7 1.7 %collective-permute-start.3 = (bf16[128,512]{1,0:T(8,128)(2,1)S(1)}, bf16[128,512]{1,0:T(8,128)(2,1)S(1)}, u32[]{:S(2)}, u32[]{:S(2)}) collective-permute-start(bf16[128,512]{1,0:T(8,128)(2,1)S(1)} %bitcast.5), channel_id=1, source_target_pairs={{0,1},{1,0},{2,3},{3,2},{4,5},{5,4},{6,7},{7,6},{8,9},{9,8},{10,11... | collective-permute-start | bytes 393224 | tf_op jit(solution)/shard_map/ppermute | solution.py:209

commit v5 on v4

v5 whole, which is shorter than its diff:
```python
import math

import jax
import jax.numpy as jnp
from jax import lax
from jax.experimental import pallas as pl
from jax.experimental.pallas import tpu as pltpu
from jax.sharding import Mesh, PartitionSpec as P

SLOT_PER = 4
SIDE = 128
CHUNK = 256
F32 = jnp.float32
BF16 = jnp.bfloat16
VMEM = pl.BlockSpec(memory_space=pltpu.VMEM)
SMEM = pl.BlockSpec(memory_space=pltpu.SMEM)
HBM = pl.BlockSpec(memory_space=pltpu.HBM)
MIB = 1024 * 1024


def params(mib):
    return pltpu.CompilerParams(vmem_limit_bytes=mib * MIB)


def cost(flops, moved, transcendentals=0):
    return pl.CostEstimate(flops=flops, bytes_accessed=moved, transcendentals=transcendentals)


def in_hbm(value):
    return pltpu.with_memory_space_constraint(value, pltpu.HBM)


def dot(lhs, rhs):
    return jnp.dot(lhs, rhs, preferred_element_type=F32)


def side_state(peak, total):
    lane = lax.broadcasted_iota(jnp.int32, (peak.shape[0], SIDE), 1)
    return jnp.where(lane == 0, peak, jnp.where(lane == 1, total, 0.0))


def side_message(peak, total):
    lane = lax.broadcasted_iota(jnp.int32, (peak.shape[0], SIDE), 1)
    out = jnp.zeros((peak.shape[0], SIDE), F32)
    for index, value in enumerate((peak, total)):
        for piece in range(3):
            part = value.astype(BF16).astype(F32)
            out = jnp.where(lane == 3 * index + piece, part, out)
            value = value - part
    return out.astype(BF16)


def read_message(side):
    value = side.astype(F32)
    return (
        value[:, 0:1] + value[:, 1:2] + value[:, 2:3],
        value[:, 3:4] + value[:, 4:5] + value[:, 5:6],
    )


def gather_kernel(place, tokens, slot_params, logits, keep, side, send, held, table, sems):
    chunks = tokens.shape[0] // CHUNK
    slots = slot_params.shape[1]
    spans = [pl.ds(i * CHUNK, CHUNK) for i in range(chunks)]
    table_copy = pltpu.make_async_copy(slot_params, table, sems.at[chunks])
    table_copy.start()
    copies = [pltpu.make_async_copy(tokens.at[span], held.at[span], sems.at[i]) for i, span in enumerate(spans)]
    for copy in copies:
        copy.start()
    high = jnp.full((8, slots), -jnp.inf, F32)
    table_copy.wait()
    for i, span in enumerate(spans):
        copies[i].wait()
        part = dot(held[span, :], table[...])
        logits[span, :] = part
        high = jnp.maximum(high, jnp.max(part.reshape(CHUNK // 8, 8, slots), axis=0))
    peak = jnp.max(high, axis=0, keepdims=True)
    total = jnp.zeros((8, slots), F32)
    turned = []
    for span in spans:
        weights = jnp.exp(logits[span, :] - peak)
        total = total + jnp.sum(weights.reshape(CHUNK // 8, 8, slots), axis=0)
        turned.append(weights.T.astype(BF16))
    sums = dot(jnp.concatenate(turned, axis=1), held[...])
    total = jnp.sum(total, axis=0, keepdims=True)
    peak = jnp.broadcast_to(peak, (8, slots)).T[:, 0:1]
    total = jnp.broadcast_to(total, (8, slots)).T[:, 0:1]
    half = sums.shape[1] // 2
    left, right = sums[:, :half], sums[:, half:]
    first = place[0] == 0
    keep[...] = jnp.where(first, left, right)
    side[...] = side_state(peak, total)
    send[:, :half] = jnp.where(first, right, left).astype(BF16)
    send[:, half:] = side_message(peak, total)


def pair_kernel(keep, side, received, combine, send):
    width = keep.shape[1]
    peak_mine, total_mine = side[:, 0:1], side[:, 1:2]
    peak_other, total_other = read_message(received[:, width:])
    peak = jnp.maximum(peak_mine, peak_other)
    scale_mine, scale_other = jnp.exp(peak_mine - peak), jnp.exp(peak_other - peak)
    total = total_mine * scale_mine + total_other * scale_other
    sums = keep[...] * scale_mine + received[:, :width].astype(F32) * scale_other
    send[:, :width] = sums.astype(BF16)
    send[:, width:] = side_message(peak, total)


def add_parts(parts, width):
    states = [read_message(part[:, width:]) for part in parts]
    peak = states[0][0]
    for other, _ in states[1:]:
        peak = jnp.maximum(peak, other)
    total = jnp.zeros_like(peak)
    sums = jnp.zeros((parts[0].shape[0], width), F32)
    for part, (peak_other, total_other) in zip(parts, states):
        scale = jnp.exp(peak_other - peak)
        total = total + total_other * scale
        sums = sums + part[:, :width].astype(F32) * scale
    return sums, peak, total


def merge_kernel(received, send):
    width = send.shape[1] - SIDE
    sums, peak, total = add_parts([received[g] for g in range(received.shape[0])], width)
    send[:, :width] = sums.astype(BF16)
    send[:, width:] = side_message(peak, total)


def finish_kernel(place, *refs):
    slot_in = refs[-1]
    half = slot_in.shape[1] // 2
    parts = (len(refs) - 2) // 2
    means = []
    for side in range(2):
        sums, _, total = add_parts([ref[...] for ref in refs[side * parts : (side + 1) * parts]], half)
        means.append((sums / total).astype(BF16))
    first = place[0] == 0
    slot_in[:, :half] = jnp.where(first, means[0], means[1])
    slot_in[:, half:] = jnp.where(first, means[1], means[0])


def load_kernel(after, weights, held, sems):
    copies = [pltpu.make_async_copy(weights.at[e], held.at[e], sems.at[e]) for e in range(held.shape[0])]
    for copy in copies:
        copy.start()
    for copy in copies:
        copy.wait()


def expert_kernel(place, slot_in, early, expert_in, expert_out, keep, send, in_held, out_held, sems):
    experts, ahead = expert_in.shape[0], early.shape[0]
    in_copies, out_copies = {}, {}
    for e in range(experts):
        if e >= ahead:
            in_copies[e] = pltpu.make_async_copy(expert_in.at[e], in_held.at[e - ahead], sems.at[0, e])
            in_copies[e].start()
        out_copies[e] = pltpu.make_async_copy(expert_out.at[e], out_held.at[e], sems.at[1, e])
        out_copies[e].start()
    row = lax.broadcasted_iota(jnp.int32, (slot_in.shape[0], 1), 0)
    result = jnp.zeros((slot_in.shape[0], expert_out.shape[2]), F32)
    hidden = [jax.nn.gelu(dot(slot_in[...], early[e])).astype(BF16) for e in range(ahead)]
    for e in range(experts):
        if e >= ahead:
            in_copies[e].wait()
            hidden.append(jax.nn.gelu(dot(slot_in[...], in_held[e - ahead])).astype(BF16))
        out_copies[e].wait()
        result = jnp.where(row // SLOT_PER == e, dot(hidden[e], out_held[e]), result)
    half = keep.shape[1]
    left, right = result[:, :half], result[:, half:]
    first = place[0] == 0
    keep[...] = jnp.where(first, left, right)
    send[...] = jnp.where(first, right, left).astype(BF16)


def combine_kernel(logits, after, combine):
    value = logits[...]
    weights = jnp.exp(value - jnp.max(value, axis=1, keepdims=True))
    combine[...] = (weights / jnp.sum(weights, axis=1, keepdims=True)).astype(BF16)


def mix_kernel(place, combine, slot_out, *refs):
    mixed, held, sems = refs[-3:]
    width = slot_out.shape[1]
    block = held.shape[0] // sems.shape[0]
    columns = pl.ds(pl.multiple_of(place[0] * width, width), width)
    copies = []
    for i in range(sems.shape[0]):
        rows = pl.ds(i * block, block)
        held[rows, :] = dot(combine[rows, :], slot_out[...]).astype(BF16)
        copies.append(pltpu.make_async_copy(held.at[rows], mixed.at[rows, columns], sems.at[i]))
        copies[-1].start()
    for copy in copies:
        copy.wait()


def mix_call(which, combine, slot_out, before=None):
    tokens, slots = combine.shape
    width = slot_out.shape[1]
    more = [] if before is None else [before]
    return pl.pallas_call(
        mix_kernel,
        out_shape=jax.ShapeDtypeStruct((tokens, 2 * width), BF16),
        in_specs=[SMEM, VMEM, VMEM] + [HBM] * len(more),
        out_specs=HBM,
        scratch_shapes=[pltpu.VMEM((tokens, width), BF16), pltpu.SemaphoreType.DMA((8,))],
        input_output_aliases={3: 0} if more else {},
        cost_estimate=cost(2 * tokens * slots * width, 2 * tokens * (width + slots)),
        compiler_params=params(16),
        name="mix",
    )(which, combine, slot_out, *more)


def move(value, axes, offsets):
    sizes = [lax.axis_size(axis) for axis in axes]
    moves = []
    for index in range(math.prod(sizes)):
        source, target, stride = index, 0, 1
        for size, offset in zip(reversed(sizes), reversed(offsets)):
            target += (source % size + offset) % size * stride
            source //= size
            stride *= size
        moves.append((index, target))
    return lax.ppermute(value, axes, moves)


def swap_pair(value):
    return move(value, ("pair",), (1,))


def shards(tokens, slot_params, expert_in, expert_out):
    count, model = tokens.shape
    slots = slot_params.shape[1]
    groups, rest = lax.axis_size("wide"), lax.axis_size("rest")
    rows = slots // groups
    half = model // 2
    place = lax.axis_index("pair").astype(jnp.int32).reshape(1)
    any_space = pl.BlockSpec(memory_space=pl.ANY)

    logits, keep, side, send = pl.pallas_call(
        gather_kernel,
        out_shape=(
            jax.ShapeDtypeStruct((count, slots), F32),
            jax.ShapeDtypeStruct((slots, half), F32),
            jax.ShapeDtypeStruct((slots, SIDE), F32),
            jax.ShapeDtypeStruct((slots, half + SIDE), BF16),
        ),
        in_specs=[SMEM, HBM, HBM],
        out_specs=(VMEM,) * 4,
        scratch_shapes=[
            pltpu.VMEM((count, model), BF16),
            pltpu.VMEM((model, slots), BF16),
            pltpu.SemaphoreType.DMA((count // CHUNK + 1,)),
        ],
        compiler_params=params(40),
        name="gather",
    )(place, in_hbm(tokens), in_hbm(slot_params))
    received = swap_pair(send)
    combine = pl.pallas_call(
        combine_kernel,
        out_shape=jax.ShapeDtypeStruct((count, slots), BF16),
        in_specs=[VMEM, any_space],
        out_specs=VMEM,
        cost_estimate=cost(8 * count * slots, 6 * count * slots, count * slots),
        compiler_params=params(16),
        name="combine",
    )(logits, send)
    send = pl.pallas_call(
        pair_kernel,
        out_shape=jax.ShapeDtypeStruct((slots, half + SIDE), BF16),
        in_specs=[VMEM] * 3 + [any_space],
        out_specs=VMEM,
        compiler_params=params(16),
        name="pair",
    )(keep, side, received, combine)
    received = lax.all_to_all(send.reshape(groups, rows, -1), "wide", split_axis=0, concat_axis=0, tiled=True)
    send = pl.pallas_call(
        merge_kernel,
        out_shape=jax.ShapeDtypeStruct((rows, half + SIDE), BF16),
        in_specs=[VMEM],
        out_specs=VMEM,
        compiler_params=params(16),
        name="merge",
    )(received)
    axes = ("rest", "pair")
    mine = [send] + [move(send, axes, (r, 0)) for r in range(1, rest)]
    others = [move(send, axes, (r, 1)) for r in reversed(range(rest))]
    ahead = expert_in.shape[0] // 2
    early = pl.pallas_call(
        load_kernel,
        out_shape=jax.ShapeDtypeStruct((ahead,) + expert_in.shape[1:], BF16),
        in_specs=[any_space, HBM],
        out_specs=VMEM,
        scratch_shapes=[pltpu.SemaphoreType.DMA((ahead,))],
        cost_estimate=cost(0, expert_in.size),
        compiler_params=params(16),
        name="load",
    )(send, in_hbm(expert_in))
    slot_in = pl.pallas_call(
        finish_kernel,
        out_shape=jax.ShapeDtypeStruct((rows, model), BF16),
        in_specs=[SMEM] + [VMEM] * (2 * rest) + [any_space],
        out_specs=VMEM,
        compiler_params=params(16),
        name="finish",
    )(place, *mine, *others, early)
    keep, send = pl.pallas_call(
        expert_kernel,
        out_shape=(jax.ShapeDtypeStruct((rows, half), F32), jax.ShapeDtypeStruct((rows, half), BF16)),
        in_specs=[SMEM, VMEM, VMEM, HBM, HBM],
        out_specs=(VMEM, VMEM),
        scratch_shapes=[
            pltpu.VMEM((expert_in.shape[0] - ahead,) + expert_in.shape[1:], BF16),
            pltpu.VMEM(expert_out.shape, BF16),
            pltpu.SemaphoreType.DMA((2, expert_in.shape[0])),
        ],
        compiler_params=params(40),
        name="experts",
    )(place, slot_in, early, in_hbm(expert_in), in_hbm(expert_out))
    partial = keep + swap_pair(send).astype(F32)
    travelling = partial.astype(BF16)
    for r in range(1, rest):
        partial = partial + move(travelling, ("rest",), (r,)).astype(F32)
    block = jnp.broadcast_to(partial.astype(BF16), (groups, rows, half))
    slot_out = lax.all_to_all(block, "wide", split_axis=0, concat_axis=0, tiled=True).reshape(slots, half)
    other = swap_pair(slot_out)
    mixed = mix_call(place, combine, slot_out)
    return mix_call(1 - place, combine, other, mixed)


def solution(mesh):
    wide, narrow = mesh.shape["wide"], mesh.shape["narrow"]
    cut = Mesh(mesh.devices.reshape(wide, narrow // 2, 2), ("wide", "rest", "pair"))
    narrow_axes = ("rest", "pair")
    return jax.shard_map(
        shards,
        mesh=cut,
        in_specs=(
            P(("wide",) + narrow_axes, None),
            P(),
            P("wide", None, narrow_axes),
            P("wide", narrow_axes, None),
        ),
        out_specs=P(("wide",) + narrow_axes, None),
        check_vma=False,
    )
```

time: 53.3 us -> 51.2 us (0.961)
  blocking collectives: 13.5 us -> 24.8 us
  waiting for transfers between devices: 12.2 us -> 5.78 us
  starting transfers between devices: 9.11 us -> 3.28 us
  Pallas kernels: 18.1 us -> 16.9 us
    all_to_all x1 -> x2, blocking collectives: 13.5 us -> 24.8 us  [the longest x1 14.7 us: shards(): lax.all_to_all(send.reshape(groups, rows, -1), 'wide', split_axis=0, conc...]
    all_to_all x1 -> x0, waiting for transfers between devices: 8.96 us -> none  [shards(): lax.all_to_all(send.reshape(groups * rest, rows, -1), ('wide', 'rest'), s...]
    all_to_all x1 -> x0, starting transfers between devices: 8.23 us -> none  [shards(): lax.all_to_all(send.reshape(groups * rest, rows, -1), ('wide', 'rest'), s...]
    ppermute x4 -> x7, waiting for transfers between devices: 3.22 us -> 5.78 us  [move(): return lax.ppermute(value, axes, moves)]
    ppermute x4 -> x7, starting transfers between devices: 0.88 us -> 3.28 us  [move(): return lax.ppermute(value, axes, moves)]
    pallas_call x1, Pallas kernels: 2.66 us -> 0.64 us  [shards(): pl.pallas_call(combine_kernel, out_shape=jax.ShapeDtypeStruct((count, slo...]
    pallas_call x3 -> x5, Pallas kernels: 5.86 us -> 7.46 us  [the longest x1 4.38 us: shards(): pl.pallas_call(gather_kernel, out_shape=(jax.ShapeDtypeStruct((count, slo...]
    pallas_call x1, Pallas kernels: 6.37 us -> 5.67 us  [shards(): pl.pallas_call(expert_kernel, out_shape=(jax.ShapeDtypeStruct((rows, half...]
  transfers between devices with their start and end apart: 5 -> 7, of which waited for: 4 -> 4; matrix products, arithmetic and copies ran while one was open for 0% -> 0% of each run, Pallas kernels for 8% -> 9%
where the time goes in v5:
time: 51.2 us; the launch traced here: 51 us
  blocking collectives  24.8 us (48%)
  Pallas kernels  16.9 us (33%)
  waiting for transfers between devices  5.78 us (11%)
  starting transfers between devices  3.28 us (6%)
    all_to_all x1, blocking collectives, shards(): lax.all_to_all(send.reshape(groups, rows, -1), 'wide', split_axis=0, conc...  14.7 us
    all_to_all x1, blocking collectives, shards(): lax.all_to_all(block, 'wide', split_axis=0, concat_axis=0, tiled=True)  10.1 us
    ppermute x7, waiting for transfers between devices, move(): return lax.ppermute(value, axes, moves)  5.78 us
    pallas_call x1, Pallas kernels, shards(): pl.pallas_call(expert_kernel, out_shape=(jax.ShapeDtypeStruct((rows, half...  5.67 us
    pallas_call x1, Pallas kernels, shards(): pl.pallas_call(gather_kernel, out_shape=(jax.ShapeDtypeStruct((count, slo...  4.38 us
    ppermute x7, starting transfers between devices, move(): return lax.ppermute(value, axes, moves)  3.28 us
    pallas_call x2, Pallas kernels, mix_call(): pl.pallas_call(mix_kernel, out_shape=jax.ShapeDtypeStruct((tokens, 2 * wi...  3.17 us
    pallas_call x1, Pallas kernels, shards(): pl.pallas_call(load_kernel, out_shape=jax.ShapeDtypeStruct((ahead,) + exp...  2.24 us
  transfers between devices with their start and end apart: 7, of which 4 were waited for; matrix products, arithmetic and copies ran while one was open for 0% of the time, Pallas kernels for 9%

profile of v5, /device:TPU:0, one launch (start us, length us, event | category | flops | bytes accessed | tf_op | source)
XLA Modules:
  0.0 51.0 jit_solution(3600173176229245974)
XLA Ops:
  0.0 4.4 %gather.1 = (f32[2048,128]{1,0:T(8,128)S(1)}, f32[128,512]{1,0:T(8,128)S(1)}, f32[128,128]{1,0:T(8,128)S(1)}, bf16[128,640]{1,0:T(8,128)(2,1)S(1)}) custom-call(s32[1]{0:T(128)} %bitcast.place, bf16[2048,1024]{1,0:T(8,128)(2,1)} %tokens.1, bf16[1024,128]{1,0:T(8,128)(2,1)} %slot_params.1), custom_call_target="tpu_custom_call" | custom-call | tf_op jit(solution)/shard_map/gather/pallas_call | solution.py:240
  4.4 0.5 %collective-permute-start = (bf16[128,640]{1,0:T(8,128)(2,1)S(1)}, bf16[128,640]{1,0:T(8,128)(2,1)S(1)}, u32[]{:S(2)}, u32[]{:S(2)}) collective-permute-start(bf16[128,640]{1,0:T(8,128)(2,1)S(1)} %get-tuple-element.12.after), channel_id=1, source_target_pairs={{0,1},{1,0},{2,3},{3,2},{4,5},{5,4},{6,7},{7,6},{8,9},{9,8},{10,11... | collective-permute-start | bytes 491528 | tf_op jit(solution)/shard_map/ppermute | solution.py:224
  4.9 0.6 %combine.1 = bf16[2048,128]{1,0:T(8,128)(2,1)S(1)} custom-call(f32[2048,128]{1,0:T(8,128)S(1)} %get-tuple-element.11.logits, bf16[128,640]{1,0:T(8,128)(2,1)S(1)} %get-tuple-element.12.after), custom_call_target="tpu_custom_call" | custom-call | flops 2097152 | bytes 1572864 | tf_op jit(solution)/shard_map/combine/pallas_call | solution.py:259
  5.5 0.4 collective-permute-done.received
  5.9 0.3 pair.1
  6.3 14.7 %all_to_all.10.received = bf16[8,16,640]{2,1,0:T(8,128)(2,1)S(1)} all-to-all(bf16[8,16,640]{2,1,0:T(8,128)(2,1)S(1)} %bitcast.3), channel_id=1, replica_groups=mesh['wide'=8,'rest'=2,'pair'=2] {'wide'}, dimensions={0} | all-to-all | bytes 327680 | tf_op jit(solution)/shard_map/all_to_all | solution.py:276
  21.0 0.3 merge.1.after.refs_0_
  21.3 0.0 collective-permute-start.3
  21.3 1.6 %collective-permute-start.2 = (bf16[16,640]{1,0:T(8,128)(2,1)S(1)}, bf16[16,640]{1,0:T(8,128)(2,1)S(1)}, u32[]{:S(2)}, u32[]{:S(2)}) collective-permute-start(bf16[16,640]{1,0:T(8,128)(2,1)S(1)} %merge.1.after.refs_0_), channel_id=1, source_target_pairs={{0,3},{1,2},{2,1},{3,0},{4,7},{5,6},{6,5},{7,4},{8,11},{9,10},{10,... | collective-permute-start | bytes 61448 | tf_op jit(solution)/shard_map/ppermute | solution.py:224
  23.0 0.5 collective-permute-start.1
  23.5 2.2 %load.1.refs_4_.early = bf16[2,1024,1024]{2,1,0:T(8,128)(2,1)S(1)} custom-call(bf16[16,640]{1,0:T(8,128)(2,1)S(1)} %merge.1.after.refs_0_, bf16[4,1024,1024]{2,1,0:T(8,128)(2,1)} %expert_in.1), custom_call_target="tpu_custom_call" | custom-call | bytes 4194304 | tf_op jit(solution)/shard_map/load/pallas_call | solution.py:289
  25.7 0.0 collective-permute-done.3.refs_3_
  25.7 0.0 collective-permute-done.2.refs_2_
  25.7 1.0 %collective-permute-done.1.refs_1_ = bf16[16,640]{1,0:T(8,128)(2,1)S(1)} collective-permute-done((bf16[16,640]{1,0:T(8,128)(2,1)S(1)}, bf16[16,640]{1,0:T(8,128)(2,1)S(1)}, u32[]{:S(2)}, u32[]{:S(2)}) %collective-permute-start.1) | collective-permute-done | bytes 20512 | tf_op jit(solution)/shard_map/ppermute | solution.py:224
  26.7 0.2 finish.1.slot_in
  27.0 5.7 %experts.1 = (f32[16,512]{1,0:T(8,128)S(1)}, bf16[16,512]{1,0:T(8,128)(2,1)S(1)}) custom-call(s32[1]{0:T(128)} %bitcast.place, bf16[16,1024]{1,0:T(8,128)(2,1)S(1)} %finish.1.slot_in, bf16[2,1024,1024]{2,1,0:T(8,128)(2,1)S(1)} %load.1.refs_4_.early, bf16[4,1024,1024]{2,1,0:T(8,128)(2,1)} %expert_in.1, bf16[4,1024,1024]{2,1,0:T(8,128)(2,1)} %expert_out.1), custom_call_target="tpu_custom_call" | custom-call | tf_op jit(solution)/shard_map/experts/pallas_call | solution.py:307
  32.7 0.1 collective-permute-start.4
  32.7 1.2 %collective-permute-done.4 = bf16[16,512]{1,0:T(8,128)(2,1)S(1)} collective-permute-done((bf16[16,512]{1,0:T(8,128)(2,1)S(1)}, bf16[16,512]{1,0:T(8,128)(2,1)S(1)}, u32[]{:S(2)}, u32[]{:S(2)}) %collective-permute-start.4) | collective-permute-done | bytes 16416 | tf_op jit(solution)/shard_map/ppermute | solution.py:224
  33.9 0.5 %collective-permute-start.5 = (bf16[16,512]{1,0:T(8,128)(2,1)S(1)}, bf16[16,512]{1,0:T(8,128)(2,1)S(1)}, u32[]{:S(2)}, u32[]{:S(2)}) collective-permute-start(bf16[16,512]{1,0:T(8,128)(2,1)S(1)} %fusion), channel_id=1, source_target_pairs={{0,2},{2,0},{1,3},{3,1},{4,6},{6,4},{5,7},{7,5},{8,10},{10,8},{9,1... | collective-permute-start | bytes 49160 | tf_op jit(solution)/shard_map/ppermute | solution.py:224
  34.4 3.2 %collective-permute-done.5 = bf16[16,512]{1,0:T(8,128)(2,1)S(1)} collective-permute-done((bf16[16,512]{1,0:T(8,128)(2,1)S(1)}, bf16[16,512]{1,0:T(8,128)(2,1)S(1)}, u32[]{:S(2)}, u32[]{:S(2)}) %collective-permute-start.5) | collective-permute-done | bytes 16416 | tf_op jit(solution)/shard_map/ppermute | solution.py:224
  37.7 10.1 %all_to_all.11 = bf16[8,16,512]{2,1,0:T(8,128)(2,1)S(1)} all-to-all(bf16[8,16,512]{2,1,0:T(8,128)(2,1)S(1)} %broadcast_in_dim.3), channel_id=1, replica_groups=mesh['wide'=8,'rest'=2,'pair'=2] {'wide'}, dimensions={0} | all-to-all | bytes 262144 | tf_op jit(solution)/shard_map/all_to_all | solution.py:325
  47.8 0.0 collective-permute-start.6
  47.8 1.6 %mix.2.refs_0_ = bf16[2048,1024]{1,0:T(8,128)(2,1)} custom-call(s32[1]{0:T(128)} %bitcast.place, bf16[2048,128]{1,0:T(8,128)(2,1)S(1)} %combine.1, bf16[128,512]{1,0:T(8,128)(2,1)S(1)} %bitcast.5), custom_call_target="tpu_custom_call" | custom-call | flops 268435456 | bytes 2621440 | tf_op jit(solution)/shard_map/mix/pallas_call | solution.py:201
  49.4 0.0 collective-permute-done.6.slot_out
  49.4 1.6 %mix.3 = bf16[2048,1024]{1,0:T(8,128)(2,1)} custom-call(s32[1]{0:T(128)S(6)} %sub.3.place, bf16[2048,128]{1,0:T(8,128)(2,1)S(1)} %combine.1, bf16[128,512]{1,0:T(8,128)(2,1)S(1)} %collective-permute-done.6.slot_out, bf16[2048,1024]{1,0:T(8,128)(2,1)} %mix.2.refs_0_), custom_call_target="tpu_custom_call", output_to_operand_aliasing={{}: (3, {})} | custom-call | flops 268435456 | bytes 2621440 | tf_op jit(solution)/shard_map/mix/pallas_call | solution.py:201
  (3 shorter events, 0.0 us)
Async XLA Ops:
  4.4 1.5 %collective-permute-start = (bf16[128,640]{1,0:T(8,128)(2,1)S(1)}, bf16[128,640]{1,0:T(8,128)(2,1)S(1)}, u32[]{:S(2)}, u32[]{:S(2)}) collective-permute-start(bf16[128,640]{1,0:T(8,128)(2,1)S(1)} %get-tuple-element.12.after), channel_id=1, source_target_pairs={{0,1},{1,0},{2,3},{3,2},{4,5},{5,4},{6,7},{7,6},{8,9},{9,8},{10,11... | collective-permute-start | bytes 491528 | tf_op jit(solution)/shard_map/ppermute | solution.py:224
  21.3 4.4 %collective-permute-start.3 = (bf16[16,640]{1,0:T(8,128)(2,1)S(1)}, bf16[16,640]{1,0:T(8,128)(2,1)S(1)}, u32[]{:S(2)}, u32[]{:S(2)}) collective-permute-start(bf16[16,640]{1,0:T(8,128)(2,1)S(1)} %merge.1.after.refs_0_), channel_id=1, source_target_pairs={{0,1},{1,0},{2,3},{3,2},{4,5},{5,4},{6,7},{7,6},{8,9},{9,8},{10,11... | collective-permute-start | bytes 61448 | tf_op jit(solution)/shard_map/ppermute | solution.py:224
  21.3 4.4 %collective-permute-start.2 = (bf16[16,640]{1,0:T(8,128)(2,1)S(1)}, bf16[16,640]{1,0:T(8,128)(2,1)S(1)}, u32[]{:S(2)}, u32[]{:S(2)}) collective-permute-start(bf16[16,640]{1,0:T(8,128)(2,1)S(1)} %merge.1.after.refs_0_), channel_id=1, source_target_pairs={{0,3},{1,2},{2,1},{3,0},{4,7},{5,6},{6,5},{7,4},{8,11},{9,10},{10,... | collective-permute-start | bytes 61448 | tf_op jit(solution)/shard_map/ppermute | solution.py:224
  23.0 3.8 %collective-permute-start.1 = (bf16[16,640]{1,0:T(8,128)(2,1)S(1)}, bf16[16,640]{1,0:T(8,128)(2,1)S(1)}, u32[]{:S(2)}, u32[]{:S(2)}) collective-permute-start(bf16[16,640]{1,0:T(8,128)(2,1)S(1)} %merge.1.after.refs_0_), channel_id=1, source_target_pairs={{0,2},{1,3},{2,0},{3,1},{4,6},{5,7},{6,4},{7,5},{8,10},{9,11},{10,... | collective-permute-start | bytes 61448 | tf_op jit(solution)/shard_map/ppermute | solution.py:224
  32.7 1.2 %collective-permute-start.4 = (bf16[16,512]{1,0:T(8,128)(2,1)S(1)}, bf16[16,512]{1,0:T(8,128)(2,1)S(1)}, u32[]{:S(2)}, u32[]{:S(2)}) collective-permute-start(bf16[16,512]{1,0:T(8,128)(2,1)S(1)} %get-tuple-element.16), channel_id=1, source_target_pairs={{0,1},{1,0},{2,3},{3,2},{4,5},{5,4},{6,7},{7,6},{8,9},{9,8},{10,11... | collective-permute-start | bytes 49160 | tf_op jit(solution)/shard_map/ppermute | solution.py:224
  33.9 3.7 %collective-permute-start.5 = (bf16[16,512]{1,0:T(8,128)(2,1)S(1)}, bf16[16,512]{1,0:T(8,128)(2,1)S(1)}, u32[]{:S(2)}, u32[]{:S(2)}) collective-permute-start(bf16[16,512]{1,0:T(8,128)(2,1)S(1)} %fusion), channel_id=1, source_target_pairs={{0,2},{2,0},{1,3},{3,1},{4,6},{6,4},{5,7},{7,5},{8,10},{10,8},{9,1... | collective-permute-start | bytes 49160 | tf_op jit(solution)/shard_map/ppermute | solution.py:224
  47.8 1.6 %collective-permute-start.6 = (bf16[128,512]{1,0:T(8,128)(2,1)S(1)}, bf16[128,512]{1,0:T(8,128)(2,1)S(1)}, u32[]{:S(2)}, u32[]{:S(2)}) collective-permute-start(bf16[128,512]{1,0:T(8,128)(2,1)S(1)} %bitcast.4), channel_id=1, source_target_pairs={{0,1},{1,0},{2,3},{3,2},{4,5},{5,4},{6,7},{7,6},{8,9},{9,8},{10,11... | collective-permute-start | bytes 393224 | tf_op jit(solution)/shard_map/ppermute | solution.py:224

commit v6 on v5

--- a/solution.py
+++ b/solution.py
@@ -1,3 +1,4 @@
+import functools
 import math
 
 import jax
@@ -9,7 +10,7 @@
 
 SLOT_PER = 4
 SIDE = 128
-CHUNK = 256
+TOKEN_GROUPS = 4
 F32 = jnp.float32
 BF16 = jnp.bfloat16
 VMEM = pl.BlockSpec(memory_space=pltpu.VMEM)
@@ -58,40 +59,54 @@
     )
 
 
-def gather_kernel(place, tokens, slot_params, logits, keep, side, send, held, table, sems):
-    chunks = tokens.shape[0] // CHUNK
+def gather_kernel(
+    place, tokens, slot_params, expert_in, logits, keep, side, send, early, held, table, sums, sems, early_sems
+):
     slots = slot_params.shape[1]
-    spans = [pl.ds(i * CHUNK, CHUNK) for i in range(chunks)]
-    table_copy = pltpu.make_async_copy(slot_params, table, sems.at[chunks])
+    groups = sums.shape[0]
+    size = tokens.shape[0] // groups
+    spans = [pl.ds(g * size, size) for g in range(groups)]
+    table_copy = pltpu.make_async_copy(slot_params, table, sems.at[groups])
     table_copy.start()
-    copies = [pltpu.make_async_copy(tokens.at[span], held.at[span], sems.at[i]) for i, span in enumerate(spans)]
+    copies = [pltpu.make_async_copy(tokens.at[span], held.at[span], sems.at[g]) for g, span in enumerate(spans)]
     for copy in copies:
         copy.start()
-    high = jnp.full((8, slots), -jnp.inf, F32)
+    early_copies = [
+        pltpu.make_async_copy(expert_in.at[e], early.at[e], early_sems.at[e]) for e in range(early.shape[0])
+    ]
+    for copy in early_copies:
+        copy.start()
     table_copy.wait()
-    for i, span in enumerate(spans):
-        copies[i].wait()
-        part = dot(held[span, :], table[...])
-        logits[span, :] = part
-        high = jnp.maximum(high, jnp.max(part.reshape(CHUNK // 8, 8, slots), axis=0))
-    peak = jnp.max(high, axis=0, keepdims=True)
-    total = jnp.zeros((8, slots), F32)
-    turned = []
-    for span in spans:
-        weights = jnp.exp(logits[span, :] - peak)
-        total = total + jnp.sum(weights.reshape(CHUNK // 8, 8, slots), axis=0)
-        turned.append(weights.T.astype(BF16))
-    sums = dot(jnp.concatenate(turned, axis=1), held[...])
-    total = jnp.sum(total, axis=0, keepdims=True)
-    peak = jnp.broadcast_to(peak, (8, slots)).T[:, 0:1]
-    total = jnp.broadcast_to(total, (8, slots)).T[:, 0:1]
-    half = sums.shape[1] // 2
-    left, right = sums[:, :half], sums[:, half:]
+    parts, peaks, totals = [], [], []
+    for g in range(groups + 1):
+        if g < groups:
+            copies[g].wait()
+            parts.append(dot(held[spans[g], :], table[...]))
+            logits[spans[g], :] = parts[g]
+            peaks.append(jnp.max(parts[g], axis=0, keepdims=True))
+        if g > 0:
+            weights = jnp.exp(parts[g - 1] - peaks[g - 1])
+            totals.append(jnp.sum(weights, axis=0, keepdims=True))
+            sums[g - 1] = dot(weights.T.astype(BF16), held[spans[g - 1], :])
+    peak = functools.reduce(jnp.maximum, peaks)
+    scales = [jnp.exp(part - peak) for part in peaks]
+    total = sum(scale * part for scale, part in zip(scales, totals))
+    row = lax.broadcasted_iota(jnp.int32, (8, slots), 0)
+    columns = jnp.zeros((8, slots), F32)
+    for index, value in enumerate([peak, total] + scales):
+        columns = jnp.where(row == index, value, columns)
+    columns = columns.T
+    peak, total = columns[:, 0:1], columns[:, 1:2]
+    result = sum(columns[:, 2 + g : 3 + g] * sums[g] for g in range(groups))
+    half = result.shape[1] // 2
+    left, right = result[:, :half], result[:, half:]
     first = place[0] == 0
     keep[...] = jnp.where(first, left, right)
     side[...] = side_state(peak, total)
     send[:, :half] = jnp.where(first, right, left).astype(BF16)
     send[:, half:] = side_message(peak, total)
+    for copy in early_copies:
+        copy.wait()
 
 
 def pair_kernel(keep, side, received, combine, send):
@@ -141,31 +156,28 @@
 
 
 def load_kernel(after, weights, held, sems):
-    copies = [pltpu.make_async_copy(weights.at[e], held.at[e], sems.at[e]) for e in range(held.shape[0])]
+    first = weights.shape[0] - held.shape[0]
+    copies = [pltpu.make_async_copy(weights.at[first + e], held.at[e], sems.at[e]) for e in range(held.shape[0])]
     for copy in copies:
         copy.start()
     for copy in copies:
         copy.wait()
 
 
-def expert_kernel(place, slot_in, early, expert_in, expert_out, keep, send, in_held, out_held, sems):
-    experts, ahead = expert_in.shape[0], early.shape[0]
-    in_copies, out_copies = {}, {}
-    for e in range(experts):
-        if e >= ahead:
-            in_copies[e] = pltpu.make_async_copy(expert_in.at[e], in_held.at[e - ahead], sems.at[0, e])
-            in_copies[e].start()
-        out_copies[e] = pltpu.make_async_copy(expert_out.at[e], out_held.at[e], sems.at[1, e])
-        out_copies[e].start()
+def expert_kernel(place, slot_in, early, later, expert_out, keep, send, held, sems):
+    experts = expert_out.shape[0]
+    copies = [pltpu.make_async_copy(expert_out.at[e], held.at[e], sems.at[e]) for e in range(experts)]
+    for copy in copies:
+        copy.start()
+    weights = [early[e] for e in range(early.shape[0])] + [later[e] for e in range(later.shape[0])]
+    hidden = [jax.nn.gelu(dot(slot_in[...], weight)).astype(BF16) for weight in weights]
     row = lax.broadcasted_iota(jnp.int32, (slot_in.shape[0], 1), 0)
     result = jnp.zeros((slot_in.shape[0], expert_out.shape[2]), F32)
-    hidden = [jax.nn.gelu(dot(slot_in[...], early[e])).astype(BF16) for e in range(ahead)]
     for e in range(experts):
-        if e >= ahead:
-            in_copies[e].wait()
-            hidden.append(jax.nn.gelu(dot(slot_in[...], in_held[e - ahead])).astype(BF16))
-        out_copies[e].wait()
-        result = jnp.where(row // SLOT_PER == e, dot(hidden[e], out_held[e]), result)
+        if e % 2 == 0:
+            for copy in copies[e : e + 2]:
+                copy.wait()
+        result = jnp.where(row // SLOT_PER == e, dot(hidden[e], held[e]), result)
     half = keep.shape[1]
     left, right = result[:, :half], result[:, half:]
     first = place[0] == 0
@@ -179,36 +191,42 @@
     combine[...] = (weights / jnp.sum(weights, axis=1, keepdims=True)).astype(BF16)
 
 
-def mix_kernel(place, combine, slot_out, *refs):
-    mixed, held, sems = refs[-3:]
+def mix_kernel(place, combine, slot_out, mixed, rest, held, sems):
     width = slot_out.shape[1]
-    block = held.shape[0] // sems.shape[0]
+    tokens, done = combine.shape[0], held.shape[0]
+    block = done // sems.shape[0]
     columns = pl.ds(pl.multiple_of(place[0] * width, width), width)
     copies = []
-    for i in range(sems.shape[0]):
+    for i in range(tokens // block):
+        rows = pl.ds(i * block, block)
+        value = dot(combine[rows, :], slot_out[...]).astype(BF16)
+        if i < sems.shape[0]:
+            held[rows, :] = value
+            copies.append(pltpu.make_async_copy(held.at[rows], mixed.at[rows, columns], sems.at[i]))
+            copies[-1].start()
+        else:
+            rest[pl.ds(i * block - done, block), :] = value
+    for copy in copies:
+        copy.wait()
+
+
+def mix_other_kernel(place, combine, slot_out, rest, before, mixed, held, sems):
+    width = slot_out.shape[1]
+    blocks = sems.shape[0] - 1
+    tokens = combine.shape[0]
+    done = tokens - rest.shape[0]
+    mine = pl.ds(pl.multiple_of(place[0] * width, width), width)
+    other = pl.ds(pl.multiple_of((1 - place[0]) * width, width), width)
+    copies = [pltpu.make_async_copy(rest, mixed.at[pl.ds(done, tokens - done), mine], sems.at[blocks])]
+    copies[0].start()
+    block = tokens // blocks
+    for i in range(blocks):
         rows = pl.ds(i * block, block)
         held[rows, :] = dot(combine[rows, :], slot_out[...]).astype(BF16)
-        copies.append(pltpu.make_async_copy(held.at[rows], mixed.at[rows, columns], sems.at[i]))
+        copies.append(pltpu.make_async_copy(held.at[rows], mixed.at[rows, other], sems.at[i]))
         copies[-1].start()
     for copy in copies:
         copy.wait()
-
-
-def mix_call(which, combine, slot_out, before=None):
-    tokens, slots = combine.shape
-    width = slot_out.shape[1]
-    more = [] if before is None else [before]
-    return pl.pallas_call(
-        mix_kernel,
-        out_shape=jax.ShapeDtypeStruct((tokens, 2 * width), BF16),
-        in_specs=[SMEM, VMEM, VMEM] + [HBM] * len(more),
-        out_specs=HBM,
-        scratch_shapes=[pltpu.VMEM((tokens, width), BF16), pltpu.SemaphoreType.DMA((8,))],
-        input_output_aliases={3: 0} if more else {},
-        cost_estimate=cost(2 * tokens * slots * width, 2 * tokens * (width + slots)),
-        compiler_params=params(16),
-        name="mix",
-    )(which, combine, slot_out, *more)
 
 
 def move(value, axes, offsets):
@@ -237,24 +255,28 @@
     place = lax.axis_index("pair").astype(jnp.int32).reshape(1)
     any_space = pl.BlockSpec(memory_space=pl.ANY)
 
-    logits, keep, side, send = pl.pallas_call(
+    ahead = expert_in.shape[0] // 2
+    logits, keep, side, send, early = pl.pallas_call(
         gather_kernel,
         out_shape=(
             jax.ShapeDtypeStruct((count, slots), F32),
             jax.ShapeDtypeStruct((slots, half), F32),
             jax.ShapeDtypeStruct((slots, SIDE), F32),
             jax.ShapeDtypeStruct((slots, half + SIDE), BF16),
+            jax.ShapeDtypeStruct((ahead,) + expert_in.shape[1:], BF16),
         ),
-        in_specs=[SMEM, HBM, HBM],
-        out_specs=(VMEM,) * 4,
+        in_specs=[SMEM, HBM, HBM, HBM],
+        out_specs=(VMEM,) * 5,
         scratch_shapes=[
             pltpu.VMEM((count, model), BF16),
             pltpu.VMEM((model, slots), BF16),
-            pltpu.SemaphoreType.DMA((count // CHUNK + 1,)),
+            pltpu.VMEM((TOKEN_GROUPS, slots, model), F32),
+            pltpu.SemaphoreType.DMA((TOKEN_GROUPS + 1,)),
+            pltpu.SemaphoreType.DMA((ahead,)),
         ],
-        compiler_params=params(40),
+        compiler_params=params(32),
         name="gather",
-    )(place, in_hbm(tokens), in_hbm(slot_params))
+    )(place, in_hbm(tokens), in_hbm(slot_params), in_hbm(expert_in))
     received = swap_pair(send)
     combine = pl.pallas_call(
         combine_kernel,
@@ -285,13 +307,12 @@
     axes = ("rest", "pair")
     mine = [send] + [move(send, axes, (r, 0)) for r in range(1, rest)]
     others = [move(send, axes, (r, 1)) for r in reversed(range(rest))]
-    ahead = expert_in.shape[0] // 2
-    early = pl.pallas_call(
+    later = pl.pallas_call(
         load_kernel,
-        out_shape=jax.ShapeDtypeStruct((ahead,) + expert_in.shape[1:], BF16),
+        out_shape=jax.ShapeDtypeStruct((expert_in.shape[0] - ahead,) + expert_in.shape[1:], BF16),
         in_specs=[any_space, HBM],
         out_specs=VMEM,
-        scratch_shapes=[pltpu.SemaphoreType.DMA((ahead,))],
+        scratch_shapes=[pltpu.SemaphoreType.DMA((expert_in.shape[0] - ahead,))],
         cost_estimate=cost(0, expert_in.size),
         compiler_params=params(16),
         name="load",
@@ -303,20 +324,19 @@
         out_specs=VMEM,
         compiler_params=params(16),
         name="finish",
-    )(place, *mine, *others, early)
+    )(place, *mine, *others, later)
     keep, send = pl.pallas_call(
         expert_kernel,
         out_shape=(jax.ShapeDtypeStruct((rows, half), F32), jax.ShapeDtypeStruct((rows, half), BF16)),
-        in_specs=[SMEM, VMEM, VMEM, HBM, HBM],
+        in_specs=[SMEM, VMEM, VMEM, VMEM, HBM],
         out_specs=(VMEM, VMEM),
         scratch_shapes=[
-            pltpu.VMEM((expert_in.shape[0] - ahead,) + expert_in.shape[1:], BF16),
             pltpu.VMEM(expert_out.shape, BF16),
-            pltpu.SemaphoreType.DMA((2, expert_in.shape[0])),
+            pltpu.SemaphoreType.DMA((expert_out.shape[0],)),
         ],
-        compiler_params=params(40),
+        compiler_params=params(24),
         name="experts",
-    )(place, slot_in, early, in_hbm(expert_in), in_hbm(expert_out))
+    )(place, slot_in, early, later, in_hbm(expert_out))
     partial = keep + swap_pair(send).astype(F32)
     travelling = partial.astype(BF16)
     for r in range(1, rest):
@@ -324,8 +344,31 @@
     block = jnp.broadcast_to(partial.astype(BF16), (groups, rows, half))
     slot_out = lax.all_to_all(block, "wide", split_axis=0, concat_axis=0, tiled=True).reshape(slots, half)
     other = swap_pair(slot_out)
-    mixed = mix_call(place, combine, slot_out)
-    return mix_call(1 - place, combine, other, mixed)
+    done, blocks = count // 2, 8
+    mixed, left = pl.pallas_call(
+        mix_kernel,
+        out_shape=(
+            pltpu.HBM((count, model), BF16),
+            jax.ShapeDtypeStruct((count - done, half), BF16),
+        ),
+        in_specs=[SMEM, VMEM, VMEM],
+        out_specs=(HBM, VMEM),
+        scratch_shapes=[pltpu.VMEM((done, half), BF16), pltpu.SemaphoreType.DMA((blocks // 2,))],
+        cost_estimate=cost(2 * count * slots * half, 2 * count * (half + slots)),
+        compiler_params=params(16),
+        name="mix",
+    )(place, combine, slot_out)
+    return pl.pallas_call(
+        mix_other_kernel,
+        out_shape=jax.ShapeDtypeStruct((count, model), BF16),
+        in_specs=[SMEM, VMEM, VMEM, VMEM, HBM],
+        out_specs=HBM,
+        scratch_shapes=[pltpu.VMEM((count, half), BF16), pltpu.SemaphoreType.DMA((blocks + 1,))],
+        input_output_aliases={4: 0},
+        cost_estimate=cost(2 * count * slots * half, 2 * count * (half + slots)),
+        compiler_params=params(16),
+        name="mix_other",
+    )(place, combine, other, left, mixed)
 
 
 def solution(mesh):

time: 51.2 us -> 51.1 us (level)
  transfers between devices with their start and end apart: 7 -> 7, of which waited for: 4 -> 5; matrix products, arithmetic and copies ran while one was open for 0% -> 0% of each run, Pallas kernels for 9% -> 8%
where the time goes in v6:
time: 51.1 us; the launch traced here: 50.9 us
  blocking collectives  24.8 us (49%)
  Pallas kernels  16.8 us (33%)
  waiting for transfers between devices  5.91 us (12%)
  starting transfers between devices  3.28 us (6%)
    all_to_all x1, blocking collectives, shards(): lax.all_to_all(send.reshape(groups, rows, -1), 'wide', split_axis=0, conc...  14.7 us
    all_to_all x1, blocking collectives, shards(): lax.all_to_all(block, 'wide', split_axis=0, concat_axis=0, tiled=True)  10.1 us
    ppermute x7, waiting for transfers between devices, move(): return lax.ppermute(value, axes, moves)  5.91 us
    pallas_call x1, Pallas kernels, shards(): pl.pallas_call(expert_kernel, out_shape=(jax.ShapeDtypeStruct((rows, half...  5.26 us
    pallas_call x1, Pallas kernels, shards(): pl.pallas_call(gather_kernel, out_shape=(jax.ShapeDtypeStruct((count, slo...  4.83 us
    ppermute x7, starting transfers between devices, move(): return lax.ppermute(value, axes, moves)  3.28 us
    pallas_call x1, Pallas kernels, shards(): pl.pallas_call(load_kernel, out_shape=jax.ShapeDtypeStruct((expert_in.sha...  2.24 us
    pallas_call x1, Pallas kernels, shards(): pl.pallas_call(mix_other_kernel, out_shape=jax.ShapeDtypeStruct((count, m...  1.74 us
  transfers between devices with their start and end apart: 7, of which 5 were waited for; matrix products, arithmetic and copies ran while one was open for 0% of the time, Pallas kernels for 8%

profile of v6, /device:TPU:0, one launch (start us, length us, event | category | flops | bytes accessed | tf_op | source)
XLA Modules:
  0.0 50.9 jit_solution(4269847632211673105)
XLA Ops:
  0.0 4.8 %gather.1 = (f32[2048,128]{1,0:T(8,128)S(1)}, f32[128,512]{1,0:T(8,128)S(1)}, f32[128,128]{1,0:T(8,128)S(1)}, bf16[128,640]{1,0:T(8,128)(2,1)S(1)}, bf16[2,1024,1024]{2,1,0:T(8,128)(2,1)S(1)}) custom-call(s32[1]{0:T(128)} %bitcast.place, bf16[2048,1024]{1,0:T(8,128)(2,1)} %tokens.1, bf16[1024,128]{1,0:T(8,128)(2,1)} %slot_params.1, ...), custom_call_target="tpu_custom_call" | custom-call | tf_op jit(solution)/shard_map/gather/pallas_call | solution.py:259
  4.8 0.5 %collective-permute-start = (bf16[128,640]{1,0:T(8,128)(2,1)S(1)}, bf16[128,640]{1,0:T(8,128)(2,1)S(1)}, u32[]{:S(2)}, u32[]{:S(2)}) collective-permute-start(bf16[128,640]{1,0:T(8,128)(2,1)S(1)} %get-tuple-element.15.after), channel_id=1, source_target_pairs={{0,1},{1,0},{2,3},{3,2},{4,5},{5,4},{6,7},{7,6},{8,9},{9,8},{10,11... | collective-permute-start | bytes 491528 | tf_op jit(solution)/shard_map/ppermute | solution.py:242
  5.4 0.6 %combine.1 = bf16[2048,128]{1,0:T(8,128)(2,1)S(1)} custom-call(f32[2048,128]{1,0:T(8,128)S(1)} %get-tuple-element.14.logits, bf16[128,640]{1,0:T(8,128)(2,1)S(1)} %get-tuple-element.15.after), custom_call_target="tpu_custom_call" | custom-call | flops 2097152 | bytes 1572864 | tf_op jit(solution)/shard_map/combine/pallas_call | solution.py:281
  6.0 0.4 collective-permute-done.received
  6.4 0.3 pair.1
  6.7 14.7 %all_to_all.10.received = bf16[8,16,640]{2,1,0:T(8,128)(2,1)S(1)} all-to-all(bf16[8,16,640]{2,1,0:T(8,128)(2,1)S(1)} %bitcast.3), channel_id=1, replica_groups=mesh['wide'=8,'rest'=2,'pair'=2] {'wide'}, dimensions={0} | all-to-all | bytes 327680 | tf_op jit(solution)/shard_map/all_to_all | solution.py:298
  21.5 0.3 merge.1.after.refs_0_
  21.7 0.0 collective-permute-start.3
  21.8 1.6 %collective-permute-start.2 = (bf16[16,640]{1,0:T(8,128)(2,1)S(1)}, bf16[16,640]{1,0:T(8,128)(2,1)S(1)}, u32[]{:S(2)}, u32[]{:S(2)}) collective-permute-start(bf16[16,640]{1,0:T(8,128)(2,1)S(1)} %merge.1.after.refs_0_), channel_id=1, source_target_pairs={{0,3},{1,2},{2,1},{3,0},{4,7},{5,6},{6,5},{7,4},{8,11},{9,10},{10,... | collective-permute-start | bytes 61448 | tf_op jit(solution)/shard_map/ppermute | solution.py:242
  23.4 0.5 collective-permute-start.1
  23.9 2.2 %load.1.refs_4_.later = bf16[2,1024,1024]{2,1,0:T(8,128)(2,1)S(1)} custom-call(bf16[16,640]{1,0:T(8,128)(2,1)S(1)} %merge.1.after.refs_0_, bf16[4,1024,1024]{2,1,0:T(8,128)(2,1)} %weights.1), custom_call_target="tpu_custom_call" | custom-call | bytes 4194304 | tf_op jit(solution)/shard_map/load/pallas_call | solution.py:310
  26.2 0.0 collective-permute-done.3.refs_3_
  26.2 0.0 collective-permute-done.2.refs_2_
  26.2 1.0 %collective-permute-done.1.refs_1_ = bf16[16,640]{1,0:T(8,128)(2,1)S(1)} collective-permute-done((bf16[16,640]{1,0:T(8,128)(2,1)S(1)}, bf16[16,640]{1,0:T(8,128)(2,1)S(1)}, u32[]{:S(2)}, u32[]{:S(2)}) %collective-permute-start.1) | collective-permute-done | bytes 20512 | tf_op jit(solution)/shard_map/ppermute | solution.py:242
  27.2 0.2 finish.1.slot_in
  27.4 5.3 %experts.1 = (f32[16,512]{1,0:T(8,128)S(1)}, bf16[16,512]{1,0:T(8,128)(2,1)S(1)}) custom-call(s32[1]{0:T(128)} %bitcast.place, bf16[16,1024]{1,0:T(8,128)(2,1)S(1)} %finish.1.slot_in, bf16[2,1024,1024]{2,1,0:T(8,128)(2,1)S(1)} %get-tuple-element.18.early, bf16[2,1024,1024]{2,1,0:T(8,128)(2,1)S(1)} %load.1.refs_4_.later, bf16[4,1024,1024]{2,1,0:T(8,128)(2,1)} %expert_out.1), custom_call_target="tpu_custom_call" | custom-call | tf_op jit(solution)/shard_map/experts/pallas_call | solution.py:328
  32.7 0.1 collective-permute-start.4
  32.8 1.2 %collective-permute-done.4 = bf16[16,512]{1,0:T(8,128)(2,1)S(1)} collective-permute-done((bf16[16,512]{1,0:T(8,128)(2,1)S(1)}, bf16[16,512]{1,0:T(8,128)(2,1)S(1)}, u32[]{:S(2)}, u32[]{:S(2)}) %collective-permute-start.4) | collective-permute-done | bytes 16416 | tf_op jit(solution)/shard_map/ppermute | solution.py:242
  34.0 0.5 %collective-permute-start.5 = (bf16[16,512]{1,0:T(8,128)(2,1)S(1)}, bf16[16,512]{1,0:T(8,128)(2,1)S(1)}, u32[]{:S(2)}, u32[]{:S(2)}) collective-permute-start(bf16[16,512]{1,0:T(8,128)(2,1)S(1)} %fusion), channel_id=1, source_target_pairs={{0,2},{2,0},{1,3},{3,1},{4,6},{6,4},{5,7},{7,5},{8,10},{10,8},{9,1... | collective-permute-start | bytes 49160 | tf_op jit(solution)/shard_map/ppermute | solution.py:242
  34.5 3.2 %collective-permute-done.5 = bf16[16,512]{1,0:T(8,128)(2,1)S(1)} collective-permute-done((bf16[16,512]{1,0:T(8,128)(2,1)S(1)}, bf16[16,512]{1,0:T(8,128)(2,1)S(1)}, u32[]{:S(2)}, u32[]{:S(2)}) %collective-permute-start.5) | collective-permute-done | bytes 16416 | tf_op jit(solution)/shard_map/ppermute | solution.py:242
  37.7 10.1 %all_to_all.11 = bf16[8,16,512]{2,1,0:T(8,128)(2,1)S(1)} all-to-all(bf16[8,16,512]{2,1,0:T(8,128)(2,1)S(1)} %broadcast_in_dim.3), channel_id=1, replica_groups=mesh['wide'=8,'rest'=2,'pair'=2] {'wide'}, dimensions={0} | all-to-all | bytes 262144 | tf_op jit(solution)/shard_map/all_to_all | solution.py:345
  47.8 0.0 collective-permute-start.6
  47.8 1.2 %mix.1 = (bf16[2048,1024]{1,0:T(8,128)(2,1)}, bf16[1024,512]{1,0:T(8,128)(2,1)S(1)}) custom-call(s32[1]{0:T(128)} %bitcast.place, bf16[2048,128]{1,0:T(8,128)(2,1)S(1)} %combine.1, bf16[128,512]{1,0:T(8,128)(2,1)S(1)} %bitcast.5), custom_call_target="tpu_custom_call" | custom-call | flops 268435456 | bytes 2621440 | tf_op jit(solution)/shard_map/mix/pallas_call | solution.py:348
  49.0 0.1 collective-permute-done.6.slot_out
  49.2 1.7 %mix_other.1 = bf16[2048,1024]{1,0:T(8,128)(2,1)} custom-call(s32[1]{0:T(128)} %bitcast.place, bf16[2048,128]{1,0:T(8,128)(2,1)S(1)} %combine.1, bf16[128,512]{1,0:T(8,128)(2,1)S(1)} %collective-permute-done.6.slot_out, bf16[1024,512]{1,0:T(8,128)(2,1)S(1)} %get-tuple-element.21.rest, ...), custom_call_target="tpu_custom_call", output_to_operand_aliasing={{}: (4, {})} | custom-call | flops 268435456 | bytes 2621440 | tf_op jit(solution)/shard_map/mix_other/pallas_call | solution.py:361
  (3 shorter events, 0.0 us)
Async XLA Ops:
  4.8 1.5 %collective-permute-start = (bf16[128,640]{1,0:T(8,128)(2,1)S(1)}, bf16[128,640]{1,0:T(8,128)(2,1)S(1)}, u32[]{:S(2)}, u32[]{:S(2)}) collective-permute-start(bf16[128,640]{1,0:T(8,128)(2,1)S(1)} %get-tuple-element.15.after), channel_id=1, source_target_pairs={{0,1},{1,0},{2,3},{3,2},{4,5},{5,4},{6,7},{7,6},{8,9},{9,8},{10,11... | collective-permute-start | bytes 491528 | tf_op jit(solution)/shard_map/ppermute | solution.py:242
  21.7 4.4 %collective-permute-start.3 = (bf16[16,640]{1,0:T(8,128)(2,1)S(1)}, bf16[16,640]{1,0:T(8,128)(2,1)S(1)}, u32[]{:S(2)}, u32[]{:S(2)}) collective-permute-start(bf16[16,640]{1,0:T(8,128)(2,1)S(1)} %merge.1.after.refs_0_), channel_id=1, source_target_pairs={{0,1},{1,0},{2,3},{3,2},{4,5},{5,4},{6,7},{7,6},{8,9},{9,8},{10,11... | collective-permute-start | bytes 61448 | tf_op jit(solution)/shard_map/ppermute | solution.py:242
  21.8 4.4 %collective-permute-start.2 = (bf16[16,640]{1,0:T(8,128)(2,1)S(1)}, bf16[16,640]{1,0:T(8,128)(2,1)S(1)}, u32[]{:S(2)}, u32[]{:S(2)}) collective-permute-start(bf16[16,640]{1,0:T(8,128)(2,1)S(1)} %merge.1.after.refs_0_), channel_id=1, source_target_pairs={{0,3},{1,2},{2,1},{3,0},{4,7},{5,6},{6,5},{7,4},{8,11},{9,10},{10,... | collective-permute-start | bytes 61448 | tf_op jit(solution)/shard_map/ppermute | solution.py:242
  23.4 3.8 %collective-permute-start.1 = (bf16[16,640]{1,0:T(8,128)(2,1)S(1)}, bf16[16,640]{1,0:T(8,128)(2,1)S(1)}, u32[]{:S(2)}, u32[]{:S(2)}) collective-permute-start(bf16[16,640]{1,0:T(8,128)(2,1)S(1)} %merge.1.after.refs_0_), channel_id=1, source_target_pairs={{0,2},{1,3},{2,0},{3,1},{4,6},{5,7},{6,4},{7,5},{8,10},{9,11},{10,... | collective-permute-start | bytes 61448 | tf_op jit(solution)/shard_map/ppermute | solution.py:242
  32.7 1.2 %collective-permute-start.4 = (bf16[16,512]{1,0:T(8,128)(2,1)S(1)}, bf16[16,512]{1,0:T(8,128)(2,1)S(1)}, u32[]{:S(2)}, u32[]{:S(2)}) collective-permute-start(bf16[16,512]{1,0:T(8,128)(2,1)S(1)} %get-tuple-element.20), channel_id=1, source_target_pairs={{0,1},{1,0},{2,3},{3,2},{4,5},{5,4},{6,7},{7,6},{8,9},{9,8},{10,11... | collective-permute-start | bytes 49160 | tf_op jit(solution)/shard_map/ppermute | solution.py:242
  34.0 3.7 %collective-permute-start.5 = (bf16[16,512]{1,0:T(8,128)(2,1)S(1)}, bf16[16,512]{1,0:T(8,128)(2,1)S(1)}, u32[]{:S(2)}, u32[]{:S(2)}) collective-permute-start(bf16[16,512]{1,0:T(8,128)(2,1)S(1)} %fusion), channel_id=1, source_target_pairs={{0,2},{2,0},{1,3},{3,1},{4,6},{6,4},{5,7},{7,5},{8,10},{10,8},{9,1... | collective-permute-start | bytes 49160 | tf_op jit(solution)/shard_map/ppermute | solution.py:242
  47.8 1.3 %collective-permute-start.6 = (bf16[128,512]{1,0:T(8,128)(2,1)S(1)}, bf16[128,512]{1,0:T(8,128)(2,1)S(1)}, u32[]{:S(2)}, u32[]{:S(2)}) collective-permute-start(bf16[128,512]{1,0:T(8,128)(2,1)S(1)} %bitcast.4), channel_id=1, source_target_pairs={{0,1},{1,0},{2,3},{3,2},{4,5},{5,4},{6,7},{7,6},{8,9},{9,8},{10,11... | collective-permute-start | bytes 393224 | tf_op jit(solution)/shard_map/ppermute | solution.py:242

commit v7 on v6

--- a/solution.py
+++ b/solution.py
@@ -74,13 +74,14 @@
     early_copies = [
         pltpu.make_async_copy(expert_in.at[e], early.at[e], early_sems.at[e]) for e in range(early.shape[0])
     ]
-    for copy in early_copies:
-        copy.start()
     table_copy.wait()
     parts, peaks, totals = [], [], []
     for g in range(groups + 1):
         if g < groups:
             copies[g].wait()
+            if g == groups // 2:
+                for copy in early_copies:
+                    copy.start()
             parts.append(dot(held[spans[g], :], table[...]))
             logits[spans[g], :] = parts[g]
             peaks.append(jnp.max(parts[g], axis=0, keepdims=True))
@@ -164,25 +165,37 @@
         copy.wait()
 
 
-def expert_kernel(place, slot_in, early, later, expert_out, keep, send, held, sems):
-    experts = expert_out.shape[0]
-    copies = [pltpu.make_async_copy(expert_out.at[e], held.at[e], sems.at[e]) for e in range(experts)]
-    for copy in copies:
-        copy.start()
+def second_product(hidden, weights):
+    row = lax.broadcasted_iota(jnp.int32, (hidden[0].shape[0], 1), 0)
+    result = 0.0
+    for e, value in enumerate(hidden):
+        result = jnp.where(row // SLOT_PER == e, dot(value, weights[e]), result)
+    return result
+
+
+def expert_kernel(place, slot_in, early, later, expert_out, hidden, own, send, held, sems):
+    experts, half = expert_out.shape[0], own.shape[2]
+    copies = []
+    for target, side in ((held, 1 - place[0]), (own, place[0])):
+        columns = pl.ds(pl.multiple_of(side * half, half), half)
+        for e in range(experts):
+            copies.append(
+                pltpu.make_async_copy(expert_out.at[e, :, columns], target.at[e], sems.at[len(copies)])
+            )
+            copies[-1].start()
     weights = [early[e] for e in range(early.shape[0])] + [later[e] for e in range(later.shape[0])]
-    hidden = [jax.nn.gelu(dot(slot_in[...], weight)).astype(BF16) for weight in weights]
-    row = lax.broadcasted_iota(jnp.int32, (slot_in.shape[0], 1), 0)
-    result = jnp.zeros((slot_in.shape[0], expert_out.shape[2]), F32)
+    values = [jax.nn.gelu(dot(slot_in[...], weight)).astype(BF16) for weight in weights]
     for e in range(experts):
-        if e % 2 == 0:
-            for copy in copies[e : e + 2]:
-                copy.wait()
-        result = jnp.where(row // SLOT_PER == e, dot(hidden[e], held[e]), result)
-    half = keep.shape[1]
-    left, right = result[:, :half], result[:, half:]
-    first = place[0] == 0
-    keep[...] = jnp.where(first, left, right)
-    send[...] = jnp.where(first, right, left).astype(BF16)
+        hidden[e] = values[e]
+    for copy in copies[:experts]:
+        copy.wait()
+    send[...] = second_product(values, held).astype(BF16)
+    for copy in copies[experts:]:
+        copy.wait()
+
+
+def own_kernel(hidden, own, after, keep):
+    keep[...] = second_product([hidden[e] for e in range(hidden.shape[0])], own)
 
 
 def combine_kernel(logits, after, combine):
@@ -325,24 +338,38 @@
         compiler_params=params(16),
         name="finish",
     )(place, *mine, *others, later)
-    keep, send = pl.pallas_call(
+    experts, units = expert_out.shape[:2]
+    hidden, own, send = pl.pallas_call(
         expert_kernel,
-        out_shape=(jax.ShapeDtypeStruct((rows, half), F32), jax.ShapeDtypeStruct((rows, half), BF16)),
+        out_shape=(
+            jax.ShapeDtypeStruct((experts, rows, units), BF16),
+            jax.ShapeDtypeStruct((experts, units, half), BF16),
+            jax.ShapeDtypeStruct((rows, half), BF16),
+        ),
         in_specs=[SMEM, VMEM, VMEM, VMEM, HBM],
-        out_specs=(VMEM, VMEM),
+        out_specs=(VMEM,) * 3,
         scratch_shapes=[
-            pltpu.VMEM(expert_out.shape, BF16),
-            pltpu.SemaphoreType.DMA((expert_out.shape[0],)),
+            pltpu.VMEM((experts, units, half), BF16),
+            pltpu.SemaphoreType.DMA((2 * experts,)),
         ],
         compiler_params=params(24),
         name="experts",
     )(place, slot_in, early, later, in_hbm(expert_out))
-    partial = keep + swap_pair(send).astype(F32)
-    travelling = partial.astype(BF16)
-    for r in range(1, rest):
-        partial = partial + move(travelling, ("rest",), (r,)).astype(F32)
-    block = jnp.broadcast_to(partial.astype(BF16), (groups, rows, half))
-    slot_out = lax.all_to_all(block, "wide", split_axis=0, concat_axis=0, tiled=True).reshape(slots, half)
+    received = swap_pair(send)
+    keep = pl.pallas_call(
+        own_kernel,
+        out_shape=jax.ShapeDtypeStruct((rows, half), F32),
+        in_specs=[VMEM, VMEM, any_space],
+        out_specs=VMEM,
+        cost_estimate=cost(2 * rows * units * half * experts, 2 * experts * units * half),
+        compiler_params=params(16),
+        name="own",
+    )(hidden, own, send)
+    partial = (keep + received.astype(F32)).astype(BF16)
+    partials = jnp.broadcast_to(partial, (groups * rest, rows, half))
+    partials = lax.all_to_all(partials, ("wide", "rest"), split_axis=0, concat_axis=0, tiled=True)
+    slot_out = jnp.sum(partials.reshape(groups, rest, rows, half).astype(F32), axis=1)
+    slot_out = slot_out.astype(BF16).reshape(slots, half)
     other = swap_pair(slot_out)
     done, blocks = count // 2, 8
     mixed, left = pl.pallas_call(

time: 51.1 us -> 49.3 us (0.965)
  waiting for transfers between devices: 5.91 us -> 2.04 us
  blocking collectives: 24.8 us -> 27.8 us
    ppermute x7 -> x6, waiting for transfers between devices: 5.91 us -> 2.04 us  [move(): return lax.ppermute(value, axes, moves)]
    all_to_all x1, blocking collectives: 10.1 us -> 13.1 us  [shards(): lax.all_to_all(partials, ('wide', 'rest'), split_axis=0, concat_axis=0, t...]
    pallas_call x1 -> x2, Pallas kernels: 5.26 us -> 4.46 us  [the longest x1 3.81 us: shards(): pl.pallas_call(expert_kernel, out_shape=(jax.ShapeDtypeStruct((experts, r...]
    ppermute x7 -> x6, starting transfers between devices: 3.28 us -> 2.83 us  [move(): return lax.ppermute(value, axes, moves)]
  transfers between devices with their start and end apart: 7 -> 6, of which waited for: 5 -> 4; matrix products, arithmetic and copies ran while one was open for 0% -> 0% of each run, Pallas kernels for 8% -> 10%
where the time goes in v7:
time: 49.3 us; the launch traced here: 49.1 us
  blocking collectives  27.8 us (56%)
  Pallas kernels  16.3 us (33%)
  starting transfers between devices  2.83 us (6%)
  waiting for transfers between devices  2.04 us (4%)
    all_to_all x1, blocking collectives, shards(): lax.all_to_all(send.reshape(groups, rows, -1), 'wide', split_axis=0, conc...  14.7 us
    all_to_all x1, blocking collectives, shards(): lax.all_to_all(partials, ('wide', 'rest'), split_axis=0, concat_axis=0, t...  13.1 us
    pallas_call x1, Pallas kernels, shards(): pl.pallas_call(gather_kernel, out_shape=(jax.ShapeDtypeStruct((count, slo...  5.13 us
    pallas_call x1, Pallas kernels, shards(): pl.pallas_call(expert_kernel, out_shape=(jax.ShapeDtypeStruct((experts, r...  3.81 us
    ppermute x6, starting transfers between devices, move(): return lax.ppermute(value, axes, moves)  2.83 us
    pallas_call x1, Pallas kernels, shards(): pl.pallas_call(load_kernel, out_shape=jax.ShapeDtypeStruct((expert_in.sha...  2.24 us
    ppermute x6, waiting for transfers between devices, move(): return lax.ppermute(value, axes, moves)  2.04 us
    pallas_call x1, Pallas kernels, shards(): pl.pallas_call(mix_other_kernel, out_shape=jax.ShapeDtypeStruct((count, m...  1.74 us
  transfers between devices with their start and end apart: 6, of which 4 were waited for; matrix products, arithmetic and copies ran while one was open for 0% of the time, Pallas kernels for 10%

profile of v7, /device:TPU:0, one launch (start us, length us, event | category | flops | bytes accessed | tf_op | source)
XLA Modules:
  0.0 49.1 jit_solution(14321367396114402170)
XLA Ops:
  0.0 5.1 %gather.1 = (f32[2048,128]{1,0:T(8,128)S(1)}, f32[128,512]{1,0:T(8,128)S(1)}, f32[128,128]{1,0:T(8,128)S(1)}, bf16[128,640]{1,0:T(8,128)(2,1)S(1)}, bf16[2,1024,1024]{2,1,0:T(8,128)(2,1)S(1)}) custom-call(s32[1]{0:T(128)} %bitcast.place, bf16[2048,1024]{1,0:T(8,128)(2,1)} %tokens.1, bf16[1024,128]{1,0:T(8,128)(2,1)} %slot_params.1, ...), custom_call_target="tpu_custom_call" | custom-call | tf_op jit(solution)/shard_map/gather/pallas_call | solution.py:272
  5.1 0.5 %collective-permute-start = (bf16[128,640]{1,0:T(8,128)(2,1)S(1)}, bf16[128,640]{1,0:T(8,128)(2,1)S(1)}, u32[]{:S(2)}, u32[]{:S(2)}) collective-permute-start(bf16[128,640]{1,0:T(8,128)(2,1)S(1)} %get-tuple-element.16.after), channel_id=1, source_target_pairs={{0,1},{1,0},{2,3},{3,2},{4,5},{5,4},{6,7},{7,6},{8,9},{9,8},{10,11... | collective-permute-start | bytes 491528 | tf_op jit(solution)/shard_map/ppermute | solution.py:255
  5.7 0.6 %combine.1 = bf16[2048,128]{1,0:T(8,128)(2,1)S(1)} custom-call(f32[2048,128]{1,0:T(8,128)S(1)} %get-tuple-element.15.logits, bf16[128,640]{1,0:T(8,128)(2,1)S(1)} %get-tuple-element.16.after), custom_call_target="tpu_custom_call" | custom-call | flops 2097152 | bytes 1572864 | tf_op jit(solution)/shard_map/combine/pallas_call | solution.py:294
  6.3 0.4 collective-permute-done.received
  6.7 0.3 pair.1
  7.0 14.7 %all_to_all.10.received = bf16[8,16,640]{2,1,0:T(8,128)(2,1)S(1)} all-to-all(bf16[8,16,640]{2,1,0:T(8,128)(2,1)S(1)} %bitcast.5), channel_id=1, replica_groups=mesh['wide'=8,'rest'=2,'pair'=2] {'wide'}, dimensions={0} | all-to-all | bytes 327680 | tf_op jit(solution)/shard_map/all_to_all | solution.py:311
  21.8 0.3 merge.1.after.refs_0_
  22.0 0.0 collective-permute-start.3
  22.1 1.6 %collective-permute-start.2 = (bf16[16,640]{1,0:T(8,128)(2,1)S(1)}, bf16[16,640]{1,0:T(8,128)(2,1)S(1)}, u32[]{:S(2)}, u32[]{:S(2)}) collective-permute-start(bf16[16,640]{1,0:T(8,128)(2,1)S(1)} %merge.1.after.refs_0_), channel_id=1, source_target_pairs={{0,3},{1,2},{2,1},{3,0},{4,7},{5,6},{6,5},{7,4},{8,11},{9,10},{10,... | collective-permute-start | bytes 61448 | tf_op jit(solution)/shard_map/ppermute | solution.py:255
  23.7 0.5 %collective-permute-start.1 = (bf16[16,640]{1,0:T(8,128)(2,1)S(1)}, bf16[16,640]{1,0:T(8,128)(2,1)S(1)}, u32[]{:S(2)}, u32[]{:S(2)}) collective-permute-start(bf16[16,640]{1,0:T(8,128)(2,1)S(1)} %merge.1.after.refs_0_), channel_id=1, source_target_pairs={{0,2},{1,3},{2,0},{3,1},{4,6},{5,7},{6,4},{7,5},{8,10},{9,11},{10,... | collective-permute-start | bytes 61448 | tf_op jit(solution)/shard_map/ppermute | solution.py:255
  24.2 2.2 %load.1.refs_4_.later = bf16[2,1024,1024]{2,1,0:T(8,128)(2,1)S(1)} custom-call(bf16[16,640]{1,0:T(8,128)(2,1)S(1)} %merge.1.after.refs_0_, bf16[4,1024,1024]{2,1,0:T(8,128)(2,1)} %weights.1), custom_call_target="tpu_custom_call" | custom-call | bytes 4194304 | tf_op jit(solution)/shard_map/load/pallas_call | solution.py:323
  26.5 0.0 collective-permute-done.3.refs_3_
  26.5 0.0 collective-permute-done.2.refs_2_
  26.5 1.0 %collective-permute-done.1.refs_1_ = bf16[16,640]{1,0:T(8,128)(2,1)S(1)} collective-permute-done((bf16[16,640]{1,0:T(8,128)(2,1)S(1)}, bf16[16,640]{1,0:T(8,128)(2,1)S(1)}, u32[]{:S(2)}, u32[]{:S(2)}) %collective-permute-start.1) | collective-permute-done | bytes 20512 | tf_op jit(solution)/shard_map/ppermute | solution.py:255
  27.5 0.2 finish.1.slot_in
  27.7 3.8 %experts.1 = (bf16[4,16,1024]{2,1,0:T(8,128)(2,1)S(1)}, bf16[4,1024,512]{2,1,0:T(8,128)(2,1)S(1)}, bf16[16,512]{1,0:T(8,128)(2,1)S(1)}) custom-call(s32[1]{0:T(128)} %bitcast.place, bf16[16,1024]{1,0:T(8,128)(2,1)S(1)} %finish.1.slot_in, bf16[2,1024,1024]{2,1,0:T(8,128)(2,1)S(1)} %get-tuple-element.19.early, bf16[2,1024,1024]{2,1,0:T(8,128)(2,1)S(1)} %load.1.refs_4_.later, ...), custom_call_target="tpu_custom_call" | custom-call | tf_op jit(solution)/shard_map/experts/pallas_call | solution.py:342
  31.6 0.1 collective-permute-start.4
  31.6 0.6 %own.1 = f32[16,512]{1,0:T(8,128)S(1)} custom-call(bf16[4,16,1024]{2,1,0:T(8,128)(2,1)S(1)} %get-tuple-element.20.hidden, bf16[4,1024,512]{2,1,0:T(8,128)(2,1)S(1)} %get-tuple-element.21.own, bf16[16,512]{1,0:T(8,128)(2,1)S(1)} %get-tuple-element.22.after), custom_call_target="tpu_custom_call" | custom-call | flops 67108864 | bytes 4194304 | tf_op jit(solution)/shard_map/own/pallas_call | solution.py:359
  32.3 0.5 %collective-permute-done.4 = bf16[16,512]{1,0:T(8,128)(2,1)S(1)} collective-permute-done((bf16[16,512]{1,0:T(8,128)(2,1)S(1)}, bf16[16,512]{1,0:T(8,128)(2,1)S(1)}, u32[]{:S(2)}, u32[]{:S(2)}) %collective-permute-start.4) | collective-permute-done | bytes 16416 | tf_op jit(solution)/shard_map/ppermute | solution.py:255
  32.8 13.1 %all_to_all.11 = bf16[16,16,512]{2,1,0:T(8,128)(2,1)S(1)} all-to-all(bf16[16,16,512]{2,1,0:T(8,128)(2,1)S(1)} %broadcast_in_dim.3), channel_id=1, replica_groups=mesh['wide'=8,'rest'=2,'pair'=2] {'wide','rest'}, dimensions={0} | all-to-all | bytes 524288 | tf_op jit(solution)/shard_map/all_to_all | solution.py:370
  45.9 0.1 collective-permute-start.5
  46.0 1.2 %mix.1 = (bf16[2048,1024]{1,0:T(8,128)(2,1)}, bf16[1024,512]{1,0:T(8,128)(2,1)S(1)}) custom-call(s32[1]{0:T(128)} %bitcast.place, bf16[2048,128]{1,0:T(8,128)(2,1)S(1)} %combine.1, bf16[128,512]{1,0:T(8,128)(2,1)S(1)} %bitcast.7), custom_call_target="tpu_custom_call" | custom-call | flops 268435456 | bytes 2621440 | tf_op jit(solution)/shard_map/mix/pallas_call | solution.py:375
  47.2 0.1 collective-permute-done.5.slot_out
  47.4 1.7 %mix_other.1 = bf16[2048,1024]{1,0:T(8,128)(2,1)} custom-call(s32[1]{0:T(128)} %bitcast.place, bf16[2048,128]{1,0:T(8,128)(2,1)S(1)} %combine.1, bf16[128,512]{1,0:T(8,128)(2,1)S(1)} %collective-permute-done.5.slot_out, bf16[1024,512]{1,0:T(8,128)(2,1)S(1)} %get-tuple-element.23.rest, ...), custom_call_target="tpu_custom_call", output_to_operand_aliasing={{}: (4, {})} | custom-call | flops 268435456 | bytes 2621440 | tf_op jit(solution)/shard_map/mix_other/pallas_call | solution.py:388
  (3 shorter events, 0.1 us)
Async XLA Ops:
  5.1 1.5 %collective-permute-start = (bf16[128,640]{1,0:T(8,128)(2,1)S(1)}, bf16[128,640]{1,0:T(8,128)(2,1)S(1)}, u32[]{:S(2)}, u32[]{:S(2)}) collective-permute-start(bf16[128,640]{1,0:T(8,128)(2,1)S(1)} %get-tuple-element.16.after), channel_id=1, source_target_pairs={{0,1},{1,0},{2,3},{3,2},{4,5},{5,4},{6,7},{7,6},{8,9},{9,8},{10,11... | collective-permute-start | bytes 491528 | tf_op jit(solution)/shard_map/ppermute | solution.py:255
  22.0 4.4 %collective-permute-start.3 = (bf16[16,640]{1,0:T(8,128)(2,1)S(1)}, bf16[16,640]{1,0:T(8,128)(2,1)S(1)}, u32[]{:S(2)}, u32[]{:S(2)}) collective-permute-start(bf16[16,640]{1,0:T(8,128)(2,1)S(1)} %merge.1.after.refs_0_), channel_id=1, source_target_pairs={{0,1},{1,0},{2,3},{3,2},{4,5},{5,4},{6,7},{7,6},{8,9},{9,8},{10,11... | collective-permute-start | bytes 61448 | tf_op jit(solution)/shard_map/ppermute | solution.py:255
  22.1 4.4 %collective-permute-start.2 = (bf16[16,640]{1,0:T(8,128)(2,1)S(1)}, bf16[16,640]{1,0:T(8,128)(2,1)S(1)}, u32[]{:S(2)}, u32[]{:S(2)}) collective-permute-start(bf16[16,640]{1,0:T(8,128)(2,1)S(1)} %merge.1.after.refs_0_), channel_id=1, source_target_pairs={{0,3},{1,2},{2,1},{3,0},{4,7},{5,6},{6,5},{7,4},{8,11},{9,10},{10,... | collective-permute-start | bytes 61448 | tf_op jit(solution)/shard_map/ppermute | solution.py:255
  23.7 3.8 %collective-permute-start.1 = (bf16[16,640]{1,0:T(8,128)(2,1)S(1)}, bf16[16,640]{1,0:T(8,128)(2,1)S(1)}, u32[]{:S(2)}, u32[]{:S(2)}) collective-permute-start(bf16[16,640]{1,0:T(8,128)(2,1)S(1)} %merge.1.after.refs_0_), channel_id=1, source_target_pairs={{0,2},{1,3},{2,0},{3,1},{4,6},{5,7},{6,4},{7,5},{8,10},{9,11},{10,... | collective-permute-start | bytes 61448 | tf_op jit(solution)/shard_map/ppermute | solution.py:255
  31.6 1.2 %collective-permute-start.4 = (bf16[16,512]{1,0:T(8,128)(2,1)S(1)}, bf16[16,512]{1,0:T(8,128)(2,1)S(1)}, u32[]{:S(2)}, u32[]{:S(2)}) collective-permute-start(bf16[16,512]{1,0:T(8,128)(2,1)S(1)} %get-tuple-element.22.after), channel_id=1, source_target_pairs={{0,1},{1,0},{2,3},{3,2},{4,5},{5,4},{6,7},{7,6},{8,9},{9,8},{10,11... | collective-permute-start | bytes 49160 | tf_op jit(solution)/shard_map/ppermute | solution.py:255
  45.9 1.4 %collective-permute-start.5 = (bf16[128,512]{1,0:T(8,128)(2,1)S(1)}, bf16[128,512]{1,0:T(8,128)(2,1)S(1)}, u32[]{:S(2)}, u32[]{:S(2)}) collective-permute-start(bf16[128,512]{1,0:T(8,128)(2,1)S(1)} %bitcast.6), channel_id=1, source_target_pairs={{0,1},{1,0},{2,3},{3,2},{4,5},{5,4},{6,7},{7,6},{8,9},{9,8},{10,11... | collective-permute-start | bytes 393224 | tf_op jit(solution)/shard_map/ppermute | solution.py:255

commit v8 on v7

--- a/solution.py
+++ b/solution.py
@@ -60,7 +60,7 @@
 
 
 def gather_kernel(
-    place, tokens, slot_params, expert_in, logits, keep, side, send, early, held, table, sums, sems, early_sems
+    place, tokens, slot_params, logits, keep, side, send, held, table, sums, sems
 ):
     slots = slot_params.shape[1]
     groups = sums.shape[0]
@@ -71,17 +71,11 @@
     copies = [pltpu.make_async_copy(tokens.at[span], held.at[span], sems.at[g]) for g, span in enumerate(spans)]
     for copy in copies:
         copy.start()
-    early_copies = [
-        pltpu.make_async_copy(expert_in.at[e], early.at[e], early_sems.at[e]) for e in range(early.shape[0])
-    ]
     table_copy.wait()
     parts, peaks, totals = [], [], []
     for g in range(groups + 1):
         if g < groups:
             copies[g].wait()
-            if g == groups // 2:
-                for copy in early_copies:
-                    copy.start()
             parts.append(dot(held[spans[g], :], table[...]))
             logits[spans[g], :] = parts[g]
             peaks.append(jnp.max(parts[g], axis=0, keepdims=True))
@@ -106,8 +100,6 @@
     side[...] = side_state(peak, total)
     send[:, :half] = jnp.where(first, right, left).astype(BF16)
     send[:, half:] = side_message(peak, total)
-    for copy in early_copies:
-        copy.wait()
 
 
 def pair_kernel(keep, side, received, combine, send):
@@ -146,7 +138,7 @@
 def finish_kernel(place, *refs):
     slot_in = refs[-1]
     half = slot_in.shape[1] // 2
-    parts = (len(refs) - 2) // 2
+    parts = (len(refs) - 1) // 2
     means = []
     for side in range(2):
         sums, _, total = add_parts([ref[...] for ref in refs[side * parts : (side + 1) * parts]], half)
@@ -156,46 +148,29 @@
     slot_in[:, half:] = jnp.where(first, means[1], means[0])
 
 
-def load_kernel(after, weights, held, sems):
-    first = weights.shape[0] - held.shape[0]
-    copies = [pltpu.make_async_copy(weights.at[first + e], held.at[e], sems.at[e]) for e in range(held.shape[0])]
-    for copy in copies:
-        copy.start()
-    for copy in copies:
-        copy.wait()
-
-
-def second_product(hidden, weights):
+def second_product(hidden, weights, columns):
     row = lax.broadcasted_iota(jnp.int32, (hidden[0].shape[0], 1), 0)
     result = 0.0
     for e, value in enumerate(hidden):
-        result = jnp.where(row // SLOT_PER == e, dot(value, weights[e]), result)
+        result = jnp.where(row // SLOT_PER == e, dot(value, weights[e, :, columns]), result)
     return result
 
 
-def expert_kernel(place, slot_in, early, later, expert_out, hidden, own, send, held, sems):
-    experts, half = expert_out.shape[0], own.shape[2]
-    copies = []
-    for target, side in ((held, 1 - place[0]), (own, place[0])):
-        columns = pl.ds(pl.multiple_of(side * half, half), half)
-        for e in range(experts):
-            copies.append(
-                pltpu.make_async_copy(expert_out.at[e, :, columns], target.at[e], sems.at[len(copies)])
-            )
-            copies[-1].start()
-    weights = [early[e] for e in range(early.shape[0])] + [later[e] for e in range(later.shape[0])]
-    values = [jax.nn.gelu(dot(slot_in[...], weight)).astype(BF16) for weight in weights]
-    for e in range(experts):
+def column_half(side, half):
+    return pl.ds(pl.multiple_of(side * half, half), half)
+
+
+def expert_kernel(place, slot_in, expert_in, expert_out, hidden, send):
+    values = []
+    for e in range(expert_in.shape[0]):
+        values.append(jax.nn.gelu(dot(slot_in[...], expert_in[e])).astype(BF16))
         hidden[e] = values[e]
-    for copy in copies[:experts]:
-        copy.wait()
-    send[...] = second_product(values, held).astype(BF16)
-    for copy in copies[experts:]:
-        copy.wait()
-
-
-def own_kernel(hidden, own, after, keep):
-    keep[...] = second_product([hidden[e] for e in range(hidden.shape[0])], own)
+    send[...] = second_product(values, expert_out, column_half(1 - place[0], send.shape[1])).astype(BF16)
+
+
+def own_kernel(place, hidden, expert_out, after, keep):
+    values = [hidden[e] for e in range(hidden.shape[0])]
+    keep[...] = second_product(values, expert_out, column_half(place[0], keep.shape[1]))
 
 
 def combine_kernel(logits, after, combine):
@@ -268,28 +243,25 @@
     place = lax.axis_index("pair").astype(jnp.int32).reshape(1)
     any_space = pl.BlockSpec(memory_space=pl.ANY)
 
-    ahead = expert_in.shape[0] // 2
-    logits, keep, side, send, early = pl.pallas_call(
+    logits, keep, side, send = pl.pallas_call(
         gather_kernel,
         out_shape=(
             jax.ShapeDtypeStruct((count, slots), F32),
             jax.ShapeDtypeStruct((slots, half), F32),
             jax.ShapeDtypeStruct((slots, SIDE), F32),
             jax.ShapeDtypeStruct((slots, half + SIDE), BF16),
-            jax.ShapeDtypeStruct((ahead,) + expert_in.shape[1:], BF16),
         ),
-        in_specs=[SMEM, HBM, HBM, HBM],
-        out_specs=(VMEM,) * 5,
+        in_specs=[SMEM, HBM, HBM],
+        out_specs=(VMEM,) * 4,
         scratch_shapes=[
             pltpu.VMEM((count, model), BF16),
             pltpu.VMEM((model, slots), BF16),
             pltpu.VMEM((TOKEN_GROUPS, slots, model), F32),
             pltpu.SemaphoreType.DMA((TOKEN_GROUPS + 1,)),
-            pltpu.SemaphoreType.DMA((ahead,)),
         ],
-        compiler_params=params(32),
+        compiler_params=params(40),
         name="gather",
-    )(place, in_hbm(tokens), in_hbm(slot_params), in_hbm(expert_in))
+    )(place, in_hbm(tokens), in_hbm(slot_params))
     received = swap_pair(send)
     combine = pl.pallas_call(
         combine_kernel,
@@ -305,6 +277,7 @@
         out_shape=jax.ShapeDtypeStruct((slots, half + SIDE), BF16),
         in_specs=[VMEM] * 3 + [any_space],
         out_specs=VMEM,
+        cost_estimate=cost(0, 6 * slots * model, 128 * slots * model),
         compiler_params=params(16),
         name="pair",
     )(keep, side, received, combine)
@@ -320,51 +293,36 @@
     axes = ("rest", "pair")
     mine = [send] + [move(send, axes, (r, 0)) for r in range(1, rest)]
     others = [move(send, axes, (r, 1)) for r in reversed(range(rest))]
-    later = pl.pallas_call(
-        load_kernel,
-        out_shape=jax.ShapeDtypeStruct((expert_in.shape[0] - ahead,) + expert_in.shape[1:], BF16),
-        in_specs=[any_space, HBM],
-        out_specs=VMEM,
-        scratch_shapes=[pltpu.SemaphoreType.DMA((expert_in.shape[0] - ahead,))],
-        cost_estimate=cost(0, expert_in.size),
-        compiler_params=params(16),
-        name="load",
-    )(send, in_hbm(expert_in))
     slot_in = pl.pallas_call(
         finish_kernel,
         out_shape=jax.ShapeDtypeStruct((rows, model), BF16),
-        in_specs=[SMEM] + [VMEM] * (2 * rest) + [any_space],
+        in_specs=[SMEM] + [VMEM] * (2 * rest),
         out_specs=VMEM,
         compiler_params=params(16),
         name="finish",
-    )(place, *mine, *others, later)
+    )(place, *mine, *others)
     experts, units = expert_out.shape[:2]
-    hidden, own, send = pl.pallas_call(
+    hidden, send = pl.pallas_call(
         expert_kernel,
         out_shape=(
             jax.ShapeDtypeStruct((experts, rows, units), BF16),
-            jax.ShapeDtypeStruct((experts, units, half), BF16),
             jax.ShapeDtypeStruct((rows, half), BF16),
         ),
-        in_specs=[SMEM, VMEM, VMEM, VMEM, HBM],
-        out_specs=(VMEM,) * 3,
-        scratch_shapes=[
-            pltpu.VMEM((experts, units, half), BF16),
-            pltpu.SemaphoreType.DMA((2 * experts,)),
-        ],
-        compiler_params=params(24),
+        in_specs=[SMEM, VMEM, VMEM, VMEM],
+        out_specs=(VMEM, VMEM),
+        compiler_params=params(8),
         name="experts",
-    )(place, slot_in, early, later, in_hbm(expert_out))
+    )(place, slot_in, expert_in, expert_out)
     received = swap_pair(send)
     keep = pl.pallas_call(
         own_kernel,
         out_shape=jax.ShapeDtypeStruct((rows, half), F32),
-        in_specs=[VMEM, VMEM, any_space],
+        in_specs=[SMEM, VMEM, VMEM, any_space],
         out_specs=VMEM,
         cost_estimate=cost(2 * rows * units * half * experts, 2 * experts * units * half),
-        compiler_params=params(16),
+        compiler_params=params(8),
         name="own",
-    )(hidden, own, send)
+    )(place, hidden, expert_out, send)
     partial = (keep + received.astype(F32)).astype(BF16)
     partials = jnp.broadcast_to(partial, (groups * rest, rows, half))
     partials = lax.all_to_all(partials, ("wide", "rest"), split_axis=0, concat_axis=0, tiled=True)

time: 49.3 us -> 47.2 us (0.957)
  Pallas kernels: 16.3 us -> 11.7 us
  waiting for transfers between devices: 2.04 us -> 4.3 us
    ppermute x6, waiting for transfers between devices: 2.04 us -> 4.3 us  [move(): return lax.ppermute(value, axes, moves)]
    pallas_call x1 -> x0, Pallas kernels: 2.24 us -> none  [shards(): pl.pallas_call(load_kernel, out_shape=jax.ShapeDtypeStruct((expert_in.sha...]
    pallas_call x1, Pallas kernels: 3.81 us -> 1.75 us  [shards(): pl.pallas_call(expert_kernel, out_shape=(jax.ShapeDtypeStruct((experts, r...]
  transfers between devices with their start and end apart: 6 -> 6, of which waited for: 4 -> 5; matrix products, arithmetic and copies ran while one was open for 0% -> 0% of each run, Pallas kernels for 10% -> 5%
where the time goes in v8:
time: 47.2 us; the launch traced here: 47 us
  blocking collectives  28.1 us (60%)
  Pallas kernels  11.7 us (25%)
  waiting for transfers between devices  4.3 us (9%)
  starting transfers between devices  2.76 us (6%)
    all_to_all x1, blocking collectives, shards(): lax.all_to_all(send.reshape(groups, rows, -1), 'wide', split_axis=0, conc...  15 us
    all_to_all x1, blocking collectives, shards(): lax.all_to_all(partials, ('wide', 'rest'), split_axis=0, concat_axis=0, t...  13.1 us
    pallas_call x1, Pallas kernels, shards(): pl.pallas_call(gather_kernel, out_shape=(jax.ShapeDtypeStruct((count, slo...  4.81 us
    ppermute x6, waiting for transfers between devices, move(): return lax.ppermute(value, axes, moves)  4.3 us
    ppermute x6, starting transfers between devices, move(): return lax.ppermute(value, axes, moves)  2.76 us
    pallas_call x1, Pallas kernels, shards(): pl.pallas_call(expert_kernel, out_shape=(jax.ShapeDtypeStruct((experts, r...  1.75 us
    pallas_call x1, Pallas kernels, shards(): pl.pallas_call(mix_other_kernel, out_shape=jax.ShapeDtypeStruct((count, m...  1.74 us
    pallas_call x1, Pallas kernels, shards(): pl.pallas_call(mix_kernel, out_shape=(pltpu.HBM((count, model), BF16), ja...  1.21 us
  transfers between devices with their start and end apart: 6, of which 5 were waited for; matrix products, arithmetic and copies ran while one was open for 0% of the time, Pallas kernels for 5%

profile of v8, /device:TPU:0, one launch (start us, length us, event | category | flops | bytes accessed | tf_op | source)
XLA Modules:
  0.0 47.0 jit_solution(17659053956736902102)
XLA Ops:
  0.0 4.8 %gather.1 = (f32[2048,128]{1,0:T(8,128)S(1)}, f32[128,512]{1,0:T(8,128)S(1)}, f32[128,128]{1,0:T(8,128)S(1)}, bf16[128,640]{1,0:T(8,128)(2,1)S(1)}) custom-call(s32[1]{0:T(128)} %bitcast.place, bf16[2048,1024]{1,0:T(8,128)(2,1)} %tokens.1, bf16[1024,128]{1,0:T(8,128)(2,1)} %slot_params.1), custom_call_target="tpu_custom_call" | custom-call | tf_op jit(solution)/shard_map/gather/pallas_call | solution.py:246
  4.8 0.5 %collective-permute-start = (bf16[128,640]{1,0:T(8,128)(2,1)S(1)}, bf16[128,640]{1,0:T(8,128)(2,1)S(1)}, u32[]{:S(2)}, u32[]{:S(2)}) collective-permute-start(bf16[128,640]{1,0:T(8,128)(2,1)S(1)} %get-tuple-element.14.after), channel_id=1, source_target_pairs={{0,1},{1,0},{2,3},{3,2},{4,5},{5,4},{6,7},{7,6},{8,9},{9,8},{10,11... | collective-permute-start | bytes 491528 | tf_op jit(solution)/shard_map/ppermute | solution.py:230
  5.3 0.6 %combine.1 = bf16[2048,128]{1,0:T(8,128)(2,1)S(1)} custom-call(f32[2048,128]{1,0:T(8,128)S(1)} %get-tuple-element.13.logits, bf16[128,640]{1,0:T(8,128)(2,1)S(1)} %get-tuple-element.14.after), custom_call_target="tpu_custom_call" | custom-call | flops 2097152 | bytes 1572864 | tf_op jit(solution)/shard_map/combine/pallas_call | solution.py:266
  6.0 0.4 collective-permute-done.received
  6.4 0.0 slice-start
  6.4 0.0 slice-start.2
  6.4 0.0 slice-start.1
  6.4 0.0 slice-start.3
  6.4 0.3 pair.1
  6.7 15.0 %all_to_all.10.received = bf16[8,16,640]{2,1,0:T(8,128)(2,1)S(1)} all-to-all(bf16[8,16,640]{2,1,0:T(8,128)(2,1)S(1)} %bitcast.9), channel_id=1, replica_groups=mesh['wide'=8,'rest'=2,'pair'=2] {'wide'}, dimensions={0} | all-to-all | bytes 327680 | tf_op jit(solution)/shard_map/all_to_all | solution.py:284
  21.7 0.3 merge.1.refs_0_
  22.0 0.0 collective-permute-start.3
  22.0 1.6 %collective-permute-start.2 = (bf16[16,640]{1,0:T(8,128)(2,1)S(1)}, bf16[16,640]{1,0:T(8,128)(2,1)S(1)}, u32[]{:S(2)}, u32[]{:S(2)}) collective-permute-start(bf16[16,640]{1,0:T(8,128)(2,1)S(1)} %merge.1.refs_0_), channel_id=1, source_target_pairs={{0,3},{1,2},{2,1},{3,0},{4,7},{5,6},{6,5},{7,4},{8,11},{9,10},{10,... | collective-permute-start | bytes 61448 | tf_op jit(solution)/shard_map/ppermute | solution.py:230
  23.7 0.5 %collective-permute-start.1 = (bf16[16,640]{1,0:T(8,128)(2,1)S(1)}, bf16[16,640]{1,0:T(8,128)(2,1)S(1)}, u32[]{:S(2)}, u32[]{:S(2)}) collective-permute-start(bf16[16,640]{1,0:T(8,128)(2,1)S(1)} %merge.1.refs_0_), channel_id=1, source_target_pairs={{0,2},{1,3},{2,0},{3,1},{4,6},{5,7},{6,4},{7,5},{8,10},{9,11},{10,... | collective-permute-start | bytes 61448 | tf_op jit(solution)/shard_map/ppermute | solution.py:230
  24.2 0.0 collective-permute-done.3.refs_3_
  24.2 1.1 %collective-permute-done.2.refs_2_ = bf16[16,640]{1,0:T(8,128)(2,1)S(1)} collective-permute-done((bf16[16,640]{1,0:T(8,128)(2,1)S(1)}, bf16[16,640]{1,0:T(8,128)(2,1)S(1)}, u32[]{:S(2)}, u32[]{:S(2)}) %collective-permute-start.2) | collective-permute-done | bytes 20512 | tf_op jit(solution)/shard_map/ppermute | solution.py:230
  25.3 2.1 %collective-permute-done.1.refs_1_ = bf16[16,640]{1,0:T(8,128)(2,1)S(1)} collective-permute-done((bf16[16,640]{1,0:T(8,128)(2,1)S(1)}, bf16[16,640]{1,0:T(8,128)(2,1)S(1)}, u32[]{:S(2)}, u32[]{:S(2)}) %collective-permute-start.1) | collective-permute-done | bytes 20512 | tf_op jit(solution)/shard_map/ppermute | solution.py:230
  27.4 0.2 finish.1.slot_in
  27.7 0.0 slice-done
  27.7 0.0 slice-done.2
  27.7 0.0 slice-done.1
  27.7 0.0 slice-done.3
  27.7 1.8 %experts.1 = (bf16[4,16,1024]{2,1,0:T(8,128)(2,1)S(1)}, bf16[16,512]{1,0:T(8,128)(2,1)S(1)}) custom-call(s32[1]{0:T(128)} %bitcast.place, bf16[16,1024]{1,0:T(8,128)(2,1)S(1)} %finish.1.slot_in, bf16[4,1024,1024]{2,1,0:T(8,128)(2,1)S(1)} %bitcast.8, bf16[4,1024,1024]{2,1,0:T(8,128)(2,1)S(1)} %bitcast.6), custom_call_target="tpu_custom_call" | custom-call | tf_op jit(solution)/shard_map/experts/pallas_call | solution.py:305
  29.5 0.0 collective-permute-start.4
  29.5 0.7 %own.1 = f32[16,512]{1,0:T(8,128)S(1)} custom-call(s32[1]{0:T(128)} %bitcast.place, bf16[4,16,1024]{2,1,0:T(8,128)(2,1)S(1)} %get-tuple-element.17.hidden, bf16[4,1024,1024]{2,1,0:T(8,128)(2,1)S(1)} %bitcast.6, bf16[16,512]{1,0:T(8,128)(2,1)S(1)} %get-tuple-element.18.after), custom_call_target="tpu_custom_call" | custom-call | flops 67108864 | bytes 4194304 | tf_op jit(solution)/shard_map/own/pallas_call | solution.py:317
  30.2 0.5 %collective-permute-done.4 = bf16[16,512]{1,0:T(8,128)(2,1)S(1)} collective-permute-done((bf16[16,512]{1,0:T(8,128)(2,1)S(1)}, bf16[16,512]{1,0:T(8,128)(2,1)S(1)}, u32[]{:S(2)}, u32[]{:S(2)}) %collective-permute-start.4) | collective-permute-done | bytes 16416 | tf_op jit(solution)/shard_map/ppermute | solution.py:230
  30.7 13.1 %all_to_all.11 = bf16[16,16,512]{2,1,0:T(8,128)(2,1)S(1)} all-to-all(bf16[16,16,512]{2,1,0:T(8,128)(2,1)S(1)} %broadcast_in_dim.3), channel_id=1, replica_groups=mesh['wide'=8,'rest'=2,'pair'=2] {'wide','rest'}, dimensions={0} | all-to-all | bytes 524288 | tf_op jit(solution)/shard_map/all_to_all | solution.py:328
  43.8 0.1 collective-permute-start.5
  43.9 1.2 %mix.1 = (bf16[2048,1024]{1,0:T(8,128)(2,1)}, bf16[1024,512]{1,0:T(8,128)(2,1)S(1)}) custom-call(s32[1]{0:T(128)} %bitcast.place, bf16[2048,128]{1,0:T(8,128)(2,1)S(1)} %combine.1, bf16[128,512]{1,0:T(8,128)(2,1)S(1)} %bitcast.11), custom_call_target="tpu_custom_call" | custom-call | flops 268435456 | bytes 2621440 | tf_op jit(solution)/shard_map/mix/pallas_call | solution.py:333
  45.1 0.1 collective-permute-done.5.slot_out
  45.2 1.7 %mix_other.1 = bf16[2048,1024]{1,0:T(8,128)(2,1)} custom-call(s32[1]{0:T(128)} %bitcast.place, bf16[2048,128]{1,0:T(8,128)(2,1)S(1)} %combine.1, bf16[128,512]{1,0:T(8,128)(2,1)S(1)} %collective-permute-done.5.slot_out, bf16[1024,512]{1,0:T(8,128)(2,1)S(1)} %get-tuple-element.19.rest, ...), custom_call_target="tpu_custom_call", output_to_operand_aliasing={{}: (4, {})} | custom-call | flops 268435456 | bytes 2621440 | tf_op jit(solution)/shard_map/mix_other/pallas_call | solution.py:346
  (5 shorter events, 0.1 us)
Async XLA Ops:
  4.8 1.5 %collective-permute-start = (bf16[128,640]{1,0:T(8,128)(2,1)S(1)}, bf16[128,640]{1,0:T(8,128)(2,1)S(1)}, u32[]{:S(2)}, u32[]{:S(2)}) collective-permute-start(bf16[128,640]{1,0:T(8,128)(2,1)S(1)} %get-tuple-element.14.after), channel_id=1, source_target_pairs={{0,1},{1,0},{2,3},{3,2},{4,5},{5,4},{6,7},{7,6},{8,9},{9,8},{10,11... | collective-permute-start | bytes 491528 | tf_op jit(solution)/shard_map/ppermute | solution.py:230
  6.4 21.3 %slice-start = ((s8[8388608]{0:T(1024)(128)(4,1)}), s8[4194304]{0:T(1024)(128)(4,1)S(1)}, s32[]{:S(2)}) async-start(s8[8388608]{0:T(1024)(128)(4,1)} %bitcast.5), calls=%async_computation.2 | async-start | bytes 8388608
  6.4 21.3 %slice-start.2 = ((s8[8388608]{0:T(1024)(128)(4,1)}), s8[4194304]{0:T(1024)(128)(4,1)S(1)}, s32[]{:S(2)}) async-start(s8[8388608]{0:T(1024)(128)(4,1)} %bitcast.7), calls=%async_computation.4 | async-start | bytes 8388608
  6.4 21.3 %slice-start.1 = ((s8[8388608]{0:T(1024)(128)(4,1)}), s8[4194304]{0:T(1024)(128)(4,1)S(1)}, s32[]{:S(2)}) async-start(s8[8388608]{0:T(1024)(128)(4,1)} %bitcast.5), calls=%async_computation.3 | async-start | bytes 8388608
  6.4 21.4 %slice-start.3 = ((s8[8388608]{0:T(1024)(128)(4,1)}), s8[4194304]{0:T(1024)(128)(4,1)S(1)}, s32[]{:S(2)}) async-start(s8[8388608]{0:T(1024)(128)(4,1)} %bitcast.7), calls=%async_computation.5 | async-start | bytes 8388608
  22.0 2.2 %collective-permute-start.3 = (bf16[16,640]{1,0:T(8,128)(2,1)S(1)}, bf16[16,640]{1,0:T(8,128)(2,1)S(1)}, u32[]{:S(2)}, u32[]{:S(2)}) collective-permute-start(bf16[16,640]{1,0:T(8,128)(2,1)S(1)} %merge.1.refs_0_), channel_id=1, source_target_pairs={{0,1},{1,0},{2,3},{3,2},{4,5},{5,4},{6,7},{7,6},{8,9},{9,8},{10,11... | collective-permute-start | bytes 61448 | tf_op jit(solution)/shard_map/ppermute | solution.py:230
  22.0 3.3 %collective-permute-start.2 = (bf16[16,640]{1,0:T(8,128)(2,1)S(1)}, bf16[16,640]{1,0:T(8,128)(2,1)S(1)}, u32[]{:S(2)}, u32[]{:S(2)}) collective-permute-start(bf16[16,640]{1,0:T(8,128)(2,1)S(1)} %merge.1.refs_0_), channel_id=1, source_target_pairs={{0,3},{1,2},{2,1},{3,0},{4,7},{5,6},{6,5},{7,4},{8,11},{9,10},{10,... | collective-permute-start | bytes 61448 | tf_op jit(solution)/shard_map/ppermute | solution.py:230
  23.7 3.8 %collective-permute-start.1 = (bf16[16,640]{1,0:T(8,128)(2,1)S(1)}, bf16[16,640]{1,0:T(8,128)(2,1)S(1)}, u32[]{:S(2)}, u32[]{:S(2)}) collective-permute-start(bf16[16,640]{1,0:T(8,128)(2,1)S(1)} %merge.1.refs_0_), channel_id=1, source_target_pairs={{0,2},{1,3},{2,0},{3,1},{4,6},{5,7},{6,4},{7,5},{8,10},{9,11},{10,... | collective-permute-start | bytes 61448 | tf_op jit(solution)/shard_map/ppermute | solution.py:230
  29.5 1.2 %collective-permute-start.4 = (bf16[16,512]{1,0:T(8,128)(2,1)S(1)}, bf16[16,512]{1,0:T(8,128)(2,1)S(1)}, u32[]{:S(2)}, u32[]{:S(2)}) collective-permute-start(bf16[16,512]{1,0:T(8,128)(2,1)S(1)} %get-tuple-element.18.after), channel_id=1, source_target_pairs={{0,1},{1,0},{2,3},{3,2},{4,5},{5,4},{6,7},{7,6},{8,9},{9,8},{10,11... | collective-permute-start | bytes 49160 | tf_op jit(solution)/shard_map/ppermute | solution.py:230
  43.8 1.4 %collective-permute-start.5 = (bf16[128,512]{1,0:T(8,128)(2,1)S(1)}, bf16[128,512]{1,0:T(8,128)(2,1)S(1)}, u32[]{:S(2)}, u32[]{:S(2)}) collective-permute-start(bf16[128,512]{1,0:T(8,128)(2,1)S(1)} %bitcast.10), channel_id=1, source_target_pairs={{0,1},{1,0},{2,3},{3,2},{4,5},{5,4},{6,7},{7,6},{8,9},{9,8},{10,11... | collective-permute-start | bytes 393224 | tf_op jit(solution)/shard_map/ppermute | solution.py:230

commit v9 on v8

--- a/solution.py
+++ b/solution.py
@@ -1,4 +1,3 @@
-import functools
 import math
 
 import jax
@@ -10,7 +9,7 @@
 
 SLOT_PER = 4
 SIDE = 128
-TOKEN_GROUPS = 4
+CHUNK = 256
 F32 = jnp.float32
 BF16 = jnp.bfloat16
 VMEM = pl.BlockSpec(memory_space=pltpu.VMEM)
@@ -59,40 +58,26 @@
     )
 
 
-def gather_kernel(
-    place, tokens, slot_params, logits, keep, side, send, held, table, sums, sems
-):
-    slots = slot_params.shape[1]
-    groups = sums.shape[0]
-    size = tokens.shape[0] // groups
-    spans = [pl.ds(g * size, size) for g in range(groups)]
-    table_copy = pltpu.make_async_copy(slot_params, table, sems.at[groups])
+def gather_kernel(place, tokens, slot_params, logits, keep, side, send, held, raw, table, sems):
+    chunks = tokens.shape[0] // CHUNK
+    spans = [pl.ds(i * CHUNK, CHUNK) for i in range(chunks)]
+    table_copy = pltpu.make_async_copy(slot_params, raw, sems.at[chunks])
     table_copy.start()
-    copies = [pltpu.make_async_copy(tokens.at[span], held.at[span], sems.at[g]) for g, span in enumerate(spans)]
+    copies = [pltpu.make_async_copy(tokens.at[span], held.at[span], sems.at[i]) for i, span in enumerate(spans)]
     for copy in copies:
         copy.start()
     table_copy.wait()
-    parts, peaks, totals = [], [], []
-    for g in range(groups + 1):
-        if g < groups:
-            copies[g].wait()
-            parts.append(dot(held[spans[g], :], table[...]))
-            logits[spans[g], :] = parts[g]
-            peaks.append(jnp.max(parts[g], axis=0, keepdims=True))
-        if g > 0:
-            weights = jnp.exp(parts[g - 1] - peaks[g - 1])
-            totals.append(jnp.sum(weights, axis=0, keepdims=True))
-            sums[g - 1] = dot(weights.T.astype(BF16), held[spans[g - 1], :])
-    peak = functools.reduce(jnp.maximum, peaks)
-    scales = [jnp.exp(part - peak) for part in peaks]
-    total = sum(scale * part for scale, part in zip(scales, totals))
-    row = lax.broadcasted_iota(jnp.int32, (8, slots), 0)
-    columns = jnp.zeros((8, slots), F32)
-    for index, value in enumerate([peak, total] + scales):
-        columns = jnp.where(row == index, value, columns)
-    columns = columns.T
-    peak, total = columns[:, 0:1], columns[:, 1:2]
-    result = sum(columns[:, 2 + g : 3 + g] * sums[g] for g in range(groups))
+    table[...] = raw[...].astype(F32).T.astype(BF16)
+    high = None
+    for copy, span in zip(copies, spans):
+        copy.wait()
+        part = lax.dot_general(table[...], held[span, :], (((1,), (1,)), ((), ())), preferred_element_type=F32)
+        logits[:, span] = part
+        high = part if high is None else jnp.maximum(high, part)
+    peak = jnp.max(high, axis=1, keepdims=True)
+    weights = jnp.exp(logits[...] - peak)
+    total = jnp.sum(weights, axis=1, keepdims=True)
+    result = dot(weights.astype(BF16), held[...])
     half = result.shape[1] // 2
     left, right = result[:, :half], result[:, half:]
     first = place[0] == 0
@@ -175,8 +160,8 @@
 
 def combine_kernel(logits, after, combine):
     value = logits[...]
-    weights = jnp.exp(value - jnp.max(value, axis=1, keepdims=True))
-    combine[...] = (weights / jnp.sum(weights, axis=1, keepdims=True)).astype(BF16)
+    weights = jnp.exp(value - jnp.max(value, axis=0, keepdims=True))
+    combine[...] = (weights / jnp.sum(weights, axis=0, keepdims=True)).T.astype(BF16)
 
 
 def mix_kernel(place, combine, slot_out, mixed, rest, held, sems):
@@ -246,7 +231,7 @@
     logits, keep, side, send = pl.pallas_call(
         gather_kernel,
         out_shape=(
-            jax.ShapeDtypeStruct((count, slots), F32),
+            jax.ShapeDtypeStruct((slots, count), F32),
             jax.ShapeDtypeStruct((slots, half), F32),
             jax.ShapeDtypeStruct((slots, SIDE), F32),
             jax.ShapeDtypeStruct((slots, half + SIDE), BF16),
@@ -256,8 +241,8 @@
         scratch_shapes=[
             pltpu.VMEM((count, model), BF16),
             pltpu.VMEM((model, slots), BF16),
-            pltpu.VMEM((TOKEN_GROUPS, slots, model), F32),
-            pltpu.SemaphoreType.DMA((TOKEN_GROUPS + 1,)),
+            pltpu.VMEM((slots, model), BF16),
+            pltpu.SemaphoreType.DMA((count // CHUNK + 1,)),
         ],
         compiler_params=params(40),
         name="gather",

time: 47.2 us -> 47.8 us (1.013)
    pallas_call x1, Pallas kernels: 4.81 us -> 5.47 us  [shards(): pl.pallas_call(gather_kernel, out_shape=(jax.ShapeDtypeStruct((slots, cou...]
where the time goes in v9:
time: 47.8 us; the launch traced here: 47.6 us
  blocking collectives  28.1 us (59%)
  Pallas kernels  12.1 us (25%)
  waiting for transfers between devices  4.54 us (9%)
  starting transfers between devices  2.76 us (6%)
    all_to_all x1, blocking collectives, shards(): lax.all_to_all(send.reshape(groups, rows, -1), 'wide', split_axis=0, conc...  15 us
    all_to_all x1, blocking collectives, shards(): lax.all_to_all(partials, ('wide', 'rest'), split_axis=0, concat_axis=0, t...  13.1 us
    pallas_call x1, Pallas kernels, shards(): pl.pallas_call(gather_kernel, out_shape=(jax.ShapeDtypeStruct((slots, cou...  5.47 us
    ppermute x6, waiting for transfers between devices, move(): return lax.ppermute(value, axes, moves)  4.54 us
    ppermute x6, starting transfers between devices, move(): return lax.ppermute(value, axes, moves)  2.76 us
    pallas_call x1, Pallas kernels, shards(): pl.pallas_call(expert_kernel, out_shape=(jax.ShapeDtypeStruct((experts, r...  1.75 us
    pallas_call x1, Pallas kernels, shards(): pl.pallas_call(mix_other_kernel, out_shape=jax.ShapeDtypeStruct((count, m...  1.74 us
    pallas_call x1, Pallas kernels, shards(): pl.pallas_call(mix_kernel, out_shape=(pltpu.HBM((count, model), BF16), ja...  1.21 us
  transfers between devices with their start and end apart: 6, of which 5 were waited for; matrix products, arithmetic and copies ran while one was open for 0% of the time, Pallas kernels for 5%

profile of v9, /device:TPU:0, one launch (start us, length us, event | category | flops | bytes accessed | tf_op | source)
XLA Modules:
  0.0 47.6 jit_solution(17982645843376084286)
XLA Ops:
  0.0 5.5 %gather.1 = (f32[128,2048]{1,0:T(8,128)S(1)}, f32[128,512]{1,0:T(8,128)S(1)}, f32[128,128]{1,0:T(8,128)S(1)}, bf16[128,640]{1,0:T(8,128)(2,1)S(1)}) custom-call(s32[1]{0:T(128)} %bitcast.place, bf16[2048,1024]{1,0:T(8,128)(2,1)} %tokens.1, bf16[1024,128]{1,0:T(8,128)(2,1)} %slot_params.1), custom_call_target="tpu_custom_call" | custom-call | tf_op jit(solution)/shard_map/gather/pallas_call | solution.py:231
  5.5 0.5 %collective-permute-start = (bf16[128,640]{1,0:T(8,128)(2,1)S(1)}, bf16[128,640]{1,0:T(8,128)(2,1)S(1)}, u32[]{:S(2)}, u32[]{:S(2)}) collective-permute-start(bf16[128,640]{1,0:T(8,128)(2,1)S(1)} %get-tuple-element.14.after), channel_id=1, source_target_pairs={{0,1},{1,0},{2,3},{3,2},{4,5},{5,4},{6,7},{7,6},{8,9},{9,8},{10,11... | collective-permute-start | bytes 491528 | tf_op jit(solution)/shard_map/ppermute | solution.py:215
  6.0 0.4 combine.1
  6.4 0.6 %collective-permute-done.received = bf16[128,640]{1,0:T(8,128)(2,1)S(1)} collective-permute-done((bf16[128,640]{1,0:T(8,128)(2,1)S(1)}, bf16[128,640]{1,0:T(8,128)(2,1)S(1)}, u32[]{:S(2)}, u32[]{:S(2)}) %collective-permute-start) | collective-permute-done | bytes 163872 | tf_op jit(solution)/shard_map/ppermute | solution.py:215
  7.0 0.0 slice-start
  7.0 0.0 slice-start.2
  7.0 0.0 slice-start.1
  7.0 0.0 slice-start.3
  7.0 0.3 pair.1
  7.4 15.0 %all_to_all.10.received = bf16[8,16,640]{2,1,0:T(8,128)(2,1)S(1)} all-to-all(bf16[8,16,640]{2,1,0:T(8,128)(2,1)S(1)} %bitcast.9), channel_id=1, replica_groups=mesh['wide'=8,'rest'=2,'pair'=2] {'wide'}, dimensions={0} | all-to-all | bytes 327680 | tf_op jit(solution)/shard_map/all_to_all | solution.py:269
  22.4 0.3 merge.1.refs_0_
  22.7 0.0 collective-permute-start.3
  22.7 1.6 %collective-permute-start.2 = (bf16[16,640]{1,0:T(8,128)(2,1)S(1)}, bf16[16,640]{1,0:T(8,128)(2,1)S(1)}, u32[]{:S(2)}, u32[]{:S(2)}) collective-permute-start(bf16[16,640]{1,0:T(8,128)(2,1)S(1)} %merge.1.refs_0_), channel_id=1, source_target_pairs={{0,3},{1,2},{2,1},{3,0},{4,7},{5,6},{6,5},{7,4},{8,11},{9,10},{10,... | collective-permute-start | bytes 61448 | tf_op jit(solution)/shard_map/ppermute | solution.py:215
  24.3 0.5 %collective-permute-start.1 = (bf16[16,640]{1,0:T(8,128)(2,1)S(1)}, bf16[16,640]{1,0:T(8,128)(2,1)S(1)}, u32[]{:S(2)}, u32[]{:S(2)}) collective-permute-start(bf16[16,640]{1,0:T(8,128)(2,1)S(1)} %merge.1.refs_0_), channel_id=1, source_target_pairs={{0,2},{1,3},{2,0},{3,1},{4,6},{5,7},{6,4},{7,5},{8,10},{9,11},{10,... | collective-permute-start | bytes 61448 | tf_op jit(solution)/shard_map/ppermute | solution.py:215
  24.8 0.0 collective-permute-done.3.refs_3_
  24.8 1.1 %collective-permute-done.2.refs_2_ = bf16[16,640]{1,0:T(8,128)(2,1)S(1)} collective-permute-done((bf16[16,640]{1,0:T(8,128)(2,1)S(1)}, bf16[16,640]{1,0:T(8,128)(2,1)S(1)}, u32[]{:S(2)}, u32[]{:S(2)}) %collective-permute-start.2) | collective-permute-done | bytes 20512 | tf_op jit(solution)/shard_map/ppermute | solution.py:215
  26.0 2.1 %collective-permute-done.1.refs_1_ = bf16[16,640]{1,0:T(8,128)(2,1)S(1)} collective-permute-done((bf16[16,640]{1,0:T(8,128)(2,1)S(1)}, bf16[16,640]{1,0:T(8,128)(2,1)S(1)}, u32[]{:S(2)}, u32[]{:S(2)}) %collective-permute-start.1) | collective-permute-done | bytes 20512 | tf_op jit(solution)/shard_map/ppermute | solution.py:215
  28.1 0.2 finish.1.slot_in
  28.4 0.0 slice-done
  28.4 0.0 slice-done.2
  28.4 0.0 slice-done.1
  28.4 0.0 slice-done.3
  28.4 1.8 %experts.1 = (bf16[4,16,1024]{2,1,0:T(8,128)(2,1)S(1)}, bf16[16,512]{1,0:T(8,128)(2,1)S(1)}) custom-call(s32[1]{0:T(128)} %bitcast.place, bf16[16,1024]{1,0:T(8,128)(2,1)S(1)} %finish.1.slot_in, bf16[4,1024,1024]{2,1,0:T(8,128)(2,1)S(1)} %bitcast.8, bf16[4,1024,1024]{2,1,0:T(8,128)(2,1)S(1)} %bitcast.6), custom_call_target="tpu_custom_call" | custom-call | tf_op jit(solution)/shard_map/experts/pallas_call | solution.py:290
  30.2 0.0 collective-permute-start.4
  30.2 0.7 %own.1 = f32[16,512]{1,0:T(8,128)S(1)} custom-call(s32[1]{0:T(128)} %bitcast.place, bf16[4,16,1024]{2,1,0:T(8,128)(2,1)S(1)} %get-tuple-element.17.hidden, bf16[4,1024,1024]{2,1,0:T(8,128)(2,1)S(1)} %bitcast.6, bf16[16,512]{1,0:T(8,128)(2,1)S(1)} %get-tuple-element.18.after), custom_call_target="tpu_custom_call" | custom-call | flops 67108864 | bytes 4194304 | tf_op jit(solution)/shard_map/own/pallas_call | solution.py:302
  30.8 0.5 %collective-permute-done.4 = bf16[16,512]{1,0:T(8,128)(2,1)S(1)} collective-permute-done((bf16[16,512]{1,0:T(8,128)(2,1)S(1)}, bf16[16,512]{1,0:T(8,128)(2,1)S(1)}, u32[]{:S(2)}, u32[]{:S(2)}) %collective-permute-start.4) | collective-permute-done | bytes 16416 | tf_op jit(solution)/shard_map/ppermute | solution.py:215
  31.4 13.1 %all_to_all.11 = bf16[16,16,512]{2,1,0:T(8,128)(2,1)S(1)} all-to-all(bf16[16,16,512]{2,1,0:T(8,128)(2,1)S(1)} %broadcast_in_dim.3), channel_id=1, replica_groups=mesh['wide'=8,'rest'=2,'pair'=2] {'wide','rest'}, dimensions={0} | all-to-all | bytes 524288 | tf_op jit(solution)/shard_map/all_to_all | solution.py:313
  44.5 0.1 collective-permute-start.5
  44.6 1.2 %mix.1 = (bf16[2048,1024]{1,0:T(8,128)(2,1)}, bf16[1024,512]{1,0:T(8,128)(2,1)S(1)}) custom-call(s32[1]{0:T(128)} %bitcast.place, bf16[2048,128]{1,0:T(8,128)(2,1)S(1)} %combine.1, bf16[128,512]{1,0:T(8,128)(2,1)S(1)} %bitcast.11), custom_call_target="tpu_custom_call" | custom-call | flops 268435456 | bytes 2621440 | tf_op jit(solution)/shard_map/mix/pallas_call | solution.py:318
  45.8 0.1 collective-permute-done.5.slot_out
  45.9 1.7 %mix_other.1 = bf16[2048,1024]{1,0:T(8,128)(2,1)} custom-call(s32[1]{0:T(128)} %bitcast.place, bf16[2048,128]{1,0:T(8,128)(2,1)S(1)} %combine.1, bf16[128,512]{1,0:T(8,128)(2,1)S(1)} %collective-permute-done.5.slot_out, bf16[1024,512]{1,0:T(8,128)(2,1)S(1)} %get-tuple-element.19.rest, ...), custom_call_target="tpu_custom_call", output_to_operand_aliasing={{}: (4, {})} | custom-call | flops 268435456 | bytes 2621440 | tf_op jit(solution)/shard_map/mix_other/pallas_call | solution.py:331
  (5 shorter events, 0.1 us)
Async XLA Ops:
  5.5 1.5 %collective-permute-start = (bf16[128,640]{1,0:T(8,128)(2,1)S(1)}, bf16[128,640]{1,0:T(8,128)(2,1)S(1)}, u32[]{:S(2)}, u32[]{:S(2)}) collective-permute-start(bf16[128,640]{1,0:T(8,128)(2,1)S(1)} %get-tuple-element.14.after), channel_id=1, source_target_pairs={{0,1},{1,0},{2,3},{3,2},{4,5},{5,4},{6,7},{7,6},{8,9},{9,8},{10,11... | collective-permute-start | bytes 491528 | tf_op jit(solution)/shard_map/ppermute | solution.py:215
  7.0 21.3 %slice-start = ((s8[8388608]{0:T(1024)(128)(4,1)}), s8[4194304]{0:T(1024)(128)(4,1)S(1)}, s32[]{:S(2)}) async-start(s8[8388608]{0:T(1024)(128)(4,1)} %bitcast.5), calls=%async_computation.2 | async-start | bytes 8388608
  7.0 21.3 %slice-start.2 = ((s8[8388608]{0:T(1024)(128)(4,1)}), s8[4194304]{0:T(1024)(128)(4,1)S(1)}, s32[]{:S(2)}) async-start(s8[8388608]{0:T(1024)(128)(4,1)} %bitcast.7), calls=%async_computation.4 | async-start | bytes 8388608
  7.0 21.3 %slice-start.1 = ((s8[8388608]{0:T(1024)(128)(4,1)}), s8[4194304]{0:T(1024)(128)(4,1)S(1)}, s32[]{:S(2)}) async-start(s8[8388608]{0:T(1024)(128)(4,1)} %bitcast.5), calls=%async_computation.3 | async-start | bytes 8388608
  7.0 21.4 %slice-start.3 = ((s8[8388608]{0:T(1024)(128)(4,1)}), s8[4194304]{0:T(1024)(128)(4,1)S(1)}, s32[]{:S(2)}) async-start(s8[8388608]{0:T(1024)(128)(4,1)} %bitcast.7), calls=%async_computation.5 | async-start | bytes 8388608
  22.7 2.2 %collective-permute-start.3 = (bf16[16,640]{1,0:T(8,128)(2,1)S(1)}, bf16[16,640]{1,0:T(8,128)(2,1)S(1)}, u32[]{:S(2)}, u32[]{:S(2)}) collective-permute-start(bf16[16,640]{1,0:T(8,128)(2,1)S(1)} %merge.1.refs_0_), channel_id=1, source_target_pairs={{0,1},{1,0},{2,3},{3,2},{4,5},{5,4},{6,7},{7,6},{8,9},{9,8},{10,11... | collective-permute-start | bytes 61448 | tf_op jit(solution)/shard_map/ppermute | solution.py:215
  22.7 3.3 %collective-permute-start.2 = (bf16[16,640]{1,0:T(8,128)(2,1)S(1)}, bf16[16,640]{1,0:T(8,128)(2,1)S(1)}, u32[]{:S(2)}, u32[]{:S(2)}) collective-permute-start(bf16[16,640]{1,0:T(8,128)(2,1)S(1)} %merge.1.refs_0_), channel_id=1, source_target_pairs={{0,3},{1,2},{2,1},{3,0},{4,7},{5,6},{6,5},{7,4},{8,11},{9,10},{10,... | collective-permute-start | bytes 61448 | tf_op jit(solution)/shard_map/ppermute | solution.py:215
  24.3 3.8 %collective-permute-start.1 = (bf16[16,640]{1,0:T(8,128)(2,1)S(1)}, bf16[16,640]{1,0:T(8,128)(2,1)S(1)}, u32[]{:S(2)}, u32[]{:S(2)}) collective-permute-start(bf16[16,640]{1,0:T(8,128)(2,1)S(1)} %merge.1.refs_0_), channel_id=1, source_target_pairs={{0,2},{1,3},{2,0},{3,1},{4,6},{5,7},{6,4},{7,5},{8,10},{9,11},{10,... | collective-permute-start | bytes 61448 | tf_op jit(solution)/shard_map/ppermute | solution.py:215
  30.2 1.2 %collective-permute-start.4 = (bf16[16,512]{1,0:T(8,128)(2,1)S(1)}, bf16[16,512]{1,0:T(8,128)(2,1)S(1)}, u32[]{:S(2)}, u32[]{:S(2)}) collective-permute-start(bf16[16,512]{1,0:T(8,128)(2,1)S(1)} %get-tuple-element.18.after), channel_id=1, source_target_pairs={{0,1},{1,0},{2,3},{3,2},{4,5},{5,4},{6,7},{7,6},{8,9},{9,8},{10,11... | collective-permute-start | bytes 49160 | tf_op jit(solution)/shard_map/ppermute | solution.py:215
  44.5 1.4 %collective-permute-start.5 = (bf16[128,512]{1,0:T(8,128)(2,1)S(1)}, bf16[128,512]{1,0:T(8,128)(2,1)S(1)}, u32[]{:S(2)}, u32[]{:S(2)}) collective-permute-start(bf16[128,512]{1,0:T(8,128)(2,1)S(1)} %bitcast.10), channel_id=1, source_target_pairs={{0,1},{1,0},{2,3},{3,2},{4,5},{5,4},{6,7},{7,6},{8,9},{9,8},{10,11... | collective-permute-start | bytes 393224 | tf_op jit(solution)/shard_map/ppermute | solution.py:215

commit v10 on v9

--- a/solution.py
+++ b/solution.py
@@ -58,36 +58,49 @@
     )
 
 
-def gather_kernel(place, tokens, slot_params, logits, keep, side, send, held, raw, table, sems):
+def column_half(side, half):
+    return pl.ds(pl.multiple_of(side * half, half), half)
+
+
+def gather_kernel(place, tokens, slot_params, logits, turned, held, side, send, table, sems):
     chunks = tokens.shape[0] // CHUNK
+    slots = slot_params.shape[1]
     spans = [pl.ds(i * CHUNK, CHUNK) for i in range(chunks)]
-    table_copy = pltpu.make_async_copy(slot_params, raw, sems.at[chunks])
+    table_copy = pltpu.make_async_copy(slot_params, table, sems.at[chunks])
     table_copy.start()
     copies = [pltpu.make_async_copy(tokens.at[span], held.at[span], sems.at[i]) for i, span in enumerate(spans)]
     for copy in copies:
         copy.start()
+    high = jnp.full((8, slots), -jnp.inf, F32)
     table_copy.wait()
-    table[...] = raw[...].astype(F32).T.astype(BF16)
-    high = None
     for copy, span in zip(copies, spans):
         copy.wait()
-        part = lax.dot_general(table[...], held[span, :], (((1,), (1,)), ((), ())), preferred_element_type=F32)
-        logits[:, span] = part
-        high = part if high is None else jnp.maximum(high, part)
-    peak = jnp.max(high, axis=1, keepdims=True)
-    weights = jnp.exp(logits[...] - peak)
-    total = jnp.sum(weights, axis=1, keepdims=True)
-    result = dot(weights.astype(BF16), held[...])
-    half = result.shape[1] // 2
-    left, right = result[:, :half], result[:, half:]
-    first = place[0] == 0
-    keep[...] = jnp.where(first, left, right)
+        part = dot(held[span, :], table[...])
+        logits[span, :] = part
+        high = jnp.maximum(high, jnp.max(part.reshape(CHUNK // 8, 8, slots), axis=0))
+    peak = jnp.max(high, axis=0, keepdims=True)
+    total = jnp.zeros((8, slots), F32)
+    columns = []
+    for span in spans:
+        weights = jnp.exp(logits[span, :] - peak)
+        total = total + jnp.sum(weights.reshape(CHUNK // 8, 8, slots), axis=0)
+        columns.append(weights.T.astype(BF16))
+    weights = jnp.concatenate(columns, axis=1)
+    turned[...] = weights
+    half = held.shape[1] // 2
+    send[:, :half] = dot(weights, held[:, column_half(1 - place[0], half)]).astype(BF16)
+    total = jnp.sum(total, axis=0, keepdims=True)
+    peak = jnp.broadcast_to(peak, (8, slots)).T[:, 0:1]
+    total = jnp.broadcast_to(total, (8, slots)).T[:, 0:1]
     side[...] = side_state(peak, total)
-    send[:, :half] = jnp.where(first, right, left).astype(BF16)
     send[:, half:] = side_message(peak, total)
 
 
-def pair_kernel(keep, side, received, combine, send):
+def own_sums_kernel(place, turned, held, after, keep):
+    keep[...] = dot(turned[...], held[:, column_half(place[0], keep.shape[1])])
+
+
+def pair_kernel(keep, side, received, send):
     width = keep.shape[1]
     peak_mine, total_mine = side[:, 0:1], side[:, 1:2]
     peak_other, total_other = read_message(received[:, width:])
@@ -123,7 +136,7 @@
 def finish_kernel(place, *refs):
     slot_in = refs[-1]
     half = slot_in.shape[1] // 2
-    parts = (len(refs) - 1) // 2
+    parts = (len(refs) - 2) // 2
     means = []
     for side in range(2):
         sums, _, total = add_parts([ref[...] for ref in refs[side * parts : (side + 1) * parts]], half)
@@ -141,10 +154,6 @@
     return result
 
 
-def column_half(side, half):
-    return pl.ds(pl.multiple_of(side * half, half), half)
-
-
 def expert_kernel(place, slot_in, expert_in, expert_out, hidden, send):
     values = []
     for e in range(expert_in.shape[0]):
@@ -160,8 +169,8 @@
 
 def combine_kernel(logits, after, combine):
     value = logits[...]
-    weights = jnp.exp(value - jnp.max(value, axis=0, keepdims=True))
-    combine[...] = (weights / jnp.sum(weights, axis=0, keepdims=True)).T.astype(BF16)
+    weights = jnp.exp(value - jnp.max(value, axis=1, keepdims=True))
+    combine[...] = (weights / jnp.sum(weights, axis=1, keepdims=True)).astype(BF16)
 
 
 def mix_kernel(place, combine, slot_out, mixed, rest, held, sems):
@@ -228,44 +237,40 @@
     place = lax.axis_index("pair").astype(jnp.int32).reshape(1)
     any_space = pl.BlockSpec(memory_space=pl.ANY)
 
-    logits, keep, side, send = pl.pallas_call(
+    logits, turned, held, side, send = pl.pallas_call(
         gather_kernel,
         out_shape=(
-            jax.ShapeDtypeStruct((slots, count), F32),
-            jax.ShapeDtypeStruct((slots, half), F32),
+            jax.ShapeDtypeStruct((count, slots), F32),
+            jax.ShapeDtypeStruct((slots, count), BF16),
+            jax.ShapeDtypeStruct((count, model), BF16),
             jax.ShapeDtypeStruct((slots, SIDE), F32),
             jax.ShapeDtypeStruct((slots, half + SIDE), BF16),
         ),
         in_specs=[SMEM, HBM, HBM],
-        out_specs=(VMEM,) * 4,
-        scratch_shapes=[
-            pltpu.VMEM((count, model), BF16),
-            pltpu.VMEM((model, slots), BF16),
-            pltpu.VMEM((slots, model), BF16),
-            pltpu.SemaphoreType.DMA((count // CHUNK + 1,)),
-        ],
-        compiler_params=params(40),
+        out_specs=(VMEM,) * 5,
+        scratch_shapes=[pltpu.VMEM((model, slots), BF16), pltpu.SemaphoreType.DMA((count // CHUNK + 1,))],
+        compiler_params=params(24),
         name="gather",
     )(place, in_hbm(tokens), in_hbm(slot_params))
     received = swap_pair(send)
-    combine = pl.pallas_call(
-        combine_kernel,
-        out_shape=jax.ShapeDtypeStruct((count, slots), BF16),
-        in_specs=[VMEM, any_space],
-        out_specs=VMEM,
-        cost_estimate=cost(8 * count * slots, 6 * count * slots, count * slots),
-        compiler_params=params(16),
-        name="combine",
-    )(logits, send)
+    keep = pl.pallas_call(
+        own_sums_kernel,
+        out_shape=jax.ShapeDtypeStruct((slots, half), F32),
+        in_specs=[SMEM, VMEM, VMEM, any_space],
+        out_specs=VMEM,
+        cost_estimate=cost(2 * slots * count * half, 2 * count * (half + slots)),
+        compiler_params=params(16),
+        name="own_sums",
+    )(place, turned, held, send)
     send = pl.pallas_call(
         pair_kernel,
         out_shape=jax.ShapeDtypeStruct((slots, half + SIDE), BF16),
-        in_specs=[VMEM] * 3 + [any_space],
+        in_specs=[VMEM] * 3,
         out_specs=VMEM,
         cost_estimate=cost(0, 6 * slots * model, 128 * slots * model),
         compiler_params=params(16),
         name="pair",
-    )(keep, side, received, combine)
+    )(keep, side, received)
     received = lax.all_to_all(send.reshape(groups, rows, -1), "wide", split_axis=0, concat_axis=0, tiled=True)
     send = pl.pallas_call(
         merge_kernel,
@@ -278,14 +283,23 @@
     axes = ("rest", "pair")
     mine = [send] + [move(send, axes, (r, 0)) for r in range(1, rest)]
     others = [move(send, axes, (r, 1)) for r in reversed(range(rest))]
+    combine = pl.pallas_call(
+        combine_kernel,
+        out_shape=jax.ShapeDtypeStruct((count, slots), BF16),
+        in_specs=[VMEM, any_space],
+        out_specs=VMEM,
+        cost_estimate=cost(8 * count * slots, 6 * count * slots, count * slots),
+        compiler_params=params(16),
+        name="combine",
+    )(logits, send)
     slot_in = pl.pallas_call(
         finish_kernel,
         out_shape=jax.ShapeDtypeStruct((rows, model), BF16),
-        in_specs=[SMEM] + [VMEM] * (2 * rest),
+        in_specs=[SMEM] + [VMEM] * (2 * rest) + [any_space],
         out_specs=VMEM,
         compiler_params=params(16),
         name="finish",
-    )(place, *mine, *others)
+    )(place, *mine, *others, combine)
     experts, units = expert_out.shape[:2]
     hidden, send = pl.pallas_call(
         expert_kernel,

time: 47.8 us -> 46.6 us (0.975)
  waiting for transfers between devices: 4.54 us -> 3.85 us
  Pallas kernels: 12.1 us -> 11.6 us
    pallas_call x1 -> x2, Pallas kernels: 5.47 us -> 4.72 us  [the longest x1 4.27 us: shards(): pl.pallas_call(gather_kernel, out_shape=(jax.ShapeDtypeStruct((count, slo...]
    ppermute x6, waiting for transfers between devices: 4.54 us -> 3.85 us  [move(): return lax.ppermute(value, axes, moves)]
  transfers between devices with their start and end apart: 6 -> 6, of which waited for: 5 -> 5; matrix products, arithmetic and copies ran while one was open for 0% -> 0% of each run, Pallas kernels for 5% -> 6%
where the time goes in v10:
time: 46.6 us; the launch traced here: 46.5 us
  blocking collectives  28.1 us (60%)
  Pallas kernels  11.6 us (25%)
  waiting for transfers between devices  3.85 us (8%)
  starting transfers between devices  2.74 us (6%)
    all_to_all x1, blocking collectives, shards(): lax.all_to_all(send.reshape(groups, rows, -1), 'wide', split_axis=0, conc...  15 us
    all_to_all x1, blocking collectives, shards(): lax.all_to_all(partials, ('wide', 'rest'), split_axis=0, concat_axis=0, t...  13.1 us
    pallas_call x1, Pallas kernels, shards(): pl.pallas_call(gather_kernel, out_shape=(jax.ShapeDtypeStruct((count, slo...  4.27 us
    ppermute x6, waiting for transfers between devices, move(): return lax.ppermute(value, axes, moves)  3.85 us
    ppermute x6, starting transfers between devices, move(): return lax.ppermute(value, axes, moves)  2.74 us
    pallas_call x1, Pallas kernels, shards(): pl.pallas_call(expert_kernel, out_shape=(jax.ShapeDtypeStruct((experts, r...  1.75 us
    pallas_call x1, Pallas kernels, shards(): pl.pallas_call(mix_other_kernel, out_shape=jax.ShapeDtypeStruct((count, m...  1.74 us
    pallas_call x1, Pallas kernels, shards(): pl.pallas_call(mix_kernel, out_shape=(pltpu.HBM((count, model), BF16), ja...  1.21 us
  transfers between devices with their start and end apart: 6, of which 5 were waited for; matrix products, arithmetic and copies ran while one was open for 0% of the time, Pallas kernels for 6%

profile of v10, /device:TPU:0, one launch (start us, length us, event | category | flops | bytes accessed | tf_op | source)
XLA Modules:
  0.0 46.5 jit_solution(1275518914879058535)
XLA Ops:
  0.0 4.3 %gather.1 = (f32[2048,128]{1,0:T(8,128)S(1)}, bf16[128,2048]{1,0:T(8,128)(2,1)S(1)}, bf16[2048,1024]{1,0:T(8,128)(2,1)S(1)}, f32[128,128]{1,0:T(8,128)S(1)}, bf16[128,640]{1,0:T(8,128)(2,1)S(1)}) custom-call(s32[1]{0:T(128)} %bitcast.place, bf16[2048,1024]{1,0:T(8,128)(2,1)} %tokens.1, bf16[1024,128]{1,0:T(8,128)(2,1)} %slot_params.1), custom_call_target="tpu_custom_call" | custom-call | tf_op jit(solution)/shard_map/gather/pallas_call | solution.py:240
  4.3 0.5 %collective-permute-start = (bf16[128,640]{1,0:T(8,128)(2,1)S(1)}, bf16[128,640]{1,0:T(8,128)(2,1)S(1)}, u32[]{:S(2)}, u32[]{:S(2)}) collective-permute-start(bf16[128,640]{1,0:T(8,128)(2,1)S(1)} %get-tuple-element.17.after), channel_id=1, source_target_pairs={{0,1},{1,0},{2,3},{3,2},{4,5},{5,4},{6,7},{7,6},{8,9},{9,8},{10,11... | collective-permute-start | bytes 491528 | tf_op jit(solution)/shard_map/ppermute | solution.py:224
  4.8 0.4 own_sums.1.keep
  5.2 0.6 %collective-permute-done.received = bf16[128,640]{1,0:T(8,128)(2,1)S(1)} collective-permute-done((bf16[128,640]{1,0:T(8,128)(2,1)S(1)}, bf16[128,640]{1,0:T(8,128)(2,1)S(1)}, u32[]{:S(2)}, u32[]{:S(2)}) %collective-permute-start) | collective-permute-done | bytes 163872 | tf_op jit(solution)/shard_map/ppermute | solution.py:224
  5.8 0.0 slice-start
  5.8 0.0 slice-start.2
  5.8 0.0 slice-start.1
  5.8 0.0 slice-start.3
  5.8 0.3 pair.1
  6.2 15.0 %all_to_all.10.received = bf16[8,16,640]{2,1,0:T(8,128)(2,1)S(1)} all-to-all(bf16[8,16,640]{2,1,0:T(8,128)(2,1)S(1)} %bitcast.9), channel_id=1, replica_groups=mesh['wide'=8,'rest'=2,'pair'=2] {'wide'}, dimensions={0} | all-to-all | bytes 327680 | tf_op jit(solution)/shard_map/all_to_all | solution.py:274
  21.2 0.3 merge.1.after.refs_0_
  21.4 0.0 collective-permute-start.3
  21.5 1.6 %collective-permute-start.2 = (bf16[16,640]{1,0:T(8,128)(2,1)S(1)}, bf16[16,640]{1,0:T(8,128)(2,1)S(1)}, u32[]{:S(2)}, u32[]{:S(2)}) collective-permute-start(bf16[16,640]{1,0:T(8,128)(2,1)S(1)} %merge.1.after.refs_0_), channel_id=1, source_target_pairs={{0,3},{1,2},{2,1},{3,0},{4,7},{5,6},{6,5},{7,4},{8,11},{9,10},{10,... | collective-permute-start | bytes 61448 | tf_op jit(solution)/shard_map/ppermute | solution.py:224
  23.1 0.5 %collective-permute-start.1 = (bf16[16,640]{1,0:T(8,128)(2,1)S(1)}, bf16[16,640]{1,0:T(8,128)(2,1)S(1)}, u32[]{:S(2)}, u32[]{:S(2)}) collective-permute-start(bf16[16,640]{1,0:T(8,128)(2,1)S(1)} %merge.1.after.refs_0_), channel_id=1, source_target_pairs={{0,2},{1,3},{2,0},{3,1},{4,6},{5,7},{6,4},{7,5},{8,10},{9,11},{10,... | collective-permute-start | bytes 61448 | tf_op jit(solution)/shard_map/ppermute | solution.py:224
  23.6 0.6 %combine.1.refs_4_ = bf16[2048,128]{1,0:T(8,128)(2,1)S(1)} custom-call(f32[2048,128]{1,0:T(8,128)S(1)} %get-tuple-element.14.logits, bf16[16,640]{1,0:T(8,128)(2,1)S(1)} %merge.1.after.refs_0_), custom_call_target="tpu_custom_call" | custom-call | flops 2097152 | bytes 1572864 | tf_op jit(solution)/shard_map/combine/pallas_call | solution.py:286
  24.3 0.0 collective-permute-done.3.refs_3_
  24.3 0.5 %collective-permute-done.2.refs_2_ = bf16[16,640]{1,0:T(8,128)(2,1)S(1)} collective-permute-done((bf16[16,640]{1,0:T(8,128)(2,1)S(1)}, bf16[16,640]{1,0:T(8,128)(2,1)S(1)}, u32[]{:S(2)}, u32[]{:S(2)}) %collective-permute-start.2) | collective-permute-done | bytes 20512 | tf_op jit(solution)/shard_map/ppermute | solution.py:224
  24.8 2.2 %collective-permute-done.1.refs_1_ = bf16[16,640]{1,0:T(8,128)(2,1)S(1)} collective-permute-done((bf16[16,640]{1,0:T(8,128)(2,1)S(1)}, bf16[16,640]{1,0:T(8,128)(2,1)S(1)}, u32[]{:S(2)}, u32[]{:S(2)}) %collective-permute-start.1) | collective-permute-done | bytes 20512 | tf_op jit(solution)/shard_map/ppermute | solution.py:224
  26.9 0.2 finish.1.slot_in
  27.2 0.0 slice-done
  27.2 0.0 slice-done.2
  27.2 0.0 slice-done.1
  27.2 0.0 slice-done.3
  27.2 1.8 %experts.1 = (bf16[4,16,1024]{2,1,0:T(8,128)(2,1)S(1)}, bf16[16,512]{1,0:T(8,128)(2,1)S(1)}) custom-call(s32[1]{0:T(128)} %bitcast.place, bf16[16,1024]{1,0:T(8,128)(2,1)S(1)} %finish.1.slot_in, bf16[4,1024,1024]{2,1,0:T(8,128)(2,1)S(1)} %bitcast.8, bf16[4,1024,1024]{2,1,0:T(8,128)(2,1)S(1)} %bitcast.6), custom_call_target="tpu_custom_call" | custom-call | tf_op jit(solution)/shard_map/experts/pallas_call | solution.py:304
  29.0 0.0 collective-permute-start.4
  29.0 0.7 %own.1 = f32[16,512]{1,0:T(8,128)S(1)} custom-call(s32[1]{0:T(128)} %bitcast.place, bf16[4,16,1024]{2,1,0:T(8,128)(2,1)S(1)} %get-tuple-element.19.hidden, bf16[4,1024,1024]{2,1,0:T(8,128)(2,1)S(1)} %bitcast.6, bf16[16,512]{1,0:T(8,128)(2,1)S(1)} %get-tuple-element.20.after), custom_call_target="tpu_custom_call" | custom-call | flops 67108864 | bytes 4194304 | tf_op jit(solution)/shard_map/own/pallas_call | solution.py:316
  29.6 0.5 %collective-permute-done.4 = bf16[16,512]{1,0:T(8,128)(2,1)S(1)} collective-permute-done((bf16[16,512]{1,0:T(8,128)(2,1)S(1)}, bf16[16,512]{1,0:T(8,128)(2,1)S(1)}, u32[]{:S(2)}, u32[]{:S(2)}) %collective-permute-start.4) | collective-permute-done | bytes 16416 | tf_op jit(solution)/shard_map/ppermute | solution.py:224
  30.2 13.1 %all_to_all.11 = bf16[16,16,512]{2,1,0:T(8,128)(2,1)S(1)} all-to-all(bf16[16,16,512]{2,1,0:T(8,128)(2,1)S(1)} %broadcast_in_dim.3), channel_id=1, replica_groups=mesh['wide'=8,'rest'=2,'pair'=2] {'wide','rest'}, dimensions={0} | all-to-all | bytes 524288 | tf_op jit(solution)/shard_map/all_to_all | solution.py:327
  43.3 0.1 collective-permute-start.5
  43.4 1.2 %mix.1 = (bf16[2048,1024]{1,0:T(8,128)(2,1)}, bf16[1024,512]{1,0:T(8,128)(2,1)S(1)}) custom-call(s32[1]{0:T(128)} %bitcast.place, bf16[2048,128]{1,0:T(8,128)(2,1)S(1)} %combine.1.refs_4_, bf16[128,512]{1,0:T(8,128)(2,1)S(1)} %bitcast.11), custom_call_target="tpu_custom_call" | custom-call | flops 268435456 | bytes 2621440 | tf_op jit(solution)/shard_map/mix/pallas_call | solution.py:332
  44.6 0.1 collective-permute-done.5.slot_out
  44.7 1.7 %mix_other.1 = bf16[2048,1024]{1,0:T(8,128)(2,1)} custom-call(s32[1]{0:T(128)} %bitcast.place, bf16[2048,128]{1,0:T(8,128)(2,1)S(1)} %combine.1.refs_4_, bf16[128,512]{1,0:T(8,128)(2,1)S(1)} %collective-permute-done.5.slot_out, bf16[1024,512]{1,0:T(8,128)(2,1)S(1)} %get-tuple-element.21.rest, ...), custom_call_target="tpu_custom_call", output_to_operand_aliasing={{}: (4, {})} | custom-call | flops 268435456 | bytes 2621440 | tf_op jit(solution)/shard_map/mix_other/pallas_call | solution.py:345
  (5 shorter events, 0.1 us)
Async XLA Ops:
  4.3 1.5 %collective-permute-start = (bf16[128,640]{1,0:T(8,128)(2,1)S(1)}, bf16[128,640]{1,0:T(8,128)(2,1)S(1)}, u32[]{:S(2)}, u32[]{:S(2)}) collective-permute-start(bf16[128,640]{1,0:T(8,128)(2,1)S(1)} %get-tuple-element.17.after), channel_id=1, source_target_pairs={{0,1},{1,0},{2,3},{3,2},{4,5},{5,4},{6,7},{7,6},{8,9},{9,8},{10,11... | collective-permute-start | bytes 491528 | tf_op jit(solution)/shard_map/ppermute | solution.py:224
  5.8 21.3 %slice-start = ((s8[8388608]{0:T(1024)(128)(4,1)}), s8[4194304]{0:T(1024)(128)(4,1)S(1)}, s32[]{:S(2)}) async-start(s8[8388608]{0:T(1024)(128)(4,1)} %bitcast.5), calls=%async_computation.2 | async-start | bytes 8388608
  5.8 21.4 %slice-start.2 = ((s8[8388608]{0:T(1024)(128)(4,1)}), s8[4194304]{0:T(1024)(128)(4,1)S(1)}, s32[]{:S(2)}) async-start(s8[8388608]{0:T(1024)(128)(4,1)} %bitcast.7), calls=%async_computation.4 | async-start | bytes 8388608
  5.8 21.4 %slice-start.1 = ((s8[8388608]{0:T(1024)(128)(4,1)}), s8[4194304]{0:T(1024)(128)(4,1)S(1)}, s32[]{:S(2)}) async-start(s8[8388608]{0:T(1024)(128)(4,1)} %bitcast.5), calls=%async_computation.3 | async-start | bytes 8388608
  5.8 21.4 %slice-start.3 = ((s8[8388608]{0:T(1024)(128)(4,1)}), s8[4194304]{0:T(1024)(128)(4,1)S(1)}, s32[]{:S(2)}) async-start(s8[8388608]{0:T(1024)(128)(4,1)} %bitcast.7), calls=%async_computation.5 | async-start | bytes 8388608
  21.4 2.8 %collective-permute-start.3 = (bf16[16,640]{1,0:T(8,128)(2,1)S(1)}, bf16[16,640]{1,0:T(8,128)(2,1)S(1)}, u32[]{:S(2)}, u32[]{:S(2)}) collective-permute-start(bf16[16,640]{1,0:T(8,128)(2,1)S(1)} %merge.1.after.refs_0_), channel_id=1, source_target_pairs={{0,1},{1,0},{2,3},{3,2},{4,5},{5,4},{6,7},{7,6},{8,9},{9,8},{10,11... | collective-permute-start | bytes 61448 | tf_op jit(solution)/shard_map/ppermute | solution.py:224
  21.5 3.3 %collective-permute-start.2 = (bf16[16,640]{1,0:T(8,128)(2,1)S(1)}, bf16[16,640]{1,0:T(8,128)(2,1)S(1)}, u32[]{:S(2)}, u32[]{:S(2)}) collective-permute-start(bf16[16,640]{1,0:T(8,128)(2,1)S(1)} %merge.1.after.refs_0_), channel_id=1, source_target_pairs={{0,3},{1,2},{2,1},{3,0},{4,7},{5,6},{6,5},{7,4},{8,11},{9,10},{10,... | collective-permute-start | bytes 61448 | tf_op jit(solution)/shard_map/ppermute | solution.py:224
  23.1 3.8 %collective-permute-start.1 = (bf16[16,640]{1,0:T(8,128)(2,1)S(1)}, bf16[16,640]{1,0:T(8,128)(2,1)S(1)}, u32[]{:S(2)}, u32[]{:S(2)}) collective-permute-start(bf16[16,640]{1,0:T(8,128)(2,1)S(1)} %merge.1.after.refs_0_), channel_id=1, source_target_pairs={{0,2},{1,3},{2,0},{3,1},{4,6},{5,7},{6,4},{7,5},{8,10},{9,11},{10,... | collective-permute-start | bytes 61448 | tf_op jit(solution)/shard_map/ppermute | solution.py:224
  29.0 1.2 %collective-permute-start.4 = (bf16[16,512]{1,0:T(8,128)(2,1)S(1)}, bf16[16,512]{1,0:T(8,128)(2,1)S(1)}, u32[]{:S(2)}, u32[]{:S(2)}) collective-permute-start(bf16[16,512]{1,0:T(8,128)(2,1)S(1)} %get-tuple-element.20.after), channel_id=1, source_target_pairs={{0,1},{1,0},{2,3},{3,2},{4,5},{5,4},{6,7},{7,6},{8,9},{9,8},{10,11... | collective-permute-start | bytes 49160 | tf_op jit(solution)/shard_map/ppermute | solution.py:224
  43.3 1.4 %collective-permute-start.5 = (bf16[128,512]{1,0:T(8,128)(2,1)S(1)}, bf16[128,512]{1,0:T(8,128)(2,1)S(1)}, u32[]{:S(2)}, u32[]{:S(2)}) collective-permute-start(bf16[128,512]{1,0:T(8,128)(2,1)S(1)} %bitcast.10), channel_id=1, source_target_pairs={{0,1},{1,0},{2,3},{3,2},{4,5},{5,4},{6,7},{7,6},{8,9},{9,8},{10,11... | collective-permute-start | bytes 393224 | tf_op jit(solution)/shard_map/ppermute | solution.py:224

commit v11 on v10

--- a/solution.py
+++ b/solution.py
@@ -84,7 +84,7 @@
     for span in spans:
         weights = jnp.exp(logits[span, :] - peak)
         total = total + jnp.sum(weights.reshape(CHUNK // 8, 8, slots), axis=0)
-        columns.append(weights.T.astype(BF16))
+        columns.append(weights.astype(BF16).T)
     weights = jnp.concatenate(columns, axis=1)
     turned[...] = weights
     half = held.shape[1] // 2

time: 46.6 us -> 46.5 us (level)
  no operation moved by 1% of the time
where the time goes in v11:
time: 46.5 us; the launch traced here: 46.3 us
  blocking collectives  28 us (60%)
  Pallas kernels  11.5 us (25%)
  waiting for transfers between devices  3.83 us (8%)
  starting transfers between devices  2.77 us (6%)
    all_to_all x1, blocking collectives, shards(): lax.all_to_all(send.reshape(groups, rows, -1), 'wide', split_axis=0, conc...  15 us
    all_to_all x1, blocking collectives, shards(): lax.all_to_all(partials, ('wide', 'rest'), split_axis=0, concat_axis=0, t...  13.1 us
    pallas_call x1, Pallas kernels, shards(): pl.pallas_call(gather_kernel, out_shape=(jax.ShapeDtypeStruct((count, slo...  4.17 us
    ppermute x6, waiting for transfers between devices, move(): return lax.ppermute(value, axes, moves)  3.83 us
    ppermute x6, starting transfers between devices, move(): return lax.ppermute(value, axes, moves)  2.77 us
    pallas_call x1, Pallas kernels, shards(): pl.pallas_call(expert_kernel, out_shape=(jax.ShapeDtypeStruct((experts, r...  1.75 us
    pallas_call x1, Pallas kernels, shards(): pl.pallas_call(mix_other_kernel, out_shape=jax.ShapeDtypeStruct((count, m...  1.74 us
    pallas_call x1, Pallas kernels, shards(): pl.pallas_call(mix_kernel, out_shape=(pltpu.HBM((count, model), BF16), ja...  1.21 us
  transfers between devices with their start and end apart: 6, of which 5 were waited for; matrix products, arithmetic and copies ran while one was open for 0% of the time, Pallas kernels for 6%

profile of v11, /device:TPU:0, one launch (start us, length us, event | category | flops | bytes accessed | tf_op | source)
XLA Modules:
  0.0 46.3 jit_solution(1396674972694518461)
XLA Ops:
  0.0 4.2 %gather.1 = (f32[2048,128]{1,0:T(8,128)S(1)}, bf16[128,2048]{1,0:T(8,128)(2,1)S(1)}, bf16[2048,1024]{1,0:T(8,128)(2,1)S(1)}, f32[128,128]{1,0:T(8,128)S(1)}, bf16[128,640]{1,0:T(8,128)(2,1)S(1)}) custom-call(s32[1]{0:T(128)} %bitcast.place, bf16[2048,1024]{1,0:T(8,128)(2,1)} %tokens.1, bf16[1024,128]{1,0:T(8,128)(2,1)} %slot_params.1), custom_call_target="tpu_custom_call" | custom-call | tf_op jit(solution)/shard_map/gather/pallas_call | solution.py:240
  4.2 0.5 %collective-permute-start = (bf16[128,640]{1,0:T(8,128)(2,1)S(1)}, bf16[128,640]{1,0:T(8,128)(2,1)S(1)}, u32[]{:S(2)}, u32[]{:S(2)}) collective-permute-start(bf16[128,640]{1,0:T(8,128)(2,1)S(1)} %get-tuple-element.17.after), channel_id=1, source_target_pairs={{0,1},{1,0},{2,3},{3,2},{4,5},{5,4},{6,7},{7,6},{8,9},{9,8},{10,11... | collective-permute-start | bytes 491528 | tf_op jit(solution)/shard_map/ppermute | solution.py:224
  4.7 0.5 own_sums.1.keep
  5.2 0.6 %collective-permute-done.received = bf16[128,640]{1,0:T(8,128)(2,1)S(1)} collective-permute-done((bf16[128,640]{1,0:T(8,128)(2,1)S(1)}, bf16[128,640]{1,0:T(8,128)(2,1)S(1)}, u32[]{:S(2)}, u32[]{:S(2)}) %collective-permute-start) | collective-permute-done | bytes 163872 | tf_op jit(solution)/shard_map/ppermute | solution.py:224
  5.7 0.0 slice-start
  5.7 0.0 slice-start.2
  5.7 0.0 slice-start.1
  5.7 0.0 slice-start.3
  5.7 0.3 pair.1
  6.1 15.0 %all_to_all.10.received = bf16[8,16,640]{2,1,0:T(8,128)(2,1)S(1)} all-to-all(bf16[8,16,640]{2,1,0:T(8,128)(2,1)S(1)} %bitcast.9), channel_id=1, replica_groups=mesh['wide'=8,'rest'=2,'pair'=2] {'wide'}, dimensions={0} | all-to-all | bytes 327680 | tf_op jit(solution)/shard_map/all_to_all | solution.py:274
  21.1 0.3 merge.1.after.refs_0_
  21.4 0.0 collective-permute-start.3
  21.4 1.6 %collective-permute-start.2 = (bf16[16,640]{1,0:T(8,128)(2,1)S(1)}, bf16[16,640]{1,0:T(8,128)(2,1)S(1)}, u32[]{:S(2)}, u32[]{:S(2)}) collective-permute-start(bf16[16,640]{1,0:T(8,128)(2,1)S(1)} %merge.1.after.refs_0_), channel_id=1, source_target_pairs={{0,3},{1,2},{2,1},{3,0},{4,7},{5,6},{6,5},{7,4},{8,11},{9,10},{10,... | collective-permute-start | bytes 61448 | tf_op jit(solution)/shard_map/ppermute | solution.py:224
  23.0 0.5 %collective-permute-start.1 = (bf16[16,640]{1,0:T(8,128)(2,1)S(1)}, bf16[16,640]{1,0:T(8,128)(2,1)S(1)}, u32[]{:S(2)}, u32[]{:S(2)}) collective-permute-start(bf16[16,640]{1,0:T(8,128)(2,1)S(1)} %merge.1.after.refs_0_), channel_id=1, source_target_pairs={{0,2},{1,3},{2,0},{3,1},{4,6},{5,7},{6,4},{7,5},{8,10},{9,11},{10,... | collective-permute-start | bytes 61448 | tf_op jit(solution)/shard_map/ppermute | solution.py:224
  23.5 0.6 %combine.1.refs_4_ = bf16[2048,128]{1,0:T(8,128)(2,1)S(1)} custom-call(f32[2048,128]{1,0:T(8,128)S(1)} %get-tuple-element.14.logits, bf16[16,640]{1,0:T(8,128)(2,1)S(1)} %merge.1.after.refs_0_), custom_call_target="tpu_custom_call" | custom-call | flops 2097152 | bytes 1572864 | tf_op jit(solution)/shard_map/combine/pallas_call | solution.py:286
  24.2 0.0 collective-permute-done.3.refs_3_
  24.2 0.5 %collective-permute-done.2.refs_2_ = bf16[16,640]{1,0:T(8,128)(2,1)S(1)} collective-permute-done((bf16[16,640]{1,0:T(8,128)(2,1)S(1)}, bf16[16,640]{1,0:T(8,128)(2,1)S(1)}, u32[]{:S(2)}, u32[]{:S(2)}) %collective-permute-start.2) | collective-permute-done | bytes 20512 | tf_op jit(solution)/shard_map/ppermute | solution.py:224
  24.7 2.1 %collective-permute-done.1.refs_1_ = bf16[16,640]{1,0:T(8,128)(2,1)S(1)} collective-permute-done((bf16[16,640]{1,0:T(8,128)(2,1)S(1)}, bf16[16,640]{1,0:T(8,128)(2,1)S(1)}, u32[]{:S(2)}, u32[]{:S(2)}) %collective-permute-start.1) | collective-permute-done | bytes 20512 | tf_op jit(solution)/shard_map/ppermute | solution.py:224
  26.8 0.2 finish.1.slot_in
  27.1 0.0 slice-done
  27.1 0.0 slice-done.2
  27.1 0.0 slice-done.1
  27.1 0.0 slice-done.3
  27.1 1.8 %experts.1 = (bf16[4,16,1024]{2,1,0:T(8,128)(2,1)S(1)}, bf16[16,512]{1,0:T(8,128)(2,1)S(1)}) custom-call(s32[1]{0:T(128)} %bitcast.place, bf16[16,1024]{1,0:T(8,128)(2,1)S(1)} %finish.1.slot_in, bf16[4,1024,1024]{2,1,0:T(8,128)(2,1)S(1)} %bitcast.8, bf16[4,1024,1024]{2,1,0:T(8,128)(2,1)S(1)} %bitcast.6), custom_call_target="tpu_custom_call" | custom-call | tf_op jit(solution)/shard_map/experts/pallas_call | solution.py:304
  28.9 0.0 collective-permute-start.4
  28.9 0.7 %own.1 = f32[16,512]{1,0:T(8,128)S(1)} custom-call(s32[1]{0:T(128)} %bitcast.place, bf16[4,16,1024]{2,1,0:T(8,128)(2,1)S(1)} %get-tuple-element.19.hidden, bf16[4,1024,1024]{2,1,0:T(8,128)(2,1)S(1)} %bitcast.6, bf16[16,512]{1,0:T(8,128)(2,1)S(1)} %get-tuple-element.20.after), custom_call_target="tpu_custom_call" | custom-call | flops 67108864 | bytes 4194304 | tf_op jit(solution)/shard_map/own/pallas_call | solution.py:316
  29.5 0.5 %collective-permute-done.4 = bf16[16,512]{1,0:T(8,128)(2,1)S(1)} collective-permute-done((bf16[16,512]{1,0:T(8,128)(2,1)S(1)}, bf16[16,512]{1,0:T(8,128)(2,1)S(1)}, u32[]{:S(2)}, u32[]{:S(2)}) %collective-permute-start.4) | collective-permute-done | bytes 16416 | tf_op jit(solution)/shard_map/ppermute | solution.py:224
  30.1 13.1 %all_to_all.11 = bf16[16,16,512]{2,1,0:T(8,128)(2,1)S(1)} all-to-all(bf16[16,16,512]{2,1,0:T(8,128)(2,1)S(1)} %broadcast_in_dim.3), channel_id=1, replica_groups=mesh['wide'=8,'rest'=2,'pair'=2] {'wide','rest'}, dimensions={0} | all-to-all | bytes 524288 | tf_op jit(solution)/shard_map/all_to_all | solution.py:327
  43.2 0.1 collective-permute-start.5
  43.3 1.2 %mix.1 = (bf16[2048,1024]{1,0:T(8,128)(2,1)}, bf16[1024,512]{1,0:T(8,128)(2,1)S(1)}) custom-call(s32[1]{0:T(128)} %bitcast.place, bf16[2048,128]{1,0:T(8,128)(2,1)S(1)} %combine.1.refs_4_, bf16[128,512]{1,0:T(8,128)(2,1)S(1)} %bitcast.11), custom_call_target="tpu_custom_call" | custom-call | flops 268435456 | bytes 2621440 | tf_op jit(solution)/shard_map/mix/pallas_call | solution.py:332
  44.5 0.1 collective-permute-done.5.slot_out
  44.6 1.7 %mix_other.1 = bf16[2048,1024]{1,0:T(8,128)(2,1)} custom-call(s32[1]{0:T(128)} %bitcast.place, bf16[2048,128]{1,0:T(8,128)(2,1)S(1)} %combine.1.refs_4_, bf16[128,512]{1,0:T(8,128)(2,1)S(1)} %collective-permute-done.5.slot_out, bf16[1024,512]{1,0:T(8,128)(2,1)S(1)} %get-tuple-element.21.rest, ...), custom_call_target="tpu_custom_call", output_to_operand_aliasing={{}: (4, {})} | custom-call | flops 268435456 | bytes 2621440 | tf_op jit(solution)/shard_map/mix_other/pallas_call | solution.py:345
  (5 shorter events, 0.1 us)
Async XLA Ops:
  4.2 1.6 %collective-permute-start = (bf16[128,640]{1,0:T(8,128)(2,1)S(1)}, bf16[128,640]{1,0:T(8,128)(2,1)S(1)}, u32[]{:S(2)}, u32[]{:S(2)}) collective-permute-start(bf16[128,640]{1,0:T(8,128)(2,1)S(1)} %get-tuple-element.17.after), channel_id=1, source_target_pairs={{0,1},{1,0},{2,3},{3,2},{4,5},{5,4},{6,7},{7,6},{8,9},{9,8},{10,11... | collective-permute-start | bytes 491528 | tf_op jit(solution)/shard_map/ppermute | solution.py:224
  5.7 21.3 %slice-start = ((s8[8388608]{0:T(1024)(128)(4,1)}), s8[4194304]{0:T(1024)(128)(4,1)S(1)}, s32[]{:S(2)}) async-start(s8[8388608]{0:T(1024)(128)(4,1)} %bitcast.5), calls=%async_computation.2 | async-start | bytes 8388608
  5.7 21.3 %slice-start.2 = ((s8[8388608]{0:T(1024)(128)(4,1)}), s8[4194304]{0:T(1024)(128)(4,1)S(1)}, s32[]{:S(2)}) async-start(s8[8388608]{0:T(1024)(128)(4,1)} %bitcast.7), calls=%async_computation.4 | async-start | bytes 8388608
  5.7 21.3 %slice-start.1 = ((s8[8388608]{0:T(1024)(128)(4,1)}), s8[4194304]{0:T(1024)(128)(4,1)S(1)}, s32[]{:S(2)}) async-start(s8[8388608]{0:T(1024)(128)(4,1)} %bitcast.5), calls=%async_computation.3 | async-start | bytes 8388608
  5.7 21.3 %slice-start.3 = ((s8[8388608]{0:T(1024)(128)(4,1)}), s8[4194304]{0:T(1024)(128)(4,1)S(1)}, s32[]{:S(2)}) async-start(s8[8388608]{0:T(1024)(128)(4,1)} %bitcast.7), calls=%async_computation.5 | async-start | bytes 8388608
  21.4 2.8 %collective-permute-start.3 = (bf16[16,640]{1,0:T(8,128)(2,1)S(1)}, bf16[16,640]{1,0:T(8,128)(2,1)S(1)}, u32[]{:S(2)}, u32[]{:S(2)}) collective-permute-start(bf16[16,640]{1,0:T(8,128)(2,1)S(1)} %merge.1.after.refs_0_), channel_id=1, source_target_pairs={{0,1},{1,0},{2,3},{3,2},{4,5},{5,4},{6,7},{7,6},{8,9},{9,8},{10,11... | collective-permute-start | bytes 61448 | tf_op jit(solution)/shard_map/ppermute | solution.py:224
  21.4 3.3 %collective-permute-start.2 = (bf16[16,640]{1,0:T(8,128)(2,1)S(1)}, bf16[16,640]{1,0:T(8,128)(2,1)S(1)}, u32[]{:S(2)}, u32[]{:S(2)}) collective-permute-start(bf16[16,640]{1,0:T(8,128)(2,1)S(1)} %merge.1.after.refs_0_), channel_id=1, source_target_pairs={{0,3},{1,2},{2,1},{3,0},{4,7},{5,6},{6,5},{7,4},{8,11},{9,10},{10,... | collective-permute-start | bytes 61448 | tf_op jit(solution)/shard_map/ppermute | solution.py:224
  23.0 3.8 %collective-permute-start.1 = (bf16[16,640]{1,0:T(8,128)(2,1)S(1)}, bf16[16,640]{1,0:T(8,128)(2,1)S(1)}, u32[]{:S(2)}, u32[]{:S(2)}) collective-permute-start(bf16[16,640]{1,0:T(8,128)(2,1)S(1)} %merge.1.after.refs_0_), channel_id=1, source_target_pairs={{0,2},{1,3},{2,0},{3,1},{4,6},{5,7},{6,4},{7,5},{8,10},{9,11},{10,... | collective-permute-start | bytes 61448 | tf_op jit(solution)/shard_map/ppermute | solution.py:224
  28.9 1.2 %collective-permute-start.4 = (bf16[16,512]{1,0:T(8,128)(2,1)S(1)}, bf16[16,512]{1,0:T(8,128)(2,1)S(1)}, u32[]{:S(2)}, u32[]{:S(2)}) collective-permute-start(bf16[16,512]{1,0:T(8,128)(2,1)S(1)} %get-tuple-element.20.after), channel_id=1, source_target_pairs={{0,1},{1,0},{2,3},{3,2},{4,5},{5,4},{6,7},{7,6},{8,9},{9,8},{10,11... | collective-permute-start | bytes 49160 | tf_op jit(solution)/shard_map/ppermute | solution.py:224
  43.2 1.4 %collective-permute-start.5 = (bf16[128,512]{1,0:T(8,128)(2,1)S(1)}, bf16[128,512]{1,0:T(8,128)(2,1)S(1)}, u32[]{:S(2)}, u32[]{:S(2)}) collective-permute-start(bf16[128,512]{1,0:T(8,128)(2,1)S(1)} %bitcast.10), channel_id=1, source_target_pairs={{0,1},{1,0},{2,3},{3,2},{4,5},{5,4},{6,7},{7,6},{8,9},{9,8},{10,11... | collective-permute-start | bytes 393224 | tf_op jit(solution)/shard_map/ppermute | solution.py:224

commit v12 on v11

--- a/solution.py
+++ b/solution.py
@@ -65,6 +65,7 @@
 def gather_kernel(place, tokens, slot_params, logits, turned, held, side, send, table, sems):
     chunks = tokens.shape[0] // CHUNK
     slots = slot_params.shape[1]
+    middle = slot_params.shape[0] // 2
     spans = [pl.ds(i * CHUNK, CHUNK) for i in range(chunks)]
     table_copy = pltpu.make_async_copy(slot_params, table, sems.at[chunks])
     table_copy.start()
@@ -75,7 +76,7 @@
     table_copy.wait()
     for copy, span in zip(copies, spans):
         copy.wait()
-        part = dot(held[span, :], table[...])
+        part = dot(held[span, :middle], table[:middle, :]) + dot(held[span, middle:], table[middle:, :])
         logits[span, :] = part
         high = jnp.maximum(high, jnp.max(part.reshape(CHUNK // 8, 8, slots), axis=0))
     peak = jnp.max(high, axis=0, keepdims=True)
@@ -328,7 +329,7 @@
     slot_out = jnp.sum(partials.reshape(groups, rest, rows, half).astype(F32), axis=1)
     slot_out = slot_out.astype(BF16).reshape(slots, half)
     other = swap_pair(slot_out)
-    done, blocks = count // 2, 8
+    done, blocks = count * 5 // 8, 16
     mixed, left = pl.pallas_call(
         mix_kernel,
         out_shape=(
@@ -337,7 +338,7 @@
         ),
         in_specs=[SMEM, VMEM, VMEM],
         out_specs=(HBM, VMEM),
-        scratch_shapes=[pltpu.VMEM((done, half), BF16), pltpu.SemaphoreType.DMA((blocks // 2,))],
+        scratch_shapes=[pltpu.VMEM((done, half), BF16), pltpu.SemaphoreType.DMA((blocks * 5 // 8,))],
         cost_estimate=cost(2 * count * slots * half, 2 * count * (half + slots)),
         compiler_params=params(16),
         name="mix",

time: 46.5 us -> 46.5 us (level)
  transfers between devices with their start and end apart: 6 -> 6, of which waited for: 5 -> 4; matrix products, arithmetic and copies ran while one was open for 0% -> 0% of each run, Pallas kernels for 6% -> 7%
where the time goes in v12:
time: 46.5 us; the launch traced here: 46.3 us
  blocking collectives  28 us (60%)
  Pallas kernels  11.5 us (25%)
  waiting for transfers between devices  3.74 us (8%)
  starting transfers between devices  2.78 us (6%)
    all_to_all x1, blocking collectives, shards(): lax.all_to_all(send.reshape(groups, rows, -1), 'wide', split_axis=0, conc...  15 us
    all_to_all x1, blocking collectives, shards(): lax.all_to_all(partials, ('wide', 'rest'), split_axis=0, concat_axis=0, t...  13.1 us
    pallas_call x1, Pallas kernels, shards(): pl.pallas_call(gather_kernel, out_shape=(jax.ShapeDtypeStruct((count, slo...  4.15 us
    ppermute x6, waiting for transfers between devices, move(): return lax.ppermute(value, axes, moves)  3.74 us
    ppermute x6, starting transfers between devices, move(): return lax.ppermute(value, axes, moves)  2.78 us
    pallas_call x1, Pallas kernels, shards(): pl.pallas_call(expert_kernel, out_shape=(jax.ShapeDtypeStruct((experts, r...  1.75 us
    pallas_call x1, Pallas kernels, shards(): pl.pallas_call(mix_other_kernel, out_shape=jax.ShapeDtypeStruct((count, m...  1.72 us
    pallas_call x1, Pallas kernels, shards(): pl.pallas_call(mix_kernel, out_shape=(pltpu.HBM((count, model), BF16), ja...  1.31 us
  transfers between devices with their start and end apart: 6, of which 4 were waited for; matrix products, arithmetic and copies ran while one was open for 0% of the time, Pallas kernels for 7%

profile of v12, /device:TPU:0, one launch (start us, length us, event | category | flops | bytes accessed | tf_op | source)
XLA Modules:
  0.0 46.3 jit_solution(10092707091017450994)
XLA Ops:
  0.0 4.1 %gather.1 = (f32[2048,128]{1,0:T(8,128)S(1)}, bf16[128,2048]{1,0:T(8,128)(2,1)S(1)}, bf16[2048,1024]{1,0:T(8,128)(2,1)S(1)}, f32[128,128]{1,0:T(8,128)S(1)}, bf16[128,640]{1,0:T(8,128)(2,1)S(1)}) custom-call(s32[1]{0:T(128)} %bitcast.place, bf16[2048,1024]{1,0:T(8,128)(2,1)} %tokens.1, bf16[1024,128]{1,0:T(8,128)(2,1)} %slot_params.1), custom_call_target="tpu_custom_call" | custom-call | tf_op jit(solution)/shard_map/gather/pallas_call | solution.py:241
  4.2 0.5 %collective-permute-start = (bf16[128,640]{1,0:T(8,128)(2,1)S(1)}, bf16[128,640]{1,0:T(8,128)(2,1)S(1)}, u32[]{:S(2)}, u32[]{:S(2)}) collective-permute-start(bf16[128,640]{1,0:T(8,128)(2,1)S(1)} %get-tuple-element.17.after), channel_id=1, source_target_pairs={{0,1},{1,0},{2,3},{3,2},{4,5},{5,4},{6,7},{7,6},{8,9},{9,8},{10,11... | collective-permute-start | bytes 491528 | tf_op jit(solution)/shard_map/ppermute | solution.py:225
  4.7 0.5 own_sums.1.keep
  5.2 0.6 %collective-permute-done.received = bf16[128,640]{1,0:T(8,128)(2,1)S(1)} collective-permute-done((bf16[128,640]{1,0:T(8,128)(2,1)S(1)}, bf16[128,640]{1,0:T(8,128)(2,1)S(1)}, u32[]{:S(2)}, u32[]{:S(2)}) %collective-permute-start) | collective-permute-done | bytes 163872 | tf_op jit(solution)/shard_map/ppermute | solution.py:225
  5.7 0.0 slice-start
  5.7 0.0 slice-start.2
  5.7 0.0 slice-start.1
  5.7 0.0 slice-start.3
  5.7 0.3 pair.1
  6.1 15.0 %all_to_all.10.received = bf16[8,16,640]{2,1,0:T(8,128)(2,1)S(1)} all-to-all(bf16[8,16,640]{2,1,0:T(8,128)(2,1)S(1)} %bitcast.9), channel_id=1, replica_groups=mesh['wide'=8,'rest'=2,'pair'=2] {'wide'}, dimensions={0} | all-to-all | bytes 327680 | tf_op jit(solution)/shard_map/all_to_all | solution.py:275
  21.1 0.3 merge.1.after.refs_0_
  21.3 0.0 collective-permute-start.3
  21.4 1.6 %collective-permute-start.2 = (bf16[16,640]{1,0:T(8,128)(2,1)S(1)}, bf16[16,640]{1,0:T(8,128)(2,1)S(1)}, u32[]{:S(2)}, u32[]{:S(2)}) collective-permute-start(bf16[16,640]{1,0:T(8,128)(2,1)S(1)} %merge.1.after.refs_0_), channel_id=1, source_target_pairs={{0,3},{1,2},{2,1},{3,0},{4,7},{5,6},{6,5},{7,4},{8,11},{9,10},{10,... | collective-permute-start | bytes 61448 | tf_op jit(solution)/shard_map/ppermute | solution.py:225
  23.0 0.5 %collective-permute-start.1 = (bf16[16,640]{1,0:T(8,128)(2,1)S(1)}, bf16[16,640]{1,0:T(8,128)(2,1)S(1)}, u32[]{:S(2)}, u32[]{:S(2)}) collective-permute-start(bf16[16,640]{1,0:T(8,128)(2,1)S(1)} %merge.1.after.refs_0_), channel_id=1, source_target_pairs={{0,2},{1,3},{2,0},{3,1},{4,6},{5,7},{6,4},{7,5},{8,10},{9,11},{10,... | collective-permute-start | bytes 61448 | tf_op jit(solution)/shard_map/ppermute | solution.py:225
  23.5 0.6 %combine.1.refs_4_ = bf16[2048,128]{1,0:T(8,128)(2,1)S(1)} custom-call(f32[2048,128]{1,0:T(8,128)S(1)} %get-tuple-element.14.logits, bf16[16,640]{1,0:T(8,128)(2,1)S(1)} %merge.1.after.refs_0_), custom_call_target="tpu_custom_call" | custom-call | flops 2097152 | bytes 1572864 | tf_op jit(solution)/shard_map/combine/pallas_call | solution.py:287
  24.2 0.0 collective-permute-done.3.refs_3_
  24.2 0.5 %collective-permute-done.2.refs_2_ = bf16[16,640]{1,0:T(8,128)(2,1)S(1)} collective-permute-done((bf16[16,640]{1,0:T(8,128)(2,1)S(1)}, bf16[16,640]{1,0:T(8,128)(2,1)S(1)}, u32[]{:S(2)}, u32[]{:S(2)}) %collective-permute-start.2) | collective-permute-done | bytes 20512 | tf_op jit(solution)/shard_map/ppermute | solution.py:225
  24.6 2.1 %collective-permute-done.1.refs_1_ = bf16[16,640]{1,0:T(8,128)(2,1)S(1)} collective-permute-done((bf16[16,640]{1,0:T(8,128)(2,1)S(1)}, bf16[16,640]{1,0:T(8,128)(2,1)S(1)}, u32[]{:S(2)}, u32[]{:S(2)}) %collective-permute-start.1) | collective-permute-done | bytes 20512 | tf_op jit(solution)/shard_map/ppermute | solution.py:225
  26.8 0.2 finish.1.slot_in
  27.0 0.0 slice-done
  27.0 0.0 slice-done.2
  27.1 0.0 slice-done.1
  27.1 0.0 slice-done.3
  27.1 1.8 %experts.1 = (bf16[4,16,1024]{2,1,0:T(8,128)(2,1)S(1)}, bf16[16,512]{1,0:T(8,128)(2,1)S(1)}) custom-call(s32[1]{0:T(128)} %bitcast.place, bf16[16,1024]{1,0:T(8,128)(2,1)S(1)} %finish.1.slot_in, bf16[4,1024,1024]{2,1,0:T(8,128)(2,1)S(1)} %bitcast.8, bf16[4,1024,1024]{2,1,0:T(8,128)(2,1)S(1)} %bitcast.6), custom_call_target="tpu_custom_call" | custom-call | tf_op jit(solution)/shard_map/experts/pallas_call | solution.py:305
  28.8 0.0 collective-permute-start.4
  28.8 0.7 %own.1 = f32[16,512]{1,0:T(8,128)S(1)} custom-call(s32[1]{0:T(128)} %bitcast.place, bf16[4,16,1024]{2,1,0:T(8,128)(2,1)S(1)} %get-tuple-element.19.hidden, bf16[4,1024,1024]{2,1,0:T(8,128)(2,1)S(1)} %bitcast.6, bf16[16,512]{1,0:T(8,128)(2,1)S(1)} %get-tuple-element.20.after), custom_call_target="tpu_custom_call" | custom-call | flops 67108864 | bytes 4194304 | tf_op jit(solution)/shard_map/own/pallas_call | solution.py:317
  29.5 0.5 %collective-permute-done.4 = bf16[16,512]{1,0:T(8,128)(2,1)S(1)} collective-permute-done((bf16[16,512]{1,0:T(8,128)(2,1)S(1)}, bf16[16,512]{1,0:T(8,128)(2,1)S(1)}, u32[]{:S(2)}, u32[]{:S(2)}) %collective-permute-start.4) | collective-permute-done | bytes 16416 | tf_op jit(solution)/shard_map/ppermute | solution.py:225
  30.1 13.1 %all_to_all.11 = bf16[16,16,512]{2,1,0:T(8,128)(2,1)S(1)} all-to-all(bf16[16,16,512]{2,1,0:T(8,128)(2,1)S(1)} %broadcast_in_dim.3), channel_id=1, replica_groups=mesh['wide'=8,'rest'=2,'pair'=2] {'wide','rest'}, dimensions={0} | all-to-all | bytes 524288 | tf_op jit(solution)/shard_map/all_to_all | solution.py:328
  43.2 0.1 collective-permute-start.5
  43.2 1.3 %mix.1 = (bf16[2048,1024]{1,0:T(8,128)(2,1)}, bf16[768,512]{1,0:T(8,128)(2,1)S(1)}) custom-call(s32[1]{0:T(128)} %bitcast.place, bf16[2048,128]{1,0:T(8,128)(2,1)S(1)} %combine.1.refs_4_, bf16[128,512]{1,0:T(8,128)(2,1)S(1)} %bitcast.11), custom_call_target="tpu_custom_call" | custom-call | flops 268435456 | bytes 2621440 | tf_op jit(solution)/shard_map/mix/pallas_call | solution.py:333
  44.6 0.0 collective-permute-done.5.slot_out
  44.6 1.7 %mix_other.1 = bf16[2048,1024]{1,0:T(8,128)(2,1)} custom-call(s32[1]{0:T(128)} %bitcast.place, bf16[2048,128]{1,0:T(8,128)(2,1)S(1)} %combine.1.refs_4_, bf16[128,512]{1,0:T(8,128)(2,1)S(1)} %collective-permute-done.5.slot_out, bf16[768,512]{1,0:T(8,128)(2,1)S(1)} %get-tuple-element.21.rest, ...), custom_call_target="tpu_custom_call", output_to_operand_aliasing={{}: (4, {})} | custom-call | flops 268435456 | bytes 2621440 | tf_op jit(solution)/shard_map/mix_other/pallas_call | solution.py:346
  (5 shorter events, 0.1 us)
Async XLA Ops:
  4.2 1.6 %collective-permute-start = (bf16[128,640]{1,0:T(8,128)(2,1)S(1)}, bf16[128,640]{1,0:T(8,128)(2,1)S(1)}, u32[]{:S(2)}, u32[]{:S(2)}) collective-permute-start(bf16[128,640]{1,0:T(8,128)(2,1)S(1)} %get-tuple-element.17.after), channel_id=1, source_target_pairs={{0,1},{1,0},{2,3},{3,2},{4,5},{5,4},{6,7},{7,6},{8,9},{9,8},{10,11... | collective-permute-start | bytes 491528 | tf_op jit(solution)/shard_map/ppermute | solution.py:225
  5.7 21.3 %slice-start = ((s8[8388608]{0:T(1024)(128)(4,1)}), s8[4194304]{0:T(1024)(128)(4,1)S(1)}, s32[]{:S(2)}) async-start(s8[8388608]{0:T(1024)(128)(4,1)} %bitcast.5), calls=%async_computation.2 | async-start | bytes 8388608
  5.7 21.3 %slice-start.2 = ((s8[8388608]{0:T(1024)(128)(4,1)}), s8[4194304]{0:T(1024)(128)(4,1)S(1)}, s32[]{:S(2)}) async-start(s8[8388608]{0:T(1024)(128)(4,1)} %bitcast.7), calls=%async_computation.4 | async-start | bytes 8388608
  5.7 21.3 %slice-start.1 = ((s8[8388608]{0:T(1024)(128)(4,1)}), s8[4194304]{0:T(1024)(128)(4,1)S(1)}, s32[]{:S(2)}) async-start(s8[8388608]{0:T(1024)(128)(4,1)} %bitcast.5), calls=%async_computation.3 | async-start | bytes 8388608
  5.7 21.3 %slice-start.3 = ((s8[8388608]{0:T(1024)(128)(4,1)}), s8[4194304]{0:T(1024)(128)(4,1)S(1)}, s32[]{:S(2)}) async-start(s8[8388608]{0:T(1024)(128)(4,1)} %bitcast.7), calls=%async_computation.5 | async-start | bytes 8388608
  21.3 2.8 %collective-permute-start.3 = (bf16[16,640]{1,0:T(8,128)(2,1)S(1)}, bf16[16,640]{1,0:T(8,128)(2,1)S(1)}, u32[]{:S(2)}, u32[]{:S(2)}) collective-permute-start(bf16[16,640]{1,0:T(8,128)(2,1)S(1)} %merge.1.after.refs_0_), channel_id=1, source_target_pairs={{0,1},{1,0},{2,3},{3,2},{4,5},{5,4},{6,7},{7,6},{8,9},{9,8},{10,11... | collective-permute-start | bytes 61448 | tf_op jit(solution)/shard_map/ppermute | solution.py:225
  21.4 3.3 %collective-permute-start.2 = (bf16[16,640]{1,0:T(8,128)(2,1)S(1)}, bf16[16,640]{1,0:T(8,128)(2,1)S(1)}, u32[]{:S(2)}, u32[]{:S(2)}) collective-permute-start(bf16[16,640]{1,0:T(8,128)(2,1)S(1)} %merge.1.after.refs_0_), channel_id=1, source_target_pairs={{0,3},{1,2},{2,1},{3,0},{4,7},{5,6},{6,5},{7,4},{8,11},{9,10},{10,... | collective-permute-start | bytes 61448 | tf_op jit(solution)/shard_map/ppermute | solution.py:225
  23.0 3.8 %collective-permute-start.1 = (bf16[16,640]{1,0:T(8,128)(2,1)S(1)}, bf16[16,640]{1,0:T(8,128)(2,1)S(1)}, u32[]{:S(2)}, u32[]{:S(2)}) collective-permute-start(bf16[16,640]{1,0:T(8,128)(2,1)S(1)} %merge.1.after.refs_0_), channel_id=1, source_target_pairs={{0,2},{1,3},{2,0},{3,1},{4,6},{5,7},{6,4},{7,5},{8,10},{9,11},{10,... | collective-permute-start | bytes 61448 | tf_op jit(solution)/shard_map/ppermute | solution.py:225
  28.8 1.2 %collective-permute-start.4 = (bf16[16,512]{1,0:T(8,128)(2,1)S(1)}, bf16[16,512]{1,0:T(8,128)(2,1)S(1)}, u32[]{:S(2)}, u32[]{:S(2)}) collective-permute-start(bf16[16,512]{1,0:T(8,128)(2,1)S(1)} %get-tuple-element.20.after), channel_id=1, source_target_pairs={{0,1},{1,0},{2,3},{3,2},{4,5},{5,4},{6,7},{7,6},{8,9},{9,8},{10,11... | collective-permute-start | bytes 49160 | tf_op jit(solution)/shard_map/ppermute | solution.py:225
  43.2 1.4 %collective-permute-start.5 = (bf16[128,512]{1,0:T(8,128)(2,1)S(1)}, bf16[128,512]{1,0:T(8,128)(2,1)S(1)}, u32[]{:S(2)}, u32[]{:S(2)}) collective-permute-start(bf16[128,512]{1,0:T(8,128)(2,1)S(1)} %bitcast.10), channel_id=1, source_target_pairs={{0,1},{1,0},{2,3},{3,2},{4,5},{5,4},{6,7},{7,6},{8,9},{9,8},{10,11... | collective-permute-start | bytes 393224 | tf_op jit(solution)/shard_map/ppermute | solution.py:225

commit v13 on v11

--- a/solution.py
+++ b/solution.py
@@ -9,7 +9,7 @@
 
 SLOT_PER = 4
 SIDE = 128
-CHUNK = 256
+CHUNK = 512
 F32 = jnp.float32
 BF16 = jnp.bfloat16
 VMEM = pl.BlockSpec(memory_space=pltpu.VMEM)
@@ -133,17 +133,16 @@
     send[:, width:] = side_message(peak, total)
 
 
-def finish_kernel(place, *refs):
-    slot_in = refs[-1]
-    half = slot_in.shape[1] // 2
-    parts = (len(refs) - 2) // 2
+def find_slot_in(place, mine, others):
+    half = mine[0].shape[1] - SIDE
     means = []
-    for side in range(2):
-        sums, _, total = add_parts([ref[...] for ref in refs[side * parts : (side + 1) * parts]], half)
+    for parts in (mine, others):
+        sums, _, total = add_parts([part[...] for part in parts], half)
         means.append((sums / total).astype(BF16))
     first = place[0] == 0
-    slot_in[:, :half] = jnp.where(first, means[0], means[1])
-    slot_in[:, half:] = jnp.where(first, means[1], means[0])
+    return jnp.concatenate(
+        [jnp.where(first, means[0], means[1]), jnp.where(first, means[1], means[0])], axis=1
+    )
 
 
 def second_product(hidden, weights, columns):
@@ -154,10 +153,13 @@
     return result
 
 
-def expert_kernel(place, slot_in, expert_in, expert_out, hidden, send):
+def expert_kernel(place, expert_in, expert_out, after, *refs):
+    parts, hidden, send = refs[:-2], refs[-2], refs[-1]
+    count = len(parts) // 2
+    slot_in = find_slot_in(place, parts[:count], parts[count:])
     values = []
     for e in range(expert_in.shape[0]):
-        values.append(jax.nn.gelu(dot(slot_in[...], expert_in[e])).astype(BF16))
+        values.append(jax.nn.gelu(dot(slot_in, expert_in[e])).astype(BF16))
         hidden[e] = values[e]
     send[...] = second_product(values, expert_out, column_half(1 - place[0], send.shape[1])).astype(BF16)
 
@@ -292,14 +294,6 @@
         compiler_params=params(16),
         name="combine",
     )(logits, send)
-    slot_in = pl.pallas_call(
-        finish_kernel,
-        out_shape=jax.ShapeDtypeStruct((rows, model), BF16),
-        in_specs=[SMEM] + [VMEM] * (2 * rest) + [any_space],
-        out_specs=VMEM,
-        compiler_params=params(16),
-        name="finish",
-    )(place, *mine, *others, combine)
     experts, units = expert_out.shape[:2]
     hidden, send = pl.pallas_call(
         expert_kernel,
@@ -307,11 +301,11 @@
             jax.ShapeDtypeStruct((experts, rows, units), BF16),
             jax.ShapeDtypeStruct((rows, half), BF16),
         ),
-        in_specs=[SMEM, VMEM, VMEM, VMEM],
+        in_specs=[SMEM, VMEM, VMEM, any_space] + [VMEM] * (2 * rest),
         out_specs=(VMEM, VMEM),
         compiler_params=params(8),
         name="experts",
-    )(place, slot_in, expert_in, expert_out)
+    )(place, expert_in, expert_out, combine, *mine, *others)
     received = swap_pair(send)
     keep = pl.pallas_call(
         own_kernel,
@@ -324,8 +318,8 @@
     )(place, hidden, expert_out, send)
     partial = (keep + received.astype(F32)).astype(BF16)
     partials = jnp.broadcast_to(partial, (groups * rest, rows, half))
-    partials = lax.all_to_all(partials, ("wide", "rest"), split_axis=0, concat_axis=0, tiled=True)
-    slot_out = jnp.sum(partials.reshape(groups, rest, rows, half).astype(F32), axis=1)
+    partials = lax.all_to_all(partials, ("rest", "wide"), split_axis=0, concat_axis=0, tiled=True)
+    slot_out = jnp.sum(partials.reshape(rest, groups, rows, half).astype(F32), axis=0)
     slot_out = slot_out.astype(BF16).reshape(slots, half)
     other = swap_pair(slot_out)
     done, blocks = count // 2, 8

time: 46.5 us -> 47.1 us (1.013)
  Pallas kernels: 11.5 us -> 12 us
    pallas_call x1, Pallas kernels: 4.17 us -> 4.76 us  [shards(): pl.pallas_call(gather_kernel, out_shape=(jax.ShapeDtypeStruct((count, slo...]
where the time goes in v13:
time: 47.1 us; the launch traced here: 46.9 us
  blocking collectives  28.1 us (60%)
  Pallas kernels  12 us (25%)
  waiting for transfers between devices  3.83 us (8%)
  starting transfers between devices  2.77 us (6%)
    all_to_all x1, blocking collectives, shards(): lax.all_to_all(send.reshape(groups, rows, -1), 'wide', split_axis=0, conc...  15 us
    all_to_all x1, blocking collectives, shards(): lax.all_to_all(partials, ('rest', 'wide'), split_axis=0, concat_axis=0, t...  13.1 us
    pallas_call x1, Pallas kernels, shards(): pl.pallas_call(gather_kernel, out_shape=(jax.ShapeDtypeStruct((count, slo...  4.76 us
    ppermute x6, waiting for transfers between devices, move(): return lax.ppermute(value, axes, moves)  3.83 us
    ppermute x6, starting transfers between devices, move(): return lax.ppermute(value, axes, moves)  2.77 us
    pallas_call x1, Pallas kernels, shards(): pl.pallas_call(expert_kernel, out_shape=(jax.ShapeDtypeStruct((experts, r...  1.96 us
    pallas_call x1, Pallas kernels, shards(): pl.pallas_call(mix_other_kernel, out_shape=jax.ShapeDtypeStruct((count, m...  1.74 us
    pallas_call x1, Pallas kernels, shards(): pl.pallas_call(mix_kernel, out_shape=(pltpu.HBM((count, model), BF16), ja...  1.21 us
  transfers between devices with their start and end apart: 6, of which 5 were waited for; matrix products, arithmetic and copies ran while one was open for 0% of the time, Pallas kernels for 6%

profile of v13, /device:TPU:0, one launch (start us, length us, event | category | flops | bytes accessed | tf_op | source)
XLA Modules:
  0.0 46.9 jit_solution(1457340201364433915)
XLA Ops:
  0.0 4.8 %gather.1 = (f32[2048,128]{1,0:T(8,128)S(1)}, bf16[128,2048]{1,0:T(8,128)(2,1)S(1)}, bf16[2048,1024]{1,0:T(8,128)(2,1)S(1)}, f32[128,128]{1,0:T(8,128)S(1)}, bf16[128,640]{1,0:T(8,128)(2,1)S(1)}) custom-call(s32[1]{0:T(128)} %bitcast.place, bf16[2048,1024]{1,0:T(8,128)(2,1)} %tokens.1, bf16[1024,128]{1,0:T(8,128)(2,1)} %slot_params.1), custom_call_target="tpu_custom_call" | custom-call | tf_op jit(solution)/shard_map/gather/pallas_call | solution.py:242
  4.8 0.5 %collective-permute-start = (bf16[128,640]{1,0:T(8,128)(2,1)S(1)}, bf16[128,640]{1,0:T(8,128)(2,1)S(1)}, u32[]{:S(2)}, u32[]{:S(2)}) collective-permute-start(bf16[128,640]{1,0:T(8,128)(2,1)S(1)} %get-tuple-element.17.after), channel_id=1, source_target_pairs={{0,1},{1,0},{2,3},{3,2},{4,5},{5,4},{6,7},{7,6},{8,9},{9,8},{10,11... | collective-permute-start | bytes 491528 | tf_op jit(solution)/shard_map/ppermute | solution.py:226
  5.3 0.5 own_sums.1.keep
  5.8 0.6 %collective-permute-done.received = bf16[128,640]{1,0:T(8,128)(2,1)S(1)} collective-permute-done((bf16[128,640]{1,0:T(8,128)(2,1)S(1)}, bf16[128,640]{1,0:T(8,128)(2,1)S(1)}, u32[]{:S(2)}, u32[]{:S(2)}) %collective-permute-start) | collective-permute-done | bytes 163872 | tf_op jit(solution)/shard_map/ppermute | solution.py:226
  6.3 0.0 slice-start
  6.3 0.0 slice-start.2
  6.3 0.0 slice-start.1
  6.3 0.0 slice-start.3
  6.3 0.3 pair.1
  6.7 15.0 %all_to_all.10.received = bf16[8,16,640]{2,1,0:T(8,128)(2,1)S(1)} all-to-all(bf16[8,16,640]{2,1,0:T(8,128)(2,1)S(1)} %bitcast.8), channel_id=1, replica_groups=mesh['wide'=8,'rest'=2,'pair'=2] {'wide'}, dimensions={0} | all-to-all | bytes 327680 | tf_op jit(solution)/shard_map/all_to_all | solution.py:276
  21.7 0.3 merge.1.after.refs_0_
  22.0 0.0 collective-permute-start.3
  22.0 1.6 %collective-permute-start.2 = (bf16[16,640]{1,0:T(8,128)(2,1)S(1)}, bf16[16,640]{1,0:T(8,128)(2,1)S(1)}, u32[]{:S(2)}, u32[]{:S(2)}) collective-permute-start(bf16[16,640]{1,0:T(8,128)(2,1)S(1)} %merge.1.after.refs_0_), channel_id=1, source_target_pairs={{0,3},{1,2},{2,1},{3,0},{4,7},{5,6},{6,5},{7,4},{8,11},{9,10},{10,... | collective-permute-start | bytes 61448 | tf_op jit(solution)/shard_map/ppermute | solution.py:226
  23.6 0.5 %collective-permute-start.1 = (bf16[16,640]{1,0:T(8,128)(2,1)S(1)}, bf16[16,640]{1,0:T(8,128)(2,1)S(1)}, u32[]{:S(2)}, u32[]{:S(2)}) collective-permute-start(bf16[16,640]{1,0:T(8,128)(2,1)S(1)} %merge.1.after.refs_0_), channel_id=1, source_target_pairs={{0,2},{1,3},{2,0},{3,1},{4,6},{5,7},{6,4},{7,5},{8,10},{9,11},{10,... | collective-permute-start | bytes 61448 | tf_op jit(solution)/shard_map/ppermute | solution.py:226
  24.1 0.6 %combine.1.after = bf16[2048,128]{1,0:T(8,128)(2,1)S(1)} custom-call(f32[2048,128]{1,0:T(8,128)S(1)} %get-tuple-element.14.logits, bf16[16,640]{1,0:T(8,128)(2,1)S(1)} %merge.1.after.refs_0_), custom_call_target="tpu_custom_call" | custom-call | flops 2097152 | bytes 1572864 | tf_op jit(solution)/shard_map/combine/pallas_call | solution.py:288
  24.8 0.0 collective-permute-done.3.refs_3_
  24.8 0.5 %collective-permute-done.2.refs_2_ = bf16[16,640]{1,0:T(8,128)(2,1)S(1)} collective-permute-done((bf16[16,640]{1,0:T(8,128)(2,1)S(1)}, bf16[16,640]{1,0:T(8,128)(2,1)S(1)}, u32[]{:S(2)}, u32[]{:S(2)}) %collective-permute-start.2) | collective-permute-done | bytes 20512 | tf_op jit(solution)/shard_map/ppermute | solution.py:226
  25.3 2.1 %collective-permute-done.1.refs_1_ = bf16[16,640]{1,0:T(8,128)(2,1)S(1)} collective-permute-done((bf16[16,640]{1,0:T(8,128)(2,1)S(1)}, bf16[16,640]{1,0:T(8,128)(2,1)S(1)}, u32[]{:S(2)}, u32[]{:S(2)}) %collective-permute-start.1) | collective-permute-done | bytes 20512 | tf_op jit(solution)/shard_map/ppermute | solution.py:226
  27.4 0.0 slice-done
  27.4 0.0 slice-done.2
  27.4 0.0 slice-done.1
  27.4 0.0 slice-done.3
  27.4 2.0 %experts.1 = (bf16[4,16,1024]{2,1,0:T(8,128)(2,1)S(1)}, bf16[16,512]{1,0:T(8,128)(2,1)S(1)}) custom-call(s32[1]{0:T(128)} %bitcast.place, bf16[4,1024,1024]{2,1,0:T(8,128)(2,1)S(1)} %bitcast.7, bf16[4,1024,1024]{2,1,0:T(8,128)(2,1)S(1)} %bitcast.5, bf16[2048,128]{1,0:T(8,128)(2,1)S(1)} %combine.1.after, bf16[16,640]{1,0:T(8,128)(2,1)S(1)} %merge.1.after.refs_0_, ...), custom_call_target="tpu_custom_call" | custom-call | tf_op jit(solution)/shard_map/experts/pallas_call | solution.py:298
  29.4 0.0 collective-permute-start.4
  29.4 0.7 %own.1 = f32[16,512]{1,0:T(8,128)S(1)} custom-call(s32[1]{0:T(128)} %bitcast.place, bf16[4,16,1024]{2,1,0:T(8,128)(2,1)S(1)} %get-tuple-element.19.hidden, bf16[4,1024,1024]{2,1,0:T(8,128)(2,1)S(1)} %bitcast.5, bf16[16,512]{1,0:T(8,128)(2,1)S(1)} %get-tuple-element.20.after), custom_call_target="tpu_custom_call" | custom-call | flops 67108864 | bytes 4194304 | tf_op jit(solution)/shard_map/own/pallas_call | solution.py:310
  30.1 0.5 %collective-permute-done.4 = bf16[16,512]{1,0:T(8,128)(2,1)S(1)} collective-permute-done((bf16[16,512]{1,0:T(8,128)(2,1)S(1)}, bf16[16,512]{1,0:T(8,128)(2,1)S(1)}, u32[]{:S(2)}, u32[]{:S(2)}) %collective-permute-start.4) | collective-permute-done | bytes 16416 | tf_op jit(solution)/shard_map/ppermute | solution.py:226
  30.6 13.1 %all_to_all.11 = bf16[16,16,512]{2,1,0:T(8,128)(2,1)S(1)} all-to-all(bf16[16,16,512]{2,1,0:T(8,128)(2,1)S(1)} %broadcast_in_dim.3), channel_id=1, replica_groups=mesh['wide'=8,'rest'=2,'pair'=2] {'rest','wide'}, dimensions={0} | all-to-all | bytes 524288 | tf_op jit(solution)/shard_map/all_to_all | solution.py:321
  43.8 0.1 collective-permute-start.5
  43.8 1.2 %mix.1 = (bf16[2048,1024]{1,0:T(8,128)(2,1)}, bf16[1024,512]{1,0:T(8,128)(2,1)S(1)}) custom-call(s32[1]{0:T(128)} %bitcast.place, bf16[2048,128]{1,0:T(8,128)(2,1)S(1)} %combine.1.after, bf16[128,512]{1,0:T(8,128)(2,1)S(1)} %bitcast.10), custom_call_target="tpu_custom_call" | custom-call | flops 268435456 | bytes 2621440 | tf_op jit(solution)/shard_map/mix/pallas_call | solution.py:326
  45.1 0.1 collective-permute-done.5.slot_out
  45.2 1.7 %mix_other.1 = bf16[2048,1024]{1,0:T(8,128)(2,1)} custom-call(s32[1]{0:T(128)} %bitcast.place, bf16[2048,128]{1,0:T(8,128)(2,1)S(1)} %combine.1.after, bf16[128,512]{1,0:T(8,128)(2,1)S(1)} %collective-permute-done.5.slot_out, bf16[1024,512]{1,0:T(8,128)(2,1)S(1)} %get-tuple-element.21.rest, ...), custom_call_target="tpu_custom_call", output_to_operand_aliasing={{}: (4, {})} | custom-call | flops 268435456 | bytes 2621440 | tf_op jit(solution)/shard_map/mix_other/pallas_call | solution.py:339
  (5 shorter events, 0.1 us)
Async XLA Ops:
  4.8 1.6 %collective-permute-start = (bf16[128,640]{1,0:T(8,128)(2,1)S(1)}, bf16[128,640]{1,0:T(8,128)(2,1)S(1)}, u32[]{:S(2)}, u32[]{:S(2)}) collective-permute-start(bf16[128,640]{1,0:T(8,128)(2,1)S(1)} %get-tuple-element.17.after), channel_id=1, source_target_pairs={{0,1},{1,0},{2,3},{3,2},{4,5},{5,4},{6,7},{7,6},{8,9},{9,8},{10,11... | collective-permute-start | bytes 491528 | tf_op jit(solution)/shard_map/ppermute | solution.py:226
  6.3 21.1 %slice-start = ((s8[8388608]{0:T(1024)(128)(4,1)}), s8[4194304]{0:T(1024)(128)(4,1)S(1)}, s32[]{:S(2)}) async-start(s8[8388608]{0:T(1024)(128)(4,1)} %bitcast.4), calls=%async_computation.2 | async-start | bytes 8388608
  6.3 21.1 %slice-start.2 = ((s8[8388608]{0:T(1024)(128)(4,1)}), s8[4194304]{0:T(1024)(128)(4,1)S(1)}, s32[]{:S(2)}) async-start(s8[8388608]{0:T(1024)(128)(4,1)} %bitcast.6), calls=%async_computation.4 | async-start | bytes 8388608
  6.3 21.1 %slice-start.1 = ((s8[8388608]{0:T(1024)(128)(4,1)}), s8[4194304]{0:T(1024)(128)(4,1)S(1)}, s32[]{:S(2)}) async-start(s8[8388608]{0:T(1024)(128)(4,1)} %bitcast.4), calls=%async_computation.3 | async-start | bytes 8388608
  6.3 21.1 %slice-start.3 = ((s8[8388608]{0:T(1024)(128)(4,1)}), s8[4194304]{0:T(1024)(128)(4,1)S(1)}, s32[]{:S(2)}) async-start(s8[8388608]{0:T(1024)(128)(4,1)} %bitcast.6), calls=%async_computation.5 | async-start | bytes 8388608
  22.0 2.8 %collective-permute-start.3 = (bf16[16,640]{1,0:T(8,128)(2,1)S(1)}, bf16[16,640]{1,0:T(8,128)(2,1)S(1)}, u32[]{:S(2)}, u32[]{:S(2)}) collective-permute-start(bf16[16,640]{1,0:T(8,128)(2,1)S(1)} %merge.1.after.refs_0_), channel_id=1, source_target_pairs={{0,1},{1,0},{2,3},{3,2},{4,5},{5,4},{6,7},{7,6},{8,9},{9,8},{10,11... | collective-permute-start | bytes 61448 | tf_op jit(solution)/shard_map/ppermute | solution.py:226
  22.0 3.3 %collective-permute-start.2 = (bf16[16,640]{1,0:T(8,128)(2,1)S(1)}, bf16[16,640]{1,0:T(8,128)(2,1)S(1)}, u32[]{:S(2)}, u32[]{:S(2)}) collective-permute-start(bf16[16,640]{1,0:T(8,128)(2,1)S(1)} %merge.1.after.refs_0_), channel_id=1, source_target_pairs={{0,3},{1,2},{2,1},{3,0},{4,7},{5,6},{6,5},{7,4},{8,11},{9,10},{10,... | collective-permute-start | bytes 61448 | tf_op jit(solution)/shard_map/ppermute | solution.py:226
  23.6 3.8 %collective-permute-start.1 = (bf16[16,640]{1,0:T(8,128)(2,1)S(1)}, bf16[16,640]{1,0:T(8,128)(2,1)S(1)}, u32[]{:S(2)}, u32[]{:S(2)}) collective-permute-start(bf16[16,640]{1,0:T(8,128)(2,1)S(1)} %merge.1.after.refs_0_), channel_id=1, source_target_pairs={{0,2},{1,3},{2,0},{3,1},{4,6},{5,7},{6,4},{7,5},{8,10},{9,11},{10,... | collective-permute-start | bytes 61448 | tf_op jit(solution)/shard_map/ppermute | solution.py:226
  29.4 1.2 %collective-permute-start.4 = (bf16[16,512]{1,0:T(8,128)(2,1)S(1)}, bf16[16,512]{1,0:T(8,128)(2,1)S(1)}, u32[]{:S(2)}, u32[]{:S(2)}) collective-permute-start(bf16[16,512]{1,0:T(8,128)(2,1)S(1)} %get-tuple-element.20.after), channel_id=1, source_target_pairs={{0,1},{1,0},{2,3},{3,2},{4,5},{5,4},{6,7},{7,6},{8,9},{9,8},{10,11... | collective-permute-start | bytes 49160 | tf_op jit(solution)/shard_map/ppermute | solution.py:226
  43.8 1.4 %collective-permute-start.5 = (bf16[128,512]{1,0:T(8,128)(2,1)S(1)}, bf16[128,512]{1,0:T(8,128)(2,1)S(1)}, u32[]{:S(2)}, u32[]{:S(2)}) collective-permute-start(bf16[128,512]{1,0:T(8,128)(2,1)S(1)} %bitcast.9), channel_id=1, source_target_pairs={{0,1},{1,0},{2,3},{3,2},{4,5},{5,4},{6,7},{7,6},{8,9},{9,8},{10,11... | collective-permute-start | bytes 393224 | tf_op jit(solution)/shard_map/ppermute | solution.py:226

commit v14 on v13

--- a/solution.py
+++ b/solution.py
@@ -9,7 +9,8 @@
 
 SLOT_PER = 4
 SIDE = 128
-CHUNK = 512
+CHUNK = 128
+ROWS, COLUMNS = 128, 256
 F32 = jnp.float32
 BF16 = jnp.bfloat16
 VMEM = pl.BlockSpec(memory_space=pltpu.VMEM)
@@ -175,39 +176,45 @@
     combine[...] = (weights / jnp.sum(weights, axis=1, keepdims=True)).astype(BF16)
 
 
+def mix_block(combine, slot_out, start, size, target, offset):
+    for row in range(start, start + size, ROWS):
+        for column in range(0, slot_out.shape[1], COLUMNS):
+            columns = pl.ds(column, COLUMNS)
+            value = dot(combine[pl.ds(row, ROWS), :], slot_out[:, columns])
+            target[pl.ds(row - offset, ROWS), columns] = value.astype(BF16)
+
+
 def mix_kernel(place, combine, slot_out, mixed, rest, held, sems):
-    width = slot_out.shape[1]
+    columns = column_half(place[0], slot_out.shape[1])
     tokens, done = combine.shape[0], held.shape[0]
     block = done // sems.shape[0]
-    columns = pl.ds(pl.multiple_of(place[0] * width, width), width)
     copies = []
     for i in range(tokens // block):
-        rows = pl.ds(i * block, block)
-        value = dot(combine[rows, :], slot_out[...]).astype(BF16)
         if i < sems.shape[0]:
-            held[rows, :] = value
+            rows = pl.ds(i * block, block)
+            mix_block(combine, slot_out, i * block, block, held, 0)
             copies.append(pltpu.make_async_copy(held.at[rows], mixed.at[rows, columns], sems.at[i]))
             copies[-1].start()
         else:
-            rest[pl.ds(i * block - done, block), :] = value
+            mix_block(combine, slot_out, i * block, block, rest, done)
     for copy in copies:
         copy.wait()
 
 
 def mix_other_kernel(place, combine, slot_out, rest, before, mixed, held, sems):
-    width = slot_out.shape[1]
+    half = slot_out.shape[1]
     blocks = sems.shape[0] - 1
     tokens = combine.shape[0]
     done = tokens - rest.shape[0]
-    mine = pl.ds(pl.multiple_of(place[0] * width, width), width)
-    other = pl.ds(pl.multiple_of((1 - place[0]) * width, width), width)
-    copies = [pltpu.make_async_copy(rest, mixed.at[pl.ds(done, tokens - done), mine], sems.at[blocks])]
+    target = mixed.at[pl.ds(done, tokens - done), column_half(place[0], half)]
+    copies = [pltpu.make_async_copy(rest, target, sems.at[blocks])]
     copies[0].start()
     block = tokens // blocks
     for i in range(blocks):
         rows = pl.ds(i * block, block)
-        held[rows, :] = dot(combine[rows, :], slot_out[...]).astype(BF16)
-        copies.append(pltpu.make_async_copy(held.at[rows], mixed.at[rows, other], sems.at[i]))
+        mix_block(combine, slot_out, i * block, block, held, 0)
+        target = mixed.at[rows, column_half(1 - place[0], half)]
+        copies.append(pltpu.make_async_copy(held.at[rows], target, sems.at[i]))
         copies[-1].start()
     for copy in copies:
         copy.wait()

time: 47.1 us -> 47.8 us (1.015)
  Pallas kernels: 12 us -> 12.7 us
    pallas_call x1, Pallas kernels: 4.76 us -> 5.46 us  [shards(): pl.pallas_call(gather_kernel, out_shape=(jax.ShapeDtypeStruct((count, slo...]
where the time goes in v14:
time: 47.8 us; the launch traced here: 47.6 us
  blocking collectives  28.1 us (59%)
  Pallas kernels  12.7 us (27%)
  waiting for transfers between devices  3.85 us (8%)
  starting transfers between devices  2.74 us (6%)
    all_to_all x1, blocking collectives, shards(): lax.all_to_all(send.reshape(groups, rows, -1), 'wide', split_axis=0, conc...  15 us
    all_to_all x1, blocking collectives, shards(): lax.all_to_all(partials, ('rest', 'wide'), split_axis=0, concat_axis=0, t...  13.1 us
    pallas_call x1, Pallas kernels, shards(): pl.pallas_call(gather_kernel, out_shape=(jax.ShapeDtypeStruct((count, slo...  5.46 us
    ppermute x6, waiting for transfers between devices, move(): return lax.ppermute(value, axes, moves)  3.85 us
    ppermute x6, starting transfers between devices, move(): return lax.ppermute(value, axes, moves)  2.74 us
    pallas_call x1, Pallas kernels, shards(): pl.pallas_call(expert_kernel, out_shape=(jax.ShapeDtypeStruct((experts, r...  1.96 us
    pallas_call x1, Pallas kernels, shards(): pl.pallas_call(mix_other_kernel, out_shape=jax.ShapeDtypeStruct((count, m...  1.74 us
    pallas_call x1, Pallas kernels, shards(): pl.pallas_call(mix_kernel, out_shape=(pltpu.HBM((count, model), BF16), ja...  1.21 us
  transfers between devices with their start and end apart: 6, of which 5 were waited for; matrix products, arithmetic and copies ran while one was open for 0% of the time, Pallas kernels for 6%

profile of v14, /device:TPU:0, one launch (start us, length us, event | category | flops | bytes accessed | tf_op | source)
XLA Modules:
  0.0 47.6 jit_solution(8957604778744905196)
XLA Ops:
  0.0 5.5 %gather.1 = (f32[2048,128]{1,0:T(8,128)S(1)}, bf16[128,2048]{1,0:T(8,128)(2,1)S(1)}, bf16[2048,1024]{1,0:T(8,128)(2,1)S(1)}, f32[128,128]{1,0:T(8,128)S(1)}, bf16[128,640]{1,0:T(8,128)(2,1)S(1)}) custom-call(s32[1]{0:T(128)} %bitcast.place, bf16[2048,1024]{1,0:T(8,128)(2,1)} %tokens.1, bf16[1024,128]{1,0:T(8,128)(2,1)} %slot_params.1), custom_call_target="tpu_custom_call" | custom-call | tf_op jit(solution)/shard_map/gather/pallas_call | solution.py:249
  5.5 0.5 %collective-permute-start = (bf16[128,640]{1,0:T(8,128)(2,1)S(1)}, bf16[128,640]{1,0:T(8,128)(2,1)S(1)}, u32[]{:S(2)}, u32[]{:S(2)}) collective-permute-start(bf16[128,640]{1,0:T(8,128)(2,1)S(1)} %get-tuple-element.17.after), channel_id=1, source_target_pairs={{0,1},{1,0},{2,3},{3,2},{4,5},{5,4},{6,7},{7,6},{8,9},{9,8},{10,11... | collective-permute-start | bytes 491528 | tf_op jit(solution)/shard_map/ppermute | solution.py:233
  6.0 0.4 own_sums.1.keep
  6.4 0.6 %collective-permute-done.received = bf16[128,640]{1,0:T(8,128)(2,1)S(1)} collective-permute-done((bf16[128,640]{1,0:T(8,128)(2,1)S(1)}, bf16[128,640]{1,0:T(8,128)(2,1)S(1)}, u32[]{:S(2)}, u32[]{:S(2)}) %collective-permute-start) | collective-permute-done | bytes 163872 | tf_op jit(solution)/shard_map/ppermute | solution.py:233
  7.0 0.0 slice-start
  7.0 0.0 slice-start.2
  7.0 0.0 slice-start.1
  7.0 0.0 slice-start.3
  7.0 0.3 pair.1
  7.4 15.0 %all_to_all.10.received = bf16[8,16,640]{2,1,0:T(8,128)(2,1)S(1)} all-to-all(bf16[8,16,640]{2,1,0:T(8,128)(2,1)S(1)} %bitcast.8), channel_id=1, replica_groups=mesh['wide'=8,'rest'=2,'pair'=2] {'wide'}, dimensions={0} | all-to-all | bytes 327680 | tf_op jit(solution)/shard_map/all_to_all | solution.py:283
  22.4 0.3 merge.1.after.refs_0_
  22.6 0.0 collective-permute-start.3
  22.7 1.6 %collective-permute-start.2 = (bf16[16,640]{1,0:T(8,128)(2,1)S(1)}, bf16[16,640]{1,0:T(8,128)(2,1)S(1)}, u32[]{:S(2)}, u32[]{:S(2)}) collective-permute-start(bf16[16,640]{1,0:T(8,128)(2,1)S(1)} %merge.1.after.refs_0_), channel_id=1, source_target_pairs={{0,3},{1,2},{2,1},{3,0},{4,7},{5,6},{6,5},{7,4},{8,11},{9,10},{10,... | collective-permute-start | bytes 61448 | tf_op jit(solution)/shard_map/ppermute | solution.py:233
  24.3 0.5 %collective-permute-start.1 = (bf16[16,640]{1,0:T(8,128)(2,1)S(1)}, bf16[16,640]{1,0:T(8,128)(2,1)S(1)}, u32[]{:S(2)}, u32[]{:S(2)}) collective-permute-start(bf16[16,640]{1,0:T(8,128)(2,1)S(1)} %merge.1.after.refs_0_), channel_id=1, source_target_pairs={{0,2},{1,3},{2,0},{3,1},{4,6},{5,7},{6,4},{7,5},{8,10},{9,11},{10,... | collective-permute-start | bytes 61448 | tf_op jit(solution)/shard_map/ppermute | solution.py:233
  24.8 0.6 %combine.1.after = bf16[2048,128]{1,0:T(8,128)(2,1)S(1)} custom-call(f32[2048,128]{1,0:T(8,128)S(1)} %get-tuple-element.14.logits, bf16[16,640]{1,0:T(8,128)(2,1)S(1)} %merge.1.after.refs_0_), custom_call_target="tpu_custom_call" | custom-call | flops 2097152 | bytes 1572864 | tf_op jit(solution)/shard_map/combine/pallas_call | solution.py:295
  25.4 0.0 collective-permute-done.3.refs_3_
  25.5 0.5 collective-permute-done.2.refs_2_
  25.9 2.2 %collective-permute-done.1.refs_1_ = bf16[16,640]{1,0:T(8,128)(2,1)S(1)} collective-permute-done((bf16[16,640]{1,0:T(8,128)(2,1)S(1)}, bf16[16,640]{1,0:T(8,128)(2,1)S(1)}, u32[]{:S(2)}, u32[]{:S(2)}) %collective-permute-start.1) | collective-permute-done | bytes 20512 | tf_op jit(solution)/shard_map/ppermute | solution.py:233
  28.1 0.0 slice-done
  28.1 0.0 slice-done.2
  28.1 0.0 slice-done.1
  28.1 0.0 slice-done.3
  28.1 2.0 %experts.1 = (bf16[4,16,1024]{2,1,0:T(8,128)(2,1)S(1)}, bf16[16,512]{1,0:T(8,128)(2,1)S(1)}) custom-call(s32[1]{0:T(128)} %bitcast.place, bf16[4,1024,1024]{2,1,0:T(8,128)(2,1)S(1)} %bitcast.7, bf16[4,1024,1024]{2,1,0:T(8,128)(2,1)S(1)} %bitcast.5, bf16[2048,128]{1,0:T(8,128)(2,1)S(1)} %combine.1.after, bf16[16,640]{1,0:T(8,128)(2,1)S(1)} %merge.1.after.refs_0_, ...), custom_call_target="tpu_custom_call" | custom-call | tf_op jit(solution)/shard_map/experts/pallas_call | solution.py:305
  30.1 0.0 collective-permute-start.4
  30.1 0.7 %own.1 = f32[16,512]{1,0:T(8,128)S(1)} custom-call(s32[1]{0:T(128)} %bitcast.place, bf16[4,16,1024]{2,1,0:T(8,128)(2,1)S(1)} %get-tuple-element.19.hidden, bf16[4,1024,1024]{2,1,0:T(8,128)(2,1)S(1)} %bitcast.5, bf16[16,512]{1,0:T(8,128)(2,1)S(1)} %get-tuple-element.20.after), custom_call_target="tpu_custom_call" | custom-call | flops 67108864 | bytes 4194304 | tf_op jit(solution)/shard_map/own/pallas_call | solution.py:317
  30.8 0.5 %collective-permute-done.4 = bf16[16,512]{1,0:T(8,128)(2,1)S(1)} collective-permute-done((bf16[16,512]{1,0:T(8,128)(2,1)S(1)}, bf16[16,512]{1,0:T(8,128)(2,1)S(1)}, u32[]{:S(2)}, u32[]{:S(2)}) %collective-permute-start.4) | collective-permute-done | bytes 16416 | tf_op jit(solution)/shard_map/ppermute | solution.py:233
  31.3 13.1 %all_to_all.11 = bf16[16,16,512]{2,1,0:T(8,128)(2,1)S(1)} all-to-all(bf16[16,16,512]{2,1,0:T(8,128)(2,1)S(1)} %broadcast_in_dim.3), channel_id=1, replica_groups=mesh['wide'=8,'rest'=2,'pair'=2] {'rest','wide'}, dimensions={0} | all-to-all | bytes 524288 | tf_op jit(solution)/shard_map/all_to_all | solution.py:328
  44.4 0.1 collective-permute-start.5
  44.5 1.2 %mix.1 = (bf16[2048,1024]{1,0:T(8,128)(2,1)}, bf16[1024,512]{1,0:T(8,128)(2,1)S(1)}) custom-call(s32[1]{0:T(128)} %bitcast.place, bf16[2048,128]{1,0:T(8,128)(2,1)S(1)} %combine.1.after, bf16[128,512]{1,0:T(8,128)(2,1)S(1)} %bitcast.10), custom_call_target="tpu_custom_call" | custom-call | flops 268435456 | bytes 2621440 | tf_op jit(solution)/shard_map/mix/pallas_call | solution.py:333
  45.7 0.1 collective-permute-done.5.slot_out
  45.8 1.7 %mix_other.1 = bf16[2048,1024]{1,0:T(8,128)(2,1)} custom-call(s32[1]{0:T(128)} %bitcast.place, bf16[2048,128]{1,0:T(8,128)(2,1)S(1)} %combine.1.after, bf16[128,512]{1,0:T(8,128)(2,1)S(1)} %collective-permute-done.5.slot_out, bf16[1024,512]{1,0:T(8,128)(2,1)S(1)} %get-tuple-element.21.rest, ...), custom_call_target="tpu_custom_call", output_to_operand_aliasing={{}: (4, {})} | custom-call | flops 268435456 | bytes 2621440 | tf_op jit(solution)/shard_map/mix_other/pallas_call | solution.py:346
  (5 shorter events, 0.1 us)
Async XLA Ops:
  5.5 1.5 %collective-permute-start = (bf16[128,640]{1,0:T(8,128)(2,1)S(1)}, bf16[128,640]{1,0:T(8,128)(2,1)S(1)}, u32[]{:S(2)}, u32[]{:S(2)}) collective-permute-start(bf16[128,640]{1,0:T(8,128)(2,1)S(1)} %get-tuple-element.17.after), channel_id=1, source_target_pairs={{0,1},{1,0},{2,3},{3,2},{4,5},{5,4},{6,7},{7,6},{8,9},{9,8},{10,11... | collective-permute-start | bytes 491528 | tf_op jit(solution)/shard_map/ppermute | solution.py:233
  7.0 21.1 %slice-start = ((s8[8388608]{0:T(1024)(128)(4,1)}), s8[4194304]{0:T(1024)(128)(4,1)S(1)}, s32[]{:S(2)}) async-start(s8[8388608]{0:T(1024)(128)(4,1)} %bitcast.4), calls=%async_computation.2 | async-start | bytes 8388608
  7.0 21.1 %slice-start.2 = ((s8[8388608]{0:T(1024)(128)(4,1)}), s8[4194304]{0:T(1024)(128)(4,1)S(1)}, s32[]{:S(2)}) async-start(s8[8388608]{0:T(1024)(128)(4,1)} %bitcast.6), calls=%async_computation.4 | async-start | bytes 8388608
  7.0 21.1 %slice-start.1 = ((s8[8388608]{0:T(1024)(128)(4,1)}), s8[4194304]{0:T(1024)(128)(4,1)S(1)}, s32[]{:S(2)}) async-start(s8[8388608]{0:T(1024)(128)(4,1)} %bitcast.4), calls=%async_computation.3 | async-start | bytes 8388608
  7.0 21.1 %slice-start.3 = ((s8[8388608]{0:T(1024)(128)(4,1)}), s8[4194304]{0:T(1024)(128)(4,1)S(1)}, s32[]{:S(2)}) async-start(s8[8388608]{0:T(1024)(128)(4,1)} %bitcast.6), calls=%async_computation.5 | async-start | bytes 8388608
  22.6 2.8 %collective-permute-start.3 = (bf16[16,640]{1,0:T(8,128)(2,1)S(1)}, bf16[16,640]{1,0:T(8,128)(2,1)S(1)}, u32[]{:S(2)}, u32[]{:S(2)}) collective-permute-start(bf16[16,640]{1,0:T(8,128)(2,1)S(1)} %merge.1.after.refs_0_), channel_id=1, source_target_pairs={{0,1},{1,0},{2,3},{3,2},{4,5},{5,4},{6,7},{7,6},{8,9},{9,8},{10,11... | collective-permute-start | bytes 61448 | tf_op jit(solution)/shard_map/ppermute | solution.py:233
  22.7 3.3 %collective-permute-start.2 = (bf16[16,640]{1,0:T(8,128)(2,1)S(1)}, bf16[16,640]{1,0:T(8,128)(2,1)S(1)}, u32[]{:S(2)}, u32[]{:S(2)}) collective-permute-start(bf16[16,640]{1,0:T(8,128)(2,1)S(1)} %merge.1.after.refs_0_), channel_id=1, source_target_pairs={{0,3},{1,2},{2,1},{3,0},{4,7},{5,6},{6,5},{7,4},{8,11},{9,10},{10,... | collective-permute-start | bytes 61448 | tf_op jit(solution)/shard_map/ppermute | solution.py:233
  24.3 3.8 %collective-permute-start.1 = (bf16[16,640]{1,0:T(8,128)(2,1)S(1)}, bf16[16,640]{1,0:T(8,128)(2,1)S(1)}, u32[]{:S(2)}, u32[]{:S(2)}) collective-permute-start(bf16[16,640]{1,0:T(8,128)(2,1)S(1)} %merge.1.after.refs_0_), channel_id=1, source_target_pairs={{0,2},{1,3},{2,0},{3,1},{4,6},{5,7},{6,4},{7,5},{8,10},{9,11},{10,... | collective-permute-start | bytes 61448 | tf_op jit(solution)/shard_map/ppermute | solution.py:233
  30.1 1.2 %collective-permute-start.4 = (bf16[16,512]{1,0:T(8,128)(2,1)S(1)}, bf16[16,512]{1,0:T(8,128)(2,1)S(1)}, u32[]{:S(2)}, u32[]{:S(2)}) collective-permute-start(bf16[16,512]{1,0:T(8,128)(2,1)S(1)} %get-tuple-element.20.after), channel_id=1, source_target_pairs={{0,1},{1,0},{2,3},{3,2},{4,5},{5,4},{6,7},{7,6},{8,9},{9,8},{10,11... | collective-permute-start | bytes 49160 | tf_op jit(solution)/shard_map/ppermute | solution.py:233
  44.4 1.4 %collective-permute-start.5 = (bf16[128,512]{1,0:T(8,128)(2,1)S(1)}, bf16[128,512]{1,0:T(8,128)(2,1)S(1)}, u32[]{:S(2)}, u32[]{:S(2)}) collective-permute-start(bf16[128,512]{1,0:T(8,128)(2,1)S(1)} %bitcast.9), channel_id=1, source_target_pairs={{0,1},{1,0},{2,3},{3,2},{4,5},{5,4},{6,7},{7,6},{8,9},{9,8},{10,11... | collective-permute-start | bytes 393224 | tf_op jit(solution)/shard_map/ppermute | solution.py:233

commit v15 on v13

--- a/solution.py
+++ b/solution.py
@@ -9,7 +9,7 @@
 
 SLOT_PER = 4
 SIDE = 128
-CHUNK = 512
+CHUNK, TOGETHER = 256, 2
 F32 = jnp.float32
 BF16 = jnp.bfloat16
 VMEM = pl.BlockSpec(memory_space=pltpu.VMEM)
@@ -73,11 +73,13 @@
         copy.start()
     high = jnp.full((8, slots), -jnp.inf, F32)
     table_copy.wait()
-    for copy, span in zip(copies, spans):
-        copy.wait()
-        part = dot(held[span, :], table[...])
-        logits[span, :] = part
-        high = jnp.maximum(high, jnp.max(part.reshape(CHUNK // 8, 8, slots), axis=0))
+    for first in range(0, chunks, TOGETHER):
+        for copy in copies[first : first + TOGETHER]:
+            copy.wait()
+        parts = [dot(held[span, :], table[...]) for span in spans[first : first + TOGETHER]]
+        for part, span in zip(parts, spans[first:]):
+            logits[span, :] = part
+            high = jnp.maximum(high, jnp.max(part.reshape(CHUNK // 8, 8, slots), axis=0))
     peak = jnp.max(high, axis=0, keepdims=True)
     total = jnp.zeros((8, slots), F32)
     columns = []

time: 47.1 us -> 46 us (0.977)
  Pallas kernels: 12 us -> 11 us
    pallas_call x1, Pallas kernels: 4.76 us -> 3.71 us  [shards(): pl.pallas_call(gather_kernel, out_shape=(jax.ShapeDtypeStruct((count, slo...]
where the time goes in v15:
time: 46 us; the launch traced here: 45.8 us
  blocking collectives  28.1 us (61%)
  Pallas kernels  11 us (24%)
  waiting for transfers between devices  3.83 us (8%)
  starting transfers between devices  2.75 us (6%)
    all_to_all x1, blocking collectives, shards(): lax.all_to_all(send.reshape(groups, rows, -1), 'wide', split_axis=0, conc...  15 us
    all_to_all x1, blocking collectives, shards(): lax.all_to_all(partials, ('rest', 'wide'), split_axis=0, concat_axis=0, t...  13.1 us
    ppermute x6, waiting for transfers between devices, move(): return lax.ppermute(value, axes, moves)  3.83 us
    pallas_call x1, Pallas kernels, shards(): pl.pallas_call(gather_kernel, out_shape=(jax.ShapeDtypeStruct((count, slo...  3.71 us
    ppermute x6, starting transfers between devices, move(): return lax.ppermute(value, axes, moves)  2.75 us
    pallas_call x1, Pallas kernels, shards(): pl.pallas_call(expert_kernel, out_shape=(jax.ShapeDtypeStruct((experts, r...  1.96 us
    pallas_call x1, Pallas kernels, shards(): pl.pallas_call(mix_other_kernel, out_shape=jax.ShapeDtypeStruct((count, m...  1.74 us
    pallas_call x1, Pallas kernels, shards(): pl.pallas_call(mix_kernel, out_shape=(pltpu.HBM((count, model), BF16), ja...  1.21 us
  transfers between devices with their start and end apart: 6, of which 5 were waited for; matrix products, arithmetic and copies ran while one was open for 0% of the time, Pallas kernels for 6%

profile of v15, /device:TPU:0, one launch (start us, length us, event | category | flops | bytes accessed | tf_op | source)
XLA Modules:
  0.0 45.8 jit_solution(7036468259864127826)
XLA Ops:
  0.0 3.7 %gather.1 = (f32[2048,128]{1,0:T(8,128)S(1)}, bf16[128,2048]{1,0:T(8,128)(2,1)S(1)}, bf16[2048,1024]{1,0:T(8,128)(2,1)S(1)}, f32[128,128]{1,0:T(8,128)S(1)}, bf16[128,640]{1,0:T(8,128)(2,1)S(1)}) custom-call(s32[1]{0:T(128)} %bitcast.place, bf16[2048,1024]{1,0:T(8,128)(2,1)} %tokens.1, bf16[1024,128]{1,0:T(8,128)(2,1)} %slot_params.1), custom_call_target="tpu_custom_call" | custom-call | tf_op jit(solution)/shard_map/gather/pallas_call | solution.py:244
  3.7 0.5 %collective-permute-start = (bf16[128,640]{1,0:T(8,128)(2,1)S(1)}, bf16[128,640]{1,0:T(8,128)(2,1)S(1)}, u32[]{:S(2)}, u32[]{:S(2)}) collective-permute-start(bf16[128,640]{1,0:T(8,128)(2,1)S(1)} %get-tuple-element.17.after), channel_id=1, source_target_pairs={{0,1},{1,0},{2,3},{3,2},{4,5},{5,4},{6,7},{7,6},{8,9},{9,8},{10,11... | collective-permute-start | bytes 491528 | tf_op jit(solution)/shard_map/ppermute | solution.py:228
  4.2 0.5 own_sums.1.keep
  4.7 0.6 %collective-permute-done.received = bf16[128,640]{1,0:T(8,128)(2,1)S(1)} collective-permute-done((bf16[128,640]{1,0:T(8,128)(2,1)S(1)}, bf16[128,640]{1,0:T(8,128)(2,1)S(1)}, u32[]{:S(2)}, u32[]{:S(2)}) %collective-permute-start) | collective-permute-done | bytes 163872 | tf_op jit(solution)/shard_map/ppermute | solution.py:228
  5.3 0.0 slice-start
  5.3 0.0 slice-start.2
  5.3 0.0 slice-start.1
  5.3 0.0 slice-start.3
  5.3 0.3 pair.1
  5.6 15.0 %all_to_all.10.received = bf16[8,16,640]{2,1,0:T(8,128)(2,1)S(1)} all-to-all(bf16[8,16,640]{2,1,0:T(8,128)(2,1)S(1)} %bitcast.8), channel_id=1, replica_groups=mesh['wide'=8,'rest'=2,'pair'=2] {'wide'}, dimensions={0} | all-to-all | bytes 327680 | tf_op jit(solution)/shard_map/all_to_all | solution.py:278
  20.6 0.3 merge.1.after.refs_0_
  20.9 0.0 collective-permute-start.3
  20.9 1.6 %collective-permute-start.2 = (bf16[16,640]{1,0:T(8,128)(2,1)S(1)}, bf16[16,640]{1,0:T(8,128)(2,1)S(1)}, u32[]{:S(2)}, u32[]{:S(2)}) collective-permute-start(bf16[16,640]{1,0:T(8,128)(2,1)S(1)} %merge.1.after.refs_0_), channel_id=1, source_target_pairs={{0,3},{1,2},{2,1},{3,0},{4,7},{5,6},{6,5},{7,4},{8,11},{9,10},{10,... | collective-permute-start | bytes 61448 | tf_op jit(solution)/shard_map/ppermute | solution.py:228
  22.6 0.5 %collective-permute-start.1 = (bf16[16,640]{1,0:T(8,128)(2,1)S(1)}, bf16[16,640]{1,0:T(8,128)(2,1)S(1)}, u32[]{:S(2)}, u32[]{:S(2)}) collective-permute-start(bf16[16,640]{1,0:T(8,128)(2,1)S(1)} %merge.1.after.refs_0_), channel_id=1, source_target_pairs={{0,2},{1,3},{2,0},{3,1},{4,6},{5,7},{6,4},{7,5},{8,10},{9,11},{10,... | collective-permute-start | bytes 61448 | tf_op jit(solution)/shard_map/ppermute | solution.py:228
  23.1 0.6 %combine.1.after = bf16[2048,128]{1,0:T(8,128)(2,1)S(1)} custom-call(f32[2048,128]{1,0:T(8,128)S(1)} %get-tuple-element.14.logits, bf16[16,640]{1,0:T(8,128)(2,1)S(1)} %merge.1.after.refs_0_), custom_call_target="tpu_custom_call" | custom-call | flops 2097152 | bytes 1572864 | tf_op jit(solution)/shard_map/combine/pallas_call | solution.py:290
  23.7 0.0 collective-permute-done.3.refs_3_
  23.7 0.5 %collective-permute-done.2.refs_2_ = bf16[16,640]{1,0:T(8,128)(2,1)S(1)} collective-permute-done((bf16[16,640]{1,0:T(8,128)(2,1)S(1)}, bf16[16,640]{1,0:T(8,128)(2,1)S(1)}, u32[]{:S(2)}, u32[]{:S(2)}) %collective-permute-start.2) | collective-permute-done | bytes 20512 | tf_op jit(solution)/shard_map/ppermute | solution.py:228
  24.2 2.1 %collective-permute-done.1.refs_1_ = bf16[16,640]{1,0:T(8,128)(2,1)S(1)} collective-permute-done((bf16[16,640]{1,0:T(8,128)(2,1)S(1)}, bf16[16,640]{1,0:T(8,128)(2,1)S(1)}, u32[]{:S(2)}, u32[]{:S(2)}) %collective-permute-start.1) | collective-permute-done | bytes 20512 | tf_op jit(solution)/shard_map/ppermute | solution.py:228
  26.3 0.0 slice-done
  26.3 0.0 slice-done.2
  26.4 0.0 slice-done.1
  26.4 0.0 slice-done.3
  26.4 2.0 %experts.1 = (bf16[4,16,1024]{2,1,0:T(8,128)(2,1)S(1)}, bf16[16,512]{1,0:T(8,128)(2,1)S(1)}) custom-call(s32[1]{0:T(128)} %bitcast.place, bf16[4,1024,1024]{2,1,0:T(8,128)(2,1)S(1)} %bitcast.7, bf16[4,1024,1024]{2,1,0:T(8,128)(2,1)S(1)} %bitcast.5, bf16[2048,128]{1,0:T(8,128)(2,1)S(1)} %combine.1.after, bf16[16,640]{1,0:T(8,128)(2,1)S(1)} %merge.1.after.refs_0_, ...), custom_call_target="tpu_custom_call" | custom-call | tf_op jit(solution)/shard_map/experts/pallas_call | solution.py:300
  28.3 0.0 collective-permute-start.4
  28.3 0.7 %own.1 = f32[16,512]{1,0:T(8,128)S(1)} custom-call(s32[1]{0:T(128)} %bitcast.place, bf16[4,16,1024]{2,1,0:T(8,128)(2,1)S(1)} %get-tuple-element.19.hidden, bf16[4,1024,1024]{2,1,0:T(8,128)(2,1)S(1)} %bitcast.5, bf16[16,512]{1,0:T(8,128)(2,1)S(1)} %get-tuple-element.20.after), custom_call_target="tpu_custom_call" | custom-call | flops 67108864 | bytes 4194304 | tf_op jit(solution)/shard_map/own/pallas_call | solution.py:312
  29.0 0.5 %collective-permute-done.4 = bf16[16,512]{1,0:T(8,128)(2,1)S(1)} collective-permute-done((bf16[16,512]{1,0:T(8,128)(2,1)S(1)}, bf16[16,512]{1,0:T(8,128)(2,1)S(1)}, u32[]{:S(2)}, u32[]{:S(2)}) %collective-permute-start.4) | collective-permute-done | bytes 16416 | tf_op jit(solution)/shard_map/ppermute | solution.py:228
  29.6 13.1 %all_to_all.11 = bf16[16,16,512]{2,1,0:T(8,128)(2,1)S(1)} all-to-all(bf16[16,16,512]{2,1,0:T(8,128)(2,1)S(1)} %broadcast_in_dim.3), channel_id=1, replica_groups=mesh['wide'=8,'rest'=2,'pair'=2] {'rest','wide'}, dimensions={0} | all-to-all | bytes 524288 | tf_op jit(solution)/shard_map/all_to_all | solution.py:323
  42.7 0.1 collective-permute-start.5
  42.8 1.2 %mix.1 = (bf16[2048,1024]{1,0:T(8,128)(2,1)}, bf16[1024,512]{1,0:T(8,128)(2,1)S(1)}) custom-call(s32[1]{0:T(128)} %bitcast.place, bf16[2048,128]{1,0:T(8,128)(2,1)S(1)} %combine.1.after, bf16[128,512]{1,0:T(8,128)(2,1)S(1)} %bitcast.10), custom_call_target="tpu_custom_call" | custom-call | flops 268435456 | bytes 2621440 | tf_op jit(solution)/shard_map/mix/pallas_call | solution.py:328
  44.0 0.1 collective-permute-done.5.slot_out
  44.1 1.7 %mix_other.1 = bf16[2048,1024]{1,0:T(8,128)(2,1)} custom-call(s32[1]{0:T(128)} %bitcast.place, bf16[2048,128]{1,0:T(8,128)(2,1)S(1)} %combine.1.after, bf16[128,512]{1,0:T(8,128)(2,1)S(1)} %collective-permute-done.5.slot_out, bf16[1024,512]{1,0:T(8,128)(2,1)S(1)} %get-tuple-element.21.rest, ...), custom_call_target="tpu_custom_call", output_to_operand_aliasing={{}: (4, {})} | custom-call | flops 268435456 | bytes 2621440 | tf_op jit(solution)/shard_map/mix_other/pallas_call | solution.py:341
  (5 shorter events, 0.1 us)
Async XLA Ops:
  3.7 1.5 %collective-permute-start = (bf16[128,640]{1,0:T(8,128)(2,1)S(1)}, bf16[128,640]{1,0:T(8,128)(2,1)S(1)}, u32[]{:S(2)}, u32[]{:S(2)}) collective-permute-start(bf16[128,640]{1,0:T(8,128)(2,1)S(1)} %get-tuple-element.17.after), channel_id=1, source_target_pairs={{0,1},{1,0},{2,3},{3,2},{4,5},{5,4},{6,7},{7,6},{8,9},{9,8},{10,11... | collective-permute-start | bytes 491528 | tf_op jit(solution)/shard_map/ppermute | solution.py:228
  5.3 21.1 %slice-start = ((s8[8388608]{0:T(1024)(128)(4,1)}), s8[4194304]{0:T(1024)(128)(4,1)S(1)}, s32[]{:S(2)}) async-start(s8[8388608]{0:T(1024)(128)(4,1)} %bitcast.4), calls=%async_computation.2 | async-start | bytes 8388608
  5.3 21.1 %slice-start.2 = ((s8[8388608]{0:T(1024)(128)(4,1)}), s8[4194304]{0:T(1024)(128)(4,1)S(1)}, s32[]{:S(2)}) async-start(s8[8388608]{0:T(1024)(128)(4,1)} %bitcast.6), calls=%async_computation.4 | async-start | bytes 8388608
  5.3 21.1 %slice-start.1 = ((s8[8388608]{0:T(1024)(128)(4,1)}), s8[4194304]{0:T(1024)(128)(4,1)S(1)}, s32[]{:S(2)}) async-start(s8[8388608]{0:T(1024)(128)(4,1)} %bitcast.4), calls=%async_computation.3 | async-start | bytes 8388608
  5.3 21.1 %slice-start.3 = ((s8[8388608]{0:T(1024)(128)(4,1)}), s8[4194304]{0:T(1024)(128)(4,1)S(1)}, s32[]{:S(2)}) async-start(s8[8388608]{0:T(1024)(128)(4,1)} %bitcast.6), calls=%async_computation.5 | async-start | bytes 8388608
  20.9 2.8 %collective-permute-start.3 = (bf16[16,640]{1,0:T(8,128)(2,1)S(1)}, bf16[16,640]{1,0:T(8,128)(2,1)S(1)}, u32[]{:S(2)}, u32[]{:S(2)}) collective-permute-start(bf16[16,640]{1,0:T(8,128)(2,1)S(1)} %merge.1.after.refs_0_), channel_id=1, source_target_pairs={{0,1},{1,0},{2,3},{3,2},{4,5},{5,4},{6,7},{7,6},{8,9},{9,8},{10,11... | collective-permute-start | bytes 61448 | tf_op jit(solution)/shard_map/ppermute | solution.py:228
  20.9 3.3 %collective-permute-start.2 = (bf16[16,640]{1,0:T(8,128)(2,1)S(1)}, bf16[16,640]{1,0:T(8,128)(2,1)S(1)}, u32[]{:S(2)}, u32[]{:S(2)}) collective-permute-start(bf16[16,640]{1,0:T(8,128)(2,1)S(1)} %merge.1.after.refs_0_), channel_id=1, source_target_pairs={{0,3},{1,2},{2,1},{3,0},{4,7},{5,6},{6,5},{7,4},{8,11},{9,10},{10,... | collective-permute-start | bytes 61448 | tf_op jit(solution)/shard_map/ppermute | solution.py:228
  22.6 3.8 %collective-permute-start.1 = (bf16[16,640]{1,0:T(8,128)(2,1)S(1)}, bf16[16,640]{1,0:T(8,128)(2,1)S(1)}, u32[]{:S(2)}, u32[]{:S(2)}) collective-permute-start(bf16[16,640]{1,0:T(8,128)(2,1)S(1)} %merge.1.after.refs_0_), channel_id=1, source_target_pairs={{0,2},{1,3},{2,0},{3,1},{4,6},{5,7},{6,4},{7,5},{8,10},{9,11},{10,... | collective-permute-start | bytes 61448 | tf_op jit(solution)/shard_map/ppermute | solution.py:228
  28.3 1.2 %collective-permute-start.4 = (bf16[16,512]{1,0:T(8,128)(2,1)S(1)}, bf16[16,512]{1,0:T(8,128)(2,1)S(1)}, u32[]{:S(2)}, u32[]{:S(2)}) collective-permute-start(bf16[16,512]{1,0:T(8,128)(2,1)S(1)} %get-tuple-element.20.after), channel_id=1, source_target_pairs={{0,1},{1,0},{2,3},{3,2},{4,5},{5,4},{6,7},{7,6},{8,9},{9,8},{10,11... | collective-permute-start | bytes 49160 | tf_op jit(solution)/shard_map/ppermute | solution.py:228
  42.7 1.4 %collective-permute-start.5 = (bf16[128,512]{1,0:T(8,128)(2,1)S(1)}, bf16[128,512]{1,0:T(8,128)(2,1)S(1)}, u32[]{:S(2)}, u32[]{:S(2)}) collective-permute-start(bf16[128,512]{1,0:T(8,128)(2,1)S(1)} %bitcast.9), channel_id=1, source_target_pairs={{0,1},{1,0},{2,3},{3,2},{4,5},{5,4},{6,7},{7,6},{8,9},{9,8},{10,11... | collective-permute-start | bytes 393224 | tf_op jit(solution)/shard_map/ppermute | solution.py:228

commit v16 on v15

--- a/solution.py
+++ b/solution.py
@@ -34,9 +34,12 @@
     return jnp.dot(lhs, rhs, preferred_element_type=F32)
 
 
-def side_state(peak, total):
-    lane = lax.broadcasted_iota(jnp.int32, (peak.shape[0], SIDE), 1)
-    return jnp.where(lane == 0, peak, jnp.where(lane == 1, total, 0.0))
+def side_state(*columns):
+    lane = lax.broadcasted_iota(jnp.int32, (columns[0].shape[0], SIDE), 1)
+    out = jnp.zeros((columns[0].shape[0], SIDE), F32)
+    for index, value in enumerate(columns):
+        out = jnp.where(lane == index, value, out)
+    return out
 
 
 def side_message(peak, total):
@@ -65,41 +68,67 @@
 def gather_kernel(place, tokens, slot_params, logits, turned, held, side, send, table, sems):
     chunks = tokens.shape[0] // CHUNK
     slots = slot_params.shape[1]
+    half = held.shape[1] // 2
     spans = [pl.ds(i * CHUNK, CHUNK) for i in range(chunks)]
     table_copy = pltpu.make_async_copy(slot_params, table, sems.at[chunks])
     table_copy.start()
     copies = [pltpu.make_async_copy(tokens.at[span], held.at[span], sems.at[i]) for i, span in enumerate(spans)]
     for copy in copies:
         copy.start()
-    high = jnp.full((8, slots), -jnp.inf, F32)
+
+    def find_peak(parts, high=None):
+        for part in parts:
+            top = jnp.max(part.reshape(CHUNK // 8, 8, slots), axis=0)
+            high = top if high is None else jnp.maximum(high, top)
+        return high
+
+    def weigh(first, parts, peak):
+        total = jnp.zeros((8, slots), F32)
+        columns = []
+        for part in parts:
+            weights = jnp.exp(part - peak)
+            total = total + jnp.sum(weights.reshape(CHUNK // 8, 8, slots), axis=0)
+            columns.append(weights.astype(BF16).T)
+        weights = jnp.concatenate(columns, axis=1)
+        span = pl.ds(first * CHUNK, len(parts) * CHUNK)
+        turned[:, span] = weights
+        sums = dot(weights, held[span, column_half(1 - place[0], half)])
+        return sums, jnp.sum(total, axis=0, keepdims=True)
+
     table_copy.wait()
+    high = None
     for first in range(0, chunks, TOGETHER):
         for copy in copies[first : first + TOGETHER]:
             copy.wait()
         parts = [dot(held[span, :], table[...]) for span in spans[first : first + TOGETHER]]
         for part, span in zip(parts, spans[first:]):
             logits[span, :] = part
-            high = jnp.maximum(high, jnp.max(part.reshape(CHUNK // 8, 8, slots), axis=0))
-    peak = jnp.max(high, axis=0, keepdims=True)
-    total = jnp.zeros((8, slots), F32)
-    columns = []
-    for span in spans:
-        weights = jnp.exp(logits[span, :] - peak)
-        total = total + jnp.sum(weights.reshape(CHUNK // 8, 8, slots), axis=0)
-        columns.append(weights.astype(BF16).T)
-    weights = jnp.concatenate(columns, axis=1)
-    turned[...] = weights
-    half = held.shape[1] // 2
-    send[:, :half] = dot(weights, held[:, column_half(1 - place[0], half)]).astype(BF16)
-    total = jnp.sum(total, axis=0, keepdims=True)
-    peak = jnp.broadcast_to(peak, (8, slots)).T[:, 0:1]
-    total = jnp.broadcast_to(total, (8, slots)).T[:, 0:1]
-    side[...] = side_state(peak, total)
+        if first + TOGETHER < chunks:
+            high = find_peak(parts, high)
+    early_peak = jnp.max(high, axis=0, keepdims=True)
+    early, early_total = weigh(0, [logits[span, :] for span in spans[:first]], early_peak)
+    late_peak = jnp.max(find_peak(parts), axis=0, keepdims=True)
+    late, late_total = weigh(first, parts, late_peak)
+    peak = jnp.maximum(early_peak, late_peak)
+    early_scale, late_scale = jnp.exp(early_peak - peak), jnp.exp(late_peak - peak)
+    total = early_total * early_scale + late_total * late_scale
+    row = lax.broadcasted_iota(jnp.int32, (8, slots), 0)
+    columns = jnp.zeros((8, slots), F32)
+    for index, value in enumerate((peak, total, early_scale, late_scale)):
+        columns = jnp.where(row == index, value, columns)
+    columns = columns.T
+    peak, total, early_scale, late_scale = [columns[:, i : i + 1] for i in range(4)]
+    send[:, :half] = (early * early_scale + late * late_scale).astype(BF16)
+    side[...] = side_state(peak, total, early_scale, late_scale)
     send[:, half:] = side_message(peak, total)
 
 
-def own_sums_kernel(place, turned, held, after, keep):
-    keep[...] = dot(turned[...], held[:, column_half(place[0], keep.shape[1])])
+def own_sums_kernel(place, turned, held, side, after, keep):
+    columns = column_half(place[0], keep.shape[1])
+    early = held.shape[0] - TOGETHER * CHUNK
+    spans = (pl.ds(0, early), pl.ds(early, TOGETHER * CHUNK))
+    early, late = [dot(turned[:, span], held[span, columns]) for span in spans]
+    keep[...] = early * side[:, 2:3] + late * side[:, 3:4]
 
 
 def pair_kernel(keep, side, received, send):
@@ -260,12 +289,12 @@
     keep = pl.pallas_call(
         own_sums_kernel,
         out_shape=jax.ShapeDtypeStruct((slots, half), F32),
-        in_specs=[SMEM, VMEM, VMEM, any_space],
+        in_specs=[SMEM, VMEM, VMEM, VMEM, any_space],
         out_specs=VMEM,
         cost_estimate=cost(2 * slots * count * half, 2 * count * (half + slots)),
         compiler_params=params(16),
         name="own_sums",
-    )(place, turned, held, send)
+    )(place, turned, held, side, send)
     send = pl.pallas_call(
         pair_kernel,
         out_shape=jax.ShapeDtypeStruct((slots, half + SIDE), BF16),

time: 46 us -> 46 us (level)
  no operation moved by 1% of the time
where the time goes in v16:
time: 46 us; the launch traced here: 45.8 us
  blocking collectives  28.1 us (61%)
  Pallas kernels  11 us (24%)
  waiting for transfers between devices  3.79 us (8%)
  starting transfers between devices  2.74 us (6%)
    all_to_all x1, blocking collectives, shards(): lax.all_to_all(send.reshape(groups, rows, -1), 'wide', split_axis=0, conc...  15 us
    all_to_all x1, blocking collectives, shards(): lax.all_to_all(partials, ('rest', 'wide'), split_axis=0, concat_axis=0, t...  13.1 us
    ppermute x6, waiting for transfers between devices, move(): return lax.ppermute(value, axes, moves)  3.79 us
    pallas_call x1, Pallas kernels, shards(): pl.pallas_call(gather_kernel, out_shape=(jax.ShapeDtypeStruct((count, slo...  3.67 us
    ppermute x6, starting transfers between devices, move(): return lax.ppermute(value, axes, moves)  2.74 us
    pallas_call x1, Pallas kernels, shards(): pl.pallas_call(expert_kernel, out_shape=(jax.ShapeDtypeStruct((experts, r...  1.96 us
    pallas_call x1, Pallas kernels, shards(): pl.pallas_call(mix_other_kernel, out_shape=jax.ShapeDtypeStruct((count, m...  1.74 us
    pallas_call x1, Pallas kernels, shards(): pl.pallas_call(mix_kernel, out_shape=(pltpu.HBM((count, model), BF16), ja...  1.21 us
  transfers between devices with their start and end apart: 6, of which 5 were waited for; matrix products, arithmetic and copies ran while one was open for 0% of the time, Pallas kernels for 6%

profile of v16, /device:TPU:0, one launch (start us, length us, event | category | flops | bytes accessed | tf_op | source)
XLA Modules:
  0.0 45.8 jit_solution(6243121663675440331)
XLA Ops:
  0.0 3.7 %gather.1 = (f32[2048,128]{1,0:T(8,128)S(1)}, bf16[128,2048]{1,0:T(8,128)(2,1)S(1)}, bf16[2048,1024]{1,0:T(8,128)(2,1)S(1)}, f32[128,128]{1,0:T(8,128)S(1)}, bf16[128,640]{1,0:T(8,128)(2,1)S(1)}) custom-call(s32[1]{0:T(128)} %bitcast.place, bf16[2048,1024]{1,0:T(8,128)(2,1)} %tokens.1, bf16[1024,128]{1,0:T(8,128)(2,1)} %slot_params.1), custom_call_target="tpu_custom_call" | custom-call | tf_op jit(solution)/shard_map/gather/pallas_call | solution.py:273
  3.7 0.5 %collective-permute-start = (bf16[128,640]{1,0:T(8,128)(2,1)S(1)}, bf16[128,640]{1,0:T(8,128)(2,1)S(1)}, u32[]{:S(2)}, u32[]{:S(2)}) collective-permute-start(bf16[128,640]{1,0:T(8,128)(2,1)S(1)} %get-tuple-element.18.after), channel_id=1, source_target_pairs={{0,1},{1,0},{2,3},{3,2},{4,5},{5,4},{6,7},{7,6},{8,9},{9,8},{10,11... | collective-permute-start | bytes 491528 | tf_op jit(solution)/shard_map/ppermute | solution.py:257
  4.2 0.0 slice-start
  4.2 0.0 slice-start.2
  4.2 0.5 own_sums.1.keep
  4.7 0.0 slice-start.1
  4.7 0.0 slice-start.3
  4.7 0.5 %collective-permute-done.received = bf16[128,640]{1,0:T(8,128)(2,1)S(1)} collective-permute-done((bf16[128,640]{1,0:T(8,128)(2,1)S(1)}, bf16[128,640]{1,0:T(8,128)(2,1)S(1)}, u32[]{:S(2)}, u32[]{:S(2)}) %collective-permute-start) | collective-permute-done | bytes 163872 | tf_op jit(solution)/shard_map/ppermute | solution.py:257
  5.2 0.3 pair.1
  5.6 15.0 %all_to_all.10.received = bf16[8,16,640]{2,1,0:T(8,128)(2,1)S(1)} all-to-all(bf16[8,16,640]{2,1,0:T(8,128)(2,1)S(1)} %bitcast.8), channel_id=1, replica_groups=mesh['wide'=8,'rest'=2,'pair'=2] {'wide'}, dimensions={0} | all-to-all | bytes 327680 | tf_op jit(solution)/shard_map/all_to_all | solution.py:307
  20.6 0.3 merge.1.after.refs_0_
  20.9 0.0 collective-permute-start.3
  20.9 1.6 %collective-permute-start.2 = (bf16[16,640]{1,0:T(8,128)(2,1)S(1)}, bf16[16,640]{1,0:T(8,128)(2,1)S(1)}, u32[]{:S(2)}, u32[]{:S(2)}) collective-permute-start(bf16[16,640]{1,0:T(8,128)(2,1)S(1)} %merge.1.after.refs_0_), channel_id=1, source_target_pairs={{0,3},{1,2},{2,1},{3,0},{4,7},{5,6},{6,5},{7,4},{8,11},{9,10},{10,... | collective-permute-start | bytes 61448 | tf_op jit(solution)/shard_map/ppermute | solution.py:257
  22.5 0.5 %collective-permute-start.1 = (bf16[16,640]{1,0:T(8,128)(2,1)S(1)}, bf16[16,640]{1,0:T(8,128)(2,1)S(1)}, u32[]{:S(2)}, u32[]{:S(2)}) collective-permute-start(bf16[16,640]{1,0:T(8,128)(2,1)S(1)} %merge.1.after.refs_0_), channel_id=1, source_target_pairs={{0,2},{1,3},{2,0},{3,1},{4,6},{5,7},{6,4},{7,5},{8,10},{9,11},{10,... | collective-permute-start | bytes 61448 | tf_op jit(solution)/shard_map/ppermute | solution.py:257
  23.0 0.6 %combine.1.after = bf16[2048,128]{1,0:T(8,128)(2,1)S(1)} custom-call(f32[2048,128]{1,0:T(8,128)S(1)} %get-tuple-element.14.logits, bf16[16,640]{1,0:T(8,128)(2,1)S(1)} %merge.1.after.refs_0_), custom_call_target="tpu_custom_call" | custom-call | flops 2097152 | bytes 1572864 | tf_op jit(solution)/shard_map/combine/pallas_call | solution.py:319
  23.7 0.0 collective-permute-done.3.refs_3_
  23.7 0.5 %collective-permute-done.2.refs_2_ = bf16[16,640]{1,0:T(8,128)(2,1)S(1)} collective-permute-done((bf16[16,640]{1,0:T(8,128)(2,1)S(1)}, bf16[16,640]{1,0:T(8,128)(2,1)S(1)}, u32[]{:S(2)}, u32[]{:S(2)}) %collective-permute-start.2) | collective-permute-done | bytes 20512 | tf_op jit(solution)/shard_map/ppermute | solution.py:257
  24.2 2.1 %collective-permute-done.1.refs_1_ = bf16[16,640]{1,0:T(8,128)(2,1)S(1)} collective-permute-done((bf16[16,640]{1,0:T(8,128)(2,1)S(1)}, bf16[16,640]{1,0:T(8,128)(2,1)S(1)}, u32[]{:S(2)}, u32[]{:S(2)}) %collective-permute-start.1) | collective-permute-done | bytes 20512 | tf_op jit(solution)/shard_map/ppermute | solution.py:257
  26.3 0.0 slice-done
  26.3 0.0 slice-done.2
  26.3 0.0 slice-done.1
  26.3 0.0 slice-done.3
  26.3 2.0 %experts.1 = (bf16[4,16,1024]{2,1,0:T(8,128)(2,1)S(1)}, bf16[16,512]{1,0:T(8,128)(2,1)S(1)}) custom-call(s32[1]{0:T(128)} %bitcast.place, bf16[4,1024,1024]{2,1,0:T(8,128)(2,1)S(1)} %bitcast.7, bf16[4,1024,1024]{2,1,0:T(8,128)(2,1)S(1)} %bitcast.5, bf16[2048,128]{1,0:T(8,128)(2,1)S(1)} %combine.1.after, bf16[16,640]{1,0:T(8,128)(2,1)S(1)} %merge.1.after.refs_0_, ...), custom_call_target="tpu_custom_call" | custom-call | tf_op jit(solution)/shard_map/experts/pallas_call | solution.py:329
  28.3 0.0 collective-permute-start.4
  28.3 0.7 %own.1 = f32[16,512]{1,0:T(8,128)S(1)} custom-call(s32[1]{0:T(128)} %bitcast.place, bf16[4,16,1024]{2,1,0:T(8,128)(2,1)S(1)} %get-tuple-element.19.hidden, bf16[4,1024,1024]{2,1,0:T(8,128)(2,1)S(1)} %bitcast.5, bf16[16,512]{1,0:T(8,128)(2,1)S(1)} %get-tuple-element.20.after), custom_call_target="tpu_custom_call" | custom-call | flops 67108864 | bytes 4194304 | tf_op jit(solution)/shard_map/own/pallas_call | solution.py:341
  29.0 0.5 %collective-permute-done.4 = bf16[16,512]{1,0:T(8,128)(2,1)S(1)} collective-permute-done((bf16[16,512]{1,0:T(8,128)(2,1)S(1)}, bf16[16,512]{1,0:T(8,128)(2,1)S(1)}, u32[]{:S(2)}, u32[]{:S(2)}) %collective-permute-start.4) | collective-permute-done | bytes 16416 | tf_op jit(solution)/shard_map/ppermute | solution.py:257
  29.5 13.1 %all_to_all.11 = bf16[16,16,512]{2,1,0:T(8,128)(2,1)S(1)} all-to-all(bf16[16,16,512]{2,1,0:T(8,128)(2,1)S(1)} %broadcast_in_dim.3), channel_id=1, replica_groups=mesh['wide'=8,'rest'=2,'pair'=2] {'rest','wide'}, dimensions={0} | all-to-all | bytes 524288 | tf_op jit(solution)/shard_map/all_to_all | solution.py:352
  42.6 0.1 collective-permute-start.5
  42.7 1.2 %mix.1 = (bf16[2048,1024]{1,0:T(8,128)(2,1)}, bf16[1024,512]{1,0:T(8,128)(2,1)S(1)}) custom-call(s32[1]{0:T(128)} %bitcast.place, bf16[2048,128]{1,0:T(8,128)(2,1)S(1)} %combine.1.after, bf16[128,512]{1,0:T(8,128)(2,1)S(1)} %bitcast.10), custom_call_target="tpu_custom_call" | custom-call | flops 268435456 | bytes 2621440 | tf_op jit(solution)/shard_map/mix/pallas_call | solution.py:357
  43.9 0.1 collective-permute-done.5.slot_out
  44.1 1.7 %mix_other.1 = bf16[2048,1024]{1,0:T(8,128)(2,1)} custom-call(s32[1]{0:T(128)} %bitcast.place, bf16[2048,128]{1,0:T(8,128)(2,1)S(1)} %combine.1.after, bf16[128,512]{1,0:T(8,128)(2,1)S(1)} %collective-permute-done.5.slot_out, bf16[1024,512]{1,0:T(8,128)(2,1)S(1)} %get-tuple-element.21.rest, ...), custom_call_target="tpu_custom_call", output_to_operand_aliasing={{}: (4, {})} | custom-call | flops 268435456 | bytes 2621440 | tf_op jit(solution)/shard_map/mix_other/pallas_call | solution.py:370
  (5 shorter events, 0.1 us)
Async XLA Ops:
  3.7 1.5 %collective-permute-start = (bf16[128,640]{1,0:T(8,128)(2,1)S(1)}, bf16[128,640]{1,0:T(8,128)(2,1)S(1)}, u32[]{:S(2)}, u32[]{:S(2)}) collective-permute-start(bf16[128,640]{1,0:T(8,128)(2,1)S(1)} %get-tuple-element.18.after), channel_id=1, source_target_pairs={{0,1},{1,0},{2,3},{3,2},{4,5},{5,4},{6,7},{7,6},{8,9},{9,8},{10,11... | collective-permute-start | bytes 491528 | tf_op jit(solution)/shard_map/ppermute | solution.py:257
  4.2 22.1 %slice-start = ((s8[8388608]{0:T(1024)(128)(4,1)}), s8[4194304]{0:T(1024)(128)(4,1)S(1)}, s32[]{:S(2)}) async-start(s8[8388608]{0:T(1024)(128)(4,1)} %bitcast.4), calls=%async_computation.2 | async-start | bytes 8388608
  4.2 22.1 %slice-start.2 = ((s8[8388608]{0:T(1024)(128)(4,1)}), s8[4194304]{0:T(1024)(128)(4,1)S(1)}, s32[]{:S(2)}) async-start(s8[8388608]{0:T(1024)(128)(4,1)} %bitcast.6), calls=%async_computation.4 | async-start | bytes 8388608
  4.7 21.7 %slice-start.1 = ((s8[8388608]{0:T(1024)(128)(4,1)}), s8[4194304]{0:T(1024)(128)(4,1)S(1)}, s32[]{:S(2)}) async-start(s8[8388608]{0:T(1024)(128)(4,1)} %bitcast.4), calls=%async_computation.3 | async-start | bytes 8388608
  4.7 21.6 %slice-start.3 = ((s8[8388608]{0:T(1024)(128)(4,1)}), s8[4194304]{0:T(1024)(128)(4,1)S(1)}, s32[]{:S(2)}) async-start(s8[8388608]{0:T(1024)(128)(4,1)} %bitcast.6), calls=%async_computation.5 | async-start | bytes 8388608
  20.9 2.8 %collective-permute-start.3 = (bf16[16,640]{1,0:T(8,128)(2,1)S(1)}, bf16[16,640]{1,0:T(8,128)(2,1)S(1)}, u32[]{:S(2)}, u32[]{:S(2)}) collective-permute-start(bf16[16,640]{1,0:T(8,128)(2,1)S(1)} %merge.1.after.refs_0_), channel_id=1, source_target_pairs={{0,1},{1,0},{2,3},{3,2},{4,5},{5,4},{6,7},{7,6},{8,9},{9,8},{10,11... | collective-permute-start | bytes 61448 | tf_op jit(solution)/shard_map/ppermute | solution.py:257
  20.9 3.3 %collective-permute-start.2 = (bf16[16,640]{1,0:T(8,128)(2,1)S(1)}, bf16[16,640]{1,0:T(8,128)(2,1)S(1)}, u32[]{:S(2)}, u32[]{:S(2)}) collective-permute-start(bf16[16,640]{1,0:T(8,128)(2,1)S(1)} %merge.1.after.refs_0_), channel_id=1, source_target_pairs={{0,3},{1,2},{2,1},{3,0},{4,7},{5,6},{6,5},{7,4},{8,11},{9,10},{10,... | collective-permute-start | bytes 61448 | tf_op jit(solution)/shard_map/ppermute | solution.py:257
  22.5 3.8 %collective-permute-start.1 = (bf16[16,640]{1,0:T(8,128)(2,1)S(1)}, bf16[16,640]{1,0:T(8,128)(2,1)S(1)}, u32[]{:S(2)}, u32[]{:S(2)}) collective-permute-start(bf16[16,640]{1,0:T(8,128)(2,1)S(1)} %merge.1.after.refs_0_), channel_id=1, source_target_pairs={{0,2},{1,3},{2,0},{3,1},{4,6},{5,7},{6,4},{7,5},{8,10},{9,11},{10,... | collective-permute-start | bytes 61448 | tf_op jit(solution)/shard_map/ppermute | solution.py:257
  28.3 1.2 %collective-permute-start.4 = (bf16[16,512]{1,0:T(8,128)(2,1)S(1)}, bf16[16,512]{1,0:T(8,128)(2,1)S(1)}, u32[]{:S(2)}, u32[]{:S(2)}) collective-permute-start(bf16[16,512]{1,0:T(8,128)(2,1)S(1)} %get-tuple-element.20.after), channel_id=1, source_target_pairs={{0,1},{1,0},{2,3},{3,2},{4,5},{5,4},{6,7},{7,6},{8,9},{9,8},{10,11... | collective-permute-start | bytes 49160 | tf_op jit(solution)/shard_map/ppermute | solution.py:257
  42.6 1.4 %collective-permute-start.5 = (bf16[128,512]{1,0:T(8,128)(2,1)S(1)}, bf16[128,512]{1,0:T(8,128)(2,1)S(1)}, u32[]{:S(2)}, u32[]{:S(2)}) collective-permute-start(bf16[128,512]{1,0:T(8,128)(2,1)S(1)} %bitcast.9), channel_id=1, source_target_pairs={{0,1},{1,0},{2,3},{3,2},{4,5},{5,4},{6,7},{7,6},{8,9},{9,8},{10,11... | collective-permute-start | bytes 393224 | tf_op jit(solution)/shard_map/ppermute | solution.py:257

commit v17 on v16

--- a/solution.py
+++ b/solution.py
@@ -164,16 +164,16 @@
     send[:, width:] = side_message(peak, total)
 
 
-def find_slot_in(place, mine, others):
-    half = mine[0].shape[1] - SIDE
-    means = []
-    for parts in (mine, others):
-        sums, _, total = add_parts([part[...] for part in parts], half)
-        means.append((sums / total).astype(BF16))
-    first = place[0] == 0
-    return jnp.concatenate(
-        [jnp.where(first, means[0], means[1]), jnp.where(first, means[1], means[0])], axis=1
-    )
+def finish_kernel(combine, *refs):
+    slot_in = refs[-1]
+    sums, _, total = add_parts([ref[...] for ref in refs[:-1]], slot_in.shape[1])
+    slot_in[...] = (sums / total).astype(BF16)
+
+
+def first_product_kernel(place, slot_in, expert_in, result):
+    half = slot_in.shape[1]
+    for e in range(expert_in.shape[0]):
+        result[e] = dot(slot_in[...], expert_in[e, column_half(place[0], half), :])
 
 
 def second_product(hidden, weights, columns):
@@ -184,15 +184,14 @@
     return result
 
 
-def expert_kernel(place, expert_in, expert_out, after, *refs):
-    parts, hidden, send = refs[:-2], refs[-2], refs[-1]
-    count = len(parts) // 2
-    slot_in = find_slot_in(place, parts[:count], parts[count:])
+def expert_kernel(place, slot_in, first, expert_in, expert_out, hidden, send):
+    half = slot_in.shape[1]
     values = []
     for e in range(expert_in.shape[0]):
-        values.append(jax.nn.gelu(dot(slot_in, expert_in[e])).astype(BF16))
+        product = first[e] + dot(slot_in[...], expert_in[e, column_half(1 - place[0], half), :])
+        values.append(jax.nn.gelu(product).astype(BF16))
         hidden[e] = values[e]
-    send[...] = second_product(values, expert_out, column_half(1 - place[0], send.shape[1])).astype(BF16)
+    send[...] = second_product(values, expert_out, column_half(1 - place[0], half)).astype(BF16)
 
 
 def own_kernel(place, hidden, expert_out, after, keep):
@@ -313,9 +312,7 @@
         compiler_params=params(16),
         name="merge",
     )(received)
-    axes = ("rest", "pair")
-    mine = [send] + [move(send, axes, (r, 0)) for r in range(1, rest)]
-    others = [move(send, axes, (r, 1)) for r in reversed(range(rest))]
+    mine = [send] + [move(send, ("rest",), (r,)) for r in range(1, rest)]
     combine = pl.pallas_call(
         combine_kernel,
         out_shape=jax.ShapeDtypeStruct((count, slots), BF16),
@@ -326,17 +323,35 @@
         name="combine",
     )(logits, send)
     experts, units = expert_out.shape[:2]
+    slot_in = pl.pallas_call(
+        finish_kernel,
+        out_shape=jax.ShapeDtypeStruct((rows, half), BF16),
+        in_specs=[any_space] + [VMEM] * rest,
+        out_specs=VMEM,
+        compiler_params=params(16),
+        name="finish",
+    )(combine, *mine)
+    other = swap_pair(slot_in)
+    first = pl.pallas_call(
+        first_product_kernel,
+        out_shape=jax.ShapeDtypeStruct((experts, rows, units), F32),
+        in_specs=[SMEM, VMEM, VMEM],
+        out_specs=VMEM,
+        cost_estimate=cost(2 * rows * units * half * experts, 2 * experts * units * half),
+        compiler_params=params(8),
+        name="first_product",
+    )(place, slot_in, expert_in)
     hidden, send = pl.pallas_call(
         expert_kernel,
         out_shape=(
             jax.ShapeDtypeStruct((experts, rows, units), BF16),
             jax.ShapeDtypeStruct((rows, half), BF16),
         ),
-        in_specs=[SMEM, VMEM, VMEM, any_space] + [VMEM] * (2 * rest),
+        in_specs=[SMEM, VMEM, VMEM, VMEM, VMEM],
         out_specs=(VMEM, VMEM),
         compiler_params=params(8),
         name="experts",
-    )(place, expert_in, expert_out, combine, *mine, *others)
+    )(place, other, first, expert_in, expert_out)
     received = swap_pair(send)
     keep = pl.pallas_call(
         own_kernel,

time: 46 us -> 46 us (level)
  blocking collectives: 28.1 us -> 29 us
  waiting for transfers between devices: 3.79 us -> 3.12 us
    all_to_all x1, blocking collectives: 13.1 us -> 14 us  [shards(): lax.all_to_all(partials, ('rest', 'wide'), split_axis=0, concat_axis=0, t...]
    pallas_call x0 -> x2, Pallas kernels: none -> 0.88 us  [the longest x1 0.65 us: shards(): pl.pallas_call(first_product_kernel, out_shape=jax.ShapeDtypeStruct((expe...]
    pallas_call x1, Pallas kernels: 1.96 us -> 1.21 us  [shards(): pl.pallas_call(expert_kernel, out_shape=(jax.ShapeDtypeStruct((experts, r...]
    ppermute x6 -> x5, waiting for transfers between devices: 3.79 us -> 3.12 us  [move(): return lax.ppermute(value, axes, moves)]
    ppermute x6 -> x5, starting transfers between devices: 2.74 us -> 2.33 us  [move(): return lax.ppermute(value, axes, moves)]
  transfers between devices with their start and end apart: 6 -> 5, of which waited for: 5 -> 5; matrix products, arithmetic and copies ran while one was open for 0% -> 0% of each run, Pallas kernels for 6% -> 8%
where the time goes in v17:
time: 46 us; the launch traced here: 45.7 us
  blocking collectives  29 us (63%)
  Pallas kernels  11.1 us (24%)
  waiting for transfers between devices  3.12 us (7%)
  starting transfers between devices  2.33 us (5%)
    all_to_all x1, blocking collectives, shards(): lax.all_to_all(send.reshape(groups, rows, -1), 'wide', split_axis=0, conc...  15 us
    all_to_all x1, blocking collectives, shards(): lax.all_to_all(partials, ('rest', 'wide'), split_axis=0, concat_axis=0, t...  14 us
    pallas_call x1, Pallas kernels, shards(): pl.pallas_call(gather_kernel, out_shape=(jax.ShapeDtypeStruct((count, slo...  3.67 us
    ppermute x5, waiting for transfers between devices, move(): return lax.ppermute(value, axes, moves)  3.12 us
    ppermute x5, starting transfers between devices, move(): return lax.ppermute(value, axes, moves)  2.33 us
    pallas_call x1, Pallas kernels, shards(): pl.pallas_call(mix_other_kernel, out_shape=jax.ShapeDtypeStruct((count, m...  1.74 us
    pallas_call x1, Pallas kernels, shards(): pl.pallas_call(mix_kernel, out_shape=(pltpu.HBM((count, model), BF16), ja...  1.21 us
    pallas_call x1, Pallas kernels, shards(): pl.pallas_call(expert_kernel, out_shape=(jax.ShapeDtypeStruct((experts, r...  1.21 us
  transfers between devices with their start and end apart: 5, of which 5 were waited for; matrix products, arithmetic and copies ran while one was open for 0% of the time, Pallas kernels for 8%

profile of v17, /device:TPU:0, one launch (start us, length us, event | category | flops | bytes accessed | tf_op | source)
XLA Modules:
  0.0 45.7 jit_solution(15873736676875839859)
XLA Ops:
  0.0 3.7 %gather.1 = (f32[2048,128]{1,0:T(8,128)S(1)}, bf16[128,2048]{1,0:T(8,128)(2,1)S(1)}, bf16[2048,1024]{1,0:T(8,128)(2,1)S(1)}, f32[128,128]{1,0:T(8,128)S(1)}, bf16[128,640]{1,0:T(8,128)(2,1)S(1)}) custom-call(s32[1]{0:T(128)} %bitcast.place, bf16[2048,1024]{1,0:T(8,128)(2,1)} %tokens.1, bf16[1024,128]{1,0:T(8,128)(2,1)} %slot_params.1), custom_call_target="tpu_custom_call" | custom-call | tf_op jit(solution)/shard_map/gather/pallas_call | solution.py:272
  3.7 0.5 %collective-permute-start = (bf16[128,640]{1,0:T(8,128)(2,1)S(1)}, bf16[128,640]{1,0:T(8,128)(2,1)S(1)}, u32[]{:S(2)}, u32[]{:S(2)}) collective-permute-start(bf16[128,640]{1,0:T(8,128)(2,1)S(1)} %get-tuple-element.18.after), channel_id=1, source_target_pairs={{0,1},{1,0},{2,3},{3,2},{4,5},{5,4},{6,7},{7,6},{8,9},{9,8},{10,11... | collective-permute-start | bytes 491528 | tf_op jit(solution)/shard_map/ppermute | solution.py:256
  4.2 0.0 slice-start
  4.2 0.0 slice-start.2
  4.2 0.5 own_sums.1.keep
  4.7 0.0 slice-start.1
  4.7 0.0 slice-start.3
  4.7 0.5 %collective-permute-done.received = bf16[128,640]{1,0:T(8,128)(2,1)S(1)} collective-permute-done((bf16[128,640]{1,0:T(8,128)(2,1)S(1)}, bf16[128,640]{1,0:T(8,128)(2,1)S(1)}, u32[]{:S(2)}, u32[]{:S(2)}) %collective-permute-start) | collective-permute-done | bytes 163872 | tf_op jit(solution)/shard_map/ppermute | solution.py:256
  5.2 0.4 pair.1
  5.6 15.0 %all_to_all.10.received = bf16[8,16,640]{2,1,0:T(8,128)(2,1)S(1)} all-to-all(bf16[8,16,640]{2,1,0:T(8,128)(2,1)S(1)} %bitcast.8), channel_id=1, replica_groups=mesh['wide'=8,'rest'=2,'pair'=2] {'wide'}, dimensions={0} | all-to-all | bytes 327680 | tf_op jit(solution)/shard_map/all_to_all | solution.py:306
  20.6 0.3 merge.1.after.refs_0_
  20.9 1.5 %collective-permute-start.1 = (bf16[16,640]{1,0:T(8,128)(2,1)S(1)}, bf16[16,640]{1,0:T(8,128)(2,1)S(1)}, u32[]{:S(2)}, u32[]{:S(2)}) collective-permute-start(bf16[16,640]{1,0:T(8,128)(2,1)S(1)} %merge.1.after.refs_0_), channel_id=1, source_target_pairs={{0,2},{2,0},{1,3},{3,1},{4,6},{6,4},{5,7},{7,5},{8,10},{10,8},{9,1... | collective-permute-start | bytes 61448 | tf_op jit(solution)/shard_map/ppermute | solution.py:256
  22.4 0.6 %combine.1 = bf16[2048,128]{1,0:T(8,128)(2,1)S(1)} custom-call(f32[2048,128]{1,0:T(8,128)S(1)} %get-tuple-element.14.logits, bf16[16,640]{1,0:T(8,128)(2,1)S(1)} %merge.1.after.refs_0_), custom_call_target="tpu_custom_call" | custom-call | flops 2097152 | bytes 1572864 | tf_op jit(solution)/shard_map/combine/pallas_call | solution.py:316
  23.0 1.6 %collective-permute-done.1.refs_1_ = bf16[16,640]{1,0:T(8,128)(2,1)S(1)} collective-permute-done((bf16[16,640]{1,0:T(8,128)(2,1)S(1)}, bf16[16,640]{1,0:T(8,128)(2,1)S(1)}, u32[]{:S(2)}, u32[]{:S(2)}) %collective-permute-start.1) | collective-permute-done | bytes 20512 | tf_op jit(solution)/shard_map/ppermute | solution.py:256
  24.7 0.2 finish.1.slot_in
  24.9 0.0 collective-permute-start.2
  24.9 0.0 slice-done
  24.9 0.0 slice-done.1
  25.0 0.7 %first_product.1.first = f32[4,16,1024]{2,1,0:T(8,128)S(1)} custom-call(s32[1]{0:T(128)} %bitcast.place, bf16[16,512]{1,0:T(8,128)(2,1)S(1)} %finish.1.slot_in, bf16[4,1024,1024]{2,1,0:T(8,128)(2,1)S(1)} %bitcast.5), custom_call_target="tpu_custom_call" | custom-call | flops 67108864 | bytes 4194304 | tf_op jit(solution)/shard_map/first_product/pallas_call | solution.py:335
  25.6 0.5 %collective-permute-done.2.slot_in = bf16[16,512]{1,0:T(8,128)(2,1)S(1)} collective-permute-done((bf16[16,512]{1,0:T(8,128)(2,1)S(1)}, bf16[16,512]{1,0:T(8,128)(2,1)S(1)}, u32[]{:S(2)}, u32[]{:S(2)}) %collective-permute-start.2) | collective-permute-done | bytes 16416 | tf_op jit(solution)/shard_map/ppermute | solution.py:256
  26.1 0.0 slice-done.2
  26.1 0.0 slice-done.3
  26.1 1.2 %experts.1 = (bf16[4,16,1024]{2,1,0:T(8,128)(2,1)S(1)}, bf16[16,512]{1,0:T(8,128)(2,1)S(1)}) custom-call(s32[1]{0:T(128)} %bitcast.place, bf16[16,512]{1,0:T(8,128)(2,1)S(1)} %collective-permute-done.2.slot_in, f32[4,16,1024]{2,1,0:T(8,128)S(1)} %first_product.1.first, bf16[4,1024,1024]{2,1,0:T(8,128)(2,1)S(1)} %bitcast.5, bf16[4,1024,1024]{2,1,0:T(8,128)(2,1)S(1)} %bitcast.7), custom_call_target="tpu_custom_call" | custom-call | tf_op jit(solution)/shard_map/experts/pallas_call | solution.py:344
  27.3 0.2 collective-permute-start.3
  27.5 0.7 %own.1 = f32[16,512]{1,0:T(8,128)S(1)} custom-call(s32[1]{0:T(128)} %bitcast.place, bf16[4,16,1024]{2,1,0:T(8,128)(2,1)S(1)} %get-tuple-element.19.hidden, bf16[4,1024,1024]{2,1,0:T(8,128)(2,1)S(1)} %bitcast.7, bf16[16,512]{1,0:T(8,128)(2,1)S(1)} %get-tuple-element.20.after), custom_call_target="tpu_custom_call" | custom-call | flops 67108864 | bytes 4194304 | tf_op jit(solution)/shard_map/own/pallas_call | solution.py:356
  28.1 0.4 collective-permute-done.3
  28.5 14.0 %all_to_all.11 = bf16[16,16,512]{2,1,0:T(8,128)(2,1)S(1)} all-to-all(bf16[16,16,512]{2,1,0:T(8,128)(2,1)S(1)} %broadcast_in_dim.3), channel_id=1, replica_groups=mesh['wide'=8,'rest'=2,'pair'=2] {'rest','wide'}, dimensions={0} | all-to-all | bytes 524288 | tf_op jit(solution)/shard_map/all_to_all | solution.py:367
  42.6 0.1 collective-permute-start.4
  42.7 1.2 %mix.1 = (bf16[2048,1024]{1,0:T(8,128)(2,1)}, bf16[1024,512]{1,0:T(8,128)(2,1)S(1)}) custom-call(s32[1]{0:T(128)} %bitcast.place, bf16[2048,128]{1,0:T(8,128)(2,1)S(1)} %combine.1, bf16[128,512]{1,0:T(8,128)(2,1)S(1)} %bitcast.10), custom_call_target="tpu_custom_call" | custom-call | flops 268435456 | bytes 2621440 | tf_op jit(solution)/shard_map/mix/pallas_call | solution.py:372
  43.9 0.1 collective-permute-done.4.slot_out
  44.0 1.7 %mix_other.1 = bf16[2048,1024]{1,0:T(8,128)(2,1)} custom-call(s32[1]{0:T(128)} %bitcast.place, bf16[2048,128]{1,0:T(8,128)(2,1)S(1)} %combine.1, bf16[128,512]{1,0:T(8,128)(2,1)S(1)} %collective-permute-done.4.slot_out, bf16[1024,512]{1,0:T(8,128)(2,1)S(1)} %get-tuple-element.21.rest, ...), custom_call_target="tpu_custom_call", output_to_operand_aliasing={{}: (4, {})} | custom-call | flops 268435456 | bytes 2621440 | tf_op jit(solution)/shard_map/mix_other/pallas_call | solution.py:385
  (5 shorter events, 0.1 us)
Async XLA Ops:
  3.7 1.5 %collective-permute-start = (bf16[128,640]{1,0:T(8,128)(2,1)S(1)}, bf16[128,640]{1,0:T(8,128)(2,1)S(1)}, u32[]{:S(2)}, u32[]{:S(2)}) collective-permute-start(bf16[128,640]{1,0:T(8,128)(2,1)S(1)} %get-tuple-element.18.after), channel_id=1, source_target_pairs={{0,1},{1,0},{2,3},{3,2},{4,5},{5,4},{6,7},{7,6},{8,9},{9,8},{10,11... | collective-permute-start | bytes 491528 | tf_op jit(solution)/shard_map/ppermute | solution.py:256
  4.2 20.8 %slice-start = ((s8[8388608]{0:T(1024)(128)(4,1)}), s8[4194304]{0:T(1024)(128)(4,1)S(1)}, s32[]{:S(2)}) async-start(s8[8388608]{0:T(1024)(128)(4,1)} %bitcast.4), calls=%async_computation.2 | async-start | bytes 8388608
  4.2 21.9 %slice-start.2 = ((s8[8388608]{0:T(1024)(128)(4,1)}), s8[4194304]{0:T(1024)(128)(4,1)S(1)}, s32[]{:S(2)}) async-start(s8[8388608]{0:T(1024)(128)(4,1)} %bitcast.6), calls=%async_computation.4 | async-start | bytes 8388608
  4.7 20.3 %slice-start.1 = ((s8[8388608]{0:T(1024)(128)(4,1)}), s8[4194304]{0:T(1024)(128)(4,1)S(1)}, s32[]{:S(2)}) async-start(s8[8388608]{0:T(1024)(128)(4,1)} %bitcast.4), calls=%async_computation.3 | async-start | bytes 8388608
  4.7 21.4 %slice-start.3 = ((s8[8388608]{0:T(1024)(128)(4,1)}), s8[4194304]{0:T(1024)(128)(4,1)S(1)}, s32[]{:S(2)}) async-start(s8[8388608]{0:T(1024)(128)(4,1)} %bitcast.6), calls=%async_computation.5 | async-start | bytes 8388608
  20.9 3.8 %collective-permute-start.1 = (bf16[16,640]{1,0:T(8,128)(2,1)S(1)}, bf16[16,640]{1,0:T(8,128)(2,1)S(1)}, u32[]{:S(2)}, u32[]{:S(2)}) collective-permute-start(bf16[16,640]{1,0:T(8,128)(2,1)S(1)} %merge.1.after.refs_0_), channel_id=1, source_target_pairs={{0,2},{2,0},{1,3},{3,1},{4,6},{6,4},{5,7},{7,5},{8,10},{10,8},{9,1... | collective-permute-start | bytes 61448 | tf_op jit(solution)/shard_map/ppermute | solution.py:256
  24.9 1.2 %collective-permute-start.2 = (bf16[16,512]{1,0:T(8,128)(2,1)S(1)}, bf16[16,512]{1,0:T(8,128)(2,1)S(1)}, u32[]{:S(2)}, u32[]{:S(2)}) collective-permute-start(bf16[16,512]{1,0:T(8,128)(2,1)S(1)} %finish.1.slot_in), channel_id=1, source_target_pairs={{0,1},{1,0},{2,3},{3,2},{4,5},{5,4},{6,7},{7,6},{8,9},{9,8},{10,11... | collective-permute-start | bytes 49160 | tf_op jit(solution)/shard_map/ppermute | solution.py:256
  27.3 1.2 %collective-permute-start.3 = (bf16[16,512]{1,0:T(8,128)(2,1)S(1)}, bf16[16,512]{1,0:T(8,128)(2,1)S(1)}, u32[]{:S(2)}, u32[]{:S(2)}) collective-permute-start(bf16[16,512]{1,0:T(8,128)(2,1)S(1)} %get-tuple-element.20.after), channel_id=1, source_target_pairs={{0,1},{1,0},{2,3},{3,2},{4,5},{5,4},{6,7},{7,6},{8,9},{9,8},{10,11... | collective-permute-start | bytes 49160 | tf_op jit(solution)/shard_map/ppermute | solution.py:256
  42.6 1.4 %collective-permute-start.4 = (bf16[128,512]{1,0:T(8,128)(2,1)S(1)}, bf16[128,512]{1,0:T(8,128)(2,1)S(1)}, u32[]{:S(2)}, u32[]{:S(2)}) collective-permute-start(bf16[128,512]{1,0:T(8,128)(2,1)S(1)} %bitcast.9), channel_id=1, source_target_pairs={{0,1},{1,0},{2,3},{3,2},{4,5},{5,4},{6,7},{7,6},{8,9},{9,8},{10,11... | collective-permute-start | bytes 393224 | tf_op jit(solution)/shard_map/ppermute | solution.py:256

commit v18 on v17

--- a/solution.py
+++ b/solution.py
@@ -131,16 +131,19 @@
     keep[...] = early * side[:, 2:3] + late * side[:, 3:4]
 
 
-def pair_kernel(keep, side, received, send):
+def pair_kernel(place, keep, side, received, *sends):
     width = keep.shape[1]
-    peak_mine, total_mine = side[:, 0:1], side[:, 1:2]
-    peak_other, total_other = read_message(received[:, width:])
-    peak = jnp.maximum(peak_mine, peak_other)
-    scale_mine, scale_other = jnp.exp(peak_mine - peak), jnp.exp(peak_other - peak)
-    total = total_mine * scale_mine + total_other * scale_other
-    sums = keep[...] * scale_mine + received[:, :width].astype(F32) * scale_other
-    send[:, :width] = sums.astype(BF16)
-    send[:, width:] = side_message(peak, total)
+    for r, send in enumerate(sends):
+        rows = send.shape[0]
+        span = pl.ds(pl.multiple_of((place[1] ^ r) * rows, rows), rows)
+        peak_mine, total_mine = side[span, 0:1], side[span, 1:2]
+        peak_other, total_other = read_message(received[span, width:])
+        peak = jnp.maximum(peak_mine, peak_other)
+        scale_mine, scale_other = jnp.exp(peak_mine - peak), jnp.exp(peak_other - peak)
+        total = total_mine * scale_mine + total_other * scale_other
+        sums = keep[span, :] * scale_mine + received[span, :width].astype(F32) * scale_other
+        send[:, :width] = sums.astype(BF16)
+        send[:, width:] = side_message(peak, total)
 
 
 def add_parts(parts, width):
@@ -157,11 +160,13 @@
     return sums, peak, total
 
 
-def merge_kernel(received, send):
-    width = send.shape[1] - SIDE
-    sums, peak, total = add_parts([received[g] for g in range(received.shape[0])], width)
-    send[:, :width] = sums.astype(BF16)
-    send[:, width:] = side_message(peak, total)
+def merge_kernel(place, *refs):
+    for n, send in enumerate(refs[-2:]):
+        rows, width = send.shape[0], send.shape[1] - SIDE
+        span = pl.ds(pl.multiple_of((place[2] ^ n) * rows, rows), rows)
+        sums, peak, total = add_parts([ref[span, :] for ref in refs[:-2]], width)
+        send[:, :width] = sums.astype(BF16)
+        send[:, width:] = side_message(peak, total)
 
 
 def finish_kernel(combine, *refs):
@@ -199,10 +204,15 @@
     keep[...] = second_product(values, expert_out, column_half(place[0], keep.shape[1]))
 
 
-def combine_kernel(logits, after, combine):
+def combine_kernel(place, logits, after, combine):
     value = logits[...]
+    slots = value.shape[1]
     weights = jnp.exp(value - jnp.max(value, axis=1, keepdims=True))
-    combine[...] = (weights / jnp.sum(weights, axis=1, keepdims=True)).astype(BF16)
+    weights = (weights / jnp.sum(weights, axis=1, keepdims=True)).astype(BF16)
+    row = lax.broadcasted_iota(jnp.int32, (slots, slots), 0)
+    column = lax.broadcasted_iota(jnp.int32, (slots, slots), 1)
+    swap = jnp.where(row == (column ^ place[3]), 1.0, 0.0).astype(BF16)
+    combine[...] = dot(weights, swap).astype(BF16)
 
 
 def mix_kernel(place, combine, slot_out, mixed, rest, held, sems):
@@ -249,7 +259,7 @@
     for index in range(math.prod(sizes)):
         source, target, stride = index, 0, 1
         for size, offset in zip(reversed(sizes), reversed(offsets)):
-            target += (source % size + offset) % size * stride
+            target += (source % size ^ offset) * stride
             source //= size
             stride *= size
         moves.append((index, target))
@@ -263,10 +273,12 @@
 def shards(tokens, slot_params, expert_in, expert_out):
     count, model = tokens.shape
     slots = slot_params.shape[1]
-    groups, rest = lax.axis_size("wide"), lax.axis_size("rest")
-    rows = slots // groups
+    far, near, rest = [lax.axis_size(axis) for axis in ("far", "near", "rest")]
+    rows = slots // (far * near)
     half = model // 2
-    place = lax.axis_index("pair").astype(jnp.int32).reshape(1)
+    far_at, near_at = lax.axis_index("far"), lax.axis_index("near")
+    place = [lax.axis_index("pair"), far_at, near_at, (far_at * near + near_at) * rows]
+    place = jnp.stack(place).astype(jnp.int32)
     any_space = pl.BlockSpec(memory_space=pl.ANY)
 
     logits, turned, held, side, send = pl.pallas_call(
@@ -294,39 +306,41 @@
         compiler_params=params(16),
         name="own_sums",
     )(place, turned, held, side, send)
-    send = pl.pallas_call(
+    sends = pl.pallas_call(
         pair_kernel,
-        out_shape=jax.ShapeDtypeStruct((slots, half + SIDE), BF16),
-        in_specs=[VMEM] * 3,
-        out_specs=VMEM,
+        out_shape=(jax.ShapeDtypeStruct((near * rows, half + SIDE), BF16),) * far,
+        in_specs=[SMEM] + [VMEM] * 3,
+        out_specs=(VMEM,) * far,
         cost_estimate=cost(0, 6 * slots * model, 128 * slots * model),
         compiler_params=params(16),
         name="pair",
-    )(keep, side, received)
-    received = lax.all_to_all(send.reshape(groups, rows, -1), "wide", split_axis=0, concat_axis=0, tiled=True)
-    send = pl.pallas_call(
+    )(place, keep, side, received)
+    parts = [sends[0]] + [move(sends[r], ("far",), (r,)) for r in range(1, far)]
+    send, their = pl.pallas_call(
         merge_kernel,
-        out_shape=jax.ShapeDtypeStruct((rows, half + SIDE), BF16),
-        in_specs=[VMEM],
-        out_specs=VMEM,
+        out_shape=(jax.ShapeDtypeStruct((rows, half + SIDE), BF16),) * 2,
+        in_specs=[SMEM] + [VMEM] * far,
+        out_specs=(VMEM, VMEM),
         compiler_params=params(16),
         name="merge",
-    )(received)
-    mine = [send] + [move(send, ("rest",), (r,)) for r in range(1, rest)]
+    )(place, *parts)
+    plane = ("near", "rest")
+    mine = [send] + [move(send, plane, (0, r)) for r in range(1, rest)]
+    mine += [move(their, plane, (1, r)) for r in range(rest)]
     combine = pl.pallas_call(
         combine_kernel,
         out_shape=jax.ShapeDtypeStruct((count, slots), BF16),
-        in_specs=[VMEM, any_space],
+        in_specs=[SMEM, VMEM, any_space],
         out_specs=VMEM,
         cost_estimate=cost(8 * count * slots, 6 * count * slots, count * slots),
         compiler_params=params(16),
         name="combine",
-    )(logits, send)
+    )(place, logits, send)
     experts, units = expert_out.shape[:2]
     slot_in = pl.pallas_call(
         finish_kernel,
         out_shape=jax.ShapeDtypeStruct((rows, half), BF16),
-        in_specs=[any_space] + [VMEM] * rest,
+        in_specs=[any_space] + [VMEM] * len(mine),
         out_specs=VMEM,
         compiler_params=params(16),
         name="finish",
@@ -363,10 +377,14 @@
         name="own",
     )(place, hidden, expert_out, send)
     partial = (keep + received.astype(F32)).astype(BF16)
-    partials = jnp.broadcast_to(partial, (groups * rest, rows, half))
-    partials = lax.all_to_all(partials, ("rest", "wide"), split_axis=0, concat_axis=0, tiled=True)
-    slot_out = jnp.sum(partials.reshape(rest, groups, rows, half).astype(F32), axis=0)
-    slot_out = slot_out.astype(BF16).reshape(slots, half)
+    own = partial.astype(F32)
+    for r in range(1, rest):
+        own = own + move(partial, plane, (0, r)).astype(F32)
+    their = jnp.zeros_like(own)
+    for r in range(rest):
+        their = their + move(partial, plane, (1, r)).astype(F32)
+    block = jnp.concatenate([own, their], axis=0).astype(BF16)
+    slot_out = jnp.concatenate([block] + [move(block, ("far",), (r,)) for r in range(1, far)], axis=0)
     other = swap_pair(slot_out)
     done, blocks = count // 2, 8
     mixed, left = pl.pallas_call(
@@ -397,17 +415,17 @@
 
 def solution(mesh):
     wide, narrow = mesh.shape["wide"], mesh.shape["narrow"]
-    cut = Mesh(mesh.devices.reshape(wide, narrow // 2, 2), ("wide", "rest", "pair"))
-    narrow_axes = ("rest", "pair")
+    cut = Mesh(mesh.devices.reshape(wide // 2, 2, narrow // 2, 2), ("far", "near", "rest", "pair"))
+    wide_axes, narrow_axes = ("far", "near"), ("rest", "pair")
     return jax.shard_map(
         shards,
         mesh=cut,
         in_specs=(
-            P(("wide",) + narrow_axes, None),
+            P(wide_axes + narrow_axes, None),
             P(),
-            P("wide", None, narrow_axes),
-            P("wide", narrow_axes, None),
+            P(wide_axes, None, narrow_axes),
+            P(wide_axes, narrow_axes, None),
         ),
-        out_specs=P(("wide",) + narrow_axes, None),
+        out_specs=P(wide_axes + narrow_axes, None),
         check_vma=False,
     )

time: 46 us -> 48.6 us (1.057)
  blocking collectives: 29 us -> 0 us
  starting transfers between devices: 2.33 us -> 17.3 us
  waiting for transfers between devices: 3.12 us -> 14.1 us
  Pallas kernels: 11.1 us -> 16.7 us
    all_to_all x2 -> x0, blocking collectives: 29 us -> none  [the longest x1 15 us: shards(): lax.all_to_all(send.reshape(groups, rows, -1), 'wide', split_axis=0, conc...]
    ppermute x5 -> x16, starting transfers between devices: 2.33 us -> 17.3 us  [move(): return lax.ppermute(value, axes, moves)]
    ppermute x5 -> x16, waiting for transfers between devices: 3.12 us -> 14.1 us  [move(): return lax.ppermute(value, axes, moves)]
    pallas_call x2, Pallas kernels: 0.62 us -> 1.75 us  [the longest x1 0.93 us: shards(): pl.pallas_call(pair_kernel, out_shape=(jax.ShapeDtypeStruct((near * rows,...]
    pallas_call x1, Pallas kernels: 0.64 us -> 1.3 us  [shards(): pl.pallas_call(combine_kernel, out_shape=jax.ShapeDtypeStruct((count, slo...]
    pallas_call x1, Pallas kernels: 1.21 us -> 1.76 us  [shards(): pl.pallas_call(expert_kernel, out_shape=(jax.ShapeDtypeStruct((experts, r...]
    pallas_call x1, Pallas kernels: 0.46 us -> 1 us  [shards(): pl.pallas_call(own_sums_kernel, out_shape=jax.ShapeDtypeStruct((slots, ha...]
    pallas_call x1, Pallas kernels: 1.74 us -> 2.28 us  [shards(): pl.pallas_call(mix_other_kernel, out_shape=jax.ShapeDtypeStruct((count, m...]
  transfers between devices with their start and end apart: 5 -> 16, of which waited for: 5 -> 9; matrix products, arithmetic and copies ran while one was open for 0% -> 0% of each run, Pallas kernels for 8% -> 13%
where the time goes in v18:
time: 48.6 us; the launch traced here: 48.5 us
  starting transfers between devices  17.3 us (36%)
  Pallas kernels  16.7 us (34%)
  waiting for transfers between devices  14.1 us (29%)
    ppermute x16, starting transfers between devices, move(): return lax.ppermute(value, axes, moves)  17.3 us
    ppermute x16, waiting for transfers between devices, move(): return lax.ppermute(value, axes, moves)  14.1 us
    pallas_call x1, Pallas kernels, shards(): pl.pallas_call(gather_kernel, out_shape=(jax.ShapeDtypeStruct((count, slo...  4.21 us
    pallas_call x1, Pallas kernels, shards(): pl.pallas_call(mix_other_kernel, out_shape=jax.ShapeDtypeStruct((count, m...  2.28 us
    pallas_call x1, Pallas kernels, shards(): pl.pallas_call(expert_kernel, out_shape=(jax.ShapeDtypeStruct((experts, r...  1.76 us
    pallas_call x1, Pallas kernels, shards(): pl.pallas_call(mix_kernel, out_shape=(pltpu.HBM((count, model), BF16), ja...  1.75 us
    pallas_call x1, Pallas kernels, shards(): pl.pallas_call(combine_kernel, out_shape=jax.ShapeDtypeStruct((count, slo...  1.3 us
    pallas_call x1, Pallas kernels, shards(): pl.pallas_call(own_kernel, out_shape=jax.ShapeDtypeStruct((rows, half), F...  1.19 us
  transfers between devices with their start and end apart: 16, of which 9 were waited for; matrix products, arithmetic and copies ran while one was open for 0% of the time, Pallas kernels for 13%

profile of v18, /device:TPU:0, one launch (start us, length us, event | category | flops | bytes accessed | tf_op | source)
XLA Modules:
  0.0 48.5 jit_solution(3233652716402329693)
XLA Ops:
  0.1 4.2 %gather.1 = (f32[2048,128]{1,0:T(8,128)S(1)}, bf16[128,2048]{1,0:T(8,128)(2,1)S(1)}, bf16[2048,1024]{1,0:T(8,128)(2,1)S(1)}, f32[128,128]{1,0:T(8,128)S(1)}, bf16[128,640]{1,0:T(8,128)(2,1)S(1)}) custom-call(s32[4]{0:T(128)S(1)} %pad_add_fusion.place, bf16[2048,1024]{1,0:T(8,128)(2,1)} %tokens.1, bf16[1024,128]{1,0:T(8,128)(2,1)} %slot_params.1), custom_call_target="tpu_custom_call" | custom-call | tf_op jit(solution)/shard_map/gather/pallas_call | solution.py:284
  4.3 0.5 %collective-permute-start = (bf16[128,640]{1,0:T(8,128)(2,1)S(1)}, bf16[128,640]{1,0:T(8,128)(2,1)S(1)}, u32[]{:S(2)}, u32[]{:S(2)}) collective-permute-start(bf16[128,640]{1,0:T(8,128)(2,1)S(1)} %get-tuple-element.24.after), channel_id=1, source_target_pairs={{0,1},{1,0},{2,3},{3,2},{4,5},{5,4},{6,7},{7,6},{8,9},{9,8},{10,11... | collective-permute-start | bytes 491528 | tf_op jit(solution)/shard_map/ppermute | solution.py:266
  4.8 1.0 %own_sums.1.keep = f32[128,512]{1,0:T(8,128)S(1)} custom-call(s32[4]{0:T(128)S(1)} %pad_add_fusion.place, bf16[128,2048]{1,0:T(8,128)(2,1)S(1)} %get-tuple-element.21.turned, bf16[2048,1024]{1,0:T(8,128)(2,1)S(1)} %get-tuple-element.22.held, f32[128,128]{1,0:T(8,128)S(1)} %get-tuple-element.23.side, bf16[128,640]{1,0:T(8,128)(2,1)S(1)} %get-tuple-element.24.after), custom_call_target="tpu_custom_call" | custom-call | flops 268435456 | bytes 2621440 | tf_op jit(solution)/shard_map/own_sums/pallas_call | solution.py:300
  5.8 0.9 %pair.1 = (bf16[32,640]{1,0:T(8,128)(2,1)S(1)}, bf16[32,640]{1,0:T(8,128)(2,1)S(1)}, bf16[32,640]{1,0:T(8,128)(2,1)S(1)}, bf16[32,640]{1,0:T(8,128)(2,1)S(1)}) custom-call(s32[4]{0:T(128)S(1)} %pad_add_fusion.place, f32[128,512]{1,0:T(8,128)S(1)} %own_sums.1.keep, f32[128,128]{1,0:T(8,128)S(1)} %get-tuple-element.23.side, ...), custom_call_target="tpu_custom_call" | custom-call | bytes 786432 | tf_op jit(solution)/shard_map/pair/pallas_call | solution.py:309
  6.8 3.0 %collective-permute-start.1 = (bf16[32,640]{1,0:T(8,128)(2,1)S(1)}, bf16[32,640]{1,0:T(8,128)(2,1)S(1)}, u32[]{:S(2)}, u32[]{:S(2)}) collective-permute-start(bf16[32,640]{1,0:T(8,128)(2,1)S(1)} %get-tuple-element.26), channel_id=1, source_target_pairs={{0,8},{8,0},{16,24},{24,16},{1,9},{9,1},{17,25},{25,17},{2,10},{10... | collective-permute-start | bytes 122888 | tf_op jit(solution)/shard_map/ppermute | solution.py:266
  9.8 2.6 %collective-permute-start.2 = (bf16[32,640]{1,0:T(8,128)(2,1)S(1)}, bf16[32,640]{1,0:T(8,128)(2,1)S(1)}, u32[]{:S(2)}, u32[]{:S(2)}) collective-permute-start(bf16[32,640]{1,0:T(8,128)(2,1)S(1)} %get-tuple-element.27), channel_id=1, source_target_pairs={{0,16},{8,24},{16,0},{24,8},{1,17},{9,25},{17,1},{25,9},{2,18},{10... | collective-permute-start | bytes 122888 | tf_op jit(solution)/shard_map/ppermute | solution.py:266
  12.4 3.1 %collective-permute-done.2.refs_2_ = bf16[32,640]{1,0:T(8,128)(2,1)S(1)} collective-permute-done((bf16[32,640]{1,0:T(8,128)(2,1)S(1)}, bf16[32,640]{1,0:T(8,128)(2,1)S(1)}, u32[]{:S(2)}, u32[]{:S(2)}) %collective-permute-start.2) | collective-permute-done | bytes 40992 | tf_op jit(solution)/shard_map/ppermute | solution.py:266
  15.5 2.7 %collective-permute-done.3.refs_3_ = bf16[32,640]{1,0:T(8,128)(2,1)S(1)} collective-permute-done((bf16[32,640]{1,0:T(8,128)(2,1)S(1)}, bf16[32,640]{1,0:T(8,128)(2,1)S(1)}, u32[]{:S(2)}, u32[]{:S(2)}) %collective-permute-start.3) | collective-permute-done | bytes 40992 | tf_op jit(solution)/shard_map/ppermute | solution.py:266
  18.2 0.8 %merge.1 = (bf16[16,640]{1,0:T(8,128)(2,1)S(1)}, bf16[16,640]{1,0:T(8,128)(2,1)S(1)}) custom-call(s32[4]{0:T(128)S(1)} %pad_add_fusion.place, bf16[32,640]{1,0:T(8,128)(2,1)S(1)} %get-tuple-element.25.refs_0_, bf16[32,640]{1,0:T(8,128)(2,1)S(1)} %collective-permute-done.1.refs_1_, bf16[32,640]{1,0:T(8,128)(2,1)S(1)} %collective-permute-done.2.refs_2_, ...), custom_call_target="tpu_custom_call" | custom-call | tf_op jit(solution)/shard_map/merge/pallas_call | solution.py:319
  19.0 2.5 %collective-permute-start.6 = (bf16[16,640]{1,0:T(8,128)(2,1)S(1)}, bf16[16,640]{1,0:T(8,128)(2,1)S(1)}, u32[]{:S(2)}, u32[]{:S(2)}) collective-permute-start(bf16[16,640]{1,0:T(8,128)(2,1)S(1)} %get-tuple-element.30), channel_id=1, source_target_pairs={{0,6},{2,4},{4,2},{6,0},{1,7},{3,5},{5,3},{7,1},{8,14},{10,12},{12... | collective-permute-start | bytes 61448 | tf_op jit(solution)/shard_map/ppermute | solution.py:266
  21.5 0.5 %collective-permute-start.5 = (bf16[16,640]{1,0:T(8,128)(2,1)S(1)}, bf16[16,640]{1,0:T(8,128)(2,1)S(1)}, u32[]{:S(2)}, u32[]{:S(2)}) collective-permute-start(bf16[16,640]{1,0:T(8,128)(2,1)S(1)} %get-tuple-element.30), channel_id=1, source_target_pairs={{0,4},{2,6},{4,0},{6,2},{1,5},{3,7},{5,1},{7,3},{8,12},{10,14},{12... | collective-permute-start | bytes 61448 | tf_op jit(solution)/shard_map/ppermute | solution.py:266
  22.0 0.5 %collective-permute-start.4 = (bf16[16,640]{1,0:T(8,128)(2,1)S(1)}, bf16[16,640]{1,0:T(8,128)(2,1)S(1)}, u32[]{:S(2)}, u32[]{:S(2)}) collective-permute-start(bf16[16,640]{1,0:T(8,128)(2,1)S(1)} %get-tuple-element.29.after.refs_0_), channel_id=1, source_target_pairs={{0,2},{2,0},{4,6},{6,4},{1,3},{3,1},{5,7},{7,5},{8,10},{10,8},{12,... | collective-permute-start | bytes 61448 | tf_op jit(solution)/shard_map/ppermute | solution.py:266
  22.5 1.3 %combine.1 = bf16[2048,128]{1,0:T(8,128)(2,1)S(1)} custom-call(s32[4]{0:T(128)S(1)} %pad_add_fusion.place, f32[2048,128]{1,0:T(8,128)S(1)} %get-tuple-element.20.logits, bf16[16,640]{1,0:T(8,128)(2,1)S(1)} %get-tuple-element.29.after.refs_0_), custom_call_target="tpu_custom_call" | custom-call | flops 2097152 | bytes 1572864 | tf_op jit(solution)/shard_map/combine/pallas_call | solution.py:330
  23.9 1.4 %collective-permute-done.5.refs_2_ = bf16[16,640]{1,0:T(8,128)(2,1)S(1)} collective-permute-done((bf16[16,640]{1,0:T(8,128)(2,1)S(1)}, bf16[16,640]{1,0:T(8,128)(2,1)S(1)}, u32[]{:S(2)}, u32[]{:S(2)}) %collective-permute-start.5) | collective-permute-done | bytes 20512 | tf_op jit(solution)/shard_map/ppermute | solution.py:266
  25.3 0.5 %collective-permute-done.4.refs_1_ = bf16[16,640]{1,0:T(8,128)(2,1)S(1)} collective-permute-done((bf16[16,640]{1,0:T(8,128)(2,1)S(1)}, bf16[16,640]{1,0:T(8,128)(2,1)S(1)}, u32[]{:S(2)}, u32[]{:S(2)}) %collective-permute-start.4) | collective-permute-done | bytes 20512 | tf_op jit(solution)/shard_map/ppermute | solution.py:266
  25.8 0.2 finish.1.slot_in
  26.1 1.2 %first_product.1.first = f32[4,16,1024]{2,1,0:T(8,128)S(1)} custom-call(s32[4]{0:T(128)S(1)} %pad_add_fusion.place, bf16[16,512]{1,0:T(8,128)(2,1)S(1)} %finish.1.slot_in, bf16[4,1024,1024]{2,1,0:T(8,128)(2,1)S(1)} %bitcast.5), custom_call_target="tpu_custom_call" | custom-call | flops 67108864 | bytes 4194304 | tf_op jit(solution)/shard_map/first_product/pallas_call | solution.py:349
  27.4 1.8 %experts.1 = (bf16[4,16,1024]{2,1,0:T(8,128)(2,1)S(1)}, bf16[16,512]{1,0:T(8,128)(2,1)S(1)}) custom-call(s32[4]{0:T(128)S(1)} %pad_add_fusion.place, bf16[16,512]{1,0:T(8,128)(2,1)S(1)} %collective-permute-done.7.slot_in, f32[4,16,1024]{2,1,0:T(8,128)S(1)} %first_product.1.first, bf16[4,1024,1024]{2,1,0:T(8,128)(2,1)S(1)} %bitcast.5, ...), custom_call_target="tpu_custom_call" | custom-call | tf_op jit(solution)/shard_map/experts/pallas_call | solution.py:358
  29.1 0.5 collective-permute-start.8
  29.6 1.2 %own.1 = f32[16,512]{1,0:T(8,128)S(1)} custom-call(s32[4]{0:T(128)S(1)} %pad_add_fusion.place, bf16[4,16,1024]{2,1,0:T(8,128)(2,1)S(1)} %get-tuple-element.31.hidden, bf16[4,1024,1024]{2,1,0:T(8,128)(2,1)S(1)} %bitcast.7, bf16[16,512]{1,0:T(8,128)(2,1)S(1)} %get-tuple-element.32.after), custom_call_target="tpu_custom_call" | custom-call | flops 67108864 | bytes 4194304 | tf_op jit(solution)/shard_map/own/pallas_call | solution.py:370
  30.8 0.6 %collective-permute-start.9 = (bf16[16,512]{1,0:T(8,128)(2,1)S(1)}, bf16[16,512]{1,0:T(8,128)(2,1)S(1)}, u32[]{:S(2)}, u32[]{:S(2)}) collective-permute-start(bf16[16,512]{1,0:T(8,128)(2,1)S(1)} %add_convert_fusion.2), channel_id=1, source_target_pairs={{0,2},{2,0},{4,6},{6,4},{1,3},{3,1},{5,7},{7,5},{8,10},{10,8},{12,... | collective-permute-start | bytes 49160 | tf_op jit(solution)/shard_map/ppermute | solution.py:266
  31.4 2.4 %collective-permute-start.11 = (bf16[16,512]{1,0:T(8,128)(2,1)S(1)}, bf16[16,512]{1,0:T(8,128)(2,1)S(1)}, u32[]{:S(2)}, u32[]{:S(2)}) collective-permute-start(bf16[16,512]{1,0:T(8,128)(2,1)S(1)} %add_convert_fusion.2), channel_id=1, source_target_pairs={{0,6},{2,4},{4,2},{6,0},{1,7},{3,5},{5,3},{7,1},{8,14},{10,12},{12... | collective-permute-start | bytes 49160 | tf_op jit(solution)/shard_map/ppermute | solution.py:266
  33.9 0.5 %collective-permute-start.10 = (bf16[16,512]{1,0:T(8,128)(2,1)S(1)}, bf16[16,512]{1,0:T(8,128)(2,1)S(1)}, u32[]{:S(2)}, u32[]{:S(2)}) collective-permute-start(bf16[16,512]{1,0:T(8,128)(2,1)S(1)} %add_convert_fusion.2), channel_id=1, source_target_pairs={{0,4},{2,6},{4,0},{6,2},{1,5},{3,7},{5,1},{7,3},{8,12},{10,14},{12... | collective-permute-start | bytes 49160 | tf_op jit(solution)/shard_map/ppermute | solution.py:266
  34.4 0.2 collective-permute-done.9
  34.7 1.6 %collective-permute-done.11 = bf16[16,512]{1,0:T(8,128)(2,1)S(1)} collective-permute-done((bf16[16,512]{1,0:T(8,128)(2,1)S(1)}, bf16[16,512]{1,0:T(8,128)(2,1)S(1)}, u32[]{:S(2)}, u32[]{:S(2)}) %collective-permute-start.11) | collective-permute-done | bytes 16416 | tf_op jit(solution)/shard_map/ppermute | solution.py:266
  36.2 1.4 %collective-permute-done.10 = bf16[16,512]{1,0:T(8,128)(2,1)S(1)} collective-permute-done((bf16[16,512]{1,0:T(8,128)(2,1)S(1)}, bf16[16,512]{1,0:T(8,128)(2,1)S(1)}, u32[]{:S(2)}, u32[]{:S(2)}) %collective-permute-start.10) | collective-permute-done | bytes 16416 | tf_op jit(solution)/shard_map/ppermute | solution.py:266
  37.7 1.7 %collective-permute-start.14 = (bf16[32,512]{1,0:T(8,128)(2,1)S(1)}, bf16[32,512]{1,0:T(8,128)(2,1)S(1)}, u32[]{:S(2)}, u32[]{:S(2)}) collective-permute-start(bf16[32,512]{1,0:T(8,128)(2,1)S(1)} %pad_maximum_fusion), channel_id=1, source_target_pairs={{0,24},{8,16},{16,8},{24,0},{1,25},{9,17},{17,9},{25,1},{2,26},{10... | collective-permute-start | bytes 98312 | tf_op jit(solution)/shard_map/ppermute | solution.py:266
  39.4 1.8 %collective-permute-start.13 = (bf16[32,512]{1,0:T(8,128)(2,1)S(1)}, bf16[32,512]{1,0:T(8,128)(2,1)S(1)}, u32[]{:S(2)}, u32[]{:S(2)}) collective-permute-start(bf16[32,512]{1,0:T(8,128)(2,1)S(1)} %pad_maximum_fusion), channel_id=1, source_target_pairs={{0,16},{8,24},{16,0},{24,8},{1,17},{9,25},{17,1},{25,9},{2,18},{10... | collective-permute-start | bytes 98312 | tf_op jit(solution)/shard_map/ppermute | solution.py:266
  41.2 0.8 %collective-permute-done.12 = bf16[32,512]{1,0:T(8,128)(2,1)S(1)} collective-permute-done((bf16[32,512]{1,0:T(8,128)(2,1)S(1)}, bf16[32,512]{1,0:T(8,128)(2,1)S(1)}, u32[]{:S(2)}, u32[]{:S(2)}) %collective-permute-start.12) | collective-permute-done | bytes 32800 | tf_op jit(solution)/shard_map/ppermute | solution.py:266
  42.0 2.3 %collective-permute-done.13 = bf16[32,512]{1,0:T(8,128)(2,1)S(1)} collective-permute-done((bf16[32,512]{1,0:T(8,128)(2,1)S(1)}, bf16[32,512]{1,0:T(8,128)(2,1)S(1)}, u32[]{:S(2)}, u32[]{:S(2)}) %collective-permute-start.13) | collective-permute-done | bytes 32800 | tf_op jit(solution)/shard_map/ppermute | solution.py:266
  44.4 1.7 %mix.1 = (bf16[2048,1024]{1,0:T(8,128)(2,1)}, bf16[1024,512]{1,0:T(8,128)(2,1)S(1)}) custom-call(s32[4]{0:T(128)S(1)} %pad_add_fusion.place, bf16[2048,128]{1,0:T(8,128)(2,1)S(1)} %combine.1, bf16[128,512]{1,0:T(8,128)(2,1)S(1)} %constant_dynamic-update-slice_fusion.slot_out), custom_call_target="tpu_custom_call" | custom-call | flops 268435456 | bytes 2621440 | tf_op jit(solution)/shard_map/mix/pallas_call | solution.py:390
  46.2 2.3 %mix_other.1 = bf16[2048,1024]{1,0:T(8,128)(2,1)} custom-call(s32[4]{0:T(128)S(1)} %pad_add_fusion.place, bf16[2048,128]{1,0:T(8,128)(2,1)S(1)} %combine.1, bf16[128,512]{1,0:T(8,128)(2,1)S(1)} %collective-permute-done.15.slot_out, bf16[1024,512]{1,0:T(8,128)(2,1)S(1)} %get-tuple-element.33.rest, ...), custom_call_target="tpu_custom_call", output_to_operand_aliasing={{}: (4, {})} | custom-call | flops 268435456 | bytes 2621440 | tf_op jit(solution)/shard_map/mix_other/pallas_call | solution.py:403
  (29 shorter events, 0.4 us)
Async XLA Ops:
  4.3 1.5 %collective-permute-start = (bf16[128,640]{1,0:T(8,128)(2,1)S(1)}, bf16[128,640]{1,0:T(8,128)(2,1)S(1)}, u32[]{:S(2)}, u32[]{:S(2)}) collective-permute-start(bf16[128,640]{1,0:T(8,128)(2,1)S(1)} %get-tuple-element.24.after), channel_id=1, source_target_pairs={{0,1},{1,0},{2,3},{3,2},{4,5},{5,4},{6,7},{7,6},{8,9},{9,8},{10,11... | collective-permute-start | bytes 491528 | tf_op jit(solution)/shard_map/ppermute | solution.py:266
  4.8 21.3 %slice-start = ((s8[8388608]{0:T(1024)(128)(4,1)}), s8[4194304]{0:T(1024)(128)(4,1)S(1)}, s32[]{:S(2)}) async-start(s8[8388608]{0:T(1024)(128)(4,1)} %bitcast.4), calls=%async_computation | async-start | bytes 8388608
  4.8 22.5 %slice-start.2 = ((s8[8388608]{0:T(1024)(128)(4,1)}), s8[4194304]{0:T(1024)(128)(4,1)S(1)}, s32[]{:S(2)}) async-start(s8[8388608]{0:T(1024)(128)(4,1)} %bitcast.6), calls=%async_computation.2 | async-start | bytes 8388608
  5.8 20.3 %slice-start.1 = ((s8[8388608]{0:T(1024)(128)(4,1)}), s8[4194304]{0:T(1024)(128)(4,1)S(1)}, s32[]{:S(2)}) async-start(s8[8388608]{0:T(1024)(128)(4,1)} %bitcast.4), calls=%async_computation.1 | async-start | bytes 8388608
  5.8 21.5 %slice-start.3 = ((s8[8388608]{0:T(1024)(128)(4,1)}), s8[4194304]{0:T(1024)(128)(4,1)S(1)}, s32[]{:S(2)}) async-start(s8[8388608]{0:T(1024)(128)(4,1)} %bitcast.6), calls=%async_computation.3 | async-start | bytes 8388608
  6.8 5.6 %collective-permute-start.1 = (bf16[32,640]{1,0:T(8,128)(2,1)S(1)}, bf16[32,640]{1,0:T(8,128)(2,1)S(1)}, u32[]{:S(2)}, u32[]{:S(2)}) collective-permute-start(bf16[32,640]{1,0:T(8,128)(2,1)S(1)} %get-tuple-element.26), channel_id=1, source_target_pairs={{0,8},{8,0},{16,24},{24,16},{1,9},{9,1},{17,25},{25,17},{2,10},{10... | collective-permute-start | bytes 122888 | tf_op jit(solution)/shard_map/ppermute | solution.py:266
  9.8 5.7 %collective-permute-start.2 = (bf16[32,640]{1,0:T(8,128)(2,1)S(1)}, bf16[32,640]{1,0:T(8,128)(2,1)S(1)}, u32[]{:S(2)}, u32[]{:S(2)}) collective-permute-start(bf16[32,640]{1,0:T(8,128)(2,1)S(1)} %get-tuple-element.27), channel_id=1, source_target_pairs={{0,16},{8,24},{16,0},{24,8},{1,17},{9,25},{17,1},{25,9},{2,18},{10... | collective-permute-start | bytes 122888 | tf_op jit(solution)/shard_map/ppermute | solution.py:266
  12.4 5.8 %collective-permute-start.3 = (bf16[32,640]{1,0:T(8,128)(2,1)S(1)}, bf16[32,640]{1,0:T(8,128)(2,1)S(1)}, u32[]{:S(2)}, u32[]{:S(2)}) collective-permute-start(bf16[32,640]{1,0:T(8,128)(2,1)S(1)} %get-tuple-element.28), channel_id=1, source_target_pairs={{0,24},{8,16},{16,8},{24,0},{1,25},{9,17},{17,9},{25,1},{2,26},{10... | collective-permute-start | bytes 122888 | tf_op jit(solution)/shard_map/ppermute | solution.py:266
  19.0 4.9 %collective-permute-start.6 = (bf16[16,640]{1,0:T(8,128)(2,1)S(1)}, bf16[16,640]{1,0:T(8,128)(2,1)S(1)}, u32[]{:S(2)}, u32[]{:S(2)}) collective-permute-start(bf16[16,640]{1,0:T(8,128)(2,1)S(1)} %get-tuple-element.30), channel_id=1, source_target_pairs={{0,6},{2,4},{4,2},{6,0},{1,7},{3,5},{5,3},{7,1},{8,14},{10,12},{12... | collective-permute-start | bytes 61448 | tf_op jit(solution)/shard_map/ppermute | solution.py:266
  21.5 3.8 %collective-permute-start.5 = (bf16[16,640]{1,0:T(8,128)(2,1)S(1)}, bf16[16,640]{1,0:T(8,128)(2,1)S(1)}, u32[]{:S(2)}, u32[]{:S(2)}) collective-permute-start(bf16[16,640]{1,0:T(8,128)(2,1)S(1)} %get-tuple-element.30), channel_id=1, source_target_pairs={{0,4},{2,6},{4,0},{6,2},{1,5},{3,7},{5,1},{7,3},{8,12},{10,14},{12... | collective-permute-start | bytes 61448 | tf_op jit(solution)/shard_map/ppermute | solution.py:266
  22.0 3.8 %collective-permute-start.4 = (bf16[16,640]{1,0:T(8,128)(2,1)S(1)}, bf16[16,640]{1,0:T(8,128)(2,1)S(1)}, u32[]{:S(2)}, u32[]{:S(2)}) collective-permute-start(bf16[16,640]{1,0:T(8,128)(2,1)S(1)} %get-tuple-element.29.after.refs_0_), channel_id=1, source_target_pairs={{0,2},{2,0},{4,6},{6,4},{1,3},{3,1},{5,7},{7,5},{8,10},{10,8},{12,... | collective-permute-start | bytes 61448 | tf_op jit(solution)/shard_map/ppermute | solution.py:266
  26.1 1.3 %collective-permute-start.7 = (bf16[16,512]{1,0:T(8,128)(2,1)S(1)}, bf16[16,512]{1,0:T(8,128)(2,1)S(1)}, u32[]{:S(2)}, u32[]{:S(2)}) collective-permute-start(bf16[16,512]{1,0:T(8,128)(2,1)S(1)} %finish.1.slot_in), channel_id=1, source_target_pairs={{0,1},{1,0},{2,3},{3,2},{4,5},{5,4},{6,7},{7,6},{8,9},{9,8},{10,11... | collective-permute-start | bytes 49160 | tf_op jit(solution)/shard_map/ppermute | solution.py:266
  29.1 1.7 %collective-permute-start.8 = (bf16[16,512]{1,0:T(8,128)(2,1)S(1)}, bf16[16,512]{1,0:T(8,128)(2,1)S(1)}, u32[]{:S(2)}, u32[]{:S(2)}) collective-permute-start(bf16[16,512]{1,0:T(8,128)(2,1)S(1)} %get-tuple-element.32.after), channel_id=1, source_target_pairs={{0,1},{1,0},{2,3},{3,2},{4,5},{5,4},{6,7},{7,6},{8,9},{9,8},{10,11... | collective-permute-start | bytes 49160 | tf_op jit(solution)/shard_map/ppermute | solution.py:266
  30.8 3.8 %collective-permute-start.9 = (bf16[16,512]{1,0:T(8,128)(2,1)S(1)}, bf16[16,512]{1,0:T(8,128)(2,1)S(1)}, u32[]{:S(2)}, u32[]{:S(2)}) collective-permute-start(bf16[16,512]{1,0:T(8,128)(2,1)S(1)} %add_convert_fusion.2), channel_id=1, source_target_pairs={{0,2},{2,0},{4,6},{6,4},{1,3},{3,1},{5,7},{7,5},{8,10},{10,8},{12,... | collective-permute-start | bytes 49160 | tf_op jit(solution)/shard_map/ppermute | solution.py:266
  31.4 4.8 %collective-permute-start.11 = (bf16[16,512]{1,0:T(8,128)(2,1)S(1)}, bf16[16,512]{1,0:T(8,128)(2,1)S(1)}, u32[]{:S(2)}, u32[]{:S(2)}) collective-permute-start(bf16[16,512]{1,0:T(8,128)(2,1)S(1)} %add_convert_fusion.2), channel_id=1, source_target_pairs={{0,6},{2,4},{4,2},{6,0},{1,7},{3,5},{5,3},{7,1},{8,14},{10,12},{12... | collective-permute-start | bytes 49160 | tf_op jit(solution)/shard_map/ppermute | solution.py:266
  33.9 3.7 %collective-permute-start.10 = (bf16[16,512]{1,0:T(8,128)(2,1)S(1)}, bf16[16,512]{1,0:T(8,128)(2,1)S(1)}, u32[]{:S(2)}, u32[]{:S(2)}) collective-permute-start(bf16[16,512]{1,0:T(8,128)(2,1)S(1)} %add_convert_fusion.2), channel_id=1, source_target_pairs={{0,4},{2,6},{4,0},{6,2},{1,5},{3,7},{5,1},{7,3},{8,12},{10,14},{12... | collective-permute-start | bytes 49160 | tf_op jit(solution)/shard_map/ppermute | solution.py:266
  37.6 4.4 %collective-permute-start.12 = (bf16[32,512]{1,0:T(8,128)(2,1)S(1)}, bf16[32,512]{1,0:T(8,128)(2,1)S(1)}, u32[]{:S(2)}, u32[]{:S(2)}) collective-permute-start(bf16[32,512]{1,0:T(8,128)(2,1)S(1)} %pad_maximum_fusion), channel_id=1, source_target_pairs={{0,8},{8,0},{16,24},{24,16},{1,9},{9,1},{17,25},{25,17},{2,10},{10... | collective-permute-start | bytes 98312 | tf_op jit(solution)/shard_map/ppermute | solution.py:266
  37.7 6.6 %collective-permute-start.14 = (bf16[32,512]{1,0:T(8,128)(2,1)S(1)}, bf16[32,512]{1,0:T(8,128)(2,1)S(1)}, u32[]{:S(2)}, u32[]{:S(2)}) collective-permute-start(bf16[32,512]{1,0:T(8,128)(2,1)S(1)} %pad_maximum_fusion), channel_id=1, source_target_pairs={{0,24},{8,16},{16,8},{24,0},{1,25},{9,17},{17,9},{25,1},{2,26},{10... | collective-permute-start | bytes 98312 | tf_op jit(solution)/shard_map/ppermute | solution.py:266
  39.4 4.9 %collective-permute-start.13 = (bf16[32,512]{1,0:T(8,128)(2,1)S(1)}, bf16[32,512]{1,0:T(8,128)(2,1)S(1)}, u32[]{:S(2)}, u32[]{:S(2)}) collective-permute-start(bf16[32,512]{1,0:T(8,128)(2,1)S(1)} %pad_maximum_fusion), channel_id=1, source_target_pairs={{0,16},{8,24},{16,0},{24,8},{1,17},{9,25},{17,1},{25,9},{2,18},{10... | collective-permute-start | bytes 98312 | tf_op jit(solution)/shard_map/ppermute | solution.py:266
  44.3 1.8 %collective-permute-start.15 = (bf16[128,512]{1,0:T(8,128)(2,1)S(1)}, bf16[128,512]{1,0:T(8,128)(2,1)S(1)}, u32[]{:S(2)}, u32[]{:S(2)}) collective-permute-start(bf16[128,512]{1,0:T(8,128)(2,1)S(1)} %constant_dynamic-update-slice_fusion.slot_out), channel_id=1, source_target_pairs={{0,1},{1,0},{2,3},{3,2},{4,5},{5,4},{6,7},{7,6},{8,9},{9,8},{10,11... | collective-permute-start | bytes 393224 | tf_op jit(solution)/shard_map/ppermute | solution.py:266

commit v19 on v18

--- a/solution.py
+++ b/solution.py
@@ -131,11 +131,11 @@
     keep[...] = early * side[:, 2:3] + late * side[:, 3:4]
 
 
-def pair_kernel(place, keep, side, received, *sends):
+def pair_kernel(far_at, keep, side, received, *sends):
     width = keep.shape[1]
     for r, send in enumerate(sends):
         rows = send.shape[0]
-        span = pl.ds(pl.multiple_of((place[1] ^ r) * rows, rows), rows)
+        span = pl.ds(pl.multiple_of((far_at[0] ^ r) * rows, rows), rows)
         peak_mine, total_mine = side[span, 0:1], side[span, 1:2]
         peak_other, total_other = read_message(received[span, width:])
         peak = jnp.maximum(peak_mine, peak_other)
@@ -160,10 +160,10 @@
     return sums, peak, total
 
 
-def merge_kernel(place, *refs):
+def merge_kernel(near_at, *refs):
     for n, send in enumerate(refs[-2:]):
         rows, width = send.shape[0], send.shape[1] - SIDE
-        span = pl.ds(pl.multiple_of((place[2] ^ n) * rows, rows), rows)
+        span = pl.ds(pl.multiple_of((near_at[0] ^ n) * rows, rows), rows)
         sums, peak, total = add_parts([ref[span, :] for ref in refs[:-2]], width)
         send[:, :width] = sums.astype(BF16)
         send[:, width:] = side_message(peak, total)
@@ -204,15 +204,10 @@
     keep[...] = second_product(values, expert_out, column_half(place[0], keep.shape[1]))
 
 
-def combine_kernel(place, logits, after, combine):
+def combine_kernel(logits, after, combine):
     value = logits[...]
-    slots = value.shape[1]
     weights = jnp.exp(value - jnp.max(value, axis=1, keepdims=True))
-    weights = (weights / jnp.sum(weights, axis=1, keepdims=True)).astype(BF16)
-    row = lax.broadcasted_iota(jnp.int32, (slots, slots), 0)
-    column = lax.broadcasted_iota(jnp.int32, (slots, slots), 1)
-    swap = jnp.where(row == (column ^ place[3]), 1.0, 0.0).astype(BF16)
-    combine[...] = dot(weights, swap).astype(BF16)
+    combine[...] = (weights / jnp.sum(weights, axis=1, keepdims=True)).astype(BF16)
 
 
 def mix_kernel(place, combine, slot_out, mixed, rest, held, sems):
@@ -276,9 +271,9 @@
     far, near, rest = [lax.axis_size(axis) for axis in ("far", "near", "rest")]
     rows = slots // (far * near)
     half = model // 2
-    far_at, near_at = lax.axis_index("far"), lax.axis_index("near")
-    place = [lax.axis_index("pair"), far_at, near_at, (far_at * near + near_at) * rows]
-    place = jnp.stack(place).astype(jnp.int32)
+    place, far_at, near_at = [
+        lax.axis_index(axis).astype(jnp.int32).reshape(1) for axis in ("pair", "far", "near")
+    ]
     any_space = pl.BlockSpec(memory_space=pl.ANY)
 
     logits, turned, held, side, send = pl.pallas_call(
@@ -314,7 +309,7 @@
         cost_estimate=cost(0, 6 * slots * model, 128 * slots * model),
         compiler_params=params(16),
         name="pair",
-    )(place, keep, side, received)
+    )(far_at, keep, side, received)
     parts = [sends[0]] + [move(sends[r], ("far",), (r,)) for r in range(1, far)]
     send, their = pl.pallas_call(
         merge_kernel,
@@ -323,19 +318,19 @@
         out_specs=(VMEM, VMEM),
         compiler_params=params(16),
         name="merge",
-    )(place, *parts)
+    )(near_at, *parts)
     plane = ("near", "rest")
     mine = [send] + [move(send, plane, (0, r)) for r in range(1, rest)]
     mine += [move(their, plane, (1, r)) for r in range(rest)]
     combine = pl.pallas_call(
         combine_kernel,
         out_shape=jax.ShapeDtypeStruct((count, slots), BF16),
-        in_specs=[SMEM, VMEM, any_space],
+        in_specs=[VMEM, any_space],
         out_specs=VMEM,
         cost_estimate=cost(8 * count * slots, 6 * count * slots, count * slots),
         compiler_params=params(16),
         name="combine",
-    )(place, logits, send)
+    )(logits, send)
     experts, units = expert_out.shape[:2]
     slot_in = pl.pallas_call(
         finish_kernel,
@@ -377,14 +372,11 @@
         name="own",
     )(place, hidden, expert_out, send)
     partial = (keep + received.astype(F32)).astype(BF16)
-    own = partial.astype(F32)
-    for r in range(1, rest):
-        own = own + move(partial, plane, (0, r)).astype(F32)
-    their = jnp.zeros_like(own)
-    for r in range(rest):
-        their = their + move(partial, plane, (1, r)).astype(F32)
-    block = jnp.concatenate([own, their], axis=0).astype(BF16)
-    slot_out = jnp.concatenate([block] + [move(block, ("far",), (r,)) for r in range(1, far)], axis=0)
+    groups = far * near
+    partials = jnp.broadcast_to(partial, (groups * rest, rows, half))
+    partials = lax.all_to_all(partials, ("rest", "far", "near"), split_axis=0, concat_axis=0, tiled=True)
+    slot_out = jnp.sum(partials.reshape(rest, groups, rows, half).astype(F32), axis=0)
+    slot_out = slot_out.astype(BF16).reshape(slots, half)
     other = swap_pair(slot_out)
     done, blocks = count // 2, 8
     mixed, left = pl.pallas_call(

time: 48.6 us -> 57.9 us (1.19)
  local copies, waits for them, and re-layouts: 0.04 us -> 14.4 us
  blocking collectives: 0 us -> 13.4 us
  starting transfers between devices: 17.3 us -> 9.86 us
  Pallas kernels: 16.7 us -> 11.1 us
  waiting for transfers between devices: 14.1 us -> 8.75 us
    unnamed x10, local copies, waits for them, and re-layouts: 0.04 us -> 14.3 us
    all_to_all x0 -> x1, blocking collectives: none -> 13.4 us  [shards(): lax.all_to_all(partials, ('rest', 'far', 'near'), split_axis=0, concat_ax...]
    ppermute x16 -> x10, starting transfers between devices: 17.3 us -> 9.86 us  [move(): return lax.ppermute(value, axes, moves)]
    ppermute x16 -> x10, waiting for transfers between devices: 14.1 us -> 8.75 us  [move(): return lax.ppermute(value, axes, moves)]
    pallas_call x1, Pallas kernels: 1.3 us -> 0.62 us  [shards(): pl.pallas_call(combine_kernel, out_shape=jax.ShapeDtypeStruct((count, slo...]
  transfers between devices with their start and end apart: 16 -> 10, of which waited for: 9 -> 7; matrix products, arithmetic and copies ran while one was open for 0% -> 0% of each run, Pallas kernels for 13% -> 6%
where the time goes in v19:
time: 57.9 us; the launch traced here: 57.6 us
  local copies, waits for them, and re-layouts  14.4 us (25%)
  blocking collectives  13.4 us (23%)
  Pallas kernels  11.1 us (19%)
  starting transfers between devices  9.86 us (17%)
  waiting for transfers between devices  8.75 us (15%)
    unnamed x10, local copies, waits for them, and re-layouts  14.3 us
    all_to_all x1, blocking collectives, shards(): lax.all_to_all(partials, ('rest', 'far', 'near'), split_axis=0, concat_ax...  13.4 us
    ppermute x10, starting transfers between devices, move(): return lax.ppermute(value, axes, moves)  9.86 us
    ppermute x10, waiting for transfers between devices, move(): return lax.ppermute(value, axes, moves)  8.75 us
    pallas_call x1, Pallas kernels, shards(): pl.pallas_call(gather_kernel, out_shape=(jax.ShapeDtypeStruct((count, slo...  3.66 us
    pallas_call x1, Pallas kernels, shards(): pl.pallas_call(mix_other_kernel, out_shape=jax.ShapeDtypeStruct((count, m...  1.74 us
    pallas_call x1, Pallas kernels, shards(): pl.pallas_call(mix_kernel, out_shape=(pltpu.HBM((count, model), BF16), ja...  1.21 us
    pallas_call x1, Pallas kernels, shards(): pl.pallas_call(expert_kernel, out_shape=(jax.ShapeDtypeStruct((experts, r...  1.2 us
  transfers between devices with their start and end apart: 10, of which 7 were waited for; matrix products, arithmetic and copies ran while one was open for 0% of the time, Pallas kernels for 6%

profile of v19, /device:TPU:0, one launch (start us, length us, event | category | flops | bytes accessed | tf_op | source)
XLA Modules:
  0.0 57.6 jit_solution(5218813799606511860)
XLA Ops:
  0.0 3.7 %gather.1 = (f32[2048,128]{1,0:T(8,128)S(1)}, bf16[128,2048]{1,0:T(8,128)(2,1)S(1)}, bf16[2048,1024]{1,0:T(8,128)(2,1)S(1)}, f32[128,128]{1,0:T(8,128)S(1)}, bf16[128,640]{1,0:T(8,128)(2,1)S(1)}) custom-call(s32[1]{0:T(128)} %bitcast.place, bf16[2048,1024]{1,0:T(8,128)(2,1)} %tokens.1, bf16[1024,128]{1,0:T(8,128)(2,1)} %slot_params.1), custom_call_target="tpu_custom_call" | custom-call | tf_op jit(solution)/shard_map/gather/pallas_call | solution.py:279
  3.7 2.0 %copy-done.3 = bf16[2048,1024]{1,0:T(8,128)(2,1)} copy-done((bf16[2048,1024]{1,0:T(8,128)(2,1)}, bf16[2048,1024]{1,0:T(8,128)(2,1)S(1)}, u32[]{:S(2)}) %copy-start.3) | copy-done | bytes 4194328
  5.7 0.4 collective-permute-start
  6.1 2.2 %copy-done.4 = bf16[2048,1024]{1,0:T(8,128)(2,1)S(1)} copy-done((bf16[2048,1024]{1,0:T(8,128)(2,1)S(1)}, bf16[2048,1024]{1,0:T(8,128)(2,1)}, u32[]{:S(2)}) %copy-start.4) | copy-done | bytes 4194328
  8.3 0.5 own_sums.1.keep
  8.8 0.4 pair.1
  9.2 2.7 %collective-permute-start.1 = (bf16[32,640]{1,0:T(8,128)(2,1)S(1)}, bf16[32,640]{1,0:T(8,128)(2,1)S(1)}, u32[]{:S(2)}, u32[]{:S(2)}) collective-permute-start(bf16[32,640]{1,0:T(8,128)(2,1)S(1)} %get-tuple-element.26), channel_id=1, source_target_pairs={{0,8},{8,0},{16,24},{24,16},{1,9},{9,1},{17,25},{25,17},{2,10},{10... | collective-permute-start | bytes 122888 | tf_op jit(solution)/shard_map/ppermute | solution.py:261
  11.8 2.6 %collective-permute-start.2 = (bf16[32,640]{1,0:T(8,128)(2,1)S(1)}, bf16[32,640]{1,0:T(8,128)(2,1)S(1)}, u32[]{:S(2)}, u32[]{:S(2)}) collective-permute-start(bf16[32,640]{1,0:T(8,128)(2,1)S(1)} %get-tuple-element.27), channel_id=1, source_target_pairs={{0,16},{8,24},{16,0},{24,8},{1,17},{9,25},{17,1},{25,9},{2,18},{10... | collective-permute-start | bytes 122888 | tf_op jit(solution)/shard_map/ppermute | solution.py:261
  14.4 3.2 %collective-permute-done.2.refs_2_ = bf16[32,640]{1,0:T(8,128)(2,1)S(1)} collective-permute-done((bf16[32,640]{1,0:T(8,128)(2,1)S(1)}, bf16[32,640]{1,0:T(8,128)(2,1)S(1)}, u32[]{:S(2)}, u32[]{:S(2)}) %collective-permute-start.2) | collective-permute-done | bytes 40992 | tf_op jit(solution)/shard_map/ppermute | solution.py:261
  17.7 2.6 %collective-permute-done.3.refs_3_ = bf16[32,640]{1,0:T(8,128)(2,1)S(1)} collective-permute-done((bf16[32,640]{1,0:T(8,128)(2,1)S(1)}, bf16[32,640]{1,0:T(8,128)(2,1)S(1)}, u32[]{:S(2)}, u32[]{:S(2)}) %collective-permute-start.3) | collective-permute-done | bytes 40992 | tf_op jit(solution)/shard_map/ppermute | solution.py:261
  20.2 0.3 merge.1
  20.5 2.5 %collective-permute-start.6 = (bf16[16,640]{1,0:T(8,128)(2,1)S(1)}, bf16[16,640]{1,0:T(8,128)(2,1)S(1)}, u32[]{:S(2)}, u32[]{:S(2)}) collective-permute-start(bf16[16,640]{1,0:T(8,128)(2,1)S(1)} %get-tuple-element.30), channel_id=1, source_target_pairs={{0,6},{2,4},{4,2},{6,0},{1,7},{3,5},{5,3},{7,1},{8,14},{10,12},{12... | collective-permute-start | bytes 61448 | tf_op jit(solution)/shard_map/ppermute | solution.py:261
  23.0 0.5 collective-permute-start.5
  23.6 0.5 collective-permute-start.4
  24.1 0.6 %combine.1 = bf16[2048,128]{1,0:T(8,128)(2,1)S(1)} custom-call(f32[2048,128]{1,0:T(8,128)S(1)} %get-tuple-element.20.logits, bf16[16,640]{1,0:T(8,128)(2,1)S(1)} %get-tuple-element.29.after.refs_0_), custom_call_target="tpu_custom_call" | custom-call | flops 2097152 | bytes 1572864 | tf_op jit(solution)/shard_map/combine/pallas_call | solution.py:325
  24.7 0.6 collective-permute-done.6.refs_3_
  25.3 1.5 %collective-permute-done.5.refs_2_ = bf16[16,640]{1,0:T(8,128)(2,1)S(1)} collective-permute-done((bf16[16,640]{1,0:T(8,128)(2,1)S(1)}, bf16[16,640]{1,0:T(8,128)(2,1)S(1)}, u32[]{:S(2)}, u32[]{:S(2)}) %collective-permute-start.5) | collective-permute-done | bytes 20512 | tf_op jit(solution)/shard_map/ppermute | solution.py:261
  26.8 0.5 collective-permute-done.4.refs_1_
  27.3 0.2 finish.1.slot_in
  27.7 3.4 %copy-done = bf16[4,1024,1024]{2,1,0:T(8,128)(2,1)S(1)} copy-done((bf16[4,1024,1024]{2,1,0:T(8,128)(2,1)S(1)}, bf16[4,1024,1024]{2,1,0:T(8,128)(2,1)}, u32[]{:S(2)}) %copy-start) | copy-done | bytes 8388632
  31.0 0.6 %first_product.1.first = f32[4,16,1024]{2,1,0:T(8,128)S(1)} custom-call(s32[1]{0:T(128)} %bitcast.place, bf16[16,512]{1,0:T(8,128)(2,1)S(1)} %finish.1.slot_in, bf16[4,1024,1024]{2,1,0:T(8,128)(2,1)S(1)} %copy-done), custom_call_target="tpu_custom_call" | custom-call | flops 67108864 | bytes 4194304 | tf_op jit(solution)/shard_map/first_product/pallas_call | solution.py:344
  31.7 3.4 %copy-done.1 = bf16[4,1024,1024]{2,1,0:T(8,128)(2,1)S(1)} copy-done((bf16[4,1024,1024]{2,1,0:T(8,128)(2,1)S(1)}, bf16[4,1024,1024]{2,1,0:T(8,128)(2,1)}, u32[]{:S(2)}) %copy-start.1) | copy-done | bytes 8388632
  35.1 3.4 %copy-done.2 = bf16[4,1024,1024]{2,1,0:T(8,128)(2,1)S(1)} copy-done((bf16[4,1024,1024]{2,1,0:T(8,128)(2,1)S(1)}, bf16[4,1024,1024]{2,1,0:T(8,128)(2,1)}, u32[]{:S(2)}) %copy-start.2) | copy-done | bytes 8388632
  38.5 1.2 %experts.1 = (bf16[4,16,1024]{2,1,0:T(8,128)(2,1)S(1)}, bf16[16,512]{1,0:T(8,128)(2,1)S(1)}) custom-call(s32[1]{0:T(128)} %bitcast.place, bf16[16,512]{1,0:T(8,128)(2,1)S(1)} %collective-permute-done.7.slot_in, f32[4,16,1024]{2,1,0:T(8,128)S(1)} %first_product.1.first, bf16[4,1024,1024]{2,1,0:T(8,128)(2,1)S(1)} %copy-done.1, bf16[4,1024,1024]{2,1,0:T(8,128)(2,1)S(1)} %copy-done.2), custom_call_target="tpu_custom_call" | custom-call | tf_op jit(solution)/shard_map/experts/pallas_call | solution.py:353
  39.7 0.5 collective-permute-start.8
  40.2 0.7 %own.1 = f32[16,512]{1,0:T(8,128)S(1)} custom-call(s32[1]{0:T(128)} %bitcast.place, bf16[4,16,1024]{2,1,0:T(8,128)(2,1)S(1)} %get-tuple-element.31.hidden, bf16[4,1024,1024]{2,1,0:T(8,128)(2,1)S(1)} %copy-done.2, bf16[16,512]{1,0:T(8,128)(2,1)S(1)} %get-tuple-element.32.after), custom_call_target="tpu_custom_call" | custom-call | flops 67108864 | bytes 4194304 | tf_op jit(solution)/shard_map/own/pallas_call | solution.py:365
  40.8 0.2 collective-permute-done.8
  41.0 13.4 %all_to_all.5 = bf16[16,16,512]{2,1,0:T(8,128)(2,1)S(1)} all-to-all(bf16[16,16,512]{2,1,0:T(8,128)(2,1)S(1)} %broadcast_in_dim.3), channel_id=1, replica_groups=mesh['far'=4,'near'=2,'rest'=2,'pair'=2] {'rest','far','near'}, dimensions={0} | all-to-all | bytes 524288 | tf_op jit(solution)/shard_map/all_to_all | solution.py:377
  54.5 0.1 collective-permute-start.9
  54.5 1.2 %mix.1 = (bf16[2048,1024]{1,0:T(8,128)(2,1)}, bf16[1024,512]{1,0:T(8,128)(2,1)S(1)}) custom-call(s32[1]{0:T(128)} %bitcast.place, bf16[2048,128]{1,0:T(8,128)(2,1)S(1)} %combine.1, bf16[128,512]{1,0:T(8,128)(2,1)S(1)} %bitcast.6), custom_call_target="tpu_custom_call" | custom-call | flops 268435456 | bytes 2621440 | tf_op jit(solution)/shard_map/mix/pallas_call | solution.py:382
  55.8 0.1 collective-permute-done.9.slot_out
  55.9 1.7 %mix_other.1 = bf16[2048,1024]{1,0:T(8,128)(2,1)} custom-call(s32[1]{0:T(128)} %bitcast.place, bf16[2048,128]{1,0:T(8,128)(2,1)S(1)} %combine.1, bf16[128,512]{1,0:T(8,128)(2,1)S(1)} %collective-permute-done.9.slot_out, bf16[1024,512]{1,0:T(8,128)(2,1)S(1)} %get-tuple-element.33.rest, ...), custom_call_target="tpu_custom_call", output_to_operand_aliasing={{}: (4, {})} | custom-call | flops 268435456 | bytes 2621440 | tf_op jit(solution)/shard_map/mix_other/pallas_call | solution.py:395
  (13 shorter events, 0.2 us)
Async XLA Ops:
  3.7 2.0 %copy-start.3 = (bf16[2048,1024]{1,0:T(8,128)(2,1)}, bf16[2048,1024]{1,0:T(8,128)(2,1)S(1)}, u32[]{:S(2)}) copy-start(bf16[2048,1024]{1,0:T(8,128)(2,1)S(1)} %get-tuple-element.22.held) | copy-start | bytes 12582916
  5.7 3.1 %collective-permute-start = (bf16[128,640]{1,0:T(8,128)(2,1)S(1)}, bf16[128,640]{1,0:T(8,128)(2,1)S(1)}, u32[]{:S(2)}, u32[]{:S(2)}) collective-permute-start(bf16[128,640]{1,0:T(8,128)(2,1)S(1)} %get-tuple-element.24.after), channel_id=1, source_target_pairs={{0,1},{1,0},{2,3},{3,2},{4,5},{5,4},{6,7},{7,6},{8,9},{9,8},{10,11... | collective-permute-start | bytes 491528 | tf_op jit(solution)/shard_map/ppermute | solution.py:261
  6.1 2.2 %copy-start.4 = (bf16[2048,1024]{1,0:T(8,128)(2,1)S(1)}, bf16[2048,1024]{1,0:T(8,128)(2,1)}, u32[]{:S(2)}) copy-start(bf16[2048,1024]{1,0:T(8,128)(2,1)} %copy-done.3) | copy-start | bytes 12582916
  9.2 5.3 %collective-permute-start.1 = (bf16[32,640]{1,0:T(8,128)(2,1)S(1)}, bf16[32,640]{1,0:T(8,128)(2,1)S(1)}, u32[]{:S(2)}, u32[]{:S(2)}) collective-permute-start(bf16[32,640]{1,0:T(8,128)(2,1)S(1)} %get-tuple-element.26), channel_id=1, source_target_pairs={{0,8},{8,0},{16,24},{24,16},{1,9},{9,1},{17,25},{25,17},{2,10},{10... | collective-permute-start | bytes 122888 | tf_op jit(solution)/shard_map/ppermute | solution.py:261
  11.8 5.8 %collective-permute-start.2 = (bf16[32,640]{1,0:T(8,128)(2,1)S(1)}, bf16[32,640]{1,0:T(8,128)(2,1)S(1)}, u32[]{:S(2)}, u32[]{:S(2)}) collective-permute-start(bf16[32,640]{1,0:T(8,128)(2,1)S(1)} %get-tuple-element.27), channel_id=1, source_target_pairs={{0,16},{8,24},{16,0},{24,8},{1,17},{9,25},{17,1},{25,9},{2,18},{10... | collective-permute-start | bytes 122888 | tf_op jit(solution)/shard_map/ppermute | solution.py:261
  14.4 5.8 %collective-permute-start.3 = (bf16[32,640]{1,0:T(8,128)(2,1)S(1)}, bf16[32,640]{1,0:T(8,128)(2,1)S(1)}, u32[]{:S(2)}, u32[]{:S(2)}) collective-permute-start(bf16[32,640]{1,0:T(8,128)(2,1)S(1)} %get-tuple-element.28), channel_id=1, source_target_pairs={{0,24},{8,16},{16,8},{24,0},{1,25},{9,17},{17,9},{25,1},{2,26},{10... | collective-permute-start | bytes 122888 | tf_op jit(solution)/shard_map/ppermute | solution.py:261
  20.5 4.7 %collective-permute-start.6 = (bf16[16,640]{1,0:T(8,128)(2,1)S(1)}, bf16[16,640]{1,0:T(8,128)(2,1)S(1)}, u32[]{:S(2)}, u32[]{:S(2)}) collective-permute-start(bf16[16,640]{1,0:T(8,128)(2,1)S(1)} %get-tuple-element.30), channel_id=1, source_target_pairs={{0,6},{2,4},{4,2},{6,0},{1,7},{3,5},{5,3},{7,1},{8,14},{10,12},{12... | collective-permute-start | bytes 61448 | tf_op jit(solution)/shard_map/ppermute | solution.py:261
  23.0 3.8 %collective-permute-start.5 = (bf16[16,640]{1,0:T(8,128)(2,1)S(1)}, bf16[16,640]{1,0:T(8,128)(2,1)S(1)}, u32[]{:S(2)}, u32[]{:S(2)}) collective-permute-start(bf16[16,640]{1,0:T(8,128)(2,1)S(1)} %get-tuple-element.30), channel_id=1, source_target_pairs={{0,4},{2,6},{4,0},{6,2},{1,5},{3,7},{5,1},{7,3},{8,12},{10,14},{12... | collective-permute-start | bytes 61448 | tf_op jit(solution)/shard_map/ppermute | solution.py:261
  23.6 3.8 %collective-permute-start.4 = (bf16[16,640]{1,0:T(8,128)(2,1)S(1)}, bf16[16,640]{1,0:T(8,128)(2,1)S(1)}, u32[]{:S(2)}, u32[]{:S(2)}) collective-permute-start(bf16[16,640]{1,0:T(8,128)(2,1)S(1)} %get-tuple-element.29.after.refs_0_), channel_id=1, source_target_pairs={{0,2},{2,0},{4,6},{6,4},{1,3},{3,1},{5,7},{7,5},{8,10},{10,8},{12,... | collective-permute-start | bytes 61448 | tf_op jit(solution)/shard_map/ppermute | solution.py:261
  27.6 4.1 %collective-permute-start.7 = (bf16[16,512]{1,0:T(8,128)(2,1)S(1)}, bf16[16,512]{1,0:T(8,128)(2,1)S(1)}, u32[]{:S(2)}, u32[]{:S(2)}) collective-permute-start(bf16[16,512]{1,0:T(8,128)(2,1)S(1)} %finish.1.slot_in), channel_id=1, source_target_pairs={{0,1},{1,0},{2,3},{3,2},{4,5},{5,4},{6,7},{7,6},{8,9},{9,8},{10,11... | collective-permute-start | bytes 49160 | tf_op jit(solution)/shard_map/ppermute | solution.py:261
  27.6 3.4 %copy-start = (bf16[4,1024,1024]{2,1,0:T(8,128)(2,1)S(1)}, bf16[4,1024,1024]{2,1,0:T(8,128)(2,1)}, u32[]{:S(2)}) copy-start(bf16[4,1024,1024]{2,1,0:T(8,128)(2,1)} %expert_in.3) | copy-start | bytes 25165828
  31.7 3.4 %copy-start.1 = (bf16[4,1024,1024]{2,1,0:T(8,128)(2,1)S(1)}, bf16[4,1024,1024]{2,1,0:T(8,128)(2,1)}, u32[]{:S(2)}) copy-start(bf16[4,1024,1024]{2,1,0:T(8,128)(2,1)} %expert_in.3) | copy-start | bytes 25165828
  35.1 3.4 %copy-start.2 = (bf16[4,1024,1024]{2,1,0:T(8,128)(2,1)S(1)}, bf16[4,1024,1024]{2,1,0:T(8,128)(2,1)}, u32[]{:S(2)}) copy-start(bf16[4,1024,1024]{2,1,0:T(8,128)(2,1)} %expert_out.3) | copy-start | bytes 25165828
  39.7 1.3 %collective-permute-start.8 = (bf16[16,512]{1,0:T(8,128)(2,1)S(1)}, bf16[16,512]{1,0:T(8,128)(2,1)S(1)}, u32[]{:S(2)}, u32[]{:S(2)}) collective-permute-start(bf16[16,512]{1,0:T(8,128)(2,1)S(1)} %get-tuple-element.32.after), channel_id=1, source_target_pairs={{0,1},{1,0},{2,3},{3,2},{4,5},{5,4},{6,7},{7,6},{8,9},{9,8},{10,11... | collective-permute-start | bytes 49160 | tf_op jit(solution)/shard_map/ppermute | solution.py:261
  54.5 1.4 %collective-permute-start.9 = (bf16[128,512]{1,0:T(8,128)(2,1)S(1)}, bf16[128,512]{1,0:T(8,128)(2,1)S(1)}, u32[]{:S(2)}, u32[]{:S(2)}) collective-permute-start(bf16[128,512]{1,0:T(8,128)(2,1)S(1)} %bitcast.5), channel_id=1, source_target_pairs={{0,1},{1,0},{2,3},{3,2},{4,5},{5,4},{6,7},{7,6},{8,9},{9,8},{10,11... | collective-permute-start | bytes 393224 | tf_op jit(solution)/shard_map/ppermute | solution.py:261

commit v20 on v19

--- a/solution.py
+++ b/solution.py
@@ -1,3 +1,4 @@
+import functools
 import math
 
 import jax
@@ -204,10 +205,15 @@
     keep[...] = second_product(values, expert_out, column_half(place[0], keep.shape[1]))
 
 
-def combine_kernel(logits, after, combine):
+def combine_kernel(rows, far_at, near_at, logits, after, combine):
     value = logits[...]
+    slots = value.shape[1]
     weights = jnp.exp(value - jnp.max(value, axis=1, keepdims=True))
-    combine[...] = (weights / jnp.sum(weights, axis=1, keepdims=True)).astype(BF16)
+    weights = (weights / jnp.sum(weights, axis=1, keepdims=True)).astype(BF16)
+    row = lax.broadcasted_iota(jnp.int32, (slots, slots), 0)
+    column = lax.broadcasted_iota(jnp.int32, (slots, slots), 1)
+    swap = jnp.where(row == (column ^ ((far_at[0] * 2 + near_at[0]) * rows)), 1.0, 0.0).astype(BF16)
+    combine[...] = dot(weights, swap).astype(BF16)
 
 
 def mix_kernel(place, combine, slot_out, mixed, rest, held, sems):
@@ -323,14 +329,14 @@
     mine = [send] + [move(send, plane, (0, r)) for r in range(1, rest)]
     mine += [move(their, plane, (1, r)) for r in range(rest)]
     combine = pl.pallas_call(
-        combine_kernel,
+        functools.partial(combine_kernel, rows),
         out_shape=jax.ShapeDtypeStruct((count, slots), BF16),
-        in_specs=[VMEM, any_space],
+        in_specs=[SMEM, SMEM, VMEM, any_space],
         out_specs=VMEM,
         cost_estimate=cost(8 * count * slots, 6 * count * slots, count * slots),
         compiler_params=params(16),
         name="combine",
-    )(logits, send)
+    )(far_at, near_at, logits, send)
     experts, units = expert_out.shape[:2]
     slot_in = pl.pallas_call(
         finish_kernel,
@@ -372,11 +378,14 @@
         name="own",
     )(place, hidden, expert_out, send)
     partial = (keep + received.astype(F32)).astype(BF16)
-    groups = far * near
-    partials = jnp.broadcast_to(partial, (groups * rest, rows, half))
-    partials = lax.all_to_all(partials, ("rest", "far", "near"), split_axis=0, concat_axis=0, tiled=True)
-    slot_out = jnp.sum(partials.reshape(rest, groups, rows, half).astype(F32), axis=0)
-    slot_out = slot_out.astype(BF16).reshape(slots, half)
+    own = partial.astype(F32)
+    for r in range(1, rest):
+        own = own + move(partial, plane, (0, r)).astype(F32)
+    their = jnp.zeros_like(own)
+    for r in range(rest):
+        their = their + move(partial, plane, (1, r)).astype(F32)
+    block = jnp.concatenate([own, their], axis=0).astype(BF16)
+    slot_out = jnp.concatenate([block] + [move(block, ("far",), (r,)) for r in range(1, far)], axis=0)
     other = swap_pair(slot_out)
     done, blocks = count // 2, 8
     mixed, left = pl.pallas_call(

time: 57.9 us -> 57.9 us (level)
  blocking collectives: 13.4 us -> 0 us
  starting transfers between devices: 9.86 us -> 16.9 us
  waiting for transfers between devices: 8.75 us -> 15 us
    all_to_all x1 -> x0, blocking collectives: 13.4 us -> none  [shards(): lax.all_to_all(partials, ('rest', 'far', 'near'), split_axis=0, concat_ax...]
    ppermute x10 -> x16, starting transfers between devices: 9.86 us -> 16.9 us  [move(): return lax.ppermute(value, axes, moves)]
    ppermute x10 -> x16, waiting for transfers between devices: 8.75 us -> 15 us  [move(): return lax.ppermute(value, axes, moves)]
    unnamed x10 -> x12, local copies, waits for them, and re-layouts: 14.3 us -> 14.4 us
  transfers between devices with their start and end apart: 10 -> 16, of which waited for: 7 -> 12; matrix products, arithmetic and copies ran while one was open for 0% -> 0% of each run, Pallas kernels for 6% -> 6%
where the time goes in v20:
time: 57.9 us; the launch traced here: 57.7 us
  starting transfers between devices  16.9 us (29%)
  waiting for transfers between devices  15 us (26%)
  local copies, waits for them, and re-layouts  14.4 us (25%)
  Pallas kernels  11.2 us (19%)
    ppermute x16, starting transfers between devices, move(): return lax.ppermute(value, axes, moves)  16.9 us
    ppermute x16, waiting for transfers between devices, move(): return lax.ppermute(value, axes, moves)  15 us
    unnamed x12, local copies, waits for them, and re-layouts  14.4 us
    pallas_call x1, Pallas kernels, shards(): pl.pallas_call(gather_kernel, out_shape=(jax.ShapeDtypeStruct((count, slo...  3.66 us
    pallas_call x1, Pallas kernels, shards(): pl.pallas_call(mix_other_kernel, out_shape=jax.ShapeDtypeStruct((count, m...  1.74 us
    pallas_call x1, Pallas kernels, shards(): pl.pallas_call(mix_kernel, out_shape=(pltpu.HBM((count, model), BF16), ja...  1.21 us
    pallas_call x1, Pallas kernels, shards(): pl.pallas_call(expert_kernel, out_shape=(jax.ShapeDtypeStruct((experts, r...  1.2 us
  transfers between devices with their start and end apart: 16, of which 12 were waited for; matrix products, arithmetic and copies ran while one was open for 0% of the time, Pallas kernels for 6%

profile of v20, /device:TPU:0, one launch (start us, length us, event | category | flops | bytes accessed | tf_op | source)
XLA Modules:
  0.0 57.7 jit_solution(5671888763201674847)
XLA Ops:
  0.0 3.7 %gather.1 = (f32[2048,128]{1,0:T(8,128)S(1)}, bf16[128,2048]{1,0:T(8,128)(2,1)S(1)}, bf16[2048,1024]{1,0:T(8,128)(2,1)S(1)}, f32[128,128]{1,0:T(8,128)S(1)}, bf16[128,640]{1,0:T(8,128)(2,1)S(1)}) custom-call(s32[1]{0:T(128)} %bitcast.place, bf16[2048,1024]{1,0:T(8,128)(2,1)} %tokens.1, bf16[1024,128]{1,0:T(8,128)(2,1)} %slot_params.1), custom_call_target="tpu_custom_call" | custom-call | tf_op jit(solution)/shard_map/gather/pallas_call | solution.py:285
  3.7 2.0 %copy-done.3 = bf16[2048,1024]{1,0:T(8,128)(2,1)} copy-done((bf16[2048,1024]{1,0:T(8,128)(2,1)}, bf16[2048,1024]{1,0:T(8,128)(2,1)S(1)}, u32[]{:S(2)}) %copy-start.3) | copy-done | bytes 4194328
  6.1 2.2 %copy-done.4 = bf16[2048,1024]{1,0:T(8,128)(2,1)S(1)} copy-done((bf16[2048,1024]{1,0:T(8,128)(2,1)S(1)}, bf16[2048,1024]{1,0:T(8,128)(2,1)}, u32[]{:S(2)}) %copy-start.4) | copy-done | bytes 4194328
  8.3 0.5 own_sums.1.keep
  9.2 2.7 %collective-permute-start.1 = (bf16[32,640]{1,0:T(8,128)(2,1)S(1)}, bf16[32,640]{1,0:T(8,128)(2,1)S(1)}, u32[]{:S(2)}, u32[]{:S(2)}) collective-permute-start(bf16[32,640]{1,0:T(8,128)(2,1)S(1)} %get-tuple-element.26), channel_id=1, source_target_pairs={{0,8},{8,0},{16,24},{24,16},{1,9},{9,1},{17,25},{25,17},{2,10},{10... | collective-permute-start | bytes 122888 | tf_op jit(solution)/shard_map/ppermute | solution.py:267
  11.8 2.6 %collective-permute-start.2 = (bf16[32,640]{1,0:T(8,128)(2,1)S(1)}, bf16[32,640]{1,0:T(8,128)(2,1)S(1)}, u32[]{:S(2)}, u32[]{:S(2)}) collective-permute-start(bf16[32,640]{1,0:T(8,128)(2,1)S(1)} %get-tuple-element.27), channel_id=1, source_target_pairs={{0,16},{8,24},{16,0},{24,8},{1,17},{9,25},{17,1},{25,9},{2,18},{10... | collective-permute-start | bytes 122888 | tf_op jit(solution)/shard_map/ppermute | solution.py:267
  14.4 3.2 %collective-permute-done.2.refs_2_ = bf16[32,640]{1,0:T(8,128)(2,1)S(1)} collective-permute-done((bf16[32,640]{1,0:T(8,128)(2,1)S(1)}, bf16[32,640]{1,0:T(8,128)(2,1)S(1)}, u32[]{:S(2)}, u32[]{:S(2)}) %collective-permute-start.2) | collective-permute-done | bytes 40992 | tf_op jit(solution)/shard_map/ppermute | solution.py:267
  17.7 2.6 %collective-permute-done.3.refs_3_ = bf16[32,640]{1,0:T(8,128)(2,1)S(1)} collective-permute-done((bf16[32,640]{1,0:T(8,128)(2,1)S(1)}, bf16[32,640]{1,0:T(8,128)(2,1)S(1)}, u32[]{:S(2)}, u32[]{:S(2)}) %collective-permute-start.3) | collective-permute-done | bytes 40992 | tf_op jit(solution)/shard_map/ppermute | solution.py:267
  20.5 2.5 %collective-permute-start.6 = (bf16[16,640]{1,0:T(8,128)(2,1)S(1)}, bf16[16,640]{1,0:T(8,128)(2,1)S(1)}, u32[]{:S(2)}, u32[]{:S(2)}) collective-permute-start(bf16[16,640]{1,0:T(8,128)(2,1)S(1)} %get-tuple-element.30), channel_id=1, source_target_pairs={{0,6},{2,4},{4,2},{6,0},{1,7},{3,5},{5,3},{7,1},{8,14},{10,12},{12... | collective-permute-start | bytes 61448 | tf_op jit(solution)/shard_map/ppermute | solution.py:267
  23.0 0.5 collective-permute-start.5
  23.6 0.5 collective-permute-start.4
  24.1 0.7 %combine.1 = bf16[2048,128]{1,0:T(8,128)(2,1)S(1)} custom-call(s32[1]{0:T(128)} %bitcast.1.far_at, s32[1]{0:T(128)} %bitcast.2.near_at, f32[2048,128]{1,0:T(8,128)S(1)} %get-tuple-element.20.logits, bf16[16,640]{1,0:T(8,128)(2,1)S(1)} %get-tuple-element.29.after.refs_0_), custom_call_target="tpu_custom_call" | custom-call | flops 2097152 | bytes 1572864 | tf_op jit(solution)/shard_map/combine/pallas_call | solution.py:331
  25.3 1.5 %collective-permute-done.5.refs_2_ = bf16[16,640]{1,0:T(8,128)(2,1)S(1)} collective-permute-done((bf16[16,640]{1,0:T(8,128)(2,1)S(1)}, bf16[16,640]{1,0:T(8,128)(2,1)S(1)}, u32[]{:S(2)}, u32[]{:S(2)}) %collective-permute-start.5) | collective-permute-done | bytes 20512 | tf_op jit(solution)/shard_map/ppermute | solution.py:267
  26.8 0.5 collective-permute-done.4.refs_1_
  27.7 3.4 %copy-done = bf16[4,1024,1024]{2,1,0:T(8,128)(2,1)S(1)} copy-done((bf16[4,1024,1024]{2,1,0:T(8,128)(2,1)S(1)}, bf16[4,1024,1024]{2,1,0:T(8,128)(2,1)}, u32[]{:S(2)}) %copy-start) | copy-done | bytes 8388632
  31.0 0.6 %first_product.1.first = f32[4,16,1024]{2,1,0:T(8,128)S(1)} custom-call(s32[1]{0:T(128)} %bitcast.place, bf16[16,512]{1,0:T(8,128)(2,1)S(1)} %finish.1.slot_in, bf16[4,1024,1024]{2,1,0:T(8,128)(2,1)S(1)} %copy-done), custom_call_target="tpu_custom_call" | custom-call | flops 67108864 | bytes 4194304 | tf_op jit(solution)/shard_map/first_product/pallas_call | solution.py:350
  31.7 3.4 %copy-done.1 = bf16[4,1024,1024]{2,1,0:T(8,128)(2,1)S(1)} copy-done((bf16[4,1024,1024]{2,1,0:T(8,128)(2,1)S(1)}, bf16[4,1024,1024]{2,1,0:T(8,128)(2,1)}, u32[]{:S(2)}) %copy-start.1) | copy-done | bytes 8388632
  35.1 3.4 %copy-done.2 = bf16[4,1024,1024]{2,1,0:T(8,128)(2,1)S(1)} copy-done((bf16[4,1024,1024]{2,1,0:T(8,128)(2,1)S(1)}, bf16[4,1024,1024]{2,1,0:T(8,128)(2,1)}, u32[]{:S(2)}) %copy-start.2) | copy-done | bytes 8388632
  38.5 1.2 %experts.1 = (bf16[4,16,1024]{2,1,0:T(8,128)(2,1)S(1)}, bf16[16,512]{1,0:T(8,128)(2,1)S(1)}) custom-call(s32[1]{0:T(128)} %bitcast.place, bf16[16,512]{1,0:T(8,128)(2,1)S(1)} %collective-permute-done.7.slot_in, f32[4,16,1024]{2,1,0:T(8,128)S(1)} %first_product.1.first, bf16[4,1024,1024]{2,1,0:T(8,128)(2,1)S(1)} %copy-done.1, bf16[4,1024,1024]{2,1,0:T(8,128)(2,1)S(1)} %copy-done.2), custom_call_target="tpu_custom_call" | custom-call | tf_op jit(solution)/shard_map/experts/pallas_call | solution.py:359
  39.7 0.5 collective-permute-start.8
  40.2 0.7 %own.1 = f32[16,512]{1,0:T(8,128)S(1)} custom-call(s32[1]{0:T(128)} %bitcast.place, bf16[4,16,1024]{2,1,0:T(8,128)(2,1)S(1)} %get-tuple-element.31.hidden, bf16[4,1024,1024]{2,1,0:T(8,128)(2,1)S(1)} %copy-done.2, bf16[16,512]{1,0:T(8,128)(2,1)S(1)} %get-tuple-element.32.after), custom_call_target="tpu_custom_call" | custom-call | flops 67108864 | bytes 4194304 | tf_op jit(solution)/shard_map/own/pallas_call | solution.py:371
  41.0 0.5 collective-permute-start.9
  41.5 2.4 %collective-permute-start.11 = (bf16[16,512]{1,0:T(8,128)(2,1)S(1)}, bf16[16,512]{1,0:T(8,128)(2,1)S(1)}, u32[]{:S(2)}, u32[]{:S(2)}) collective-permute-start(bf16[16,512]{1,0:T(8,128)(2,1)S(1)} %add_convert_fusion.2), channel_id=1, source_target_pairs={{0,6},{2,4},{4,2},{6,0},{1,7},{3,5},{5,3},{7,1},{8,14},{10,12},{12... | collective-permute-start | bytes 49160 | tf_op jit(solution)/shard_map/ppermute | solution.py:267
  44.0 0.5 collective-permute-start.10
  44.8 1.4 %collective-permute-done.11 = bf16[16,512]{1,0:T(8,128)(2,1)S(1)} collective-permute-done((bf16[16,512]{1,0:T(8,128)(2,1)S(1)}, bf16[16,512]{1,0:T(8,128)(2,1)S(1)}, u32[]{:S(2)}, u32[]{:S(2)}) %collective-permute-start.11) | collective-permute-done | bytes 16416 | tf_op jit(solution)/shard_map/ppermute | solution.py:267
  46.2 1.5 %collective-permute-done.10 = bf16[16,512]{1,0:T(8,128)(2,1)S(1)} collective-permute-done((bf16[16,512]{1,0:T(8,128)(2,1)S(1)}, bf16[16,512]{1,0:T(8,128)(2,1)S(1)}, u32[]{:S(2)}, u32[]{:S(2)}) %collective-permute-start.10) | collective-permute-done | bytes 16416 | tf_op jit(solution)/shard_map/ppermute | solution.py:267
  47.8 1.9 %collective-permute-start.14 = (bf16[32,512]{1,0:T(8,128)(2,1)S(1)}, bf16[32,512]{1,0:T(8,128)(2,1)S(1)}, u32[]{:S(2)}, u32[]{:S(2)}) collective-permute-start(bf16[32,512]{1,0:T(8,128)(2,1)S(1)} %pad_maximum_fusion), channel_id=1, source_target_pairs={{0,24},{8,16},{16,8},{24,0},{1,25},{9,17},{17,9},{25,1},{2,26},{10... | collective-permute-start | bytes 98312 | tf_op jit(solution)/shard_map/ppermute | solution.py:267
  49.7 1.6 %collective-permute-start.13 = (bf16[32,512]{1,0:T(8,128)(2,1)S(1)}, bf16[32,512]{1,0:T(8,128)(2,1)S(1)}, u32[]{:S(2)}, u32[]{:S(2)}) collective-permute-start(bf16[32,512]{1,0:T(8,128)(2,1)S(1)} %pad_maximum_fusion), channel_id=1, source_target_pairs={{0,16},{8,24},{16,0},{24,8},{1,17},{9,25},{17,1},{25,9},{2,18},{10... | collective-permute-start | bytes 98312 | tf_op jit(solution)/shard_map/ppermute | solution.py:267
  51.3 0.7 %collective-permute-done.12 = bf16[32,512]{1,0:T(8,128)(2,1)S(1)} collective-permute-done((bf16[32,512]{1,0:T(8,128)(2,1)S(1)}, bf16[32,512]{1,0:T(8,128)(2,1)S(1)}, u32[]{:S(2)}, u32[]{:S(2)}) %collective-permute-start.12) | collective-permute-done | bytes 32800 | tf_op jit(solution)/shard_map/ppermute | solution.py:267
  52.0 2.5 %collective-permute-done.13 = bf16[32,512]{1,0:T(8,128)(2,1)S(1)} collective-permute-done((bf16[32,512]{1,0:T(8,128)(2,1)S(1)}, bf16[32,512]{1,0:T(8,128)(2,1)S(1)}, u32[]{:S(2)}, u32[]{:S(2)}) %collective-permute-start.13) | collective-permute-done | bytes 32800 | tf_op jit(solution)/shard_map/ppermute | solution.py:267
  54.6 1.2 %mix.1 = (bf16[2048,1024]{1,0:T(8,128)(2,1)}, bf16[1024,512]{1,0:T(8,128)(2,1)S(1)}) custom-call(s32[1]{0:T(128)} %bitcast.place, bf16[2048,128]{1,0:T(8,128)(2,1)S(1)} %combine.1, bf16[128,512]{1,0:T(8,128)(2,1)S(1)} %constant_dynamic-update-slice_fusion.slot_out), custom_call_target="tpu_custom_call" | custom-call | flops 268435456 | bytes 2621440 | tf_op jit(solution)/shard_map/mix/pallas_call | solution.py:391
  55.9 1.7 %mix_other.1 = bf16[2048,1024]{1,0:T(8,128)(2,1)} custom-call(s32[1]{0:T(128)} %bitcast.place, bf16[2048,128]{1,0:T(8,128)(2,1)S(1)} %combine.1, bf16[128,512]{1,0:T(8,128)(2,1)S(1)} %collective-permute-done.15.slot_out, bf16[1024,512]{1,0:T(8,128)(2,1)S(1)} %get-tuple-element.33.rest, ...), custom_call_target="tpu_custom_call", output_to_operand_aliasing={{}: (4, {})} | custom-call | flops 268435456 | bytes 2621440 | tf_op jit(solution)/shard_map/mix_other/pallas_call | solution.py:404
  (28 shorter events, 2.6 us)
Async XLA Ops:
  3.7 2.0 %copy-start.3 = (bf16[2048,1024]{1,0:T(8,128)(2,1)}, bf16[2048,1024]{1,0:T(8,128)(2,1)S(1)}, u32[]{:S(2)}) copy-start(bf16[2048,1024]{1,0:T(8,128)(2,1)S(1)} %get-tuple-element.22.held) | copy-start | bytes 12582916
  5.7 3.1 %collective-permute-start = (bf16[128,640]{1,0:T(8,128)(2,1)S(1)}, bf16[128,640]{1,0:T(8,128)(2,1)S(1)}, u32[]{:S(2)}, u32[]{:S(2)}) collective-permute-start(bf16[128,640]{1,0:T(8,128)(2,1)S(1)} %get-tuple-element.24.after), channel_id=1, source_target_pairs={{0,1},{1,0},{2,3},{3,2},{4,5},{5,4},{6,7},{7,6},{8,9},{9,8},{10,11... | collective-permute-start | bytes 491528 | tf_op jit(solution)/shard_map/ppermute | solution.py:267
  6.1 2.2 %copy-start.4 = (bf16[2048,1024]{1,0:T(8,128)(2,1)S(1)}, bf16[2048,1024]{1,0:T(8,128)(2,1)}, u32[]{:S(2)}) copy-start(bf16[2048,1024]{1,0:T(8,128)(2,1)} %copy-done.3) | copy-start | bytes 12582916
  9.2 5.3 %collective-permute-start.1 = (bf16[32,640]{1,0:T(8,128)(2,1)S(1)}, bf16[32,640]{1,0:T(8,128)(2,1)S(1)}, u32[]{:S(2)}, u32[]{:S(2)}) collective-permute-start(bf16[32,640]{1,0:T(8,128)(2,1)S(1)} %get-tuple-element.26), channel_id=1, source_target_pairs={{0,8},{8,0},{16,24},{24,16},{1,9},{9,1},{17,25},{25,17},{2,10},{10... | collective-permute-start | bytes 122888 | tf_op jit(solution)/shard_map/ppermute | solution.py:267
  11.8 5.8 %collective-permute-start.2 = (bf16[32,640]{1,0:T(8,128)(2,1)S(1)}, bf16[32,640]{1,0:T(8,128)(2,1)S(1)}, u32[]{:S(2)}, u32[]{:S(2)}) collective-permute-start(bf16[32,640]{1,0:T(8,128)(2,1)S(1)} %get-tuple-element.27), channel_id=1, source_target_pairs={{0,16},{8,24},{16,0},{24,8},{1,17},{9,25},{17,1},{25,9},{2,18},{10... | collective-permute-start | bytes 122888 | tf_op jit(solution)/shard_map/ppermute | solution.py:267
  14.4 5.8 %collective-permute-start.3 = (bf16[32,640]{1,0:T(8,128)(2,1)S(1)}, bf16[32,640]{1,0:T(8,128)(2,1)S(1)}, u32[]{:S(2)}, u32[]{:S(2)}) collective-permute-start(bf16[32,640]{1,0:T(8,128)(2,1)S(1)} %get-tuple-element.28), channel_id=1, source_target_pairs={{0,24},{8,16},{16,8},{24,0},{1,25},{9,17},{17,9},{25,1},{2,26},{10... | collective-permute-start | bytes 122888 | tf_op jit(solution)/shard_map/ppermute | solution.py:267
  20.5 4.7 %collective-permute-start.6 = (bf16[16,640]{1,0:T(8,128)(2,1)S(1)}, bf16[16,640]{1,0:T(8,128)(2,1)S(1)}, u32[]{:S(2)}, u32[]{:S(2)}) collective-permute-start(bf16[16,640]{1,0:T(8,128)(2,1)S(1)} %get-tuple-element.30), channel_id=1, source_target_pairs={{0,6},{2,4},{4,2},{6,0},{1,7},{3,5},{5,3},{7,1},{8,14},{10,12},{12... | collective-permute-start | bytes 61448 | tf_op jit(solution)/shard_map/ppermute | solution.py:267
  23.0 3.8 %collective-permute-start.5 = (bf16[16,640]{1,0:T(8,128)(2,1)S(1)}, bf16[16,640]{1,0:T(8,128)(2,1)S(1)}, u32[]{:S(2)}, u32[]{:S(2)}) collective-permute-start(bf16[16,640]{1,0:T(8,128)(2,1)S(1)} %get-tuple-element.30), channel_id=1, source_target_pairs={{0,4},{2,6},{4,0},{6,2},{1,5},{3,7},{5,1},{7,3},{8,12},{10,14},{12... | collective-permute-start | bytes 61448 | tf_op jit(solution)/shard_map/ppermute | solution.py:267
  23.6 3.8 %collective-permute-start.4 = (bf16[16,640]{1,0:T(8,128)(2,1)S(1)}, bf16[16,640]{1,0:T(8,128)(2,1)S(1)}, u32[]{:S(2)}, u32[]{:S(2)}) collective-permute-start(bf16[16,640]{1,0:T(8,128)(2,1)S(1)} %get-tuple-element.29.after.refs_0_), channel_id=1, source_target_pairs={{0,2},{2,0},{4,6},{6,4},{1,3},{3,1},{5,7},{7,5},{8,10},{10,8},{12,... | collective-permute-start | bytes 61448 | tf_op jit(solution)/shard_map/ppermute | solution.py:267
  27.6 4.1 %collective-permute-start.7 = (bf16[16,512]{1,0:T(8,128)(2,1)S(1)}, bf16[16,512]{1,0:T(8,128)(2,1)S(1)}, u32[]{:S(2)}, u32[]{:S(2)}) collective-permute-start(bf16[16,512]{1,0:T(8,128)(2,1)S(1)} %finish.1.slot_in), channel_id=1, source_target_pairs={{0,1},{1,0},{2,3},{3,2},{4,5},{5,4},{6,7},{7,6},{8,9},{9,8},{10,11... | collective-permute-start | bytes 49160 | tf_op jit(solution)/shard_map/ppermute | solution.py:267
  27.6 3.4 %copy-start = (bf16[4,1024,1024]{2,1,0:T(8,128)(2,1)S(1)}, bf16[4,1024,1024]{2,1,0:T(8,128)(2,1)}, u32[]{:S(2)}) copy-start(bf16[4,1024,1024]{2,1,0:T(8,128)(2,1)} %expert_in.3) | copy-start | bytes 25165828
  31.7 3.4 %copy-start.1 = (bf16[4,1024,1024]{2,1,0:T(8,128)(2,1)S(1)}, bf16[4,1024,1024]{2,1,0:T(8,128)(2,1)}, u32[]{:S(2)}) copy-start(bf16[4,1024,1024]{2,1,0:T(8,128)(2,1)} %expert_in.3) | copy-start | bytes 25165828
  35.1 3.4 %copy-start.2 = (bf16[4,1024,1024]{2,1,0:T(8,128)(2,1)S(1)}, bf16[4,1024,1024]{2,1,0:T(8,128)(2,1)}, u32[]{:S(2)}) copy-start(bf16[4,1024,1024]{2,1,0:T(8,128)(2,1)} %expert_out.3) | copy-start | bytes 25165828
  39.7 1.3 %collective-permute-start.8 = (bf16[16,512]{1,0:T(8,128)(2,1)S(1)}, bf16[16,512]{1,0:T(8,128)(2,1)S(1)}, u32[]{:S(2)}, u32[]{:S(2)}) collective-permute-start(bf16[16,512]{1,0:T(8,128)(2,1)S(1)} %get-tuple-element.32.after), channel_id=1, source_target_pairs={{0,1},{1,0},{2,3},{3,2},{4,5},{5,4},{6,7},{7,6},{8,9},{9,8},{10,11... | collective-permute-start | bytes 49160 | tf_op jit(solution)/shard_map/ppermute | solution.py:267
  41.0 3.7 %collective-permute-start.9 = (bf16[16,512]{1,0:T(8,128)(2,1)S(1)}, bf16[16,512]{1,0:T(8,128)(2,1)S(1)}, u32[]{:S(2)}, u32[]{:S(2)}) collective-permute-start(bf16[16,512]{1,0:T(8,128)(2,1)S(1)} %add_convert_fusion.2), channel_id=1, source_target_pairs={{0,2},{2,0},{4,6},{6,4},{1,3},{3,1},{5,7},{7,5},{8,10},{10,8},{12,... | collective-permute-start | bytes 49160 | tf_op jit(solution)/shard_map/ppermute | solution.py:267
  41.5 4.6 %collective-permute-start.11 = (bf16[16,512]{1,0:T(8,128)(2,1)S(1)}, bf16[16,512]{1,0:T(8,128)(2,1)S(1)}, u32[]{:S(2)}, u32[]{:S(2)}) collective-permute-start(bf16[16,512]{1,0:T(8,128)(2,1)S(1)} %add_convert_fusion.2), channel_id=1, source_target_pairs={{0,6},{2,4},{4,2},{6,0},{1,7},{3,5},{5,3},{7,1},{8,14},{10,12},{12... | collective-permute-start | bytes 49160 | tf_op jit(solution)/shard_map/ppermute | solution.py:267
  44.0 3.7 %collective-permute-start.10 = (bf16[16,512]{1,0:T(8,128)(2,1)S(1)}, bf16[16,512]{1,0:T(8,128)(2,1)S(1)}, u32[]{:S(2)}, u32[]{:S(2)}) collective-permute-start(bf16[16,512]{1,0:T(8,128)(2,1)S(1)} %add_convert_fusion.2), channel_id=1, source_target_pairs={{0,4},{2,6},{4,0},{6,2},{1,5},{3,7},{5,1},{7,3},{8,12},{10,14},{12... | collective-permute-start | bytes 49160 | tf_op jit(solution)/shard_map/ppermute | solution.py:267
  47.7 4.3 %collective-permute-start.12 = (bf16[32,512]{1,0:T(8,128)(2,1)S(1)}, bf16[32,512]{1,0:T(8,128)(2,1)S(1)}, u32[]{:S(2)}, u32[]{:S(2)}) collective-permute-start(bf16[32,512]{1,0:T(8,128)(2,1)S(1)} %pad_maximum_fusion), channel_id=1, source_target_pairs={{0,8},{8,0},{16,24},{24,16},{1,9},{9,1},{17,25},{25,17},{2,10},{10... | collective-permute-start | bytes 98312 | tf_op jit(solution)/shard_map/ppermute | solution.py:267
  47.8 6.7 %collective-permute-start.14 = (bf16[32,512]{1,0:T(8,128)(2,1)S(1)}, bf16[32,512]{1,0:T(8,128)(2,1)S(1)}, u32[]{:S(2)}, u32[]{:S(2)}) collective-permute-start(bf16[32,512]{1,0:T(8,128)(2,1)S(1)} %pad_maximum_fusion), channel_id=1, source_target_pairs={{0,24},{8,16},{16,8},{24,0},{1,25},{9,17},{17,9},{25,1},{2,26},{10... | collective-permute-start | bytes 98312 | tf_op jit(solution)/shard_map/ppermute | solution.py:267
  49.7 4.8 %collective-permute-start.13 = (bf16[32,512]{1,0:T(8,128)(2,1)S(1)}, bf16[32,512]{1,0:T(8,128)(2,1)S(1)}, u32[]{:S(2)}, u32[]{:S(2)}) collective-permute-start(bf16[32,512]{1,0:T(8,128)(2,1)S(1)} %pad_maximum_fusion), channel_id=1, source_target_pairs={{0,16},{8,24},{16,0},{24,8},{1,17},{9,25},{17,1},{25,9},{2,18},{10... | collective-permute-start | bytes 98312 | tf_op jit(solution)/shard_map/ppermute | solution.py:267
  54.5 1.4 %collective-permute-start.15 = (bf16[128,512]{1,0:T(8,128)(2,1)S(1)}, bf16[128,512]{1,0:T(8,128)(2,1)S(1)}, u32[]{:S(2)}, u32[]{:S(2)}) collective-permute-start(bf16[128,512]{1,0:T(8,128)(2,1)S(1)} %constant_dynamic-update-slice_fusion.slot_out), channel_id=1, source_target_pairs={{0,1},{1,0},{2,3},{3,2},{4,5},{5,4},{6,7},{7,6},{8,9},{9,8},{10,11... | collective-permute-start | bytes 393224 | tf_op jit(solution)/shard_map/ppermute | solution.py:267

commit v21 on v19

--- a/solution.py
+++ b/solution.py
@@ -1,3 +1,4 @@
+import functools
 import math
 
 import jax
@@ -59,6 +60,18 @@
         value[:, 0:1] + value[:, 1:2] + value[:, 2:3],
         value[:, 3:4] + value[:, 4:5] + value[:, 5:6],
     )
+
+
+def pair_at(place):
+    return place[0] & 1
+
+
+def near_at(place, rest):
+    return place[0] // (2 * rest) & 1
+
+
+def far_at(place, rest):
+    return place[0] // (4 * rest)
 
 
 def column_half(side, half):
@@ -92,7 +105,7 @@
         weights = jnp.concatenate(columns, axis=1)
         span = pl.ds(first * CHUNK, len(parts) * CHUNK)
         turned[:, span] = weights
-        sums = dot(weights, held[span, column_half(1 - place[0], half)])
+        sums = dot(weights, held[span, column_half(1 - pair_at(place), half)])
         return sums, jnp.sum(total, axis=0, keepdims=True)
 
     table_copy.wait()
@@ -124,18 +137,18 @@
 
 
 def own_sums_kernel(place, turned, held, side, after, keep):
-    columns = column_half(place[0], keep.shape[1])
+    columns = column_half(pair_at(place), keep.shape[1])
     early = held.shape[0] - TOGETHER * CHUNK
     spans = (pl.ds(0, early), pl.ds(early, TOGETHER * CHUNK))
     early, late = [dot(turned[:, span], held[span, columns]) for span in spans]
     keep[...] = early * side[:, 2:3] + late * side[:, 3:4]
 
 
-def pair_kernel(far_at, keep, side, received, *sends):
+def pair_kernel(rest, place, keep, side, received, *sends):
     width = keep.shape[1]
     for r, send in enumerate(sends):
         rows = send.shape[0]
-        span = pl.ds(pl.multiple_of((far_at[0] ^ r) * rows, rows), rows)
+        span = pl.ds(pl.multiple_of((far_at(place, rest) ^ r) * rows, rows), rows)
         peak_mine, total_mine = side[span, 0:1], side[span, 1:2]
         peak_other, total_other = read_message(received[span, width:])
         peak = jnp.maximum(peak_mine, peak_other)
@@ -160,10 +173,10 @@
     return sums, peak, total
 
 
-def merge_kernel(near_at, *refs):
+def merge_kernel(rest, place, *refs):
     for n, send in enumerate(refs[-2:]):
         rows, width = send.shape[0], send.shape[1] - SIDE
-        span = pl.ds(pl.multiple_of((near_at[0] ^ n) * rows, rows), rows)
+        span = pl.ds(pl.multiple_of((near_at(place, rest) ^ n) * rows, rows), rows)
         sums, peak, total = add_parts([ref[span, :] for ref in refs[:-2]], width)
         send[:, :width] = sums.astype(BF16)
         send[:, width:] = side_message(peak, total)
@@ -178,7 +191,7 @@
 def first_product_kernel(place, slot_in, expert_in, result):
     half = slot_in.shape[1]
     for e in range(expert_in.shape[0]):
-        result[e] = dot(slot_in[...], expert_in[e, column_half(place[0], half), :])
+        result[e] = dot(slot_in[...], expert_in[e, column_half(pair_at(place), half), :])
 
 
 def second_product(hidden, weights, columns):
@@ -193,15 +206,15 @@
     half = slot_in.shape[1]
     values = []
     for e in range(expert_in.shape[0]):
-        product = first[e] + dot(slot_in[...], expert_in[e, column_half(1 - place[0], half), :])
+        product = first[e] + dot(slot_in[...], expert_in[e, column_half(1 - pair_at(place), half), :])
         values.append(jax.nn.gelu(product).astype(BF16))
         hidden[e] = values[e]
-    send[...] = second_product(values, expert_out, column_half(1 - place[0], half)).astype(BF16)
+    send[...] = second_product(values, expert_out, column_half(1 - pair_at(place), half)).astype(BF16)
 
 
 def own_kernel(place, hidden, expert_out, after, keep):
     values = [hidden[e] for e in range(hidden.shape[0])]
-    keep[...] = second_product(values, expert_out, column_half(place[0], keep.shape[1]))
+    keep[...] = second_product(values, expert_out, column_half(pair_at(place), keep.shape[1]))
 
 
 def combine_kernel(logits, after, combine):
@@ -214,7 +227,7 @@
     width = slot_out.shape[1]
     tokens, done = combine.shape[0], held.shape[0]
     block = done // sems.shape[0]
-    columns = pl.ds(pl.multiple_of(place[0] * width, width), width)
+    columns = pl.ds(pl.multiple_of(pair_at(place) * width, width), width)
     copies = []
     for i in range(tokens // block):
         rows = pl.ds(i * block, block)
@@ -234,8 +247,8 @@
     blocks = sems.shape[0] - 1
     tokens = combine.shape[0]
     done = tokens - rest.shape[0]
-    mine = pl.ds(pl.multiple_of(place[0] * width, width), width)
-    other = pl.ds(pl.multiple_of((1 - place[0]) * width, width), width)
+    mine = pl.ds(pl.multiple_of(pair_at(place) * width, width), width)
+    other = pl.ds(pl.multiple_of((1 - pair_at(place)) * width, width), width)
     copies = [pltpu.make_async_copy(rest, mixed.at[pl.ds(done, tokens - done), mine], sems.at[blocks])]
     copies[0].start()
     block = tokens // blocks
@@ -271,9 +284,7 @@
     far, near, rest = [lax.axis_size(axis) for axis in ("far", "near", "rest")]
     rows = slots // (far * near)
     half = model // 2
-    place, far_at, near_at = [
-        lax.axis_index(axis).astype(jnp.int32).reshape(1) for axis in ("pair", "far", "near")
-    ]
+    place = lax.axis_index(("far", "near", "rest", "pair")).astype(jnp.int32).reshape(1)
     any_space = pl.BlockSpec(memory_space=pl.ANY)
 
     logits, turned, held, side, send = pl.pallas_call(
@@ -302,23 +313,23 @@
         name="own_sums",
     )(place, turned, held, side, send)
     sends = pl.pallas_call(
-        pair_kernel,
+        functools.partial(pair_kernel, rest),
         out_shape=(jax.ShapeDtypeStruct((near * rows, half + SIDE), BF16),) * far,
         in_specs=[SMEM] + [VMEM] * 3,
         out_specs=(VMEM,) * far,
         cost_estimate=cost(0, 6 * slots * model, 128 * slots * model),
         compiler_params=params(16),
         name="pair",
-    )(far_at, keep, side, received)
+    )(place, keep, side, received)
     parts = [sends[0]] + [move(sends[r], ("far",), (r,)) for r in range(1, far)]
     send, their = pl.pallas_call(
-        merge_kernel,
+        functools.partial(merge_kernel, rest),
         out_shape=(jax.ShapeDtypeStruct((rows, half + SIDE), BF16),) * 2,
         in_specs=[SMEM] + [VMEM] * far,
         out_specs=(VMEM, VMEM),
         compiler_params=params(16),
         name="merge",
-    )(near_at, *parts)
+    )(place, *parts)
     plane = ("near", "rest")
     mine = [send] + [move(send, plane, (0, r)) for r in range(1, rest)]
     mine += [move(their, plane, (1, r)) for r in range(rest)]

time: 57.9 us -> 44.5 us (0.77)
  local copies, waits for them, and re-layouts: 14.4 us -> 0.04 us
  waiting for transfers between devices: 8.75 us -> 9.93 us
    unnamed x10 -> x8, local copies, waits for them, and re-layouts: 14.3 us -> 0.02 us
    ppermute x10, waiting for transfers between devices: 8.75 us -> 9.93 us  [move(): return lax.ppermute(value, axes, moves)]
  transfers between devices with their start and end apart: 10 -> 10, of which waited for: 7 -> 9; matrix products, arithmetic and copies ran while one was open for 0% -> 0% of each run, Pallas kernels for 6% -> 8%
where the time goes in v21:
time: 44.5 us; the launch traced here: 44.3 us
  blocking collectives  13.1 us (29%)
  Pallas kernels  11.1 us (25%)
  starting transfers between devices  9.96 us (22%)
  waiting for transfers between devices  9.93 us (22%)
    all_to_all x1, blocking collectives, shards(): lax.all_to_all(partials, ('rest', 'far', 'near'), split_axis=0, concat_ax...  13.1 us
    ppermute x10, starting transfers between devices, move(): return lax.ppermute(value, axes, moves)  9.96 us
    ppermute x10, waiting for transfers between devices, move(): return lax.ppermute(value, axes, moves)  9.93 us
    pallas_call x1, Pallas kernels, shards(): pl.pallas_call(gather_kernel, out_shape=(jax.ShapeDtypeStruct((count, slo...  3.67 us
    pallas_call x1, Pallas kernels, shards(): pl.pallas_call(mix_other_kernel, out_shape=jax.ShapeDtypeStruct((count, m...  1.74 us
    pallas_call x1, Pallas kernels, shards(): pl.pallas_call(expert_kernel, out_shape=(jax.ShapeDtypeStruct((experts, r...  1.21 us
    pallas_call x1, Pallas kernels, shards(): pl.pallas_call(mix_kernel, out_shape=(pltpu.HBM((count, model), BF16), ja...  1.21 us
  transfers between devices with their start and end apart: 10, of which 9 were waited for; matrix products, arithmetic and copies ran while one was open for 0% of the time, Pallas kernels for 8%

profile of v21, /device:TPU:0, one launch (start us, length us, event | category | flops | bytes accessed | tf_op | source)
XLA Modules:
  0.0 44.3 jit_solution(4972051525364157414)
XLA Ops:
  0.0 3.7 %gather.1 = (f32[2048,128]{1,0:T(8,128)S(1)}, bf16[128,2048]{1,0:T(8,128)(2,1)S(1)}, bf16[2048,1024]{1,0:T(8,128)(2,1)S(1)}, f32[128,128]{1,0:T(8,128)S(1)}, bf16[128,640]{1,0:T(8,128)(2,1)S(1)}) custom-call(s32[1]{0:T(128)} %bitcast.place, bf16[2048,1024]{1,0:T(8,128)(2,1)} %tokens.1, bf16[1024,128]{1,0:T(8,128)(2,1)} %slot_params.1), custom_call_target="tpu_custom_call" | custom-call | tf_op jit(solution)/shard_map/gather/pallas_call | solution.py:290
  3.7 0.5 %collective-permute-start = (bf16[128,640]{1,0:T(8,128)(2,1)S(1)}, bf16[128,640]{1,0:T(8,128)(2,1)S(1)}, u32[]{:S(2)}, u32[]{:S(2)}) collective-permute-start(bf16[128,640]{1,0:T(8,128)(2,1)S(1)} %get-tuple-element.24.after), channel_id=1, source_target_pairs={{0,1},{1,0},{2,3},{3,2},{4,5},{5,4},{6,7},{7,6},{8,9},{9,8},{10,11... | collective-permute-start | bytes 491528 | tf_op jit(solution)/shard_map/ppermute | solution.py:274
  4.2 0.5 %own_sums.1.keep = f32[128,512]{1,0:T(8,128)S(1)} custom-call(s32[1]{0:T(128)} %bitcast.place, bf16[128,2048]{1,0:T(8,128)(2,1)S(1)} %get-tuple-element.21.turned, bf16[2048,1024]{1,0:T(8,128)(2,1)S(1)} %get-tuple-element.22.held, f32[128,128]{1,0:T(8,128)S(1)} %get-tuple-element.23.side, bf16[128,640]{1,0:T(8,128)(2,1)S(1)} %get-tuple-element.24.after), custom_call_target="tpu_custom_call" | custom-call | flops 268435456 | bytes 2621440 | tf_op jit(solution)/shard_map/own_sums/pallas_call | solution.py:306
  4.6 0.0 slice-start.1
  4.7 0.0 slice-start.3
  4.7 0.5 %collective-permute-done.received = bf16[128,640]{1,0:T(8,128)(2,1)S(1)} collective-permute-done((bf16[128,640]{1,0:T(8,128)(2,1)S(1)}, bf16[128,640]{1,0:T(8,128)(2,1)S(1)}, u32[]{:S(2)}, u32[]{:S(2)}) %collective-permute-start) | collective-permute-done | bytes 163872 | tf_op jit(solution)/shard_map/ppermute | solution.py:274
  5.2 0.4 pair.1
  5.6 3.0 %collective-permute-start.1 = (bf16[32,640]{1,0:T(8,128)(2,1)S(1)}, bf16[32,640]{1,0:T(8,128)(2,1)S(1)}, u32[]{:S(2)}, u32[]{:S(2)}) collective-permute-start(bf16[32,640]{1,0:T(8,128)(2,1)S(1)} %get-tuple-element.26), channel_id=1, source_target_pairs={{0,8},{8,0},{16,24},{24,16},{1,9},{9,1},{17,25},{25,17},{2,10},{10... | collective-permute-start | bytes 122888 | tf_op jit(solution)/shard_map/ppermute | solution.py:274
  8.6 2.6 %collective-permute-start.2 = (bf16[32,640]{1,0:T(8,128)(2,1)S(1)}, bf16[32,640]{1,0:T(8,128)(2,1)S(1)}, u32[]{:S(2)}, u32[]{:S(2)}) collective-permute-start(bf16[32,640]{1,0:T(8,128)(2,1)S(1)} %get-tuple-element.27), channel_id=1, source_target_pairs={{0,16},{8,24},{16,0},{24,8},{1,17},{9,25},{17,1},{25,9},{2,18},{10... | collective-permute-start | bytes 122888 | tf_op jit(solution)/shard_map/ppermute | solution.py:274
  11.2 3.1 %collective-permute-done.2.refs_2_ = bf16[32,640]{1,0:T(8,128)(2,1)S(1)} collective-permute-done((bf16[32,640]{1,0:T(8,128)(2,1)S(1)}, bf16[32,640]{1,0:T(8,128)(2,1)S(1)}, u32[]{:S(2)}, u32[]{:S(2)}) %collective-permute-start.2) | collective-permute-done | bytes 40992 | tf_op jit(solution)/shard_map/ppermute | solution.py:274
  14.4 2.7 %collective-permute-done.3.refs_3_ = bf16[32,640]{1,0:T(8,128)(2,1)S(1)} collective-permute-done((bf16[32,640]{1,0:T(8,128)(2,1)S(1)}, bf16[32,640]{1,0:T(8,128)(2,1)S(1)}, u32[]{:S(2)}, u32[]{:S(2)}) %collective-permute-start.3) | collective-permute-done | bytes 40992 | tf_op jit(solution)/shard_map/ppermute | solution.py:274
  17.0 0.3 merge.1
  17.3 2.5 %collective-permute-start.6 = (bf16[16,640]{1,0:T(8,128)(2,1)S(1)}, bf16[16,640]{1,0:T(8,128)(2,1)S(1)}, u32[]{:S(2)}, u32[]{:S(2)}) collective-permute-start(bf16[16,640]{1,0:T(8,128)(2,1)S(1)} %get-tuple-element.30), channel_id=1, source_target_pairs={{0,6},{2,4},{4,2},{6,0},{1,7},{3,5},{5,3},{7,1},{8,14},{10,12},{12... | collective-permute-start | bytes 61448 | tf_op jit(solution)/shard_map/ppermute | solution.py:274
  19.8 0.5 %collective-permute-start.5 = (bf16[16,640]{1,0:T(8,128)(2,1)S(1)}, bf16[16,640]{1,0:T(8,128)(2,1)S(1)}, u32[]{:S(2)}, u32[]{:S(2)}) collective-permute-start(bf16[16,640]{1,0:T(8,128)(2,1)S(1)} %get-tuple-element.30), channel_id=1, source_target_pairs={{0,4},{2,6},{4,0},{6,2},{1,5},{3,7},{5,1},{7,3},{8,12},{10,14},{12... | collective-permute-start | bytes 61448 | tf_op jit(solution)/shard_map/ppermute | solution.py:274
  20.3 0.5 %collective-permute-start.4 = (bf16[16,640]{1,0:T(8,128)(2,1)S(1)}, bf16[16,640]{1,0:T(8,128)(2,1)S(1)}, u32[]{:S(2)}, u32[]{:S(2)}) collective-permute-start(bf16[16,640]{1,0:T(8,128)(2,1)S(1)} %get-tuple-element.29.after.refs_0_), channel_id=1, source_target_pairs={{0,2},{2,0},{4,6},{6,4},{1,3},{3,1},{5,7},{7,5},{8,10},{10,8},{12,... | collective-permute-start | bytes 61448 | tf_op jit(solution)/shard_map/ppermute | solution.py:274
  20.8 0.6 %combine.1 = bf16[2048,128]{1,0:T(8,128)(2,1)S(1)} custom-call(f32[2048,128]{1,0:T(8,128)S(1)} %get-tuple-element.20.logits, bf16[16,640]{1,0:T(8,128)(2,1)S(1)} %get-tuple-element.29.after.refs_0_), custom_call_target="tpu_custom_call" | custom-call | flops 2097152 | bytes 1572864 | tf_op jit(solution)/shard_map/combine/pallas_call | solution.py:336
  21.5 0.5 %collective-permute-done.6.refs_3_ = bf16[16,640]{1,0:T(8,128)(2,1)S(1)} collective-permute-done((bf16[16,640]{1,0:T(8,128)(2,1)S(1)}, bf16[16,640]{1,0:T(8,128)(2,1)S(1)}, u32[]{:S(2)}, u32[]{:S(2)}) %collective-permute-start.6) | collective-permute-done | bytes 20512 | tf_op jit(solution)/shard_map/ppermute | solution.py:274
  22.0 1.5 %collective-permute-done.5.refs_2_ = bf16[16,640]{1,0:T(8,128)(2,1)S(1)} collective-permute-done((bf16[16,640]{1,0:T(8,128)(2,1)S(1)}, bf16[16,640]{1,0:T(8,128)(2,1)S(1)}, u32[]{:S(2)}, u32[]{:S(2)}) %collective-permute-start.5) | collective-permute-done | bytes 20512 | tf_op jit(solution)/shard_map/ppermute | solution.py:274
  23.6 0.5 %collective-permute-done.4.refs_1_ = bf16[16,640]{1,0:T(8,128)(2,1)S(1)} collective-permute-done((bf16[16,640]{1,0:T(8,128)(2,1)S(1)}, bf16[16,640]{1,0:T(8,128)(2,1)S(1)}, u32[]{:S(2)}, u32[]{:S(2)}) %collective-permute-start.4) | collective-permute-done | bytes 20512 | tf_op jit(solution)/shard_map/ppermute | solution.py:274
  24.1 0.2 finish.1.slot_in
  24.4 0.1 collective-permute-start.7
  24.4 0.7 %first_product.1.first = f32[4,16,1024]{2,1,0:T(8,128)S(1)} custom-call(s32[1]{0:T(128)} %bitcast.place, bf16[16,512]{1,0:T(8,128)(2,1)S(1)} %finish.1.slot_in, bf16[4,1024,1024]{2,1,0:T(8,128)(2,1)S(1)} %bitcast.4), custom_call_target="tpu_custom_call" | custom-call | flops 67108864 | bytes 4194304 | tf_op jit(solution)/shard_map/first_product/pallas_call | solution.py:355
  25.1 0.5 %collective-permute-done.7.slot_in = bf16[16,512]{1,0:T(8,128)(2,1)S(1)} collective-permute-done((bf16[16,512]{1,0:T(8,128)(2,1)S(1)}, bf16[16,512]{1,0:T(8,128)(2,1)S(1)}, u32[]{:S(2)}, u32[]{:S(2)}) %collective-permute-start.7) | collective-permute-done | bytes 16416 | tf_op jit(solution)/shard_map/ppermute | solution.py:274
  25.6 1.2 %experts.1 = (bf16[4,16,1024]{2,1,0:T(8,128)(2,1)S(1)}, bf16[16,512]{1,0:T(8,128)(2,1)S(1)}) custom-call(s32[1]{0:T(128)} %bitcast.place, bf16[16,512]{1,0:T(8,128)(2,1)S(1)} %collective-permute-done.7.slot_in, f32[4,16,1024]{2,1,0:T(8,128)S(1)} %first_product.1.first, bf16[4,1024,1024]{2,1,0:T(8,128)(2,1)S(1)} %bitcast.4, bf16[4,1024,1024]{2,1,0:T(8,128)(2,1)S(1)} %bitcast.6), custom_call_target="tpu_custom_call" | custom-call | tf_op jit(solution)/shard_map/experts/pallas_call | solution.py:364
  26.8 0.2 collective-permute-start.8
  27.0 0.7 %own.1 = f32[16,512]{1,0:T(8,128)S(1)} custom-call(s32[1]{0:T(128)} %bitcast.place, bf16[4,16,1024]{2,1,0:T(8,128)(2,1)S(1)} %get-tuple-element.31.hidden, bf16[4,1024,1024]{2,1,0:T(8,128)(2,1)S(1)} %bitcast.6, bf16[16,512]{1,0:T(8,128)(2,1)S(1)} %get-tuple-element.32.after), custom_call_target="tpu_custom_call" | custom-call | flops 67108864 | bytes 4194304 | tf_op jit(solution)/shard_map/own/pallas_call | solution.py:376
  27.6 0.4 collective-permute-done.8
  28.0 13.1 %all_to_all.5 = bf16[16,16,512]{2,1,0:T(8,128)(2,1)S(1)} all-to-all(bf16[16,16,512]{2,1,0:T(8,128)(2,1)S(1)} %broadcast_in_dim.3), channel_id=1, replica_groups=mesh['far'=4,'near'=2,'rest'=2,'pair'=2] {'rest','far','near'}, dimensions={0} | all-to-all | bytes 524288 | tf_op jit(solution)/shard_map/all_to_all | solution.py:388
  41.2 0.1 collective-permute-start.9
  41.2 1.2 %mix.1 = (bf16[2048,1024]{1,0:T(8,128)(2,1)}, bf16[1024,512]{1,0:T(8,128)(2,1)S(1)}) custom-call(s32[1]{0:T(128)} %bitcast.place, bf16[2048,128]{1,0:T(8,128)(2,1)S(1)} %combine.1, bf16[128,512]{1,0:T(8,128)(2,1)S(1)} %bitcast.8), custom_call_target="tpu_custom_call" | custom-call | flops 268435456 | bytes 2621440 | tf_op jit(solution)/shard_map/mix/pallas_call | solution.py:393
  42.4 0.1 collective-permute-done.9.slot_out
  42.6 1.7 %mix_other.1 = bf16[2048,1024]{1,0:T(8,128)(2,1)} custom-call(s32[1]{0:T(128)} %bitcast.place, bf16[2048,128]{1,0:T(8,128)(2,1)S(1)} %combine.1, bf16[128,512]{1,0:T(8,128)(2,1)S(1)} %collective-permute-done.9.slot_out, bf16[1024,512]{1,0:T(8,128)(2,1)S(1)} %get-tuple-element.33.rest, ...), custom_call_target="tpu_custom_call", output_to_operand_aliasing={{}: (4, {})} | custom-call | flops 268435456 | bytes 2621440 | tf_op jit(solution)/shard_map/mix_other/pallas_call | solution.py:406
  (13 shorter events, 0.1 us)
Async XLA Ops:
  3.7 1.5 %collective-permute-start = (bf16[128,640]{1,0:T(8,128)(2,1)S(1)}, bf16[128,640]{1,0:T(8,128)(2,1)S(1)}, u32[]{:S(2)}, u32[]{:S(2)}) collective-permute-start(bf16[128,640]{1,0:T(8,128)(2,1)S(1)} %get-tuple-element.24.after), channel_id=1, source_target_pairs={{0,1},{1,0},{2,3},{3,2},{4,5},{5,4},{6,7},{7,6},{8,9},{9,8},{10,11... | collective-permute-start | bytes 491528 | tf_op jit(solution)/shard_map/ppermute | solution.py:274
  4.2 20.2 %slice-start = ((s8[8388608]{0:T(1024)(128)(4,1)}), s8[4194304]{0:T(1024)(128)(4,1)S(1)}, s32[]{:S(2)}) async-start(s8[8388608]{0:T(1024)(128)(4,1)} %bitcast.3), calls=%async_computation.1 | async-start | bytes 8388608
  4.2 21.4 %slice-start.2 = ((s8[8388608]{0:T(1024)(128)(4,1)}), s8[4194304]{0:T(1024)(128)(4,1)S(1)}, s32[]{:S(2)}) async-start(s8[8388608]{0:T(1024)(128)(4,1)} %bitcast.5), calls=%async_computation.3 | async-start | bytes 8388608
  4.6 19.8 %slice-start.1 = ((s8[8388608]{0:T(1024)(128)(4,1)}), s8[4194304]{0:T(1024)(128)(4,1)S(1)}, s32[]{:S(2)}) async-start(s8[8388608]{0:T(1024)(128)(4,1)} %bitcast.3), calls=%async_computation.2 | async-start | bytes 8388608
  4.7 20.9 %slice-start.3 = ((s8[8388608]{0:T(1024)(128)(4,1)}), s8[4194304]{0:T(1024)(128)(4,1)S(1)}, s32[]{:S(2)}) async-start(s8[8388608]{0:T(1024)(128)(4,1)} %bitcast.5), calls=%async_computation.4 | async-start | bytes 8388608
  5.6 5.6 %collective-permute-start.1 = (bf16[32,640]{1,0:T(8,128)(2,1)S(1)}, bf16[32,640]{1,0:T(8,128)(2,1)S(1)}, u32[]{:S(2)}, u32[]{:S(2)}) collective-permute-start(bf16[32,640]{1,0:T(8,128)(2,1)S(1)} %get-tuple-element.26), channel_id=1, source_target_pairs={{0,8},{8,0},{16,24},{24,16},{1,9},{9,1},{17,25},{25,17},{2,10},{10... | collective-permute-start | bytes 122888 | tf_op jit(solution)/shard_map/ppermute | solution.py:274
  8.6 5.7 %collective-permute-start.2 = (bf16[32,640]{1,0:T(8,128)(2,1)S(1)}, bf16[32,640]{1,0:T(8,128)(2,1)S(1)}, u32[]{:S(2)}, u32[]{:S(2)}) collective-permute-start(bf16[32,640]{1,0:T(8,128)(2,1)S(1)} %get-tuple-element.27), channel_id=1, source_target_pairs={{0,16},{8,24},{16,0},{24,8},{1,17},{9,25},{17,1},{25,9},{2,18},{10... | collective-permute-start | bytes 122888 | tf_op jit(solution)/shard_map/ppermute | solution.py:274
  11.2 5.8 %collective-permute-start.3 = (bf16[32,640]{1,0:T(8,128)(2,1)S(1)}, bf16[32,640]{1,0:T(8,128)(2,1)S(1)}, u32[]{:S(2)}, u32[]{:S(2)}) collective-permute-start(bf16[32,640]{1,0:T(8,128)(2,1)S(1)} %get-tuple-element.28), channel_id=1, source_target_pairs={{0,24},{8,16},{16,8},{24,0},{1,25},{9,17},{17,9},{25,1},{2,26},{10... | collective-permute-start | bytes 122888 | tf_op jit(solution)/shard_map/ppermute | solution.py:274
  17.3 4.7 %collective-permute-start.6 = (bf16[16,640]{1,0:T(8,128)(2,1)S(1)}, bf16[16,640]{1,0:T(8,128)(2,1)S(1)}, u32[]{:S(2)}, u32[]{:S(2)}) collective-permute-start(bf16[16,640]{1,0:T(8,128)(2,1)S(1)} %get-tuple-element.30), channel_id=1, source_target_pairs={{0,6},{2,4},{4,2},{6,0},{1,7},{3,5},{5,3},{7,1},{8,14},{10,12},{12... | collective-permute-start | bytes 61448 | tf_op jit(solution)/shard_map/ppermute | solution.py:274
  19.8 3.8 %collective-permute-start.5 = (bf16[16,640]{1,0:T(8,128)(2,1)S(1)}, bf16[16,640]{1,0:T(8,128)(2,1)S(1)}, u32[]{:S(2)}, u32[]{:S(2)}) collective-permute-start(bf16[16,640]{1,0:T(8,128)(2,1)S(1)} %get-tuple-element.30), channel_id=1, source_target_pairs={{0,4},{2,6},{4,0},{6,2},{1,5},{3,7},{5,1},{7,3},{8,12},{10,14},{12... | collective-permute-start | bytes 61448 | tf_op jit(solution)/shard_map/ppermute | solution.py:274
  20.3 3.8 %collective-permute-start.4 = (bf16[16,640]{1,0:T(8,128)(2,1)S(1)}, bf16[16,640]{1,0:T(8,128)(2,1)S(1)}, u32[]{:S(2)}, u32[]{:S(2)}) collective-permute-start(bf16[16,640]{1,0:T(8,128)(2,1)S(1)} %get-tuple-element.29.after.refs_0_), channel_id=1, source_target_pairs={{0,2},{2,0},{4,6},{6,4},{1,3},{3,1},{5,7},{7,5},{8,10},{10,8},{12,... | collective-permute-start | bytes 61448 | tf_op jit(solution)/shard_map/ppermute | solution.py:274
  24.4 1.2 %collective-permute-start.7 = (bf16[16,512]{1,0:T(8,128)(2,1)S(1)}, bf16[16,512]{1,0:T(8,128)(2,1)S(1)}, u32[]{:S(2)}, u32[]{:S(2)}) collective-permute-start(bf16[16,512]{1,0:T(8,128)(2,1)S(1)} %finish.1.slot_in), channel_id=1, source_target_pairs={{0,1},{1,0},{2,3},{3,2},{4,5},{5,4},{6,7},{7,6},{8,9},{9,8},{10,11... | collective-permute-start | bytes 49160 | tf_op jit(solution)/shard_map/ppermute | solution.py:274
  26.8 1.2 %collective-permute-start.8 = (bf16[16,512]{1,0:T(8,128)(2,1)S(1)}, bf16[16,512]{1,0:T(8,128)(2,1)S(1)}, u32[]{:S(2)}, u32[]{:S(2)}) collective-permute-start(bf16[16,512]{1,0:T(8,128)(2,1)S(1)} %get-tuple-element.32.after), channel_id=1, source_target_pairs={{0,1},{1,0},{2,3},{3,2},{4,5},{5,4},{6,7},{7,6},{8,9},{9,8},{10,11... | collective-permute-start | bytes 49160 | tf_op jit(solution)/shard_map/ppermute | solution.py:274
  41.2 1.4 %collective-permute-start.9 = (bf16[128,512]{1,0:T(8,128)(2,1)S(1)}, bf16[128,512]{1,0:T(8,128)(2,1)S(1)}, u32[]{:S(2)}, u32[]{:S(2)}) collective-permute-start(bf16[128,512]{1,0:T(8,128)(2,1)S(1)} %bitcast.7), channel_id=1, source_target_pairs={{0,1},{1,0},{2,3},{3,2},{4,5},{5,4},{6,7},{7,6},{8,9},{9,8},{10,11... | collective-permute-start | bytes 393224 | tf_op jit(solution)/shard_map/ppermute | solution.py:274

commit v22 on v21

--- a/solution.py
+++ b/solution.py
@@ -10,7 +10,7 @@
 
 SLOT_PER = 4
 SIDE = 128
-CHUNK, TOGETHER = 256, 2
+CHUNK = 256
 F32 = jnp.float32
 BF16 = jnp.bfloat16
 VMEM = pl.BlockSpec(memory_space=pltpu.VMEM)
@@ -110,13 +110,14 @@
 
     table_copy.wait()
     high = None
-    for first in range(0, chunks, TOGETHER):
-        for copy in copies[first : first + TOGETHER]:
+    starts = [0] + list(range(1, chunks, 2))
+    for first, end in zip(starts, starts[1:] + [chunks]):
+        for copy in copies[first:end]:
             copy.wait()
-        parts = [dot(held[span, :], table[...]) for span in spans[first : first + TOGETHER]]
-        for part, span in zip(parts, spans[first:]):
+        parts = [dot(held[span, :], table[...]) for span in spans[first:end]]
+        for part, span in zip(parts, spans[first:end]):
             logits[span, :] = part
-        if first + TOGETHER < chunks:
+        if end < chunks:
             high = find_peak(parts, high)
     early_peak = jnp.max(high, axis=0, keepdims=True)
     early, early_total = weigh(0, [logits[span, :] for span in spans[:first]], early_peak)
@@ -138,8 +139,8 @@
 
 def own_sums_kernel(place, turned, held, side, after, keep):
     columns = column_half(pair_at(place), keep.shape[1])
-    early = held.shape[0] - TOGETHER * CHUNK
-    spans = (pl.ds(0, early), pl.ds(early, TOGETHER * CHUNK))
+    early = held.shape[0] - CHUNK
+    spans = (pl.ds(0, early), pl.ds(early, CHUNK))
     early, late = [dot(turned[:, span], held[span, columns]) for span in spans]
     keep[...] = early * side[:, 2:3] + late * side[:, 3:4]
 
@@ -331,8 +332,8 @@
         name="merge",
     )(place, *parts)
     plane = ("near", "rest")
-    mine = [send] + [move(send, plane, (0, r)) for r in range(1, rest)]
-    mine += [move(their, plane, (1, r)) for r in range(rest)]
+    mine = [move(their, plane, (1, r)) for r in reversed(range(rest))]
+    mine = [send] + [move(send, plane, (0, r)) for r in range(1, rest)] + mine
     combine = pl.pallas_call(
         combine_kernel,
         out_shape=jax.ShapeDtypeStruct((count, slots), BF16),

time: 44.5 us -> 44.5 us (level)
  transfers between devices with their start and end apart: 10 -> 10, of which waited for: 9 -> 8; matrix products, arithmetic and copies ran while one was open for 0% -> 0% of each run, Pallas kernels for 8% -> 8%
where the time goes in v22:
time: 44.5 us; the launch traced here: 44.3 us
  blocking collectives  13.1 us (29%)
  Pallas kernels  11.1 us (25%)
  starting transfers between devices  9.96 us (22%)
  waiting for transfers between devices  9.92 us (22%)
    all_to_all x1, blocking collectives, shards(): lax.all_to_all(partials, ('rest', 'far', 'near'), split_axis=0, concat_ax...  13.1 us
    ppermute x10, starting transfers between devices, move(): return lax.ppermute(value, axes, moves)  9.96 us
    ppermute x10, waiting for transfers between devices, move(): return lax.ppermute(value, axes, moves)  9.92 us
    pallas_call x1, Pallas kernels, shards(): pl.pallas_call(gather_kernel, out_shape=(jax.ShapeDtypeStruct((count, slo...  3.65 us
    pallas_call x1, Pallas kernels, shards(): pl.pallas_call(mix_other_kernel, out_shape=jax.ShapeDtypeStruct((count, m...  1.74 us
    pallas_call x1, Pallas kernels, shards(): pl.pallas_call(expert_kernel, out_shape=(jax.ShapeDtypeStruct((experts, r...  1.21 us
    pallas_call x1, Pallas kernels, shards(): pl.pallas_call(mix_kernel, out_shape=(pltpu.HBM((count, model), BF16), ja...  1.21 us
  transfers between devices with their start and end apart: 10, of which 8 were waited for; matrix products, arithmetic and copies ran while one was open for 0% of the time, Pallas kernels for 8%

profile of v22, /device:TPU:0, one launch (start us, length us, event | category | flops | bytes accessed | tf_op | source)
XLA Modules:
  0.0 44.3 jit_solution(13913250919601073343)
XLA Ops:
  0.0 3.7 %gather.1 = (f32[2048,128]{1,0:T(8,128)S(1)}, bf16[128,2048]{1,0:T(8,128)(2,1)S(1)}, bf16[2048,1024]{1,0:T(8,128)(2,1)S(1)}, f32[128,128]{1,0:T(8,128)S(1)}, bf16[128,640]{1,0:T(8,128)(2,1)S(1)}) custom-call(s32[1]{0:T(128)} %bitcast.place, bf16[2048,1024]{1,0:T(8,128)(2,1)} %tokens.1, bf16[1024,128]{1,0:T(8,128)(2,1)} %slot_params.1), custom_call_target="tpu_custom_call" | custom-call | tf_op jit(solution)/shard_map/gather/pallas_call | solution.py:291
  3.7 0.5 %collective-permute-start = (bf16[128,640]{1,0:T(8,128)(2,1)S(1)}, bf16[128,640]{1,0:T(8,128)(2,1)S(1)}, u32[]{:S(2)}, u32[]{:S(2)}) collective-permute-start(bf16[128,640]{1,0:T(8,128)(2,1)S(1)} %get-tuple-element.24.after), channel_id=1, source_target_pairs={{0,1},{1,0},{2,3},{3,2},{4,5},{5,4},{6,7},{7,6},{8,9},{9,8},{10,11... | collective-permute-start | bytes 491528 | tf_op jit(solution)/shard_map/ppermute | solution.py:275
  4.2 0.5 %own_sums.1.keep = f32[128,512]{1,0:T(8,128)S(1)} custom-call(s32[1]{0:T(128)} %bitcast.place, bf16[128,2048]{1,0:T(8,128)(2,1)S(1)} %get-tuple-element.21.turned, bf16[2048,1024]{1,0:T(8,128)(2,1)S(1)} %get-tuple-element.22.held, f32[128,128]{1,0:T(8,128)S(1)} %get-tuple-element.23.side, bf16[128,640]{1,0:T(8,128)(2,1)S(1)} %get-tuple-element.24.after), custom_call_target="tpu_custom_call" | custom-call | flops 268435456 | bytes 2621440 | tf_op jit(solution)/shard_map/own_sums/pallas_call | solution.py:307
  4.6 0.0 slice-start.1
  4.6 0.0 slice-start.3
  4.7 0.5 %collective-permute-done.received = bf16[128,640]{1,0:T(8,128)(2,1)S(1)} collective-permute-done((bf16[128,640]{1,0:T(8,128)(2,1)S(1)}, bf16[128,640]{1,0:T(8,128)(2,1)S(1)}, u32[]{:S(2)}, u32[]{:S(2)}) %collective-permute-start) | collective-permute-done | bytes 163872 | tf_op jit(solution)/shard_map/ppermute | solution.py:275
  5.2 0.4 pair.1
  5.6 3.0 %collective-permute-start.1 = (bf16[32,640]{1,0:T(8,128)(2,1)S(1)}, bf16[32,640]{1,0:T(8,128)(2,1)S(1)}, u32[]{:S(2)}, u32[]{:S(2)}) collective-permute-start(bf16[32,640]{1,0:T(8,128)(2,1)S(1)} %get-tuple-element.26), channel_id=1, source_target_pairs={{0,8},{8,0},{16,24},{24,16},{1,9},{9,1},{17,25},{25,17},{2,10},{10... | collective-permute-start | bytes 122888 | tf_op jit(solution)/shard_map/ppermute | solution.py:275
  8.6 2.6 %collective-permute-start.2 = (bf16[32,640]{1,0:T(8,128)(2,1)S(1)}, bf16[32,640]{1,0:T(8,128)(2,1)S(1)}, u32[]{:S(2)}, u32[]{:S(2)}) collective-permute-start(bf16[32,640]{1,0:T(8,128)(2,1)S(1)} %get-tuple-element.27), channel_id=1, source_target_pairs={{0,16},{8,24},{16,0},{24,8},{1,17},{9,25},{17,1},{25,9},{2,18},{10... | collective-permute-start | bytes 122888 | tf_op jit(solution)/shard_map/ppermute | solution.py:275
  11.2 0.0 collective-permute-start.3
  11.2 3.1 %collective-permute-done.2.refs_2_ = bf16[32,640]{1,0:T(8,128)(2,1)S(1)} collective-permute-done((bf16[32,640]{1,0:T(8,128)(2,1)S(1)}, bf16[32,640]{1,0:T(8,128)(2,1)S(1)}, u32[]{:S(2)}, u32[]{:S(2)}) %collective-permute-start.2) | collective-permute-done | bytes 40992 | tf_op jit(solution)/shard_map/ppermute | solution.py:275
  14.3 2.6 %collective-permute-done.3.refs_3_ = bf16[32,640]{1,0:T(8,128)(2,1)S(1)} collective-permute-done((bf16[32,640]{1,0:T(8,128)(2,1)S(1)}, bf16[32,640]{1,0:T(8,128)(2,1)S(1)}, u32[]{:S(2)}, u32[]{:S(2)}) %collective-permute-start.3) | collective-permute-done | bytes 40992 | tf_op jit(solution)/shard_map/ppermute | solution.py:275
  17.0 0.3 merge.1
  17.3 1.6 %collective-permute-start.6 = (bf16[16,640]{1,0:T(8,128)(2,1)S(1)}, bf16[16,640]{1,0:T(8,128)(2,1)S(1)}, u32[]{:S(2)}, u32[]{:S(2)}) collective-permute-start(bf16[16,640]{1,0:T(8,128)(2,1)S(1)} %get-tuple-element.30), channel_id=1, source_target_pairs={{0,4},{2,6},{4,0},{6,2},{1,5},{3,7},{5,1},{7,3},{8,12},{10,14},{12... | collective-permute-start | bytes 61448 | tf_op jit(solution)/shard_map/ppermute | solution.py:275
  18.8 1.5 %collective-permute-start.5 = (bf16[16,640]{1,0:T(8,128)(2,1)S(1)}, bf16[16,640]{1,0:T(8,128)(2,1)S(1)}, u32[]{:S(2)}, u32[]{:S(2)}) collective-permute-start(bf16[16,640]{1,0:T(8,128)(2,1)S(1)} %get-tuple-element.30), channel_id=1, source_target_pairs={{0,6},{2,4},{4,2},{6,0},{1,7},{3,5},{5,3},{7,1},{8,14},{10,12},{12... | collective-permute-start | bytes 61448 | tf_op jit(solution)/shard_map/ppermute | solution.py:275
  20.3 0.5 %collective-permute-start.4 = (bf16[16,640]{1,0:T(8,128)(2,1)S(1)}, bf16[16,640]{1,0:T(8,128)(2,1)S(1)}, u32[]{:S(2)}, u32[]{:S(2)}) collective-permute-start(bf16[16,640]{1,0:T(8,128)(2,1)S(1)} %get-tuple-element.29.after.refs_0_), channel_id=1, source_target_pairs={{0,2},{2,0},{4,6},{6,4},{1,3},{3,1},{5,7},{7,5},{8,10},{10,8},{12,... | collective-permute-start | bytes 61448 | tf_op jit(solution)/shard_map/ppermute | solution.py:275
  20.8 0.6 %combine.1 = bf16[2048,128]{1,0:T(8,128)(2,1)S(1)} custom-call(f32[2048,128]{1,0:T(8,128)S(1)} %get-tuple-element.20.logits, bf16[16,640]{1,0:T(8,128)(2,1)S(1)} %get-tuple-element.29.after.refs_0_), custom_call_target="tpu_custom_call" | custom-call | flops 2097152 | bytes 1572864 | tf_op jit(solution)/shard_map/combine/pallas_call | solution.py:337
  21.5 2.0 %collective-permute-done.5.refs_2_ = bf16[16,640]{1,0:T(8,128)(2,1)S(1)} collective-permute-done((bf16[16,640]{1,0:T(8,128)(2,1)S(1)}, bf16[16,640]{1,0:T(8,128)(2,1)S(1)}, u32[]{:S(2)}, u32[]{:S(2)}) %collective-permute-start.5) | collective-permute-done | bytes 20512 | tf_op jit(solution)/shard_map/ppermute | solution.py:275
  23.5 0.6 %collective-permute-done.4.refs_1_ = bf16[16,640]{1,0:T(8,128)(2,1)S(1)} collective-permute-done((bf16[16,640]{1,0:T(8,128)(2,1)S(1)}, bf16[16,640]{1,0:T(8,128)(2,1)S(1)}, u32[]{:S(2)}, u32[]{:S(2)}) %collective-permute-start.4) | collective-permute-done | bytes 20512 | tf_op jit(solution)/shard_map/ppermute | solution.py:275
  24.1 0.2 finish.1.slot_in
  24.3 0.1 collective-permute-start.7
  24.4 0.7 %first_product.1.first = f32[4,16,1024]{2,1,0:T(8,128)S(1)} custom-call(s32[1]{0:T(128)} %bitcast.place, bf16[16,512]{1,0:T(8,128)(2,1)S(1)} %finish.1.slot_in, bf16[4,1024,1024]{2,1,0:T(8,128)(2,1)S(1)} %bitcast.4), custom_call_target="tpu_custom_call" | custom-call | flops 67108864 | bytes 4194304 | tf_op jit(solution)/shard_map/first_product/pallas_call | solution.py:356
  25.1 0.5 %collective-permute-done.7.slot_in = bf16[16,512]{1,0:T(8,128)(2,1)S(1)} collective-permute-done((bf16[16,512]{1,0:T(8,128)(2,1)S(1)}, bf16[16,512]{1,0:T(8,128)(2,1)S(1)}, u32[]{:S(2)}, u32[]{:S(2)}) %collective-permute-start.7) | collective-permute-done | bytes 16416 | tf_op jit(solution)/shard_map/ppermute | solution.py:275
  25.6 1.2 %experts.1 = (bf16[4,16,1024]{2,1,0:T(8,128)(2,1)S(1)}, bf16[16,512]{1,0:T(8,128)(2,1)S(1)}) custom-call(s32[1]{0:T(128)} %bitcast.place, bf16[16,512]{1,0:T(8,128)(2,1)S(1)} %collective-permute-done.7.slot_in, f32[4,16,1024]{2,1,0:T(8,128)S(1)} %first_product.1.first, bf16[4,1024,1024]{2,1,0:T(8,128)(2,1)S(1)} %bitcast.4, bf16[4,1024,1024]{2,1,0:T(8,128)(2,1)S(1)} %bitcast.6), custom_call_target="tpu_custom_call" | custom-call | tf_op jit(solution)/shard_map/experts/pallas_call | solution.py:365
  26.8 0.2 collective-permute-start.8
  27.0 0.7 %own.1 = f32[16,512]{1,0:T(8,128)S(1)} custom-call(s32[1]{0:T(128)} %bitcast.place, bf16[4,16,1024]{2,1,0:T(8,128)(2,1)S(1)} %get-tuple-element.31.hidden, bf16[4,1024,1024]{2,1,0:T(8,128)(2,1)S(1)} %bitcast.6, bf16[16,512]{1,0:T(8,128)(2,1)S(1)} %get-tuple-element.32.after), custom_call_target="tpu_custom_call" | custom-call | flops 67108864 | bytes 4194304 | tf_op jit(solution)/shard_map/own/pallas_call | solution.py:377
  27.6 0.4 collective-permute-done.8
  28.0 13.1 %all_to_all.5 = bf16[16,16,512]{2,1,0:T(8,128)(2,1)S(1)} all-to-all(bf16[16,16,512]{2,1,0:T(8,128)(2,1)S(1)} %broadcast_in_dim.3), channel_id=1, replica_groups=mesh['far'=4,'near'=2,'rest'=2,'pair'=2] {'rest','far','near'}, dimensions={0} | all-to-all | bytes 524288 | tf_op jit(solution)/shard_map/all_to_all | solution.py:389
  41.1 0.1 collective-permute-start.9
  41.2 1.2 %mix.1 = (bf16[2048,1024]{1,0:T(8,128)(2,1)}, bf16[1024,512]{1,0:T(8,128)(2,1)S(1)}) custom-call(s32[1]{0:T(128)} %bitcast.place, bf16[2048,128]{1,0:T(8,128)(2,1)S(1)} %combine.1, bf16[128,512]{1,0:T(8,128)(2,1)S(1)} %bitcast.8), custom_call_target="tpu_custom_call" | custom-call | flops 268435456 | bytes 2621440 | tf_op jit(solution)/shard_map/mix/pallas_call | solution.py:394
  42.4 0.1 collective-permute-done.9.slot_out
  42.5 1.7 %mix_other.1 = bf16[2048,1024]{1,0:T(8,128)(2,1)} custom-call(s32[1]{0:T(128)} %bitcast.place, bf16[2048,128]{1,0:T(8,128)(2,1)S(1)} %combine.1, bf16[128,512]{1,0:T(8,128)(2,1)S(1)} %collective-permute-done.9.slot_out, bf16[1024,512]{1,0:T(8,128)(2,1)S(1)} %get-tuple-element.33.rest, ...), custom_call_target="tpu_custom_call", output_to_operand_aliasing={{}: (4, {})} | custom-call | flops 268435456 | bytes 2621440 | tf_op jit(solution)/shard_map/mix_other/pallas_call | solution.py:407
  (13 shorter events, 0.1 us)
Async XLA Ops:
  3.7 1.5 %collective-permute-start = (bf16[128,640]{1,0:T(8,128)(2,1)S(1)}, bf16[128,640]{1,0:T(8,128)(2,1)S(1)}, u32[]{:S(2)}, u32[]{:S(2)}) collective-permute-start(bf16[128,640]{1,0:T(8,128)(2,1)S(1)} %get-tuple-element.24.after), channel_id=1, source_target_pairs={{0,1},{1,0},{2,3},{3,2},{4,5},{5,4},{6,7},{7,6},{8,9},{9,8},{10,11... | collective-permute-start | bytes 491528 | tf_op jit(solution)/shard_map/ppermute | solution.py:275
  4.2 20.2 %slice-start = ((s8[8388608]{0:T(1024)(128)(4,1)}), s8[4194304]{0:T(1024)(128)(4,1)S(1)}, s32[]{:S(2)}) async-start(s8[8388608]{0:T(1024)(128)(4,1)} %bitcast.3), calls=%async_computation.1 | async-start | bytes 8388608
  4.2 21.4 %slice-start.2 = ((s8[8388608]{0:T(1024)(128)(4,1)}), s8[4194304]{0:T(1024)(128)(4,1)S(1)}, s32[]{:S(2)}) async-start(s8[8388608]{0:T(1024)(128)(4,1)} %bitcast.5), calls=%async_computation.3 | async-start | bytes 8388608
  4.6 19.8 %slice-start.1 = ((s8[8388608]{0:T(1024)(128)(4,1)}), s8[4194304]{0:T(1024)(128)(4,1)S(1)}, s32[]{:S(2)}) async-start(s8[8388608]{0:T(1024)(128)(4,1)} %bitcast.3), calls=%async_computation.2 | async-start | bytes 8388608
  4.6 20.9 %slice-start.3 = ((s8[8388608]{0:T(1024)(128)(4,1)}), s8[4194304]{0:T(1024)(128)(4,1)S(1)}, s32[]{:S(2)}) async-start(s8[8388608]{0:T(1024)(128)(4,1)} %bitcast.5), calls=%async_computation.4 | async-start | bytes 8388608
  5.6 5.6 %collective-permute-start.1 = (bf16[32,640]{1,0:T(8,128)(2,1)S(1)}, bf16[32,640]{1,0:T(8,128)(2,1)S(1)}, u32[]{:S(2)}, u32[]{:S(2)}) collective-permute-start(bf16[32,640]{1,0:T(8,128)(2,1)S(1)} %get-tuple-element.26), channel_id=1, source_target_pairs={{0,8},{8,0},{16,24},{24,16},{1,9},{9,1},{17,25},{25,17},{2,10},{10... | collective-permute-start | bytes 122888 | tf_op jit(solution)/shard_map/ppermute | solution.py:275
  8.6 5.7 %collective-permute-start.2 = (bf16[32,640]{1,0:T(8,128)(2,1)S(1)}, bf16[32,640]{1,0:T(8,128)(2,1)S(1)}, u32[]{:S(2)}, u32[]{:S(2)}) collective-permute-start(bf16[32,640]{1,0:T(8,128)(2,1)S(1)} %get-tuple-element.27), channel_id=1, source_target_pairs={{0,16},{8,24},{16,0},{24,8},{1,17},{9,25},{17,1},{25,9},{2,18},{10... | collective-permute-start | bytes 122888 | tf_op jit(solution)/shard_map/ppermute | solution.py:275
  11.2 5.8 %collective-permute-start.3 = (bf16[32,640]{1,0:T(8,128)(2,1)S(1)}, bf16[32,640]{1,0:T(8,128)(2,1)S(1)}, u32[]{:S(2)}, u32[]{:S(2)}) collective-permute-start(bf16[32,640]{1,0:T(8,128)(2,1)S(1)} %get-tuple-element.28), channel_id=1, source_target_pairs={{0,24},{8,16},{16,8},{24,0},{1,25},{9,17},{17,9},{25,1},{2,26},{10... | collective-permute-start | bytes 122888 | tf_op jit(solution)/shard_map/ppermute | solution.py:275
  17.3 4.2 %collective-permute-start.6 = (bf16[16,640]{1,0:T(8,128)(2,1)S(1)}, bf16[16,640]{1,0:T(8,128)(2,1)S(1)}, u32[]{:S(2)}, u32[]{:S(2)}) collective-permute-start(bf16[16,640]{1,0:T(8,128)(2,1)S(1)} %get-tuple-element.30), channel_id=1, source_target_pairs={{0,4},{2,6},{4,0},{6,2},{1,5},{3,7},{5,1},{7,3},{8,12},{10,14},{12... | collective-permute-start | bytes 61448 | tf_op jit(solution)/shard_map/ppermute | solution.py:275
  18.8 4.7 %collective-permute-start.5 = (bf16[16,640]{1,0:T(8,128)(2,1)S(1)}, bf16[16,640]{1,0:T(8,128)(2,1)S(1)}, u32[]{:S(2)}, u32[]{:S(2)}) collective-permute-start(bf16[16,640]{1,0:T(8,128)(2,1)S(1)} %get-tuple-element.30), channel_id=1, source_target_pairs={{0,6},{2,4},{4,2},{6,0},{1,7},{3,5},{5,3},{7,1},{8,14},{10,12},{12... | collective-permute-start | bytes 61448 | tf_op jit(solution)/shard_map/ppermute | solution.py:275
  20.3 3.8 %collective-permute-start.4 = (bf16[16,640]{1,0:T(8,128)(2,1)S(1)}, bf16[16,640]{1,0:T(8,128)(2,1)S(1)}, u32[]{:S(2)}, u32[]{:S(2)}) collective-permute-start(bf16[16,640]{1,0:T(8,128)(2,1)S(1)} %get-tuple-element.29.after.refs_0_), channel_id=1, source_target_pairs={{0,2},{2,0},{4,6},{6,4},{1,3},{3,1},{5,7},{7,5},{8,10},{10,8},{12,... | collective-permute-start | bytes 61448 | tf_op jit(solution)/shard_map/ppermute | solution.py:275
  24.3 1.2 %collective-permute-start.7 = (bf16[16,512]{1,0:T(8,128)(2,1)S(1)}, bf16[16,512]{1,0:T(8,128)(2,1)S(1)}, u32[]{:S(2)}, u32[]{:S(2)}) collective-permute-start(bf16[16,512]{1,0:T(8,128)(2,1)S(1)} %finish.1.slot_in), channel_id=1, source_target_pairs={{0,1},{1,0},{2,3},{3,2},{4,5},{5,4},{6,7},{7,6},{8,9},{9,8},{10,11... | collective-permute-start | bytes 49160 | tf_op jit(solution)/shard_map/ppermute | solution.py:275
  26.8 1.2 %collective-permute-start.8 = (bf16[16,512]{1,0:T(8,128)(2,1)S(1)}, bf16[16,512]{1,0:T(8,128)(2,1)S(1)}, u32[]{:S(2)}, u32[]{:S(2)}) collective-permute-start(bf16[16,512]{1,0:T(8,128)(2,1)S(1)} %get-tuple-element.32.after), channel_id=1, source_target_pairs={{0,1},{1,0},{2,3},{3,2},{4,5},{5,4},{6,7},{7,6},{8,9},{9,8},{10,11... | collective-permute-start | bytes 49160 | tf_op jit(solution)/shard_map/ppermute | solution.py:275
  41.1 1.4 %collective-permute-start.9 = (bf16[128,512]{1,0:T(8,128)(2,1)S(1)}, bf16[128,512]{1,0:T(8,128)(2,1)S(1)}, u32[]{:S(2)}, u32[]{:S(2)}) collective-permute-start(bf16[128,512]{1,0:T(8,128)(2,1)S(1)} %bitcast.7), channel_id=1, source_target_pairs={{0,1},{1,0},{2,3},{3,2},{4,5},{5,4},{6,7},{7,6},{8,9},{9,8},{10,11... | collective-permute-start | bytes 393224 | tf_op jit(solution)/shard_map/ppermute | solution.py:275

commit v23 on v22

--- a/solution.py
+++ b/solution.py
@@ -383,12 +383,13 @@
         compiler_params=params(8),
         name="own",
     )(place, hidden, expert_out, send)
-    partial = (keep + received.astype(F32)).astype(BF16)
-    groups = far * near
-    partials = jnp.broadcast_to(partial, (groups * rest, rows, half))
-    partials = lax.all_to_all(partials, ("rest", "far", "near"), split_axis=0, concat_axis=0, tiled=True)
-    slot_out = jnp.sum(partials.reshape(rest, groups, rows, half).astype(F32), axis=0)
-    slot_out = slot_out.astype(BF16).reshape(slots, half)
+    partial = keep + received.astype(F32)
+    travelling = partial.astype(BF16)
+    for r in range(1, rest):
+        partial = partial + move(travelling, ("rest",), (r,)).astype(F32)
+    block = jnp.broadcast_to(partial.astype(BF16), (far * near, rows, half))
+    slot_out = lax.all_to_all(block, ("far", "near"), split_axis=0, concat_axis=0, tiled=True)
+    slot_out = slot_out.reshape(slots, half)
     other = swap_pair(slot_out)
     done, blocks = count // 2, 8
     mixed, left = pl.pallas_call(

time: 44.5 us -> 45 us (1.011)
  blocking collectives: 13.1 us -> 10 us
  waiting for transfers between devices: 9.92 us -> 12.7 us
  starting transfers between devices: 9.96 us -> 10.8 us
    all_to_all x1, blocking collectives: 13.1 us -> 10 us  [shards(): lax.all_to_all(block, ('far', 'near'), split_axis=0, concat_axis=0, tiled...]
    ppermute x10 -> x11, waiting for transfers between devices: 9.92 us -> 12.7 us  [move(): return lax.ppermute(value, axes, moves)]
    ppermute x10 -> x11, starting transfers between devices: 9.96 us -> 10.8 us  [move(): return lax.ppermute(value, axes, moves)]
  transfers between devices with their start and end apart: 10 -> 11, of which waited for: 8 -> 9; matrix products, arithmetic and copies ran while one was open for 0% -> 0% of each run, Pallas kernels for 8% -> 8%
where the time goes in v23:
time: 45 us; the launch traced here: 44.8 us
  waiting for transfers between devices  12.7 us (28%)
  Pallas kernels  11.1 us (25%)
  starting transfers between devices  10.8 us (24%)
  blocking collectives  10 us (22%)
    ppermute x11, waiting for transfers between devices, move(): return lax.ppermute(value, axes, moves)  12.7 us
    ppermute x11, starting transfers between devices, move(): return lax.ppermute(value, axes, moves)  10.8 us
    all_to_all x1, blocking collectives, shards(): lax.all_to_all(block, ('far', 'near'), split_axis=0, concat_axis=0, tiled...  10 us
    pallas_call x1, Pallas kernels, shards(): pl.pallas_call(gather_kernel, out_shape=(jax.ShapeDtypeStruct((count, slo...  3.65 us
    pallas_call x1, Pallas kernels, shards(): pl.pallas_call(mix_other_kernel, out_shape=jax.ShapeDtypeStruct((count, m...  1.74 us
    pallas_call x1, Pallas kernels, shards(): pl.pallas_call(expert_kernel, out_shape=(jax.ShapeDtypeStruct((experts, r...  1.21 us
    pallas_call x1, Pallas kernels, shards(): pl.pallas_call(mix_kernel, out_shape=(pltpu.HBM((count, model), BF16), ja...  1.21 us
  transfers between devices with their start and end apart: 11, of which 9 were waited for; matrix products, arithmetic and copies ran while one was open for 0% of the time, Pallas kernels for 8%

profile of v23, /device:TPU:0, one launch (start us, length us, event | category | flops | bytes accessed | tf_op | source)
XLA Modules:
  0.0 44.8 jit_solution(9917265682619438561)
XLA Ops:
  0.0 3.7 %gather.1 = (f32[2048,128]{1,0:T(8,128)S(1)}, bf16[128,2048]{1,0:T(8,128)(2,1)S(1)}, bf16[2048,1024]{1,0:T(8,128)(2,1)S(1)}, f32[128,128]{1,0:T(8,128)S(1)}, bf16[128,640]{1,0:T(8,128)(2,1)S(1)}) custom-call(s32[1]{0:T(128)} %bitcast.place, bf16[2048,1024]{1,0:T(8,128)(2,1)} %tokens.1, bf16[1024,128]{1,0:T(8,128)(2,1)} %slot_params.1), custom_call_target="tpu_custom_call" | custom-call | tf_op jit(solution)/shard_map/gather/pallas_call | solution.py:291
  3.7 0.5 %collective-permute-start = (bf16[128,640]{1,0:T(8,128)(2,1)S(1)}, bf16[128,640]{1,0:T(8,128)(2,1)S(1)}, u32[]{:S(2)}, u32[]{:S(2)}) collective-permute-start(bf16[128,640]{1,0:T(8,128)(2,1)S(1)} %get-tuple-element.24.after), channel_id=1, source_target_pairs={{0,1},{1,0},{2,3},{3,2},{4,5},{5,4},{6,7},{7,6},{8,9},{9,8},{10,11... | collective-permute-start | bytes 491528 | tf_op jit(solution)/shard_map/ppermute | solution.py:275
  4.2 0.5 %own_sums.1.keep = f32[128,512]{1,0:T(8,128)S(1)} custom-call(s32[1]{0:T(128)} %bitcast.place, bf16[128,2048]{1,0:T(8,128)(2,1)S(1)} %get-tuple-element.21.turned, bf16[2048,1024]{1,0:T(8,128)(2,1)S(1)} %get-tuple-element.22.held, f32[128,128]{1,0:T(8,128)S(1)} %get-tuple-element.23.side, bf16[128,640]{1,0:T(8,128)(2,1)S(1)} %get-tuple-element.24.after), custom_call_target="tpu_custom_call" | custom-call | flops 268435456 | bytes 2621440 | tf_op jit(solution)/shard_map/own_sums/pallas_call | solution.py:307
  4.6 0.0 slice-start.1
  4.6 0.0 slice-start.3
  4.7 0.5 %collective-permute-done.received = bf16[128,640]{1,0:T(8,128)(2,1)S(1)} collective-permute-done((bf16[128,640]{1,0:T(8,128)(2,1)S(1)}, bf16[128,640]{1,0:T(8,128)(2,1)S(1)}, u32[]{:S(2)}, u32[]{:S(2)}) %collective-permute-start) | collective-permute-done | bytes 163872 | tf_op jit(solution)/shard_map/ppermute | solution.py:275
  5.2 0.4 pair.1
  5.6 3.0 %collective-permute-start.1 = (bf16[32,640]{1,0:T(8,128)(2,1)S(1)}, bf16[32,640]{1,0:T(8,128)(2,1)S(1)}, u32[]{:S(2)}, u32[]{:S(2)}) collective-permute-start(bf16[32,640]{1,0:T(8,128)(2,1)S(1)} %get-tuple-element.26), channel_id=1, source_target_pairs={{0,8},{8,0},{16,24},{24,16},{1,9},{9,1},{17,25},{25,17},{2,10},{10... | collective-permute-start | bytes 122888 | tf_op jit(solution)/shard_map/ppermute | solution.py:275
  8.6 2.6 %collective-permute-start.2 = (bf16[32,640]{1,0:T(8,128)(2,1)S(1)}, bf16[32,640]{1,0:T(8,128)(2,1)S(1)}, u32[]{:S(2)}, u32[]{:S(2)}) collective-permute-start(bf16[32,640]{1,0:T(8,128)(2,1)S(1)} %get-tuple-element.27), channel_id=1, source_target_pairs={{0,16},{8,24},{16,0},{24,8},{1,17},{9,25},{17,1},{25,9},{2,18},{10... | collective-permute-start | bytes 122888 | tf_op jit(solution)/shard_map/ppermute | solution.py:275
  11.2 3.1 %collective-permute-done.2.refs_2_ = bf16[32,640]{1,0:T(8,128)(2,1)S(1)} collective-permute-done((bf16[32,640]{1,0:T(8,128)(2,1)S(1)}, bf16[32,640]{1,0:T(8,128)(2,1)S(1)}, u32[]{:S(2)}, u32[]{:S(2)}) %collective-permute-start.2) | collective-permute-done | bytes 40992 | tf_op jit(solution)/shard_map/ppermute | solution.py:275
  14.3 2.6 %collective-permute-done.3.refs_3_ = bf16[32,640]{1,0:T(8,128)(2,1)S(1)} collective-permute-done((bf16[32,640]{1,0:T(8,128)(2,1)S(1)}, bf16[32,640]{1,0:T(8,128)(2,1)S(1)}, u32[]{:S(2)}, u32[]{:S(2)}) %collective-permute-start.3) | collective-permute-done | bytes 40992 | tf_op jit(solution)/shard_map/ppermute | solution.py:275
  17.0 0.3 merge.1
  17.3 1.6 %collective-permute-start.6 = (bf16[16,640]{1,0:T(8,128)(2,1)S(1)}, bf16[16,640]{1,0:T(8,128)(2,1)S(1)}, u32[]{:S(2)}, u32[]{:S(2)}) collective-permute-start(bf16[16,640]{1,0:T(8,128)(2,1)S(1)} %get-tuple-element.30), channel_id=1, source_target_pairs={{0,4},{2,6},{4,0},{6,2},{1,5},{3,7},{5,1},{7,3},{8,12},{10,14},{12... | collective-permute-start | bytes 61448 | tf_op jit(solution)/shard_map/ppermute | solution.py:275
  18.8 1.5 %collective-permute-start.5 = (bf16[16,640]{1,0:T(8,128)(2,1)S(1)}, bf16[16,640]{1,0:T(8,128)(2,1)S(1)}, u32[]{:S(2)}, u32[]{:S(2)}) collective-permute-start(bf16[16,640]{1,0:T(8,128)(2,1)S(1)} %get-tuple-element.30), channel_id=1, source_target_pairs={{0,6},{2,4},{4,2},{6,0},{1,7},{3,5},{5,3},{7,1},{8,14},{10,12},{12... | collective-permute-start | bytes 61448 | tf_op jit(solution)/shard_map/ppermute | solution.py:275
  20.3 0.5 %collective-permute-start.4 = (bf16[16,640]{1,0:T(8,128)(2,1)S(1)}, bf16[16,640]{1,0:T(8,128)(2,1)S(1)}, u32[]{:S(2)}, u32[]{:S(2)}) collective-permute-start(bf16[16,640]{1,0:T(8,128)(2,1)S(1)} %get-tuple-element.29.after.refs_0_), channel_id=1, source_target_pairs={{0,2},{2,0},{4,6},{6,4},{1,3},{3,1},{5,7},{7,5},{8,10},{10,8},{12,... | collective-permute-start | bytes 61448 | tf_op jit(solution)/shard_map/ppermute | solution.py:275
  20.8 0.6 %combine.1 = bf16[2048,128]{1,0:T(8,128)(2,1)S(1)} custom-call(f32[2048,128]{1,0:T(8,128)S(1)} %get-tuple-element.20.logits, bf16[16,640]{1,0:T(8,128)(2,1)S(1)} %get-tuple-element.29.after.refs_0_), custom_call_target="tpu_custom_call" | custom-call | flops 2097152 | bytes 1572864 | tf_op jit(solution)/shard_map/combine/pallas_call | solution.py:337
  21.5 2.0 %collective-permute-done.5.refs_2_ = bf16[16,640]{1,0:T(8,128)(2,1)S(1)} collective-permute-done((bf16[16,640]{1,0:T(8,128)(2,1)S(1)}, bf16[16,640]{1,0:T(8,128)(2,1)S(1)}, u32[]{:S(2)}, u32[]{:S(2)}) %collective-permute-start.5) | collective-permute-done | bytes 20512 | tf_op jit(solution)/shard_map/ppermute | solution.py:275
  23.5 0.6 %collective-permute-done.4.refs_1_ = bf16[16,640]{1,0:T(8,128)(2,1)S(1)} collective-permute-done((bf16[16,640]{1,0:T(8,128)(2,1)S(1)}, bf16[16,640]{1,0:T(8,128)(2,1)S(1)}, u32[]{:S(2)}, u32[]{:S(2)}) %collective-permute-start.4) | collective-permute-done | bytes 20512 | tf_op jit(solution)/shard_map/ppermute | solution.py:275
  24.1 0.2 finish.1.slot_in
  24.3 0.1 collective-permute-start.7
  24.4 0.7 %first_product.1.first = f32[4,16,1024]{2,1,0:T(8,128)S(1)} custom-call(s32[1]{0:T(128)} %bitcast.place, bf16[16,512]{1,0:T(8,128)(2,1)S(1)} %finish.1.slot_in, bf16[4,1024,1024]{2,1,0:T(8,128)(2,1)S(1)} %bitcast.3), custom_call_target="tpu_custom_call" | custom-call | flops 67108864 | bytes 4194304 | tf_op jit(solution)/shard_map/first_product/pallas_call | solution.py:356
  25.1 0.5 %collective-permute-done.7.slot_in = bf16[16,512]{1,0:T(8,128)(2,1)S(1)} collective-permute-done((bf16[16,512]{1,0:T(8,128)(2,1)S(1)}, bf16[16,512]{1,0:T(8,128)(2,1)S(1)}, u32[]{:S(2)}, u32[]{:S(2)}) %collective-permute-start.7) | collective-permute-done | bytes 16416 | tf_op jit(solution)/shard_map/ppermute | solution.py:275
  25.6 1.2 %experts.1 = (bf16[4,16,1024]{2,1,0:T(8,128)(2,1)S(1)}, bf16[16,512]{1,0:T(8,128)(2,1)S(1)}) custom-call(s32[1]{0:T(128)} %bitcast.place, bf16[16,512]{1,0:T(8,128)(2,1)S(1)} %collective-permute-done.7.slot_in, f32[4,16,1024]{2,1,0:T(8,128)S(1)} %first_product.1.first, bf16[4,1024,1024]{2,1,0:T(8,128)(2,1)S(1)} %bitcast.3, bf16[4,1024,1024]{2,1,0:T(8,128)(2,1)S(1)} %bitcast.5), custom_call_target="tpu_custom_call" | custom-call | tf_op jit(solution)/shard_map/experts/pallas_call | solution.py:365
  26.8 0.2 collective-permute-start.8
  27.0 0.7 %own.1 = f32[16,512]{1,0:T(8,128)S(1)} custom-call(s32[1]{0:T(128)} %bitcast.place, bf16[4,16,1024]{2,1,0:T(8,128)(2,1)S(1)} %get-tuple-element.31.hidden, bf16[4,1024,1024]{2,1,0:T(8,128)(2,1)S(1)} %bitcast.5, bf16[16,512]{1,0:T(8,128)(2,1)S(1)} %get-tuple-element.32.after), custom_call_target="tpu_custom_call" | custom-call | flops 67108864 | bytes 4194304 | tf_op jit(solution)/shard_map/own/pallas_call | solution.py:377
  27.6 0.4 collective-permute-done.8
  28.0 0.9 %collective-permute-start.9 = (bf16[16,512]{1,0:T(8,128)(2,1)S(1)}, bf16[16,512]{1,0:T(8,128)(2,1)S(1)}, u32[]{:S(2)}, u32[]{:S(2)}) collective-permute-start(bf16[16,512]{1,0:T(8,128)(2,1)S(1)} %fusion), channel_id=1, source_target_pairs={{0,2},{2,0},{1,3},{3,1},{4,6},{6,4},{5,7},{7,5},{8,10},{10,8},{9,1... | collective-permute-start | bytes 49160 | tf_op jit(solution)/shard_map/ppermute | solution.py:275
  28.9 2.8 %collective-permute-done.9 = bf16[16,512]{1,0:T(8,128)(2,1)S(1)} collective-permute-done((bf16[16,512]{1,0:T(8,128)(2,1)S(1)}, bf16[16,512]{1,0:T(8,128)(2,1)S(1)}, u32[]{:S(2)}, u32[]{:S(2)}) %collective-permute-start.9) | collective-permute-done | bytes 16416 | tf_op jit(solution)/shard_map/ppermute | solution.py:275
  31.8 10.0 %all_to_all.5 = bf16[8,16,512]{2,1,0:T(8,128)(2,1)S(1)} all-to-all(bf16[8,16,512]{2,1,0:T(8,128)(2,1)S(1)} %broadcast_in_dim.3), channel_id=1, replica_groups=mesh['far'=4,'near'=2,'rest'=2,'pair'=2] {'far','near'}, dimensions={0} | all-to-all | bytes 262144 | tf_op jit(solution)/shard_map/all_to_all | solution.py:391
  41.8 1.2 %mix.1 = (bf16[2048,1024]{1,0:T(8,128)(2,1)}, bf16[1024,512]{1,0:T(8,128)(2,1)S(1)}) custom-call(s32[1]{0:T(128)} %bitcast.place, bf16[2048,128]{1,0:T(8,128)(2,1)S(1)} %combine.1, bf16[128,512]{1,0:T(8,128)(2,1)S(1)} %bitcast.7), custom_call_target="tpu_custom_call" | custom-call | flops 268435456 | bytes 2621440 | tf_op jit(solution)/shard_map/mix/pallas_call | solution.py:395
  43.0 0.1 collective-permute-done.10.slot_out
  43.1 1.7 %mix_other.1 = bf16[2048,1024]{1,0:T(8,128)(2,1)} custom-call(s32[1]{0:T(128)} %bitcast.place, bf16[2048,128]{1,0:T(8,128)(2,1)S(1)} %combine.1, bf16[128,512]{1,0:T(8,128)(2,1)S(1)} %collective-permute-done.10.slot_out, bf16[1024,512]{1,0:T(8,128)(2,1)S(1)} %get-tuple-element.33.rest, ...), custom_call_target="tpu_custom_call", output_to_operand_aliasing={{}: (4, {})} | custom-call | flops 268435456 | bytes 2621440 | tf_op jit(solution)/shard_map/mix_other/pallas_call | solution.py:408
  (15 shorter events, 0.0 us)
Async XLA Ops:
  3.7 1.5 %collective-permute-start = (bf16[128,640]{1,0:T(8,128)(2,1)S(1)}, bf16[128,640]{1,0:T(8,128)(2,1)S(1)}, u32[]{:S(2)}, u32[]{:S(2)}) collective-permute-start(bf16[128,640]{1,0:T(8,128)(2,1)S(1)} %get-tuple-element.24.after), channel_id=1, source_target_pairs={{0,1},{1,0},{2,3},{3,2},{4,5},{5,4},{6,7},{7,6},{8,9},{9,8},{10,11... | collective-permute-start | bytes 491528 | tf_op jit(solution)/shard_map/ppermute | solution.py:275
  4.2 20.2 %slice-start = ((s8[8388608]{0:T(1024)(128)(4,1)}), s8[4194304]{0:T(1024)(128)(4,1)S(1)}, s32[]{:S(2)}) async-start(s8[8388608]{0:T(1024)(128)(4,1)} %bitcast.2), calls=%async_computation.1 | async-start | bytes 8388608
  4.2 21.4 %slice-start.2 = ((s8[8388608]{0:T(1024)(128)(4,1)}), s8[4194304]{0:T(1024)(128)(4,1)S(1)}, s32[]{:S(2)}) async-start(s8[8388608]{0:T(1024)(128)(4,1)} %bitcast.4), calls=%async_computation.3 | async-start | bytes 8388608
  4.6 19.8 %slice-start.1 = ((s8[8388608]{0:T(1024)(128)(4,1)}), s8[4194304]{0:T(1024)(128)(4,1)S(1)}, s32[]{:S(2)}) async-start(s8[8388608]{0:T(1024)(128)(4,1)} %bitcast.2), calls=%async_computation.2 | async-start | bytes 8388608
  4.6 20.9 %slice-start.3 = ((s8[8388608]{0:T(1024)(128)(4,1)}), s8[4194304]{0:T(1024)(128)(4,1)S(1)}, s32[]{:S(2)}) async-start(s8[8388608]{0:T(1024)(128)(4,1)} %bitcast.4), calls=%async_computation.4 | async-start | bytes 8388608
  5.6 5.6 %collective-permute-start.1 = (bf16[32,640]{1,0:T(8,128)(2,1)S(1)}, bf16[32,640]{1,0:T(8,128)(2,1)S(1)}, u32[]{:S(2)}, u32[]{:S(2)}) collective-permute-start(bf16[32,640]{1,0:T(8,128)(2,1)S(1)} %get-tuple-element.26), channel_id=1, source_target_pairs={{0,8},{8,0},{16,24},{24,16},{1,9},{9,1},{17,25},{25,17},{2,10},{10... | collective-permute-start | bytes 122888 | tf_op jit(solution)/shard_map/ppermute | solution.py:275
  8.6 5.7 %collective-permute-start.2 = (bf16[32,640]{1,0:T(8,128)(2,1)S(1)}, bf16[32,640]{1,0:T(8,128)(2,1)S(1)}, u32[]{:S(2)}, u32[]{:S(2)}) collective-permute-start(bf16[32,640]{1,0:T(8,128)(2,1)S(1)} %get-tuple-element.27), channel_id=1, source_target_pairs={{0,16},{8,24},{16,0},{24,8},{1,17},{9,25},{17,1},{25,9},{2,18},{10... | collective-permute-start | bytes 122888 | tf_op jit(solution)/shard_map/ppermute | solution.py:275
  11.2 5.8 %collective-permute-start.3 = (bf16[32,640]{1,0:T(8,128)(2,1)S(1)}, bf16[32,640]{1,0:T(8,128)(2,1)S(1)}, u32[]{:S(2)}, u32[]{:S(2)}) collective-permute-start(bf16[32,640]{1,0:T(8,128)(2,1)S(1)} %get-tuple-element.28), channel_id=1, source_target_pairs={{0,24},{8,16},{16,8},{24,0},{1,25},{9,17},{17,9},{25,1},{2,26},{10... | collective-permute-start | bytes 122888 | tf_op jit(solution)/shard_map/ppermute | solution.py:275
  17.3 4.2 %collective-permute-start.6 = (bf16[16,640]{1,0:T(8,128)(2,1)S(1)}, bf16[16,640]{1,0:T(8,128)(2,1)S(1)}, u32[]{:S(2)}, u32[]{:S(2)}) collective-permute-start(bf16[16,640]{1,0:T(8,128)(2,1)S(1)} %get-tuple-element.30), channel_id=1, source_target_pairs={{0,4},{2,6},{4,0},{6,2},{1,5},{3,7},{5,1},{7,3},{8,12},{10,14},{12... | collective-permute-start | bytes 61448 | tf_op jit(solution)/shard_map/ppermute | solution.py:275
  18.8 4.7 %collective-permute-start.5 = (bf16[16,640]{1,0:T(8,128)(2,1)S(1)}, bf16[16,640]{1,0:T(8,128)(2,1)S(1)}, u32[]{:S(2)}, u32[]{:S(2)}) collective-permute-start(bf16[16,640]{1,0:T(8,128)(2,1)S(1)} %get-tuple-element.30), channel_id=1, source_target_pairs={{0,6},{2,4},{4,2},{6,0},{1,7},{3,5},{5,3},{7,1},{8,14},{10,12},{12... | collective-permute-start | bytes 61448 | tf_op jit(solution)/shard_map/ppermute | solution.py:275
  20.3 3.8 %collective-permute-start.4 = (bf16[16,640]{1,0:T(8,128)(2,1)S(1)}, bf16[16,640]{1,0:T(8,128)(2,1)S(1)}, u32[]{:S(2)}, u32[]{:S(2)}) collective-permute-start(bf16[16,640]{1,0:T(8,128)(2,1)S(1)} %get-tuple-element.29.after.refs_0_), channel_id=1, source_target_pairs={{0,2},{2,0},{4,6},{6,4},{1,3},{3,1},{5,7},{7,5},{8,10},{10,8},{12,... | collective-permute-start | bytes 61448 | tf_op jit(solution)/shard_map/ppermute | solution.py:275
  24.3 1.2 %collective-permute-start.7 = (bf16[16,512]{1,0:T(8,128)(2,1)S(1)}, bf16[16,512]{1,0:T(8,128)(2,1)S(1)}, u32[]{:S(2)}, u32[]{:S(2)}) collective-permute-start(bf16[16,512]{1,0:T(8,128)(2,1)S(1)} %finish.1.slot_in), channel_id=1, source_target_pairs={{0,1},{1,0},{2,3},{3,2},{4,5},{5,4},{6,7},{7,6},{8,9},{9,8},{10,11... | collective-permute-start | bytes 49160 | tf_op jit(solution)/shard_map/ppermute | solution.py:275
  26.8 1.2 %collective-permute-start.8 = (bf16[16,512]{1,0:T(8,128)(2,1)S(1)}, bf16[16,512]{1,0:T(8,128)(2,1)S(1)}, u32[]{:S(2)}, u32[]{:S(2)}) collective-permute-start(bf16[16,512]{1,0:T(8,128)(2,1)S(1)} %get-tuple-element.32.after), channel_id=1, source_target_pairs={{0,1},{1,0},{2,3},{3,2},{4,5},{5,4},{6,7},{7,6},{8,9},{9,8},{10,11... | collective-permute-start | bytes 49160 | tf_op jit(solution)/shard_map/ppermute | solution.py:275
  28.0 3.7 %collective-permute-start.9 = (bf16[16,512]{1,0:T(8,128)(2,1)S(1)}, bf16[16,512]{1,0:T(8,128)(2,1)S(1)}, u32[]{:S(2)}, u32[]{:S(2)}) collective-permute-start(bf16[16,512]{1,0:T(8,128)(2,1)S(1)} %fusion), channel_id=1, source_target_pairs={{0,2},{2,0},{1,3},{3,1},{4,6},{6,4},{5,7},{7,5},{8,10},{10,8},{9,1... | collective-permute-start | bytes 49160 | tf_op jit(solution)/shard_map/ppermute | solution.py:275
  41.8 1.3 %collective-permute-start.10 = (bf16[128,512]{1,0:T(8,128)(2,1)S(1)}, bf16[128,512]{1,0:T(8,128)(2,1)S(1)}, u32[]{:S(2)}, u32[]{:S(2)}) collective-permute-start(bf16[128,512]{1,0:T(8,128)(2,1)S(1)} %bitcast.6), channel_id=1, source_target_pairs={{0,1},{1,0},{2,3},{3,2},{4,5},{5,4},{6,7},{7,6},{8,9},{9,8},{10,11... | collective-permute-start | bytes 393224 | tf_op jit(solution)/shard_map/ppermute | solution.py:275

commit v24 on v22

--- a/solution.py
+++ b/solution.py
@@ -322,7 +322,8 @@
         compiler_params=params(16),
         name="pair",
     )(place, keep, side, received)
-    parts = [sends[0]] + [move(sends[r], ("far",), (r,)) for r in range(1, far)]
+    order = [0] + list(range(2, far)) + [1]
+    parts = [sends[0]] + [move(sends[r], ("far",), (r,)) for r in order[1:]]
     send, their = pl.pallas_call(
         functools.partial(merge_kernel, rest),
         out_shape=(jax.ShapeDtypeStruct((rows, half + SIDE), BF16),) * 2,

time: 44.5 us -> 44.4 us (level)
  waiting for transfers between devices: 9.92 us -> 8.35 us
  blocking collectives: 13.1 us -> 14.5 us
    ppermute x10, waiting for transfers between devices: 9.92 us -> 8.35 us  [move(): return lax.ppermute(value, axes, moves)]
    all_to_all x1, blocking collectives: 13.1 us -> 14.5 us  [shards(): lax.all_to_all(partials, ('rest', 'far', 'near'), split_axis=0, concat_ax...]
where the time goes in v24:
time: 44.4 us; the launch traced here: 44.2 us
  blocking collectives  14.5 us (33%)
  Pallas kernels  11.1 us (25%)
  starting transfers between devices  9.96 us (22%)
  waiting for transfers between devices  8.35 us (19%)
    all_to_all x1, blocking collectives, shards(): lax.all_to_all(partials, ('rest', 'far', 'near'), split_axis=0, concat_ax...  14.5 us
    ppermute x10, starting transfers between devices, move(): return lax.ppermute(value, axes, moves)  9.96 us
    ppermute x10, waiting for transfers between devices, move(): return lax.ppermute(value, axes, moves)  8.35 us
    pallas_call x1, Pallas kernels, shards(): pl.pallas_call(gather_kernel, out_shape=(jax.ShapeDtypeStruct((count, slo...  3.65 us
    pallas_call x1, Pallas kernels, shards(): pl.pallas_call(mix_other_kernel, out_shape=jax.ShapeDtypeStruct((count, m...  1.74 us
    pallas_call x1, Pallas kernels, shards(): pl.pallas_call(mix_kernel, out_shape=(pltpu.HBM((count, model), BF16), ja...  1.21 us
    pallas_call x1, Pallas kernels, shards(): pl.pallas_call(expert_kernel, out_shape=(jax.ShapeDtypeStruct((experts, r...  1.21 us
  transfers between devices with their start and end apart: 10, of which 8 were waited for; matrix products, arithmetic and copies ran while one was open for 0% of the time, Pallas kernels for 8%

profile of v24, /device:TPU:0, one launch (start us, length us, event | category | flops | bytes accessed | tf_op | source)
XLA Modules:
  0.0 44.2 jit_solution(1577432015129788969)
XLA Ops:
  0.0 3.7 %gather.1 = (f32[2048,128]{1,0:T(8,128)S(1)}, bf16[128,2048]{1,0:T(8,128)(2,1)S(1)}, bf16[2048,1024]{1,0:T(8,128)(2,1)S(1)}, f32[128,128]{1,0:T(8,128)S(1)}, bf16[128,640]{1,0:T(8,128)(2,1)S(1)}) custom-call(s32[1]{0:T(128)} %bitcast.place, bf16[2048,1024]{1,0:T(8,128)(2,1)} %tokens.1, bf16[1024,128]{1,0:T(8,128)(2,1)} %slot_params.1), custom_call_target="tpu_custom_call" | custom-call | tf_op jit(solution)/shard_map/gather/pallas_call | solution.py:291
  3.7 0.5 %collective-permute-start = (bf16[128,640]{1,0:T(8,128)(2,1)S(1)}, bf16[128,640]{1,0:T(8,128)(2,1)S(1)}, u32[]{:S(2)}, u32[]{:S(2)}) collective-permute-start(bf16[128,640]{1,0:T(8,128)(2,1)S(1)} %get-tuple-element.24.after), channel_id=1, source_target_pairs={{0,1},{1,0},{2,3},{3,2},{4,5},{5,4},{6,7},{7,6},{8,9},{9,8},{10,11... | collective-permute-start | bytes 491528 | tf_op jit(solution)/shard_map/ppermute | solution.py:275
  4.2 0.5 %own_sums.1.keep = f32[128,512]{1,0:T(8,128)S(1)} custom-call(s32[1]{0:T(128)} %bitcast.place, bf16[128,2048]{1,0:T(8,128)(2,1)S(1)} %get-tuple-element.21.turned, bf16[2048,1024]{1,0:T(8,128)(2,1)S(1)} %get-tuple-element.22.held, f32[128,128]{1,0:T(8,128)S(1)} %get-tuple-element.23.side, bf16[128,640]{1,0:T(8,128)(2,1)S(1)} %get-tuple-element.24.after), custom_call_target="tpu_custom_call" | custom-call | flops 268435456 | bytes 2621440 | tf_op jit(solution)/shard_map/own_sums/pallas_call | solution.py:307
  4.6 0.0 slice-start.1
  4.6 0.0 slice-start.3
  4.7 0.5 %collective-permute-done.received = bf16[128,640]{1,0:T(8,128)(2,1)S(1)} collective-permute-done((bf16[128,640]{1,0:T(8,128)(2,1)S(1)}, bf16[128,640]{1,0:T(8,128)(2,1)S(1)}, u32[]{:S(2)}, u32[]{:S(2)}) %collective-permute-start) | collective-permute-done | bytes 163872 | tf_op jit(solution)/shard_map/ppermute | solution.py:275
  5.2 0.4 pair.1
  5.6 4.0 %collective-permute-start.1 = (bf16[32,640]{1,0:T(8,128)(2,1)S(1)}, bf16[32,640]{1,0:T(8,128)(2,1)S(1)}, u32[]{:S(2)}, u32[]{:S(2)}) collective-permute-start(bf16[32,640]{1,0:T(8,128)(2,1)S(1)} %get-tuple-element.26), channel_id=1, source_target_pairs={{0,16},{8,24},{16,0},{24,8},{1,17},{9,25},{17,1},{25,9},{2,18},{10... | collective-permute-start | bytes 122888 | tf_op jit(solution)/shard_map/ppermute | solution.py:275
  9.6 1.4 %collective-permute-start.2 = (bf16[32,640]{1,0:T(8,128)(2,1)S(1)}, bf16[32,640]{1,0:T(8,128)(2,1)S(1)}, u32[]{:S(2)}, u32[]{:S(2)}) collective-permute-start(bf16[32,640]{1,0:T(8,128)(2,1)S(1)} %get-tuple-element.27), channel_id=1, source_target_pairs={{0,24},{8,16},{16,8},{24,0},{1,25},{9,17},{17,9},{25,1},{2,26},{10... | collective-permute-start | bytes 122888 | tf_op jit(solution)/shard_map/ppermute | solution.py:275
  11.0 0.2 collective-permute-start.3
  11.2 0.4 collective-permute-done.1.refs_1_
  11.6 3.8 %collective-permute-done.2.refs_2_ = bf16[32,640]{1,0:T(8,128)(2,1)S(1)} collective-permute-done((bf16[32,640]{1,0:T(8,128)(2,1)S(1)}, bf16[32,640]{1,0:T(8,128)(2,1)S(1)}, u32[]{:S(2)}, u32[]{:S(2)}) %collective-permute-start.2) | collective-permute-done | bytes 40992 | tf_op jit(solution)/shard_map/ppermute | solution.py:275
  15.4 0.3 merge.1
  15.7 1.6 %collective-permute-start.6 = (bf16[16,640]{1,0:T(8,128)(2,1)S(1)}, bf16[16,640]{1,0:T(8,128)(2,1)S(1)}, u32[]{:S(2)}, u32[]{:S(2)}) collective-permute-start(bf16[16,640]{1,0:T(8,128)(2,1)S(1)} %get-tuple-element.30), channel_id=1, source_target_pairs={{0,4},{2,6},{4,0},{6,2},{1,5},{3,7},{5,1},{7,3},{8,12},{10,14},{12... | collective-permute-start | bytes 61448 | tf_op jit(solution)/shard_map/ppermute | solution.py:275
  17.2 1.5 %collective-permute-start.5 = (bf16[16,640]{1,0:T(8,128)(2,1)S(1)}, bf16[16,640]{1,0:T(8,128)(2,1)S(1)}, u32[]{:S(2)}, u32[]{:S(2)}) collective-permute-start(bf16[16,640]{1,0:T(8,128)(2,1)S(1)} %get-tuple-element.30), channel_id=1, source_target_pairs={{0,6},{2,4},{4,2},{6,0},{1,7},{3,5},{5,3},{7,1},{8,14},{10,12},{12... | collective-permute-start | bytes 61448 | tf_op jit(solution)/shard_map/ppermute | solution.py:275
  18.7 0.5 %collective-permute-start.4 = (bf16[16,640]{1,0:T(8,128)(2,1)S(1)}, bf16[16,640]{1,0:T(8,128)(2,1)S(1)}, u32[]{:S(2)}, u32[]{:S(2)}) collective-permute-start(bf16[16,640]{1,0:T(8,128)(2,1)S(1)} %get-tuple-element.29.after.refs_0_), channel_id=1, source_target_pairs={{0,2},{2,0},{4,6},{6,4},{1,3},{3,1},{5,7},{7,5},{8,10},{10,8},{12,... | collective-permute-start | bytes 61448 | tf_op jit(solution)/shard_map/ppermute | solution.py:275
  19.2 0.6 %combine.1 = bf16[2048,128]{1,0:T(8,128)(2,1)S(1)} custom-call(f32[2048,128]{1,0:T(8,128)S(1)} %get-tuple-element.20.logits, bf16[16,640]{1,0:T(8,128)(2,1)S(1)} %get-tuple-element.29.after.refs_0_), custom_call_target="tpu_custom_call" | custom-call | flops 2097152 | bytes 1572864 | tf_op jit(solution)/shard_map/combine/pallas_call | solution.py:338
  19.9 2.0 %collective-permute-done.5.refs_2_ = bf16[16,640]{1,0:T(8,128)(2,1)S(1)} collective-permute-done((bf16[16,640]{1,0:T(8,128)(2,1)S(1)}, bf16[16,640]{1,0:T(8,128)(2,1)S(1)}, u32[]{:S(2)}, u32[]{:S(2)}) %collective-permute-start.5) | collective-permute-done | bytes 20512 | tf_op jit(solution)/shard_map/ppermute | solution.py:275
  21.9 0.6 %collective-permute-done.4.refs_1_ = bf16[16,640]{1,0:T(8,128)(2,1)S(1)} collective-permute-done((bf16[16,640]{1,0:T(8,128)(2,1)S(1)}, bf16[16,640]{1,0:T(8,128)(2,1)S(1)}, u32[]{:S(2)}, u32[]{:S(2)}) %collective-permute-start.4) | collective-permute-done | bytes 20512 | tf_op jit(solution)/shard_map/ppermute | solution.py:275
  22.5 0.2 finish.1.slot_in
  22.8 0.1 collective-permute-start.7
  22.9 0.7 %first_product.1.first = f32[4,16,1024]{2,1,0:T(8,128)S(1)} custom-call(s32[1]{0:T(128)} %bitcast.place, bf16[16,512]{1,0:T(8,128)(2,1)S(1)} %finish.1.slot_in, bf16[4,1024,1024]{2,1,0:T(8,128)(2,1)S(1)} %bitcast.4), custom_call_target="tpu_custom_call" | custom-call | flops 67108864 | bytes 4194304 | tf_op jit(solution)/shard_map/first_product/pallas_call | solution.py:357
  23.5 0.5 %collective-permute-done.7.slot_in = bf16[16,512]{1,0:T(8,128)(2,1)S(1)} collective-permute-done((bf16[16,512]{1,0:T(8,128)(2,1)S(1)}, bf16[16,512]{1,0:T(8,128)(2,1)S(1)}, u32[]{:S(2)}, u32[]{:S(2)}) %collective-permute-start.7) | collective-permute-done | bytes 16416 | tf_op jit(solution)/shard_map/ppermute | solution.py:275
  24.0 1.2 %experts.1 = (bf16[4,16,1024]{2,1,0:T(8,128)(2,1)S(1)}, bf16[16,512]{1,0:T(8,128)(2,1)S(1)}) custom-call(s32[1]{0:T(128)} %bitcast.place, bf16[16,512]{1,0:T(8,128)(2,1)S(1)} %collective-permute-done.7.slot_in, f32[4,16,1024]{2,1,0:T(8,128)S(1)} %first_product.1.first, bf16[4,1024,1024]{2,1,0:T(8,128)(2,1)S(1)} %bitcast.4, bf16[4,1024,1024]{2,1,0:T(8,128)(2,1)S(1)} %bitcast.6), custom_call_target="tpu_custom_call" | custom-call | tf_op jit(solution)/shard_map/experts/pallas_call | solution.py:366
  25.2 0.2 collective-permute-start.8
  25.4 0.7 %own.1 = f32[16,512]{1,0:T(8,128)S(1)} custom-call(s32[1]{0:T(128)} %bitcast.place, bf16[4,16,1024]{2,1,0:T(8,128)(2,1)S(1)} %get-tuple-element.31.hidden, bf16[4,1024,1024]{2,1,0:T(8,128)(2,1)S(1)} %bitcast.6, bf16[16,512]{1,0:T(8,128)(2,1)S(1)} %get-tuple-element.32.after), custom_call_target="tpu_custom_call" | custom-call | flops 67108864 | bytes 4194304 | tf_op jit(solution)/shard_map/own/pallas_call | solution.py:378
  26.0 0.4 collective-permute-done.8
  26.4 14.5 %all_to_all.5 = bf16[16,16,512]{2,1,0:T(8,128)(2,1)S(1)} all-to-all(bf16[16,16,512]{2,1,0:T(8,128)(2,1)S(1)} %broadcast_in_dim.3), channel_id=1, replica_groups=mesh['far'=4,'near'=2,'rest'=2,'pair'=2] {'rest','far','near'}, dimensions={0} | all-to-all | bytes 524288 | tf_op jit(solution)/shard_map/all_to_all | solution.py:390
  41.0 0.1 collective-permute-start.9
  41.1 1.2 %mix.1 = (bf16[2048,1024]{1,0:T(8,128)(2,1)}, bf16[1024,512]{1,0:T(8,128)(2,1)S(1)}) custom-call(s32[1]{0:T(128)} %bitcast.place, bf16[2048,128]{1,0:T(8,128)(2,1)S(1)} %combine.1, bf16[128,512]{1,0:T(8,128)(2,1)S(1)} %bitcast.8), custom_call_target="tpu_custom_call" | custom-call | flops 268435456 | bytes 2621440 | tf_op jit(solution)/shard_map/mix/pallas_call | solution.py:395
  42.3 0.1 collective-permute-done.9.slot_out
  42.5 1.7 %mix_other.1 = bf16[2048,1024]{1,0:T(8,128)(2,1)} custom-call(s32[1]{0:T(128)} %bitcast.place, bf16[2048,128]{1,0:T(8,128)(2,1)S(1)} %combine.1, bf16[128,512]{1,0:T(8,128)(2,1)S(1)} %collective-permute-done.9.slot_out, bf16[1024,512]{1,0:T(8,128)(2,1)S(1)} %get-tuple-element.33.rest, ...), custom_call_target="tpu_custom_call", output_to_operand_aliasing={{}: (4, {})} | custom-call | flops 268435456 | bytes 2621440 | tf_op jit(solution)/shard_map/mix_other/pallas_call | solution.py:408
  (13 shorter events, 0.1 us)
Async XLA Ops:
  3.7 1.5 %collective-permute-start = (bf16[128,640]{1,0:T(8,128)(2,1)S(1)}, bf16[128,640]{1,0:T(8,128)(2,1)S(1)}, u32[]{:S(2)}, u32[]{:S(2)}) collective-permute-start(bf16[128,640]{1,0:T(8,128)(2,1)S(1)} %get-tuple-element.24.after), channel_id=1, source_target_pairs={{0,1},{1,0},{2,3},{3,2},{4,5},{5,4},{6,7},{7,6},{8,9},{9,8},{10,11... | collective-permute-start | bytes 491528 | tf_op jit(solution)/shard_map/ppermute | solution.py:275
  4.2 18.7 %slice-start = ((s8[8388608]{0:T(1024)(128)(4,1)}), s8[4194304]{0:T(1024)(128)(4,1)S(1)}, s32[]{:S(2)}) async-start(s8[8388608]{0:T(1024)(128)(4,1)} %bitcast.3), calls=%async_computation.1 | async-start | bytes 8388608
  4.2 19.8 %slice-start.2 = ((s8[8388608]{0:T(1024)(128)(4,1)}), s8[4194304]{0:T(1024)(128)(4,1)S(1)}, s32[]{:S(2)}) async-start(s8[8388608]{0:T(1024)(128)(4,1)} %bitcast.5), calls=%async_computation.3 | async-start | bytes 8388608
  4.6 18.2 %slice-start.1 = ((s8[8388608]{0:T(1024)(128)(4,1)}), s8[4194304]{0:T(1024)(128)(4,1)S(1)}, s32[]{:S(2)}) async-start(s8[8388608]{0:T(1024)(128)(4,1)} %bitcast.3), calls=%async_computation.2 | async-start | bytes 8388608
  4.6 19.4 %slice-start.3 = ((s8[8388608]{0:T(1024)(128)(4,1)}), s8[4194304]{0:T(1024)(128)(4,1)S(1)}, s32[]{:S(2)}) async-start(s8[8388608]{0:T(1024)(128)(4,1)} %bitcast.5), calls=%async_computation.4 | async-start | bytes 8388608
  5.6 6.0 %collective-permute-start.1 = (bf16[32,640]{1,0:T(8,128)(2,1)S(1)}, bf16[32,640]{1,0:T(8,128)(2,1)S(1)}, u32[]{:S(2)}, u32[]{:S(2)}) collective-permute-start(bf16[32,640]{1,0:T(8,128)(2,1)S(1)} %get-tuple-element.26), channel_id=1, source_target_pairs={{0,16},{8,24},{16,0},{24,8},{1,17},{9,25},{17,1},{25,9},{2,18},{10... | collective-permute-start | bytes 122888 | tf_op jit(solution)/shard_map/ppermute | solution.py:275
  9.6 5.8 %collective-permute-start.2 = (bf16[32,640]{1,0:T(8,128)(2,1)S(1)}, bf16[32,640]{1,0:T(8,128)(2,1)S(1)}, u32[]{:S(2)}, u32[]{:S(2)}) collective-permute-start(bf16[32,640]{1,0:T(8,128)(2,1)S(1)} %get-tuple-element.27), channel_id=1, source_target_pairs={{0,24},{8,16},{16,8},{24,0},{1,25},{9,17},{17,9},{25,1},{2,26},{10... | collective-permute-start | bytes 122888 | tf_op jit(solution)/shard_map/ppermute | solution.py:275
  11.0 4.5 %collective-permute-start.3 = (bf16[32,640]{1,0:T(8,128)(2,1)S(1)}, bf16[32,640]{1,0:T(8,128)(2,1)S(1)}, u32[]{:S(2)}, u32[]{:S(2)}) collective-permute-start(bf16[32,640]{1,0:T(8,128)(2,1)S(1)} %get-tuple-element.28), channel_id=1, source_target_pairs={{0,8},{8,0},{16,24},{24,16},{1,9},{9,1},{17,25},{25,17},{2,10},{10... | collective-permute-start | bytes 122888 | tf_op jit(solution)/shard_map/ppermute | solution.py:275
  15.7 4.2 %collective-permute-start.6 = (bf16[16,640]{1,0:T(8,128)(2,1)S(1)}, bf16[16,640]{1,0:T(8,128)(2,1)S(1)}, u32[]{:S(2)}, u32[]{:S(2)}) collective-permute-start(bf16[16,640]{1,0:T(8,128)(2,1)S(1)} %get-tuple-element.30), channel_id=1, source_target_pairs={{0,4},{2,6},{4,0},{6,2},{1,5},{3,7},{5,1},{7,3},{8,12},{10,14},{12... | collective-permute-start | bytes 61448 | tf_op jit(solution)/shard_map/ppermute | solution.py:275
  17.2 4.7 %collective-permute-start.5 = (bf16[16,640]{1,0:T(8,128)(2,1)S(1)}, bf16[16,640]{1,0:T(8,128)(2,1)S(1)}, u32[]{:S(2)}, u32[]{:S(2)}) collective-permute-start(bf16[16,640]{1,0:T(8,128)(2,1)S(1)} %get-tuple-element.30), channel_id=1, source_target_pairs={{0,6},{2,4},{4,2},{6,0},{1,7},{3,5},{5,3},{7,1},{8,14},{10,12},{12... | collective-permute-start | bytes 61448 | tf_op jit(solution)/shard_map/ppermute | solution.py:275
  18.7 3.8 %collective-permute-start.4 = (bf16[16,640]{1,0:T(8,128)(2,1)S(1)}, bf16[16,640]{1,0:T(8,128)(2,1)S(1)}, u32[]{:S(2)}, u32[]{:S(2)}) collective-permute-start(bf16[16,640]{1,0:T(8,128)(2,1)S(1)} %get-tuple-element.29.after.refs_0_), channel_id=1, source_target_pairs={{0,2},{2,0},{4,6},{6,4},{1,3},{3,1},{5,7},{7,5},{8,10},{10,8},{12,... | collective-permute-start | bytes 61448 | tf_op jit(solution)/shard_map/ppermute | solution.py:275
  22.8 1.2 %collective-permute-start.7 = (bf16[16,512]{1,0:T(8,128)(2,1)S(1)}, bf16[16,512]{1,0:T(8,128)(2,1)S(1)}, u32[]{:S(2)}, u32[]{:S(2)}) collective-permute-start(bf16[16,512]{1,0:T(8,128)(2,1)S(1)} %finish.1.slot_in), channel_id=1, source_target_pairs={{0,1},{1,0},{2,3},{3,2},{4,5},{5,4},{6,7},{7,6},{8,9},{9,8},{10,11... | collective-permute-start | bytes 49160 | tf_op jit(solution)/shard_map/ppermute | solution.py:275
  25.2 1.2 %collective-permute-start.8 = (bf16[16,512]{1,0:T(8,128)(2,1)S(1)}, bf16[16,512]{1,0:T(8,128)(2,1)S(1)}, u32[]{:S(2)}, u32[]{:S(2)}) collective-permute-start(bf16[16,512]{1,0:T(8,128)(2,1)S(1)} %get-tuple-element.32.after), channel_id=1, source_target_pairs={{0,1},{1,0},{2,3},{3,2},{4,5},{5,4},{6,7},{7,6},{8,9},{9,8},{10,11... | collective-permute-start | bytes 49160 | tf_op jit(solution)/shard_map/ppermute | solution.py:275
  41.0 1.4 %collective-permute-start.9 = (bf16[128,512]{1,0:T(8,128)(2,1)S(1)}, bf16[128,512]{1,0:T(8,128)(2,1)S(1)}, u32[]{:S(2)}, u32[]{:S(2)}) collective-permute-start(bf16[128,512]{1,0:T(8,128)(2,1)S(1)} %bitcast.7), channel_id=1, source_target_pairs={{0,1},{1,0},{2,3},{3,2},{4,5},{5,4},{6,7},{7,6},{8,9},{9,8},{10,11... | collective-permute-start | bytes 393224 | tf_op jit(solution)/shard_map/ppermute | solution.py:275

commit v25 on v24

--- a/solution.py
+++ b/solution.py
@@ -322,7 +322,7 @@
         compiler_params=params(16),
         name="pair",
     )(place, keep, side, received)
-    order = [0] + list(range(2, far)) + [1]
+    order = [0] + list(range(far - 1, 0, -1))
     parts = [sends[0]] + [move(sends[r], ("far",), (r,)) for r in order[1:]]
     send, their = pl.pallas_call(
         functools.partial(merge_kernel, rest),

time: 44.4 us -> 44.3 us (level)
  no operation moved by 1% of the time
where the time goes in v25:
time: 44.3 us; the launch traced here: 44.1 us
  blocking collectives  14.3 us (32%)
  Pallas kernels  11.1 us (25%)
  starting transfers between devices  10 us (23%)
  waiting for transfers between devices  8.39 us (19%)
    all_to_all x1, blocking collectives, shards(): lax.all_to_all(partials, ('rest', 'far', 'near'), split_axis=0, concat_ax...  14.3 us
    ppermute x10, starting transfers between devices, move(): return lax.ppermute(value, axes, moves)  10 us
    ppermute x10, waiting for transfers between devices, move(): return lax.ppermute(value, axes, moves)  8.39 us
    pallas_call x1, Pallas kernels, shards(): pl.pallas_call(gather_kernel, out_shape=(jax.ShapeDtypeStruct((count, slo...  3.65 us
    pallas_call x1, Pallas kernels, shards(): pl.pallas_call(mix_other_kernel, out_shape=jax.ShapeDtypeStruct((count, m...  1.74 us
    pallas_call x1, Pallas kernels, shards(): pl.pallas_call(expert_kernel, out_shape=(jax.ShapeDtypeStruct((experts, r...  1.21 us
    pallas_call x1, Pallas kernels, shards(): pl.pallas_call(mix_kernel, out_shape=(pltpu.HBM((count, model), BF16), ja...  1.21 us
  transfers between devices with their start and end apart: 10, of which 8 were waited for; matrix products, arithmetic and copies ran while one was open for 0% of the time, Pallas kernels for 8%

profile of v25, /device:TPU:0, one launch (start us, length us, event | category | flops | bytes accessed | tf_op | source)
XLA Modules:
  0.0 44.1 jit_solution(5598567956589484835)
XLA Ops:
  0.0 3.7 %gather.1 = (f32[2048,128]{1,0:T(8,128)S(1)}, bf16[128,2048]{1,0:T(8,128)(2,1)S(1)}, bf16[2048,1024]{1,0:T(8,128)(2,1)S(1)}, f32[128,128]{1,0:T(8,128)S(1)}, bf16[128,640]{1,0:T(8,128)(2,1)S(1)}) custom-call(s32[1]{0:T(128)} %bitcast.place, bf16[2048,1024]{1,0:T(8,128)(2,1)} %tokens.1, bf16[1024,128]{1,0:T(8,128)(2,1)} %slot_params.1), custom_call_target="tpu_custom_call" | custom-call | tf_op jit(solution)/shard_map/gather/pallas_call | solution.py:291
  3.7 0.5 %collective-permute-start = (bf16[128,640]{1,0:T(8,128)(2,1)S(1)}, bf16[128,640]{1,0:T(8,128)(2,1)S(1)}, u32[]{:S(2)}, u32[]{:S(2)}) collective-permute-start(bf16[128,640]{1,0:T(8,128)(2,1)S(1)} %get-tuple-element.24.after), channel_id=1, source_target_pairs={{0,1},{1,0},{2,3},{3,2},{4,5},{5,4},{6,7},{7,6},{8,9},{9,8},{10,11... | collective-permute-start | bytes 491528 | tf_op jit(solution)/shard_map/ppermute | solution.py:275
  4.2 0.5 %own_sums.1.keep = f32[128,512]{1,0:T(8,128)S(1)} custom-call(s32[1]{0:T(128)} %bitcast.place, bf16[128,2048]{1,0:T(8,128)(2,1)S(1)} %get-tuple-element.21.turned, bf16[2048,1024]{1,0:T(8,128)(2,1)S(1)} %get-tuple-element.22.held, f32[128,128]{1,0:T(8,128)S(1)} %get-tuple-element.23.side, bf16[128,640]{1,0:T(8,128)(2,1)S(1)} %get-tuple-element.24.after), custom_call_target="tpu_custom_call" | custom-call | flops 268435456 | bytes 2621440 | tf_op jit(solution)/shard_map/own_sums/pallas_call | solution.py:307
  4.6 0.0 slice-start.1
  4.6 0.0 slice-start.3
  4.7 0.5 %collective-permute-done.received = bf16[128,640]{1,0:T(8,128)(2,1)S(1)} collective-permute-done((bf16[128,640]{1,0:T(8,128)(2,1)S(1)}, bf16[128,640]{1,0:T(8,128)(2,1)S(1)}, u32[]{:S(2)}, u32[]{:S(2)}) %collective-permute-start) | collective-permute-done | bytes 163872 | tf_op jit(solution)/shard_map/ppermute | solution.py:275
  5.2 0.4 pair.1
  5.6 5.0 %collective-permute-start.1 = (bf16[32,640]{1,0:T(8,128)(2,1)S(1)}, bf16[32,640]{1,0:T(8,128)(2,1)S(1)}, u32[]{:S(2)}, u32[]{:S(2)}) collective-permute-start(bf16[32,640]{1,0:T(8,128)(2,1)S(1)} %get-tuple-element.26), channel_id=1, source_target_pairs={{0,24},{8,16},{16,8},{24,0},{1,25},{9,17},{17,9},{25,1},{2,26},{10... | collective-permute-start | bytes 122888 | tf_op jit(solution)/shard_map/ppermute | solution.py:275
  10.6 0.0 collective-permute-start.2
  10.6 0.6 %collective-permute-start.3 = (bf16[32,640]{1,0:T(8,128)(2,1)S(1)}, bf16[32,640]{1,0:T(8,128)(2,1)S(1)}, u32[]{:S(2)}, u32[]{:S(2)}) collective-permute-start(bf16[32,640]{1,0:T(8,128)(2,1)S(1)} %get-tuple-element.28), channel_id=1, source_target_pairs={{0,8},{8,0},{16,24},{24,16},{1,9},{9,1},{17,25},{25,17},{2,10},{10... | collective-permute-start | bytes 122888 | tf_op jit(solution)/shard_map/ppermute | solution.py:275
  11.3 1.4 %collective-permute-done.1.refs_1_ = bf16[32,640]{1,0:T(8,128)(2,1)S(1)} collective-permute-done((bf16[32,640]{1,0:T(8,128)(2,1)S(1)}, bf16[32,640]{1,0:T(8,128)(2,1)S(1)}, u32[]{:S(2)}, u32[]{:S(2)}) %collective-permute-start.1) | collective-permute-done | bytes 40992 | tf_op jit(solution)/shard_map/ppermute | solution.py:275
  12.7 2.9 %collective-permute-done.2.refs_2_ = bf16[32,640]{1,0:T(8,128)(2,1)S(1)} collective-permute-done((bf16[32,640]{1,0:T(8,128)(2,1)S(1)}, bf16[32,640]{1,0:T(8,128)(2,1)S(1)}, u32[]{:S(2)}, u32[]{:S(2)}) %collective-permute-start.2) | collective-permute-done | bytes 40992 | tf_op jit(solution)/shard_map/ppermute | solution.py:275
  15.5 0.3 merge.1
  15.8 1.6 %collective-permute-start.6 = (bf16[16,640]{1,0:T(8,128)(2,1)S(1)}, bf16[16,640]{1,0:T(8,128)(2,1)S(1)}, u32[]{:S(2)}, u32[]{:S(2)}) collective-permute-start(bf16[16,640]{1,0:T(8,128)(2,1)S(1)} %get-tuple-element.30), channel_id=1, source_target_pairs={{0,4},{2,6},{4,0},{6,2},{1,5},{3,7},{5,1},{7,3},{8,12},{10,14},{12... | collective-permute-start | bytes 61448 | tf_op jit(solution)/shard_map/ppermute | solution.py:275
  17.4 1.5 %collective-permute-start.5 = (bf16[16,640]{1,0:T(8,128)(2,1)S(1)}, bf16[16,640]{1,0:T(8,128)(2,1)S(1)}, u32[]{:S(2)}, u32[]{:S(2)}) collective-permute-start(bf16[16,640]{1,0:T(8,128)(2,1)S(1)} %get-tuple-element.30), channel_id=1, source_target_pairs={{0,6},{2,4},{4,2},{6,0},{1,7},{3,5},{5,3},{7,1},{8,14},{10,12},{12... | collective-permute-start | bytes 61448 | tf_op jit(solution)/shard_map/ppermute | solution.py:275
  18.8 0.5 %collective-permute-start.4 = (bf16[16,640]{1,0:T(8,128)(2,1)S(1)}, bf16[16,640]{1,0:T(8,128)(2,1)S(1)}, u32[]{:S(2)}, u32[]{:S(2)}) collective-permute-start(bf16[16,640]{1,0:T(8,128)(2,1)S(1)} %get-tuple-element.29.after.refs_0_), channel_id=1, source_target_pairs={{0,2},{2,0},{4,6},{6,4},{1,3},{3,1},{5,7},{7,5},{8,10},{10,8},{12,... | collective-permute-start | bytes 61448 | tf_op jit(solution)/shard_map/ppermute | solution.py:275
  19.4 0.6 %combine.1 = bf16[2048,128]{1,0:T(8,128)(2,1)S(1)} custom-call(f32[2048,128]{1,0:T(8,128)S(1)} %get-tuple-element.20.logits, bf16[16,640]{1,0:T(8,128)(2,1)S(1)} %get-tuple-element.29.after.refs_0_), custom_call_target="tpu_custom_call" | custom-call | flops 2097152 | bytes 1572864 | tf_op jit(solution)/shard_map/combine/pallas_call | solution.py:338
  20.0 2.0 %collective-permute-done.5.refs_2_ = bf16[16,640]{1,0:T(8,128)(2,1)S(1)} collective-permute-done((bf16[16,640]{1,0:T(8,128)(2,1)S(1)}, bf16[16,640]{1,0:T(8,128)(2,1)S(1)}, u32[]{:S(2)}, u32[]{:S(2)}) %collective-permute-start.5) | collective-permute-done | bytes 20512 | tf_op jit(solution)/shard_map/ppermute | solution.py:275
  22.0 0.6 %collective-permute-done.4.refs_1_ = bf16[16,640]{1,0:T(8,128)(2,1)S(1)} collective-permute-done((bf16[16,640]{1,0:T(8,128)(2,1)S(1)}, bf16[16,640]{1,0:T(8,128)(2,1)S(1)}, u32[]{:S(2)}, u32[]{:S(2)}) %collective-permute-start.4) | collective-permute-done | bytes 20512 | tf_op jit(solution)/shard_map/ppermute | solution.py:275
  22.6 0.2 finish.1.slot_in
  22.9 0.1 collective-permute-start.7
  23.0 0.7 %first_product.1.first = f32[4,16,1024]{2,1,0:T(8,128)S(1)} custom-call(s32[1]{0:T(128)} %bitcast.place, bf16[16,512]{1,0:T(8,128)(2,1)S(1)} %finish.1.slot_in, bf16[4,1024,1024]{2,1,0:T(8,128)(2,1)S(1)} %bitcast.4), custom_call_target="tpu_custom_call" | custom-call | flops 67108864 | bytes 4194304 | tf_op jit(solution)/shard_map/first_product/pallas_call | solution.py:357
  23.6 0.5 %collective-permute-done.7.slot_in = bf16[16,512]{1,0:T(8,128)(2,1)S(1)} collective-permute-done((bf16[16,512]{1,0:T(8,128)(2,1)S(1)}, bf16[16,512]{1,0:T(8,128)(2,1)S(1)}, u32[]{:S(2)}, u32[]{:S(2)}) %collective-permute-start.7) | collective-permute-done | bytes 16416 | tf_op jit(solution)/shard_map/ppermute | solution.py:275
  24.1 1.2 %experts.1 = (bf16[4,16,1024]{2,1,0:T(8,128)(2,1)S(1)}, bf16[16,512]{1,0:T(8,128)(2,1)S(1)}) custom-call(s32[1]{0:T(128)} %bitcast.place, bf16[16,512]{1,0:T(8,128)(2,1)S(1)} %collective-permute-done.7.slot_in, f32[4,16,1024]{2,1,0:T(8,128)S(1)} %first_product.1.first, bf16[4,1024,1024]{2,1,0:T(8,128)(2,1)S(1)} %bitcast.4, bf16[4,1024,1024]{2,1,0:T(8,128)(2,1)S(1)} %bitcast.6), custom_call_target="tpu_custom_call" | custom-call | tf_op jit(solution)/shard_map/experts/pallas_call | solution.py:366
  25.3 0.2 collective-permute-start.8
  25.5 0.7 %own.1 = f32[16,512]{1,0:T(8,128)S(1)} custom-call(s32[1]{0:T(128)} %bitcast.place, bf16[4,16,1024]{2,1,0:T(8,128)(2,1)S(1)} %get-tuple-element.31.hidden, bf16[4,1024,1024]{2,1,0:T(8,128)(2,1)S(1)} %bitcast.6, bf16[16,512]{1,0:T(8,128)(2,1)S(1)} %get-tuple-element.32.after), custom_call_target="tpu_custom_call" | custom-call | flops 67108864 | bytes 4194304 | tf_op jit(solution)/shard_map/own/pallas_call | solution.py:378
  26.1 0.4 collective-permute-done.8
  26.6 14.3 %all_to_all.5 = bf16[16,16,512]{2,1,0:T(8,128)(2,1)S(1)} all-to-all(bf16[16,16,512]{2,1,0:T(8,128)(2,1)S(1)} %broadcast_in_dim.3), channel_id=1, replica_groups=mesh['far'=4,'near'=2,'rest'=2,'pair'=2] {'rest','far','near'}, dimensions={0} | all-to-all | bytes 524288 | tf_op jit(solution)/shard_map/all_to_all | solution.py:390
  40.9 0.1 collective-permute-start.9
  41.0 1.2 %mix.1 = (bf16[2048,1024]{1,0:T(8,128)(2,1)}, bf16[1024,512]{1,0:T(8,128)(2,1)S(1)}) custom-call(s32[1]{0:T(128)} %bitcast.place, bf16[2048,128]{1,0:T(8,128)(2,1)S(1)} %combine.1, bf16[128,512]{1,0:T(8,128)(2,1)S(1)} %bitcast.8), custom_call_target="tpu_custom_call" | custom-call | flops 268435456 | bytes 2621440 | tf_op jit(solution)/shard_map/mix/pallas_call | solution.py:395
  42.2 0.1 collective-permute-done.9.slot_out
  42.3 1.7 %mix_other.1 = bf16[2048,1024]{1,0:T(8,128)(2,1)} custom-call(s32[1]{0:T(128)} %bitcast.place, bf16[2048,128]{1,0:T(8,128)(2,1)S(1)} %combine.1, bf16[128,512]{1,0:T(8,128)(2,1)S(1)} %collective-permute-done.9.slot_out, bf16[1024,512]{1,0:T(8,128)(2,1)S(1)} %get-tuple-element.33.rest, ...), custom_call_target="tpu_custom_call", output_to_operand_aliasing={{}: (4, {})} | custom-call | flops 268435456 | bytes 2621440 | tf_op jit(solution)/shard_map/mix_other/pallas_call | solution.py:408
  (13 shorter events, 0.1 us)
Async XLA Ops:
  3.7 1.5 %collective-permute-start = (bf16[128,640]{1,0:T(8,128)(2,1)S(1)}, bf16[128,640]{1,0:T(8,128)(2,1)S(1)}, u32[]{:S(2)}, u32[]{:S(2)}) collective-permute-start(bf16[128,640]{1,0:T(8,128)(2,1)S(1)} %get-tuple-element.24.after), channel_id=1, source_target_pairs={{0,1},{1,0},{2,3},{3,2},{4,5},{5,4},{6,7},{7,6},{8,9},{9,8},{10,11... | collective-permute-start | bytes 491528 | tf_op jit(solution)/shard_map/ppermute | solution.py:275
  4.2 18.8 %slice-start = ((s8[8388608]{0:T(1024)(128)(4,1)}), s8[4194304]{0:T(1024)(128)(4,1)S(1)}, s32[]{:S(2)}) async-start(s8[8388608]{0:T(1024)(128)(4,1)} %bitcast.3), calls=%async_computation.1 | async-start | bytes 8388608
  4.2 19.9 %slice-start.2 = ((s8[8388608]{0:T(1024)(128)(4,1)}), s8[4194304]{0:T(1024)(128)(4,1)S(1)}, s32[]{:S(2)}) async-start(s8[8388608]{0:T(1024)(128)(4,1)} %bitcast.5), calls=%async_computation.3 | async-start | bytes 8388608
  4.6 18.3 %slice-start.1 = ((s8[8388608]{0:T(1024)(128)(4,1)}), s8[4194304]{0:T(1024)(128)(4,1)S(1)}, s32[]{:S(2)}) async-start(s8[8388608]{0:T(1024)(128)(4,1)} %bitcast.3), calls=%async_computation.2 | async-start | bytes 8388608
  4.6 19.5 %slice-start.3 = ((s8[8388608]{0:T(1024)(128)(4,1)}), s8[4194304]{0:T(1024)(128)(4,1)S(1)}, s32[]{:S(2)}) async-start(s8[8388608]{0:T(1024)(128)(4,1)} %bitcast.5), calls=%async_computation.4 | async-start | bytes 8388608
  5.6 7.1 %collective-permute-start.1 = (bf16[32,640]{1,0:T(8,128)(2,1)S(1)}, bf16[32,640]{1,0:T(8,128)(2,1)S(1)}, u32[]{:S(2)}, u32[]{:S(2)}) collective-permute-start(bf16[32,640]{1,0:T(8,128)(2,1)S(1)} %get-tuple-element.26), channel_id=1, source_target_pairs={{0,24},{8,16},{16,8},{24,0},{1,25},{9,17},{17,9},{25,1},{2,26},{10... | collective-permute-start | bytes 122888 | tf_op jit(solution)/shard_map/ppermute | solution.py:275
  10.6 4.9 %collective-permute-start.2 = (bf16[32,640]{1,0:T(8,128)(2,1)S(1)}, bf16[32,640]{1,0:T(8,128)(2,1)S(1)}, u32[]{:S(2)}, u32[]{:S(2)}) collective-permute-start(bf16[32,640]{1,0:T(8,128)(2,1)S(1)} %get-tuple-element.27), channel_id=1, source_target_pairs={{0,16},{8,24},{16,0},{24,8},{1,17},{9,25},{17,1},{25,9},{2,18},{10... | collective-permute-start | bytes 122888 | tf_op jit(solution)/shard_map/ppermute | solution.py:275
  10.6 4.9 %collective-permute-start.3 = (bf16[32,640]{1,0:T(8,128)(2,1)S(1)}, bf16[32,640]{1,0:T(8,128)(2,1)S(1)}, u32[]{:S(2)}, u32[]{:S(2)}) collective-permute-start(bf16[32,640]{1,0:T(8,128)(2,1)S(1)} %get-tuple-element.28), channel_id=1, source_target_pairs={{0,8},{8,0},{16,24},{24,16},{1,9},{9,1},{17,25},{25,17},{2,10},{10... | collective-permute-start | bytes 122888 | tf_op jit(solution)/shard_map/ppermute | solution.py:275
  15.8 4.2 %collective-permute-start.6 = (bf16[16,640]{1,0:T(8,128)(2,1)S(1)}, bf16[16,640]{1,0:T(8,128)(2,1)S(1)}, u32[]{:S(2)}, u32[]{:S(2)}) collective-permute-start(bf16[16,640]{1,0:T(8,128)(2,1)S(1)} %get-tuple-element.30), channel_id=1, source_target_pairs={{0,4},{2,6},{4,0},{6,2},{1,5},{3,7},{5,1},{7,3},{8,12},{10,14},{12... | collective-permute-start | bytes 61448 | tf_op jit(solution)/shard_map/ppermute | solution.py:275
  17.4 4.7 %collective-permute-start.5 = (bf16[16,640]{1,0:T(8,128)(2,1)S(1)}, bf16[16,640]{1,0:T(8,128)(2,1)S(1)}, u32[]{:S(2)}, u32[]{:S(2)}) collective-permute-start(bf16[16,640]{1,0:T(8,128)(2,1)S(1)} %get-tuple-element.30), channel_id=1, source_target_pairs={{0,6},{2,4},{4,2},{6,0},{1,7},{3,5},{5,3},{7,1},{8,14},{10,12},{12... | collective-permute-start | bytes 61448 | tf_op jit(solution)/shard_map/ppermute | solution.py:275
  18.8 3.8 %collective-permute-start.4 = (bf16[16,640]{1,0:T(8,128)(2,1)S(1)}, bf16[16,640]{1,0:T(8,128)(2,1)S(1)}, u32[]{:S(2)}, u32[]{:S(2)}) collective-permute-start(bf16[16,640]{1,0:T(8,128)(2,1)S(1)} %get-tuple-element.29.after.refs_0_), channel_id=1, source_target_pairs={{0,2},{2,0},{4,6},{6,4},{1,3},{3,1},{5,7},{7,5},{8,10},{10,8},{12,... | collective-permute-start | bytes 61448 | tf_op jit(solution)/shard_map/ppermute | solution.py:275
  22.9 1.2 %collective-permute-start.7 = (bf16[16,512]{1,0:T(8,128)(2,1)S(1)}, bf16[16,512]{1,0:T(8,128)(2,1)S(1)}, u32[]{:S(2)}, u32[]{:S(2)}) collective-permute-start(bf16[16,512]{1,0:T(8,128)(2,1)S(1)} %finish.1.slot_in), channel_id=1, source_target_pairs={{0,1},{1,0},{2,3},{3,2},{4,5},{5,4},{6,7},{7,6},{8,9},{9,8},{10,11... | collective-permute-start | bytes 49160 | tf_op jit(solution)/shard_map/ppermute | solution.py:275
  25.3 1.2 %collective-permute-start.8 = (bf16[16,512]{1,0:T(8,128)(2,1)S(1)}, bf16[16,512]{1,0:T(8,128)(2,1)S(1)}, u32[]{:S(2)}, u32[]{:S(2)}) collective-permute-start(bf16[16,512]{1,0:T(8,128)(2,1)S(1)} %get-tuple-element.32.after), channel_id=1, source_target_pairs={{0,1},{1,0},{2,3},{3,2},{4,5},{5,4},{6,7},{7,6},{8,9},{9,8},{10,11... | collective-permute-start | bytes 49160 | tf_op jit(solution)/shard_map/ppermute | solution.py:275
  40.9 1.4 %collective-permute-start.9 = (bf16[128,512]{1,0:T(8,128)(2,1)S(1)}, bf16[128,512]{1,0:T(8,128)(2,1)S(1)}, u32[]{:S(2)}, u32[]{:S(2)}) collective-permute-start(bf16[128,512]{1,0:T(8,128)(2,1)S(1)} %bitcast.7), channel_id=1, source_target_pairs={{0,1},{1,0},{2,3},{3,2},{4,5},{5,4},{6,7},{7,6},{8,9},{9,8},{10,11... | collective-permute-start | bytes 393224 | tf_op jit(solution)/shard_map/ppermute | solution.py:275
